TPU v7x, 32 devices: a whole 2x2x4 slice. The times are simulated.
32 devices in a mesh: row: 8 (over z, core), col: 2 (over y), feat: 2 (over x).
Axes of the slice: x: 2, y: 2, z: 4, core: 2. Of those that a mesh axis runs over, the one named last changes fastest.
Arguments:
- features: bfloat16 [8192, 256], P(('col', 'row'), 'feat'), may hold values from -6 to 6
- tile_rows: int32 [8, 2, 256], P('row', 'col'), may hold values from 0 to 7, as said below
- tile_cols: int32 [8, 2, 256], P('row', 'col'), may hold values from 0 to 31
- tile_count: int32 [8, 2], P('row', 'col'), may hold values from 64 to 256, as said below
- tile_values: bfloat16 [8, 2, 256, 128, 128], P('row', 'col'), may hold values from -0.21875 to 0.21875
- weights: bfloat16 [256, 256], replicated, may hold values from -0.375 to 0.375
- cotangent: bfloat16 [8192, 256], P(('row', 'col'), 'feat'), may hold values from -6 to 6
Outputs:
- activated: bfloat16 [8192, 256], P(('row', 'col'), 'feat')
- feature_grad: bfloat16 [8192, 256], P(('col', 'row'), 'feat')
- weight_grad: float32 [256, 256], P('feat')
Inputs may be any that keep to these rules, and one draw needn't show every extreme that they name: `tile_rows`: block rows of a cell, unevenly loaded. `tile_count`: some cell has all 256 slots live.
All inputs are finite; a program needn't handle non-finite values.
Results may differ from a plain program's by a relative error of at most 0.027.
Values may be sent and summed in bfloat16 or wider, within the bound.
No kernel may reach another device: no remote copies, remote signals or barrier semaphores. Data moves between devices by JAX's collectives and lax.ppermute only.
A program may use at most 128 MiB of HBM per device.

v0:
```python
import jax
import jax.numpy as jnp
from jax import lax
from jax.sharding import PartitionSpec as P


def shards(features, tile_rows, tile_cols, tile_count, tile_values, weights, cotangent):
    width = tile_values.shape[-1]
    slots = tile_values.shape[2]
    local_tiles = tile_values[0, 0]
    block_rows = tile_rows[0, 0]
    block_cols = tile_cols[0, 0]
    live_mask = (jnp.arange(slots) < tile_count[0, 0]).astype(jnp.float32)
    n_rowdev = lax.axis_size("row")
    n_coldev = lax.axis_size("col")
    local_blocks = features.shape[0] // width
    feat_half = features.shape[1]
    feat_index = lax.axis_index("feat")
    row_blocks = local_blocks * n_coldev
    col_blocks = local_blocks * n_rowdev
    node_total = features.shape[0] * n_rowdev * n_coldev
    panel = lax.all_gather(features, "row", axis=0, tiled=True)
    gathered = panel.reshape(col_blocks, width, feat_half)[block_cols]
    products = jnp.einsum("tij,tjf->tif", local_tiles, gathered, preferred_element_type=jnp.float32)
    products = products * live_mask[:, None, None]
    partial_value = (
        jnp.zeros((row_blocks, width, feat_half), jnp.float32).at[block_rows].add(products)
    )
    summed = lax.psum_scatter(
        partial_value.reshape(row_blocks * width, feat_half).astype(jnp.bfloat16),
        "col",
        scatter_dimension=0,
        tiled=True,
    )
    weight_rows = lax.dynamic_slice_in_dim(weights, feat_index * feat_half, feat_half, 0)
    mix_term = jnp.dot(summed, weight_rows, preferred_element_type=jnp.float32)
    hidden = lax.psum_scatter(
        mix_term.astype(jnp.bfloat16), "feat", scatter_dimension=1, tiled=True
    ).astype(jnp.float32)
    negative = jnp.minimum(hidden, 0.0)
    activated = jnp.where(hidden > 0, hidden, jnp.expm1(negative)).astype(jnp.bfloat16)
    slope_factor = jnp.where(hidden > 0, 1.0, jnp.exp(negative))
    grad_out = (cotangent.astype(jnp.float32) * slope_factor).astype(jnp.bfloat16)
    grad_whole = lax.all_gather(grad_out, "feat", axis=1, tiled=True)
    weight_term = lax.dot_general(
        summed, grad_whole, (((0,), (0,)), ((), ())), preferred_element_type=jnp.float32
    )
    weight_grad = lax.psum(weight_term, ("row", "col")) * node_total ** (-0.5)
    spread = lax.dot_general(
        grad_whole, weight_rows, (((1,), (1,)), ((), ())), preferred_element_type=jnp.float32
    ).astype(jnp.bfloat16)
    spread_panel = lax.all_gather(spread, "col", axis=0, tiled=True)
    spread_blocks = spread_panel.reshape(row_blocks, width, feat_half)[block_rows]
    back_products = jnp.einsum(
        "tji,tjf->tif", local_tiles, spread_blocks, preferred_element_type=jnp.float32
    )
    back_products = back_products * live_mask[:, None, None]
    back_partial = (
        jnp.zeros((col_blocks, width, feat_half), jnp.float32).at[block_cols].add(back_products)
    )
    back_summed = lax.psum_scatter(
        back_partial.reshape(col_blocks * width, feat_half).astype(jnp.bfloat16),
        "row",
        scatter_dimension=0,
        tiled=True,
    )
    return (activated, back_summed, weight_grad)


def solution(mesh):
    return jax.shard_map(
        shards,
        mesh=mesh,
        in_specs=(
            P(("col", "row"), "feat"),
            P("row", "col", None),
            P("row", "col", None),
            P("row", "col"),
            P("row", "col", None, None, None),
            P(),
            P(("row", "col"), "feat"),
        ),
        out_specs=(P(("row", "col"), "feat"), P(("col", "row"), "feat"), P("feat", None)),
        check_vma=False,
    )
```

profile of v0, /device:TPU:0, one launch (start us, length us, event | category | flops | bytes accessed | tf_op | source)
XLA Modules:
  0.0 279.7 jit_solution(13035599672791697739)
XLA Ops:
  7.2 0.0 copy-start
  7.2 0.0 all-gather.2.cloned.1.call-start
  7.2 0.7 all-gather.2.cloned.1.call-update
  7.9 0.0 reduce-scatter.6.cloned.1.call-start
  8.6 0.7 compare_select_fusion
  9.3 0.7 compare_select_fusion.1
  10.0 24.5 %all-gather.2.cloned.1.call-done = bf16[4096,128]{1,0:T(8,128)(2,1)} async-done(((bf16[512,128]{1,0:T(8,128)(2,1)}), bf16[4096,128]{1,0:T(8,128)(2,1)}) %all-gather.2.cloned.1.call-update) | async-done | bytes 1048592 | tf_op jit(solution)/shard_map/all_gather | solution.py:22
  34.4 9.8 %gather_fusion = bf16[256,128,128]{2,1,0:T(8,128)(2,1)} fusion(bf16[32,128,128]{2,1,0:T(8,128)(2,1)} %bitcast.30, s32[1024]{0:T(1024)S(1)} %pad_clamp_fusion.1), kind=kCustom, calls=%fused_computation | custom fusion | bytes 16778240 | tf_op jit(solution)/shard_map/gather | solution.py:23
  44.3 13.0 %multiply_bitcast_fusion.1 = f32[256,128,128]{1,2,0:T(8,128)} fusion(bf16[256,128,128]{2,1,0:T(8,128)(2,1)} %gather_fusion, bf16[1,1,256,128,128]{4,3,2,1,0:T(8,128)(2,1)} %param.11, f32[256]{0:T(256)S(1)} %compare_convert_fusion), kind=kOutput, calls=%fused_computation.5 | convolution fusion | flops 1077936128 | bytes 33555456 | tf_op jit(solution)/shard_map/tij,tjf->tif/dot_general | solution.py:24
  57.3 17.5 %copy.17 = f32[256,128,128]{2,1,0:T(8,128)} copy(f32[256,128,128]{1,2,0:T(8,128)} %multiply_bitcast_fusion.1) | data formatting | bytes 33554432 | tf_op jit(solution)/shard_map/mul | solution.py:25
  74.8 0.0 copy-start.2
  74.8 33.1 %scatter_fusion = f32[8,128,128]{2,1,0:T(8,128)S(1)} fusion(f32[8,128,128]{2,1,0:T(8,128)S(1)} %broadcast_in_dim.8, s32[256]{0:T(256)S(1)} %bitcast.37, f32[256,128,128]{2,1,0:T(8,128)} %copy.17), kind=kCustom, calls=%fused_computation.2 | custom fusion | flops 4194304 | bytes 50332672 | tf_op jit(solution)/shard_map/scatter-add | solution.py:27
  107.9 0.7 convert_element_type.38
  108.7 0.0 reduce-scatter.6.cloned.1.call-update
  108.7 0.0 reduce-scatter.10.cloned.1.call-start
  108.7 11.4 %reduce-scatter.6.cloned.1.call-done = bf16[512,128]{1,0:T(8,128)(2,1)} async-done(((bf16[1024,128]{1,0:T(8,128)(2,1)}), bf16[512,128]{1,0:T(8,128)(2,1)}) %reduce-scatter.6.cloned.1.call-update) | async-done | bytes 131088 | tf_op jit(solution)/shard_map/reduce_scatter | solution.py:29
  120.1 0.0 copy-done
  120.1 1.1 convolution_convert_fusion
  121.2 0.8 copy.22
  122.1 0.0 reduce-scatter.10.cloned.1.call-update
  122.1 0.0 all-reduce.2.cloned.1.call-start
  122.2 12.0 %reduce-scatter.10.cloned.1.call-done = bf16[128,512]{1,0:T(8,128)(2,1)} async-done(((bf16[256,512]{1,0:T(8,128)(2,1)}), bf16[128,512]{1,0:T(8,128)(2,1)}) %reduce-scatter.10.cloned.1.call-update) | async-done | bytes 131088
  134.2 1.0 copy.23
  135.2 0.0 copy-done.2
  135.2 0.8 fusion.6
  136.0 5.9 %all_gather.10 = bf16[512,256]{1,0:T(8,128)(2,1)S(1)} all-gather(bf16[512,128]{1,0:T(8,128)(2,1)S(1)} %get-tuple-element.3), channel_id=1, replica_groups=mesh['row'=8,'col'=2,'feat'=2] {'feat'}, dimensions={1}, use_global_device_ids=true | all-gather | bytes 393216 | tf_op jit(solution)/shard_map/all_gather | solution.py:44
  141.9 0.2 convolution_convert_fusion.1
  142.2 5.6 %all_gather.11 = bf16[1024,128]{1,0:T(8,128)(2,1)S(1)} all-gather(bf16[512,128]{1,0:T(8,128)(2,1)S(1)} %convolution_convert_fusion.1), channel_id=1, replica_groups=mesh['row'=8,'col'=2,'feat'=2] {'col'}, dimensions={0}, use_global_device_ids=true | all-gather | bytes 393216 | tf_op jit(solution)/shard_map/all_gather | solution.py:52
  147.8 1.8 fusion.12
  149.6 0.0 all-reduce.2.cloned.1.call-update
  149.6 0.2 reduce-scatter.8.cloned.1.call-start
  149.8 8.6 %gather_fusion.1 = bf16[256,128,128]{2,1,0:T(8,128)(2,1)} fusion(bf16[8,128,128]{2,1,0:T(8,128)(2,1)S(1)} %bitcast.29, s32[1024]{0:T(1024)S(1)} %pad_clamp_fusion), kind=kCustom, calls=%fused_computation.1 | custom fusion | bytes 16778240 | tf_op jit(solution)/shard_map/gather | solution.py:53
  158.4 15.4 %multiply_bitcast_fusion = f32[256,128,128]{1,2,0:T(8,128)} fusion(bf16[256,128,128]{2,1,0:T(8,128)(2,1)} %gather_fusion.1, bf16[1,1,256,128,128]{4,3,2,1,0:T(8,128)(2,1)} %param.11, f32[256]{0:T(256)S(1)} %compare_convert_fusion), kind=kOutput, calls=%fused_computation.4 | convolution fusion | flops 1077936128 | bytes 33555456 | tf_op jit(solution)/shard_map/tji,tjf->tif/dot_general | solution.py:54
  173.8 17.5 %copy.19 = f32[256,128,128]{2,1,0:T(8,128)} copy(f32[256,128,128]{1,2,0:T(8,128)} %multiply_bitcast_fusion) | data formatting | bytes 33554432 | tf_op jit(solution)/shard_map/mul | solution.py:57
  191.3 0.2 broadcast_in_dim.9
  191.6 0.0 copy-start.1
  191.6 33.2 %scatter_fusion.1 = f32[32,128,128]{2,1,0:T(8,128)S(1)} fusion(f32[32,128,128]{2,1,0:T(8,128)S(1)} %broadcast_in_dim.9, s32[256]{0:T(256)S(1)} %bitcast.36, f32[256,128,128]{2,1,0:T(8,128)} %copy.19), kind=kCustom, calls=%fused_computation.3 | custom fusion | flops 4194304 | bytes 50332672 | tf_op jit(solution)/shard_map/scatter-add | solution.py:59
  224.8 1.1 convert_element_type.46
  226.0 0.0 reduce-scatter.8.cloned.1.call-update
  226.0 10.7 %all-reduce.2.cloned.1.call-done = f32[128,256]{1,0:T(8,128)} async-done(((f32[128,256]{1,0:T(8,128)}), f32[128,256]{1,0:T(8,128)}) %all-reduce.2.cloned.1.call-update) | async-done | bytes 131088 | tf_op jit(solution)/shard_map/psum | solution.py:48
  236.7 1.6 broadcast_multiply_fusion
  238.3 34.9 %reduce-scatter.8.cloned.1.call-done = bf16[512,128]{1,0:T(8,128)(2,1)} async-done(((bf16[4096,128]{1,0:T(8,128)(2,1)}), bf16[512,128]{1,0:T(8,128)(2,1)}) %reduce-scatter.8.cloned.1.call-update) | async-done | bytes 131088 | tf_op jit(solution)/shard_map/reduce_scatter | solution.py:61
  273.2 0.0 copy-done.1
  (4 shorter events, 0.1 us)
Async XLA Ops:
  7.2 113.0 %copy-start = (bf16[256,256]{1,0:T(8,128)(2,1)S(1)}, bf16[256,256]{1,0:T(8,128)(2,1)}, u32[]{:S(2)}) copy-start(bf16[256,256]{1,0:T(8,128)(2,1)} %param.12) | copy-start | bytes 393220
  7.2 27.3 %all-gather.2.cloned.1.call-start = ((), (), s32[]{:S(2)}) async-start(), calls=%async_computation.3 | async-start | bytes 1179648 | tf_op jit(solution)/shard_map/all_gather | solution.py:22
  7.9 112.2 %reduce-scatter.6.cloned.1.call-start = ((), (), s32[]{:S(2)}) async-start(), calls=%async_computation.4 | async-start | bytes 393216 | tf_op jit(solution)/shard_map/reduce_scatter | solution.py:29
  74.8 60.4 %copy-start.2 = (bf16[512,128]{1,0:T(8,128)(2,1)S(1)}, bf16[512,128]{1,0:T(8,128)(2,1)}, u32[]{:S(2)}) copy-start(bf16[512,128]{1,0:T(8,128)(2,1)} %param.13) | copy-start | bytes 393220
  108.7 25.5 %reduce-scatter.10.cloned.1.call-start = ((), (), s32[]{:S(2)}) async-start(), calls=%async_computation.7 | async-start | bytes 393216
  122.1 114.6 %all-reduce.2.cloned.1.call-start = ((), (), s32[]{:S(2)}) async-start(), calls=%async_computation.6 | async-start | bytes 262144 | tf_op jit(solution)/shard_map/psum | solution.py:48
  149.6 123.6 %reduce-scatter.8.cloned.1.call-start = ((), (), s32[]{:S(2)}) async-start(), calls=%async_computation.5 | async-start | bytes 1179648 | tf_op jit(solution)/shard_map/reduce_scatter | solution.py:61
  191.6 81.6 %copy-start.1 = (bf16[256,256]{1,0:T(8,128)(2,1)S(1)}, bf16[256,256]{1,0:T(8,128)(2,1)}, u32[]{:S(2)}) copy-start(bf16[256,256]{1,0:T(8,128)(2,1)} %param.12) | copy-start | bytes 393220
Sparse Core Ops, SparseCore 0:
  9.6 24.7 all-gather.1
  108.8 11.2 reduce-scatter.5
  122.4 11.6 reduce-scatter.9
  149.7 86.9 all-reduce.1
  239.4 33.7 reduce-scatter.7
where the time goes:
time: 282 us; the launch traced here: 280 us
  waiting for transfers between devices  94.2 us (33%)
  other arithmetic  72 us (26%)
  local copies, waits for them, and re-layouts  55.5 us (20%)
  matrix products  31.6 us (11%)
  between operations  14.5 us (5%)
  blocking collectives  11.6 us (4%)
    reduce_scatter x1, waiting for transfers between devices, shards(): lax.psum_scatter(back_partial.reshape(col_blocks * width, feat_half).asty...  34.9 us
    scatter-add x1, other arithmetic, shards(): jnp.zeros((col_blocks, width, feat_half), jnp.float32).at[block_cols]  33.2 us
    scatter-add x1, other arithmetic, shards(): jnp.zeros((row_blocks, width, feat_half), jnp.float32).at[block_rows]  33.1 us
    all_gather x1, waiting for transfers between devices, shards(): panel = lax.all_gather(features, 'row', axis=0, tiled=True)  24.5 us
    mul x1, local copies, waits for them, and re-layouts, shards(): back_products = back_products * live_mask[:, None, None]  17.5 us
    mul x1, local copies, waits for them, and re-layouts, shards(): products = products * live_mask[:, None, None]  17.5 us
    dot_general x1, matrix products, shards(): jnp.einsum('tji,tjf->tif', local_tiles, spread_blocks, preferred_element_...  15.4 us
    dot_general x1, matrix products, shards(): jnp.einsum('tij,tjf->tif', local_tiles, gathered, preferred_element_type=...  13 us
  transfers between devices with their start and end apart: 5, of which 5 were waited for; matrix products, arithmetic and copies ran while one was open for 28% of the time, Pallas kernels for 0%

commit v1 on v0

v1 whole, which is shorter than its diff:
```python
import functools

import jax
import jax.numpy as jnp
from jax import lax
from jax.experimental import pallas as pl
from jax.experimental.pallas import tpu as pltpu
from jax.sharding import PartitionSpec as P

F32 = jnp.float32
BF16 = jnp.bfloat16
VMEM_LIMIT = 48 * 1024 * 1024


def params(*semantics):
    return pltpu.CompilerParams(vmem_limit_bytes=VMEM_LIMIT)


def vmem():
    return pl.BlockSpec(memory_space=pltpu.VMEM)


def smem():
    return pl.BlockSpec(memory_space=pltpu.SMEM)


def densify_kernel(
    dims, info, rows, cols, count, tiles, out, buffer, head, following, sems
):
    n_z, n_col, blocks, slots, groups = dims
    chunk = pl.program_id(0)
    per_chunk = n_col * blocks * blocks
    per_group = slots // groups

    def copy(g):
        part = pl.ds(g * per_group, per_group)
        return pltpu.make_async_copy(tiles.at[part], buffer.at[part], sems.at[g])

    @pl.when(chunk == 0)
    def _():
        for g in range(groups):
            copy(g).start()
        z, core, c = info[0], info[1], info[2]

        def clear(i, carry):
            head[i] = slots
            return carry

        lax.fori_loop(0, 2 * n_z * per_chunk, clear, 0, unroll=8)
        following[slots] = slots
        buffer[slots] = jnp.zeros(buffer.shape[1:], buffer.dtype)

        def link(slot, carry):
            block_row, block_col = rows[0, 0, slot], cols[0, 0, slot]
            source, owner = block_col // blocks, block_row // blocks
            shift = z - source // 2
            shift = jnp.where(shift < 0, shift + n_z, shift)
            j = 2 * shift + ((source + core) & 1)
            t = c - owner
            t = jnp.where(t < 0, t + n_col, t)
            place = ((j * n_col + t) * blocks + block_row % blocks) * blocks + block_col % blocks
            following[slot] = head[place]
            head[place] = slot
            return carry

        lax.fori_loop(0, count[0, 0], link, 0)
        for g in range(groups):
            copy(g).wait()

    tile = buffer.shape[1]

    def fill(i, carry):
        first = head[chunk * per_chunk + i]
        t = i // (blocks * blocks)
        a = pl.multiple_of((i // blocks) % blocks * tile, tile)
        b = pl.multiple_of(i % blocks * tile, tile)
        where = (0, t, pl.ds(a, tile), pl.ds(b, tile))
        out[where] = buffer[first]
        second = following[first]

        @pl.when(second != slots)
        def _():
            def more(state):
                slot, total = state
                return following[slot], total + buffer[slot].astype(F32)

            _, total = lax.while_loop(
                lambda state: state[0] != slots,
                more,
                (second, buffer[first].astype(F32)),
            )
            out[where] = total.astype(BF16)

        return carry

    lax.fori_loop(0, per_chunk, fill, 0)


def densify(info, rows, cols, count, tiles, n_z, n_col, blocks):
    slots, tile = tiles.shape[0], tiles.shape[1]
    n_src = 2 * n_z
    groups = 8
    side = blocks * tile
    shape = (n_src, n_col, side, side)
    return pl.pallas_call(
        functools.partial(densify_kernel, (n_z, n_col, blocks, slots, groups)),
        grid=(n_src,),
        out_shape=jax.ShapeDtypeStruct(shape, BF16),
        in_specs=[smem(), smem(), smem(), smem(), pl.BlockSpec(memory_space=pl.ANY)],
        out_specs=pl.BlockSpec((1, n_col, side, side), lambda j: (j, 0, 0, 0)),
        scratch_shapes=[
            pltpu.VMEM((slots + 1, tile, tile), BF16),
            pltpu.SMEM((n_src * n_col * blocks * blocks,), jnp.int32),
            pltpu.SMEM((slots + 1,), jnp.int32),
            pltpu.SemaphoreType.DMA((groups,)),
        ],
        compiler_params=params(),
        cost_estimate=pl.CostEstimate(
            flops=0, bytes_accessed=24 * 1024 * 1024, transcendentals=0
        ),
        name="densify",
    )(info, rows, cols, count, tiles)


def forward_kernel(first, a, x0, x1, *rest):

    j = pl.program_id(1)

    @pl.when(j == 0)
    def _():
        value = jnp.dot(a[0, 0], x0[...], preferred_element_type=F32)
        if not first:
            value = value + rest[0][...]
        rest[-1][...] = value

    @pl.when(j == 1)
    def _():
        rest[-1][...] += jnp.dot(a[0, 0], x1[...], preferred_element_type=F32)


def forward(dense, shift, x0, x1, total):
    _, n_col, side, _ = dense.shape
    feats = x0.shape[1]
    first = total is None
    block = pl.BlockSpec((side, feats), lambda t, j: (t, 0))
    return pl.pallas_call(
        functools.partial(forward_kernel, first),
        grid=(n_col, 2),
        out_shape=jax.ShapeDtypeStruct((n_col * side, feats), F32),
        in_specs=[
            pl.BlockSpec((1, 1, side, side), lambda t, j: (2 * shift + j, t, 0, 0)),
            vmem(),
            vmem(),
        ]
        + ([] if first else [block]),
        out_specs=block,
        compiler_params=params(),
        cost_estimate=pl.CostEstimate(
            flops=4 * n_col * side * side * feats,
            bytes_accessed=4 * n_col * side * side,
            transcendentals=0,
        ),
        name="forward",
    )(dense, x0, x1, *([] if first else [total]))


def middle_kernel(n_col, info, weights, cot_own, cot_other, *refs):
    own = refs[:n_col]
    other = refs[n_col : 2 * n_col]
    activated, spread, keep, send = refs[2 * n_col :]
    half = cot_own.shape[1]
    core, f = info[1], info[3]
    mine = pl.ds(pl.multiple_of(f * half, half), half)
    theirs = pl.ds(pl.multiple_of((1 - f) * half, half), half)

    def gather(parts):
        total = parts[0][...].astype(F32)
        for part in parts[1:]:
            total = total + part[...].astype(F32)
        return total.astype(BF16)

    agg_own, agg_other = gather(own), gather(other)

    def hidden(columns):
        return jnp.dot(
            agg_own, weights[mine, columns], preferred_element_type=F32
        ) + jnp.dot(agg_other, weights[theirs, columns], preferred_element_type=F32)

    h = hidden(mine)
    decay = jnp.exp(jnp.minimum(h, 0.0))
    activated[...] = jnp.where(h > 0, h, decay - 1.0).astype(BF16)
    g_own = (cot_own[...].astype(F32) * decay).astype(BF16)
    h = hidden(theirs)
    decay = jnp.exp(jnp.minimum(h, 0.0))
    g_other = (cot_other[...].astype(F32) * decay).astype(BF16)
    across = (((1,), (1,)), ((), ()))
    spread[...] = (
        lax.dot_general(g_own, weights[mine, mine], across, preferred_element_type=F32)
        + lax.dot_general(g_other, weights[mine, theirs], across, preferred_element_type=F32)
    ).astype(BF16)
    down = (((0,), (0,)), ((), ()))
    rows = half // 2
    for columns, g in ((mine, g_own), (theirs, g_other)):
        term = lax.dot_general(agg_own, g, down, preferred_element_type=F32).astype(BF16)

        @pl.when(core == 0)
        def _():
            keep[:, columns] = term[:rows]
            send[:, columns] = term[rows:]

        @pl.when(core == 1)
        def _():
            keep[:, columns] = term[rows:]
            send[:, columns] = term[:rows]


def middle(info, weights, cot_own, cot_other, own, other):
    nodes, half = cot_own.shape
    whole = weights.shape[1]
    n_col = len(own)
    return pl.pallas_call(
        functools.partial(middle_kernel, n_col),
        out_shape=(
            jax.ShapeDtypeStruct((nodes, half), BF16),
            jax.ShapeDtypeStruct((nodes, half), BF16),
            jax.ShapeDtypeStruct((half // 2, whole), BF16),
            jax.ShapeDtypeStruct((half // 2, whole), BF16),
        ),
        in_specs=[smem()] + [vmem()] * (3 + 2 * n_col),
        out_specs=(vmem(),) * 4,
        compiler_params=params(),
        cost_estimate=pl.CostEstimate(
            flops=8 * nodes * half * whole, bytes_accessed=1024 * 1024, transcendentals=nodes * whole
        ),
        name="middle",
    )(info, weights, cot_own, cot_other, *own, *other)


def backward_kernel(n_col, a, *refs):
    pieces, out, turned = refs[:n_col], refs[n_col], refs[n_col + 1]

    @pl.when(pl.program_id(0) == 0)
    def _():
        for t in range(n_col):
            turned[t] = pieces[t][...].astype(F32).T.astype(BF16)

    total = jnp.dot(turned[0], a[0, 0], preferred_element_type=F32)
    for t in range(1, n_col):
        total = total + jnp.dot(turned[t], a[0, t], preferred_element_type=F32)
    out[0] = total.T.astype(BF16)


def backward(dense, parity, pieces):
    n_src, n_col, side, _ = dense.shape
    feats = pieces[0].shape[1]
    n_z = n_src // 2
    return pl.pallas_call(
        functools.partial(backward_kernel, n_col),
        grid=(n_z,),
        out_shape=jax.ShapeDtypeStruct((n_z, side, feats), BF16),
        in_specs=[pl.BlockSpec((1, n_col, side, side), lambda s: (2 * s + parity, 0, 0, 0))]
        + [vmem()] * n_col,
        out_specs=pl.BlockSpec((1, side, feats), lambda s: (s, 0, 0)),
        scratch_shapes=[pltpu.VMEM((n_col, feats, side), BF16)],
        compiler_params=params(),
        cost_estimate=pl.CostEstimate(
            flops=2 * n_z * n_col * side * side * feats,
            bytes_accessed=2 * n_z * n_col * side * side,
            transcendentals=0,
        ),
        name="backward",
    )(dense, *pieces)


def pair_kernel(own, arrived, *outs):
    for s, out in enumerate(outs):
        out[...] = (own[s].astype(F32) + arrived[s].astype(F32)).astype(BF16)


def pair_sums(own, arrived):
    n_z, side, feats = own.shape
    return pl.pallas_call(
        pair_kernel,
        out_shape=(jax.ShapeDtypeStruct((side, feats), BF16),) * n_z,
        in_specs=[vmem()] * 2,
        out_specs=(vmem(),) * n_z,
        compiler_params=params(),
        name="pair_sums",
    )(own, arrived)


def shards(features, tile_rows, tile_cols, tile_count, tile_values, weights, cotangent):
    tile = tile_values.shape[-1]
    n_row, n_col = lax.axis_size("row"), lax.axis_size("col")
    n_z = n_row // 2
    nodes, half = features.shape
    blocks = nodes // tile
    node_total = nodes * n_row * n_col
    r, c, f = lax.axis_index("row"), lax.axis_index("col"), lax.axis_index("feat")
    info = jnp.stack([r // 2, r % 2, c, f]).astype(jnp.int32)

    def sibling(v):
        return lax.ppermute(v, "row", [(i, i ^ 1) for i in range(n_row)])

    def along_z(v, s):
        return lax.ppermute(v, "row", [(i, (i + 2 * s) % n_row) for i in range(n_row)])

    def other_feat(v):
        return lax.ppermute(v, "feat", [(0, 1), (1, 0)])

    def to_group(v, shift, flip):
        pairs = []
        for cc in range(n_col):
            for ff in range(2):
                pairs.append((2 * cc + ff, 2 * ((cc + shift) % n_col) + (ff ^ flip)))
        return lax.ppermute(v, ("col", "feat"), pairs)

    same = [features] + [along_z(features, s) for s in range(1, n_z)]
    cross = [sibling(v) for v in same]
    cot_other = other_feat(cotangent)

    dense = densify(
        info, tile_rows, tile_cols, tile_count, tile_values[0, 0], n_z, n_col, blocks
    )
    total = None
    for s in range(n_z):
        total = forward(dense, s, same[s], cross[s], total)
    parts = total.astype(BF16).reshape(n_col, nodes, half)

    own = [parts[0]] + [to_group(parts[t], -t, 0) for t in range(1, n_col)]
    other = [to_group(parts[t], -t, 1) for t in range(n_col)]
    activated, spread, keep, send = middle(info, weights, cotangent, cot_other, own, other)

    term = (keep.astype(F32) + sibling(send).astype(F32)).astype(BF16)
    pieces = [spread] + [
        lax.ppermute(spread, "col", [(i, (i + t) % n_col) for i in range(n_col)])
        for t in range(1, n_col)
    ]
    gathered = [along_z(term, s) for s in range(1, n_z)]

    odd = backward(dense, 1, pieces)
    arrived = sibling(odd)
    even = backward(dense, 0, pieces)
    sums = pair_sums(even, arrived)
    back = sums[0].astype(F32)
    for s in range(1, n_z):
        back = back + along_z(sums[s], -s).astype(F32)

    grad = term.astype(F32)
    for v in gathered:
        grad = grad + v.astype(F32)
    grad = grad.astype(BF16)
    across = grad.astype(F32)
    for t in range(1, n_col):
        across = across + lax.ppermute(
            grad, "col", [(i, (i + t) % n_col) for i in range(n_col)]
        ).astype(F32)
    kept = across.astype(BF16)
    swapped = sibling(kept)
    lower = jnp.where(r % 2 == 0, kept, swapped)
    upper = jnp.where(r % 2 == 0, swapped, kept)
    weight_grad = jnp.concatenate([lower, upper], axis=0).astype(F32) * node_total ** (-0.5)
    return (activated, back.astype(BF16), weight_grad)


def solution(mesh):
    return jax.shard_map(
        shards,
        mesh=mesh,
        in_specs=(
            P(("col", "row"), "feat"),
            P("row", "col", None),
            P("row", "col", None),
            P("row", "col"),
            P("row", "col", None, None, None),
            P(),
            P(("row", "col"), "feat"),
        ),
        out_specs=(P(("row", "col"), "feat"), P(("col", "row"), "feat"), P("feat", None)),
        check_vma=False,
    )
```

time: 282 us -> 94.5 us (0.34)
  other arithmetic: 72 us -> 1.55 us
  waiting for transfers between devices: 94.2 us -> 25 us
  local copies, waits for them, and re-layouts: 55.5 us -> 1.39 us
  Pallas kernels: 0 us -> 34.7 us
  matrix products: 31.6 us -> 0 us
  starting transfers between devices: 0.38 us -> 30.1 us
  between operations: 14.5 us -> 1.51 us
  blocking collectives: 11.6 us -> 0 us
    scatter-add x2 -> x0, other arithmetic: 66.4 us -> none  [the longest x1 33.2 us: shards(): jnp.zeros((col_blocks, width, feat_half), jnp.float32).at[block_cols]]
    reduce_scatter x2 -> x0, waiting for transfers between devices: 46.3 us -> none  [the longest x1 34.9 us: shards(): lax.psum_scatter(back_partial.reshape(col_blocks * width, feat_half).asty...]
    mul x2 -> x0, local copies, waits for them, and re-layouts: 35 us -> none  [the longest x1 17.5 us: shards(): back_products = back_products * live_mask[:, None, None]]
    pallas_call x0 -> x9, Pallas kernels: none -> 34.7 us  [the longest x1 12.5 us: densify(): pl.pallas_call(functools.partial(densify_kernel, (n_z, n_col, blocks, slo...]
    dot_general x5 -> x0, matrix products: 31.6 us -> none  [the longest x1 15.4 us: shards(): jnp.einsum('tji,tjf->tif', local_tiles, spread_blocks, preferred_element_...]
    ppermute x0 -> x22, starting transfers between devices: none -> 30.1 us  [the longest x9 18 us: along_z(): lax.ppermute(v, 'row', [(i, (i + 2 * s) % n_row) for i in range(n_row)])]
    ppermute x0 -> x22, waiting for transfers between devices: none -> 25 us  [the longest x9 16.8 us: along_z(): lax.ppermute(v, 'row', [(i, (i + 2 * s) % n_row) for i in range(n_row)])]
    all_gather x1 -> x0, waiting for transfers between devices: 24.5 us -> none  [shards(): panel = lax.all_gather(features, 'row', axis=0, tiled=True)]
  transfers between devices with their start and end apart: 5 -> 22, of which waited for: 5 -> 9; matrix products, arithmetic and copies ran while one was open for 28% -> 1% of each run, Pallas kernels for 0% -> 35%
where the time goes in v1:
time: 94.5 us; the launch traced here: 94.1 us
  Pallas kernels  34.7 us (37%)
  starting transfers between devices  30.1 us (32%)
  waiting for transfers between devices  25 us (26%)
  other arithmetic  1.55 us (2%)
  between operations  1.51 us (2%)
  local copies, waits for them, and re-layouts  1.39 us (1%)
    ppermute x9, starting transfers between devices, along_z(): lax.ppermute(v, 'row', [(i, (i + 2 * s) % n_row) for i in range(n_row)])  18 us
    ppermute x9, waiting for transfers between devices, along_z(): lax.ppermute(v, 'row', [(i, (i + 2 * s) % n_row) for i in range(n_row)])  16.8 us
    pallas_call x1, Pallas kernels, densify(): pl.pallas_call(functools.partial(densify_kernel, (n_z, n_col, blocks, slo...  12.5 us
    pallas_call x4, Pallas kernels, forward(): pl.pallas_call(functools.partial(forward_kernel, first), grid=(n_col, 2),...  12.4 us
    pallas_call x2, Pallas kernels, backward(): pl.pallas_call(functools.partial(backward_kernel, n_col), grid=(n_z,), ou...  7.7 us
    ppermute x3, starting transfers between devices, to_group(): return lax.ppermute(v, ('col', 'feat'), pairs)  7.58 us
    ppermute x3, waiting for transfers between devices, to_group(): return lax.ppermute(v, ('col', 'feat'), pairs)  5.25 us
    ppermute x1, waiting for transfers between devices, shards(): lax.ppermute(grad, 'col', [(i, (i + t) % n_col) for i in range(n_col)])  2.74 us
  transfers between devices with their start and end apart: 22, of which 9 were waited for; matrix products, arithmetic and copies ran while one was open for 1% of the time, Pallas kernels for 35%

profile of v1, /device:TPU:0, one launch (start us, length us, event | category | flops | bytes accessed | tf_op | source)
XLA Modules:
  0.0 94.1 jit_solution(10481441215863427175)
XLA Ops:
  0.6 3.1 %collective-permute-start.5 = (bf16[512,128]{1,0:T(8,128)(2,1)}, bf16[512,128]{1,0:T(8,128)(2,1)S(1)}, u32[]{:S(2)}, u32[]{:S(2)}) collective-permute-start(bf16[512,128]{1,0:T(8,128)(2,1)} %x0.1), channel_id=1, source_target_pairs={{0,8},{4,12},{8,16},{12,20},{16,24},{20,28},{24,0},{28,4},{1,9},{5... | collective-permute-start | bytes 393224 | tf_op jit(solution)/shard_map/ppermute | solution.py:306
  3.7 2.6 %collective-permute-start.3 = (bf16[512,128]{1,0:T(8,128)(2,1)}, bf16[512,128]{1,0:T(8,128)(2,1)S(1)}, u32[]{:S(2)}, u32[]{:S(2)}) collective-permute-start(bf16[512,128]{1,0:T(8,128)(2,1)} %x0.1), channel_id=1, source_target_pairs={{0,16},{4,20},{8,24},{12,28},{16,0},{20,4},{24,8},{28,12},{1,17},{... | collective-permute-start | bytes 393224 | tf_op jit(solution)/shard_map/ppermute | solution.py:306
  6.3 1.3 %collective-permute-start.1 = (bf16[512,128]{1,0:T(8,128)(2,1)}, bf16[512,128]{1,0:T(8,128)(2,1)S(1)}, u32[]{:S(2)}, u32[]{:S(2)}) collective-permute-start(bf16[512,128]{1,0:T(8,128)(2,1)} %x0.1), channel_id=1, source_target_pairs={{0,24},{4,28},{8,0},{12,4},{16,8},{20,12},{24,16},{28,20},{1,25},{... | collective-permute-start | bytes 393224 | tf_op jit(solution)/shard_map/ppermute | solution.py:306
  7.6 0.0 collective-permute-start.7
  7.6 1.5 %collective-permute-start = (bf16[512,128]{1,0:T(8,128)(2,1)}, bf16[512,128]{1,0:T(8,128)(2,1)S(1)}, u32[]{:S(2)}, u32[]{:S(2)}) collective-permute-start(bf16[512,128]{1,0:T(8,128)(2,1)} %cot_own.1), channel_id=1, source_target_pairs={{0,1},{1,0},{2,3},{3,2},{4,5},{5,4},{6,7},{7,6},{8,9},{9,8},{10,11... | collective-permute-start | bytes 393224 | tf_op jit(solution)/shard_map/ppermute | solution.py:309
  9.1 1.2 %collective-permute-done.5.x0 = bf16[512,128]{1,0:T(8,128)(2,1)S(1)} collective-permute-done((bf16[512,128]{1,0:T(8,128)(2,1)}, bf16[512,128]{1,0:T(8,128)(2,1)S(1)}, u32[]{:S(2)}, u32[]{:S(2)}) %collective-permute-start.5) | collective-permute-done | bytes 131104 | tf_op jit(solution)/shard_map/ppermute | solution.py:306
  10.4 0.0 collective-permute-start.6
  10.4 4.8 %collective-permute-done.3.x0 = bf16[512,128]{1,0:T(8,128)(2,1)S(1)} collective-permute-done((bf16[512,128]{1,0:T(8,128)(2,1)}, bf16[512,128]{1,0:T(8,128)(2,1)S(1)}, u32[]{:S(2)}, u32[]{:S(2)}) %collective-permute-start.3) | collective-permute-done | bytes 131104 | tf_op jit(solution)/shard_map/ppermute | solution.py:306
  15.2 0.0 collective-permute-start.4
  15.2 0.0 collective-permute-done.1.x0
  15.2 0.5 collective-permute-start.2
  15.7 0.1 pad_add_fusion.info
  16.4 0.0 copy-start.3
  16.4 0.7 copy-done.3
  17.1 0.7 copy-done.4
  17.8 12.5 %densify.1.a = bf16[8,2,512,512]{3,2,1,0:T(8,128)(2,1)} custom-call(s32[4]{0:T(128)S(1)} %pad_add_fusion.info, s32[1,1,256]{2,1,0:T(1,128)S(1)} %copy-done.3, s32[1,1,256]{2,1,0:T(1,128)S(1)} %copy-done.4, s32[1,1]{1,0:T(1,128)S(6)} %copy.10.count, bf16[256,128,128]{2,1,0:T(8,128)(2,1)} %bitcast.5), custom_call_target="tpu_custom_call" | custom-call | bytes 25165824 | tf_op jit(solution)/shard_map/densify/pallas_call | solution.py:105
  30.3 0.0 collective-permute-done.7.x1
  30.3 0.0 copy-done
  30.3 3.1 %forward.4.rest_0_ = f32[1024,128]{1,0:T(8,128)S(1)} custom-call(bf16[8,2,512,512]{3,2,1,0:T(8,128)(2,1)} %densify.1.a, bf16[512,128]{1,0:T(8,128)(2,1)S(1)} %copy-done, bf16[512,128]{1,0:T(8,128)(2,1)S(1)} %collective-permute-done.7.x1), custom_call_target="tpu_custom_call" | custom-call | flops 268435456 | bytes 2097152 | tf_op jit(solution)/shard_map/forward/pallas_call | solution.py:146
  33.4 0.0 collective-permute-done.6.x1
  33.4 3.1 %forward.5.rest_0_ = f32[1024,128]{1,0:T(8,128)S(1)} custom-call(bf16[8,2,512,512]{3,2,1,0:T(8,128)(2,1)} %densify.1.a, bf16[512,128]{1,0:T(8,128)(2,1)S(1)} %collective-permute-done.5.x0, bf16[512,128]{1,0:T(8,128)(2,1)S(1)} %collective-permute-done.6.x1, f32[1024,128]{1,0:T(8,128)S(1)} %forward.4.rest_0_), custom_call_target="tpu_custom_call" | custom-call | flops 268435456 | bytes 2097152 | tf_op jit(solution)/shard_map/forward/pallas_call | solution.py:146
  36.5 0.0 copy-start.1
  36.5 0.0 copy-start.2
  36.5 0.0 collective-permute-done.4.x1
  36.5 3.2 %forward.6.rest_0_ = f32[1024,128]{1,0:T(8,128)S(1)} custom-call(bf16[8,2,512,512]{3,2,1,0:T(8,128)(2,1)} %densify.1.a, bf16[512,128]{1,0:T(8,128)(2,1)S(1)} %collective-permute-done.3.x0, bf16[512,128]{1,0:T(8,128)(2,1)S(1)} %collective-permute-done.4.x1, f32[1024,128]{1,0:T(8,128)S(1)} %forward.5.rest_0_), custom_call_target="tpu_custom_call" | custom-call | flops 268435456 | bytes 2097152 | tf_op jit(solution)/shard_map/forward/pallas_call | solution.py:146
  39.7 0.0 collective-permute-done.2.x1
  39.7 3.1 %forward.7 = f32[1024,128]{1,0:T(8,128)S(1)} custom-call(bf16[8,2,512,512]{3,2,1,0:T(8,128)(2,1)} %densify.1.a, bf16[512,128]{1,0:T(8,128)(2,1)S(1)} %collective-permute-done.1.x0, bf16[512,128]{1,0:T(8,128)(2,1)S(1)} %collective-permute-done.2.x1, f32[1024,128]{1,0:T(8,128)S(1)} %forward.6.rest_0_), custom_call_target="tpu_custom_call" | custom-call | flops 268435456 | bytes 2097152 | tf_op jit(solution)/shard_map/forward/pallas_call | solution.py:146
  42.8 6.9 %collective-permute-start.10 = (bf16[512,128]{1,0:T(8,128)(2,1)S(1)}, bf16[512,128]{1,0:T(8,128)(2,1)S(1)}, u32[]{:S(2)}, u32[]{:S(2)}) collective-permute-start(bf16[512,128]{1,0:T(8,128)(2,1)S(1)} %get-tuple-element.19), channel_id=1, source_target_pairs={{0,3},{1,2},{2,1},{3,0},{4,7},{5,6},{6,5},{7,4},{8,11},{9,10},{10,... | collective-permute-start | bytes 393224 | tf_op jit(solution)/shard_map/ppermute | solution.py:316
  49.8 0.0 collective-permute-start.8
  49.8 0.6 collective-permute-start.9
  50.4 0.0 collective-permute-done.cot_other
  50.4 3.7 %collective-permute-done.10.refs_3_ = bf16[512,128]{1,0:T(8,128)(2,1)S(1)} collective-permute-done((bf16[512,128]{1,0:T(8,128)(2,1)S(1)}, bf16[512,128]{1,0:T(8,128)(2,1)S(1)}, u32[]{:S(2)}, u32[]{:S(2)}) %collective-permute-start.10) | collective-permute-done | bytes 131104 | tf_op jit(solution)/shard_map/ppermute | solution.py:316
  54.2 1.4 %collective-permute-done.8.refs_1_ = bf16[512,128]{1,0:T(8,128)(2,1)S(1)} collective-permute-done((bf16[512,128]{1,0:T(8,128)(2,1)S(1)}, bf16[512,128]{1,0:T(8,128)(2,1)S(1)}, u32[]{:S(2)}, u32[]{:S(2)}) %collective-permute-start.8) | collective-permute-done | bytes 131104 | tf_op jit(solution)/shard_map/ppermute | solution.py:316
  55.6 0.1 collective-permute-done.9.refs_2_
  55.7 0.0 copy-done.1
  55.7 0.0 copy-done.2
  55.7 1.9 %middle.1 = (bf16[512,128]{1,0:T(8,128)(2,1)}, bf16[512,128]{1,0:T(8,128)(2,1)S(1)}, bf16[64,256]{1,0:T(8,128)(2,1)S(1)}, bf16[64,256]{1,0:T(8,128)(2,1)S(1)}) custom-call(s32[4]{0:T(128)S(1)} %pad_add_fusion.info, bf16[256,256]{1,0:T(8,128)(2,1)S(1)} %copy-done.1, bf16[512,128]{1,0:T(8,128)(2,1)S(1)} %copy-done.2, ...), custom_call_target="tpu_custom_call" | custom-call | flops 134217728 | bytes 1048576 | tf_op jit(solution)/shard_map/middle/pallas_call | solution.py:221
  57.6 0.0 collective-permute-start.16
  57.6 1.1 %collective-permute-start.11 = (bf16[512,128]{1,0:T(8,128)(2,1)S(1)}, bf16[512,128]{1,0:T(8,128)(2,1)S(1)}, u32[]{:S(2)}, u32[]{:S(2)}) collective-permute-start(bf16[512,128]{1,0:T(8,128)(2,1)S(1)} %get-tuple-element.12.refs_0_), channel_id=1, source_target_pairs={{0,2},{2,0},{1,3},{3,1},{4,6},{6,4},{5,7},{7,5},{8,10},{10,8},{9,1... | collective-permute-start | bytes 393224 | tf_op jit(solution)/shard_map/ppermute | solution.py:336
  58.7 0.1 collective-permute-done.16
  58.9 3.9 %collective-permute-start.17 = (bf16[64,256]{1,0:T(8,128)(2,1)S(1)}, bf16[64,256]{1,0:T(8,128)(2,1)S(1)}, u32[]{:S(2)}, u32[]{:S(2)}) collective-permute-start(bf16[64,256]{1,0:T(8,128)(2,1)S(1)} %add_convert_fusion.3), channel_id=1, source_target_pairs={{0,8},{4,12},{8,16},{12,20},{16,24},{20,28},{24,0},{28,4},{1,9},{5... | collective-permute-start | bytes 98312 | tf_op jit(solution)/shard_map/ppermute | solution.py:306
  62.7 2.4 %collective-permute-start.18 = (bf16[64,256]{1,0:T(8,128)(2,1)S(1)}, bf16[64,256]{1,0:T(8,128)(2,1)S(1)}, u32[]{:S(2)}, u32[]{:S(2)}) collective-permute-start(bf16[64,256]{1,0:T(8,128)(2,1)S(1)} %add_convert_fusion.3), channel_id=1, source_target_pairs={{0,16},{4,20},{8,24},{12,28},{16,0},{20,4},{24,8},{28,12},{1,17},{... | collective-permute-start | bytes 98312 | tf_op jit(solution)/shard_map/ppermute | solution.py:306
  65.1 0.1 collective-permute-start.19
  65.2 0.0 collective-permute-done.11.refs_1_
  65.2 3.8 %backward.3 = bf16[4,512,128]{2,1,0:T(8,128)(2,1)S(1)} custom-call(bf16[8,2,512,512]{3,2,1,0:T(8,128)(2,1)} %densify.1.a, bf16[512,128]{1,0:T(8,128)(2,1)S(1)} %get-tuple-element.12.refs_0_, bf16[512,128]{1,0:T(8,128)(2,1)S(1)} %collective-permute-done.11.refs_1_), custom_call_target="tpu_custom_call" | custom-call | flops 536870912 | bytes 4194304 | tf_op jit(solution)/shard_map/backward/pallas_call | solution.py:257
  69.0 0.1 collective-permute-start.12
  69.1 0.0 collective-permute-done.17
  69.1 0.0 collective-permute-done.18
  69.1 0.0 collective-permute-done.19
  69.1 1.2 %collective-permute-start.20 = (bf16[64,256]{1,0:T(8,128)(2,1)S(1)}, bf16[64,256]{1,0:T(8,128)(2,1)S(1)}, u32[]{:S(2)}, u32[]{:S(2)}) collective-permute-start(bf16[64,256]{1,0:T(8,128)(2,1)S(1)} %add_convert_fusion.2), channel_id=1, source_target_pairs={{0,2},{2,0},{1,3},{3,1},{4,6},{6,4},{5,7},{7,5},{8,10},{10,8},{9,1... | collective-permute-start | bytes 98312 | tf_op jit(solution)/shard_map/ppermute | solution.py:355
  70.4 2.7 %collective-permute-done.20 = bf16[64,256]{1,0:T(8,128)(2,1)S(1)} collective-permute-done((bf16[64,256]{1,0:T(8,128)(2,1)S(1)}, bf16[64,256]{1,0:T(8,128)(2,1)S(1)}, u32[]{:S(2)}, u32[]{:S(2)}) %collective-permute-start.20) | collective-permute-done | bytes 32800 | tf_op jit(solution)/shard_map/ppermute | solution.py:355
  73.1 0.1 collective-permute-start.21
  73.2 3.9 %backward.2.own = bf16[4,512,128]{2,1,0:T(8,128)(2,1)S(1)} custom-call(bf16[8,2,512,512]{3,2,1,0:T(8,128)(2,1)} %densify.1.a, bf16[512,128]{1,0:T(8,128)(2,1)S(1)} %get-tuple-element.12.refs_0_, bf16[512,128]{1,0:T(8,128)(2,1)S(1)} %collective-permute-done.11.refs_1_), custom_call_target="tpu_custom_call" | custom-call | flops 536870912 | bytes 4194304 | tf_op jit(solution)/shard_map/backward/pallas_call | solution.py:257
  77.1 0.0 collective-permute-done.12.arrived
  77.1 0.1 pair_sums.1
  77.2 4.0 %collective-permute-start.13 = (bf16[512,128]{1,0:T(8,128)(2,1)S(1)}, bf16[512,128]{1,0:T(8,128)(2,1)S(1)}, u32[]{:S(2)}, u32[]{:S(2)}) collective-permute-start(bf16[512,128]{1,0:T(8,128)(2,1)S(1)} %get-tuple-element.14), channel_id=1, source_target_pairs={{0,24},{4,28},{8,0},{12,4},{16,8},{20,12},{24,16},{28,20},{1,25},{... | collective-permute-start | bytes 393224 | tf_op jit(solution)/shard_map/ppermute | solution.py:306
  81.3 0.0 collective-permute-start.14
  81.3 0.6 collective-permute-start.15
  81.9 0.0 collective-permute-done.21
  81.9 0.7 convert_multiply_fusion
  82.6 2.6 %collective-permute-done.13 = bf16[512,128]{1,0:T(8,128)(2,1)S(1)} collective-permute-done((bf16[512,128]{1,0:T(8,128)(2,1)S(1)}, bf16[512,128]{1,0:T(8,128)(2,1)S(1)}, u32[]{:S(2)}, u32[]{:S(2)}) %collective-permute-start.13) | collective-permute-done | bytes 131104 | tf_op jit(solution)/shard_map/ppermute | solution.py:306
  85.2 8.2 %collective-permute-done.14 = bf16[512,128]{1,0:T(8,128)(2,1)S(1)} collective-permute-done((bf16[512,128]{1,0:T(8,128)(2,1)S(1)}, bf16[512,128]{1,0:T(8,128)(2,1)S(1)}, u32[]{:S(2)}, u32[]{:S(2)}) %collective-permute-start.14) | collective-permute-done | bytes 131104 | tf_op jit(solution)/shard_map/ppermute | solution.py:306
  93.4 0.0 collective-permute-done.15
  93.4 0.7 add_convert_fusion
  (8 shorter events, 0.1 us)
Async XLA Ops:
  0.6 9.7 %collective-permute-start.5 = (bf16[512,128]{1,0:T(8,128)(2,1)}, bf16[512,128]{1,0:T(8,128)(2,1)S(1)}, u32[]{:S(2)}, u32[]{:S(2)}) collective-permute-start(bf16[512,128]{1,0:T(8,128)(2,1)} %x0.1), channel_id=1, source_target_pairs={{0,8},{4,12},{8,16},{12,20},{16,24},{20,28},{24,0},{28,4},{1,9},{5... | collective-permute-start | bytes 393224 | tf_op jit(solution)/shard_map/ppermute | solution.py:306
  3.7 11.4 %collective-permute-start.3 = (bf16[512,128]{1,0:T(8,128)(2,1)}, bf16[512,128]{1,0:T(8,128)(2,1)S(1)}, u32[]{:S(2)}, u32[]{:S(2)}) collective-permute-start(bf16[512,128]{1,0:T(8,128)(2,1)} %x0.1), channel_id=1, source_target_pairs={{0,16},{4,20},{8,24},{12,28},{16,0},{20,4},{24,8},{28,12},{1,17},{... | collective-permute-start | bytes 393224 | tf_op jit(solution)/shard_map/ppermute | solution.py:306
  6.3 8.9 %collective-permute-start.1 = (bf16[512,128]{1,0:T(8,128)(2,1)}, bf16[512,128]{1,0:T(8,128)(2,1)S(1)}, u32[]{:S(2)}, u32[]{:S(2)}) collective-permute-start(bf16[512,128]{1,0:T(8,128)(2,1)} %x0.1), channel_id=1, source_target_pairs={{0,24},{4,28},{8,0},{12,4},{16,8},{20,12},{24,16},{28,20},{1,25},{... | collective-permute-start | bytes 393224 | tf_op jit(solution)/shard_map/ppermute | solution.py:306
  7.6 22.6 %collective-permute-start.7 = (bf16[512,128]{1,0:T(8,128)(2,1)}, bf16[512,128]{1,0:T(8,128)(2,1)S(1)}, u32[]{:S(2)}, u32[]{:S(2)}) collective-permute-start(bf16[512,128]{1,0:T(8,128)(2,1)} %x0.1), channel_id=1, source_target_pairs={{0,4},{4,0},{8,12},{12,8},{16,20},{20,16},{24,28},{28,24},{1,5},{5... | collective-permute-start | bytes 393224 | tf_op jit(solution)/shard_map/ppermute | solution.py:303
  7.6 42.8 %collective-permute-start = (bf16[512,128]{1,0:T(8,128)(2,1)}, bf16[512,128]{1,0:T(8,128)(2,1)S(1)}, u32[]{:S(2)}, u32[]{:S(2)}) collective-permute-start(bf16[512,128]{1,0:T(8,128)(2,1)} %cot_own.1), channel_id=1, source_target_pairs={{0,1},{1,0},{2,3},{3,2},{4,5},{5,4},{6,7},{7,6},{8,9},{9,8},{10,11... | collective-permute-start | bytes 393224 | tf_op jit(solution)/shard_map/ppermute | solution.py:309
  10.4 23.0 %collective-permute-start.6 = (bf16[512,128]{1,0:T(8,128)(2,1)S(1)}, bf16[512,128]{1,0:T(8,128)(2,1)S(1)}, u32[]{:S(2)}, u32[]{:S(2)}) collective-permute-start(bf16[512,128]{1,0:T(8,128)(2,1)S(1)} %collective-permute-done.5.x0), channel_id=1, source_target_pairs={{0,4},{4,0},{8,12},{12,8},{16,20},{20,16},{24,28},{28,24},{1,5},{5... | collective-permute-start | bytes 393224 | tf_op jit(solution)/shard_map/ppermute | solution.py:303
  15.2 21.3 %collective-permute-start.4 = (bf16[512,128]{1,0:T(8,128)(2,1)S(1)}, bf16[512,128]{1,0:T(8,128)(2,1)S(1)}, u32[]{:S(2)}, u32[]{:S(2)}) collective-permute-start(bf16[512,128]{1,0:T(8,128)(2,1)S(1)} %collective-permute-done.3.x0), channel_id=1, source_target_pairs={{0,4},{4,0},{8,12},{12,8},{16,20},{20,16},{24,28},{28,24},{1,5},{5... | collective-permute-start | bytes 393224 | tf_op jit(solution)/shard_map/ppermute | solution.py:303
  15.2 24.5 %collective-permute-start.2 = (bf16[512,128]{1,0:T(8,128)(2,1)S(1)}, bf16[512,128]{1,0:T(8,128)(2,1)S(1)}, u32[]{:S(2)}, u32[]{:S(2)}) collective-permute-start(bf16[512,128]{1,0:T(8,128)(2,1)S(1)} %collective-permute-done.1.x0), channel_id=1, source_target_pairs={{0,4},{4,0},{8,12},{12,8},{16,20},{20,16},{24,28},{28,24},{1,5},{5... | collective-permute-start | bytes 393224 | tf_op jit(solution)/shard_map/ppermute | solution.py:303
  16.4 0.7 copy-start.3
  17.1 0.7 copy-start.4
  17.8 12.5 %copy-start = (bf16[512,128]{1,0:T(8,128)(2,1)S(1)}, bf16[512,128]{1,0:T(8,128)(2,1)}, u32[]{:S(2)}) copy-start(bf16[512,128]{1,0:T(8,128)(2,1)} %x0.1) | copy-start | bytes 393220
  36.5 19.2 %copy-start.1 = (bf16[256,256]{1,0:T(8,128)(2,1)S(1)}, bf16[256,256]{1,0:T(8,128)(2,1)}, u32[]{:S(2)}) copy-start(bf16[256,256]{1,0:T(8,128)(2,1)} %weights.1) | copy-start | bytes 393220
  36.5 19.2 %copy-start.2 = (bf16[512,128]{1,0:T(8,128)(2,1)S(1)}, bf16[512,128]{1,0:T(8,128)(2,1)}, u32[]{:S(2)}) copy-start(bf16[512,128]{1,0:T(8,128)(2,1)} %cot_own.1) | copy-start | bytes 393220
  42.8 11.3 %collective-permute-start.10 = (bf16[512,128]{1,0:T(8,128)(2,1)S(1)}, bf16[512,128]{1,0:T(8,128)(2,1)S(1)}, u32[]{:S(2)}, u32[]{:S(2)}) collective-permute-start(bf16[512,128]{1,0:T(8,128)(2,1)S(1)} %get-tuple-element.19), channel_id=1, source_target_pairs={{0,3},{1,2},{2,1},{3,0},{4,7},{5,6},{6,5},{7,4},{8,11},{9,10},{10,... | collective-permute-start | bytes 393224 | tf_op jit(solution)/shard_map/ppermute | solution.py:316
  49.8 5.8 %collective-permute-start.8 = (bf16[512,128]{1,0:T(8,128)(2,1)S(1)}, bf16[512,128]{1,0:T(8,128)(2,1)S(1)}, u32[]{:S(2)}, u32[]{:S(2)}) collective-permute-start(bf16[512,128]{1,0:T(8,128)(2,1)S(1)} %get-tuple-element.19), channel_id=1, source_target_pairs={{0,2},{1,3},{2,0},{3,1},{4,6},{5,7},{6,4},{7,5},{8,10},{9,11},{10,... | collective-permute-start | bytes 393224 | tf_op jit(solution)/shard_map/ppermute | solution.py:316
  49.8 5.9 %collective-permute-start.9 = (bf16[512,128]{1,0:T(8,128)(2,1)S(1)}, bf16[512,128]{1,0:T(8,128)(2,1)S(1)}, u32[]{:S(2)}, u32[]{:S(2)}) collective-permute-start(bf16[512,128]{1,0:T(8,128)(2,1)S(1)} %get-tuple-element.20.refs_0_), channel_id=1, source_target_pairs={{0,1},{1,0},{2,3},{3,2},{4,5},{5,4},{6,7},{7,6},{8,9},{9,8},{10,11... | collective-permute-start | bytes 393224 | tf_op jit(solution)/shard_map/ppermute | solution.py:316
  57.6 1.2 %collective-permute-start.16 = (bf16[64,256]{1,0:T(8,128)(2,1)S(1)}, bf16[64,256]{1,0:T(8,128)(2,1)S(1)}, u32[]{:S(2)}, u32[]{:S(2)}) collective-permute-start(bf16[64,256]{1,0:T(8,128)(2,1)S(1)} %get-tuple-element.18), channel_id=1, source_target_pairs={{0,4},{4,0},{8,12},{12,8},{16,20},{20,16},{24,28},{28,24},{1,5},{5... | collective-permute-start | bytes 98312 | tf_op jit(solution)/shard_map/ppermute | solution.py:303
  57.6 7.5 %collective-permute-start.11 = (bf16[512,128]{1,0:T(8,128)(2,1)S(1)}, bf16[512,128]{1,0:T(8,128)(2,1)S(1)}, u32[]{:S(2)}, u32[]{:S(2)}) collective-permute-start(bf16[512,128]{1,0:T(8,128)(2,1)S(1)} %get-tuple-element.12.refs_0_), channel_id=1, source_target_pairs={{0,2},{2,0},{1,3},{3,1},{4,6},{6,4},{5,7},{7,5},{8,10},{10,8},{9,1... | collective-permute-start | bytes 393224 | tf_op jit(solution)/shard_map/ppermute | solution.py:336
  58.9 10.2 %collective-permute-start.17 = (bf16[64,256]{1,0:T(8,128)(2,1)S(1)}, bf16[64,256]{1,0:T(8,128)(2,1)S(1)}, u32[]{:S(2)}, u32[]{:S(2)}) collective-permute-start(bf16[64,256]{1,0:T(8,128)(2,1)S(1)} %add_convert_fusion.3), channel_id=1, source_target_pairs={{0,8},{4,12},{8,16},{12,20},{16,24},{20,28},{24,0},{28,4},{1,9},{5... | collective-permute-start | bytes 98312 | tf_op jit(solution)/shard_map/ppermute | solution.py:306
  62.7 6.4 %collective-permute-start.18 = (bf16[64,256]{1,0:T(8,128)(2,1)S(1)}, bf16[64,256]{1,0:T(8,128)(2,1)S(1)}, u32[]{:S(2)}, u32[]{:S(2)}) collective-permute-start(bf16[64,256]{1,0:T(8,128)(2,1)S(1)} %add_convert_fusion.3), channel_id=1, source_target_pairs={{0,16},{4,20},{8,24},{12,28},{16,0},{20,4},{24,8},{28,12},{1,17},{... | collective-permute-start | bytes 98312 | tf_op jit(solution)/shard_map/ppermute | solution.py:306
  65.1 4.0 %collective-permute-start.19 = (bf16[64,256]{1,0:T(8,128)(2,1)S(1)}, bf16[64,256]{1,0:T(8,128)(2,1)S(1)}, u32[]{:S(2)}, u32[]{:S(2)}) collective-permute-start(bf16[64,256]{1,0:T(8,128)(2,1)S(1)} %add_convert_fusion.3), channel_id=1, source_target_pairs={{0,24},{4,28},{8,0},{12,4},{16,8},{20,12},{24,16},{28,20},{1,25},{... | collective-permute-start | bytes 98312 | tf_op jit(solution)/shard_map/ppermute | solution.py:306
  69.0 8.1 %collective-permute-start.12 = (bf16[4,512,128]{2,1,0:T(8,128)(2,1)S(1)}, bf16[4,512,128]{2,1,0:T(8,128)(2,1)S(1)}, u32[]{:S(2)}, u32[]{:S(2)}) collective-permute-start(bf16[4,512,128]{2,1,0:T(8,128)(2,1)S(1)} %backward.3), channel_id=1, source_target_pairs={{0,4},{4,0},{8,12},{12,8},{16,20},{20,16},{24,28},{28,24},{1,5},{5... | collective-permute-start | bytes 1572872 | tf_op jit(solution)/shard_map/ppermute | solution.py:303
  69.1 4.0 %collective-permute-start.20 = (bf16[64,256]{1,0:T(8,128)(2,1)S(1)}, bf16[64,256]{1,0:T(8,128)(2,1)S(1)}, u32[]{:S(2)}, u32[]{:S(2)}) collective-permute-start(bf16[64,256]{1,0:T(8,128)(2,1)S(1)} %add_convert_fusion.2), channel_id=1, source_target_pairs={{0,2},{2,0},{1,3},{3,1},{4,6},{6,4},{5,7},{7,5},{8,10},{10,8},{9,1... | collective-permute-start | bytes 98312 | tf_op jit(solution)/shard_map/ppermute | solution.py:355
  73.1 8.8 %collective-permute-start.21 = (bf16[64,256]{1,0:T(8,128)(2,1)S(1)}, bf16[64,256]{1,0:T(8,128)(2,1)S(1)}, u32[]{:S(2)}, u32[]{:S(2)}) collective-permute-start(bf16[64,256]{1,0:T(8,128)(2,1)S(1)} %add_convert_fusion.1), channel_id=1, source_target_pairs={{0,4},{4,0},{8,12},{12,8},{16,20},{20,16},{24,28},{28,24},{1,5},{5... | collective-permute-start | bytes 98312 | tf_op jit(solution)/shard_map/ppermute | solution.py:303
  77.2 7.9 %collective-permute-start.13 = (bf16[512,128]{1,0:T(8,128)(2,1)S(1)}, bf16[512,128]{1,0:T(8,128)(2,1)S(1)}, u32[]{:S(2)}, u32[]{:S(2)}) collective-permute-start(bf16[512,128]{1,0:T(8,128)(2,1)S(1)} %get-tuple-element.14), channel_id=1, source_target_pairs={{0,24},{4,28},{8,0},{12,4},{16,8},{20,12},{24,16},{28,20},{1,25},{... | collective-permute-start | bytes 393224 | tf_op jit(solution)/shard_map/ppermute | solution.py:306
  81.3 12.1 %collective-permute-start.14 = (bf16[512,128]{1,0:T(8,128)(2,1)S(1)}, bf16[512,128]{1,0:T(8,128)(2,1)S(1)}, u32[]{:S(2)}, u32[]{:S(2)}) collective-permute-start(bf16[512,128]{1,0:T(8,128)(2,1)S(1)} %get-tuple-element.15), channel_id=1, source_target_pairs={{0,16},{4,20},{8,24},{12,28},{16,0},{20,4},{24,8},{28,12},{1,17},{... | collective-permute-start | bytes 393224 | tf_op jit(solution)/shard_map/ppermute | solution.py:306
  81.3 12.1 %collective-permute-start.15 = (bf16[512,128]{1,0:T(8,128)(2,1)S(1)}, bf16[512,128]{1,0:T(8,128)(2,1)S(1)}, u32[]{:S(2)}, u32[]{:S(2)}) collective-permute-start(bf16[512,128]{1,0:T(8,128)(2,1)S(1)} %get-tuple-element.16), channel_id=1, source_target_pairs={{0,8},{4,12},{8,16},{12,20},{16,24},{20,28},{24,0},{28,4},{1,9},{5... | collective-permute-start | bytes 393224 | tf_op jit(solution)/shard_map/ppermute | solution.py:306

commit v2 on v1

--- a/solution.py
+++ b/solution.py
@@ -9,11 +9,11 @@
 
 F32 = jnp.float32
 BF16 = jnp.bfloat16
-VMEM_LIMIT = 48 * 1024 * 1024
-
-
-def params(*semantics):
-    return pltpu.CompilerParams(vmem_limit_bytes=VMEM_LIMIT)
+MIB = 1024 * 1024
+
+
+def params(mib=48):
+    return pltpu.CompilerParams(vmem_limit_bytes=mib * MIB)
 
 
 def vmem():
@@ -24,7 +24,173 @@
     return pl.BlockSpec(memory_space=pltpu.SMEM)
 
 
-def densify_kernel(
+def place_of(dims, info, block_row, block_col):
+    n_z, n_col, blocks = dims
+    z, core, c = info[0], info[1], info[2]
+    source, owner = block_col // blocks, block_row // blocks
+    j = 2 * (z ^ (source // 2)) + ((source + core) & 1)
+    t = c - owner
+    t = jnp.where(t < 0, t + n_col, t)
+    return ((j * n_col + t) * blocks + block_row % blocks) * blocks + block_col % blocks
+
+
+def densify_kernel(dims, groups, info, rows, cols, count, tiles, out, buffer, total, sems):
+    n_z, n_col, blocks = dims
+    slots, tile = buffer.shape[0], buffer.shape[1]
+    per_group = slots // groups
+    places = total.shape[0] - 1
+    live = count[0, 0]
+
+    def copy(g):
+        part = pl.ds(g * per_group, per_group)
+        return pltpu.make_async_copy(tiles.at[part], buffer.at[part], sems.at[g])
+
+    def each_group(action):
+        for g in range(groups):
+
+            @pl.when(g * per_group < live)
+            def _():
+                action(g)
+
+    each_group(lambda g: copy(g).start())
+
+    def clear(i, carry):
+        total[i] = jnp.zeros((tile, tile), F32)
+        return carry
+
+    lax.fori_loop(0, places, clear, 0, unroll=4)
+
+    def add_group(g):
+        copy(g).wait()
+
+        def add(i, carry):
+            slot = g * per_group + i
+            place = place_of(dims, info, rows[0, 0, slot], cols[0, 0, slot])
+            place = jnp.where(slot < live, place, places)
+            total[place] += buffer[slot].astype(F32)
+            return carry
+
+        lax.fori_loop(0, per_group, add, 0, unroll=4)
+
+    each_group(add_group)
+
+    def settle(j, carry):
+        for t in range(n_col):
+            for a in range(blocks):
+                for b in range(blocks):
+                    value = total[((j * n_col + t) * blocks + a) * blocks + b]
+                    out[j, t, a * tile : (a + 1) * tile, b * tile : (b + 1) * tile] = value.astype(BF16)
+        return carry
+
+    lax.fori_loop(0, 2 * n_z, settle, 0)
+
+
+def densify(info, rows, cols, count, tiles, n_z, n_col, blocks):
+    slots, tile = tiles.shape[0], tiles.shape[1]
+    n_src = 2 * n_z
+    groups = 8
+    side = blocks * tile
+    places = n_src * n_col * blocks * blocks
+    return pl.pallas_call(
+        functools.partial(densify_kernel, (n_z, n_col, blocks), groups),
+        out_shape=pltpu.VMEM((n_src, n_col, side, side), BF16),
+        in_specs=[smem(), smem(), smem(), smem(), pl.BlockSpec(memory_space=pl.ANY)],
+        out_specs=vmem(),
+        scratch_shapes=[
+            pltpu.VMEM((slots, tile, tile), BF16),
+            pltpu.VMEM((places + 1, tile, tile), F32),
+            pltpu.SemaphoreType.DMA((groups,)),
+        ],
+        compiler_params=params(),
+        cost_estimate=pl.CostEstimate(
+            flops=0, bytes_accessed=24 * 1024 * 1024, transcendentals=0
+        ),
+        name="densify",
+    )(info, rows, cols, count, tiles)
+
+
+def resident(dense):
+    return pltpu.with_memory_space_constraint(dense, pltpu.VMEM)
+
+
+def hold(arrays, dense):
+    n = len(arrays)
+    outs = pl.pallas_call(
+        lambda *refs: None,
+        out_shape=tuple(jax.ShapeDtypeStruct(v.shape, v.dtype) for v in arrays),
+        in_specs=[pl.BlockSpec(memory_space=pl.ANY)] * n + [vmem()],
+        out_specs=(pl.BlockSpec(memory_space=pl.ANY),) * n,
+        input_output_aliases={i: i for i in range(n)},
+        compiler_params=params(1),
+        name="hold",
+    )(*arrays, resident(dense))
+    return list(outs)
+
+
+def forward_kernel(places, last, dense, *refs):
+    n = len(places)
+    xs, refs = refs[:n], refs[n:]
+    n_col, side = dense.shape[1], dense.shape[2]
+    outs = refs[-n_col:]
+    for t in range(n_col):
+        total = jnp.dot(dense[places[0], t], xs[0][...], preferred_element_type=F32)
+        for j, x in zip(places[1:], xs[1:]):
+            total = total + jnp.dot(dense[j, t], x[...], preferred_element_type=F32)
+        if len(refs) > n_col:
+            total = total + refs[t][...]
+        outs[t][...] = total.astype(BF16) if last else total
+
+
+def forward(dense, places, xs, totals, last):
+    _, n_col, side, _ = dense.shape
+    feats = xs[0].shape[1]
+    shape = jax.ShapeDtypeStruct((side, feats), BF16 if last else F32)
+    return pl.pallas_call(
+        functools.partial(forward_kernel, places, last),
+        out_shape=(shape,) * n_col,
+        in_specs=[vmem()] * (1 + len(xs) + len(totals)),
+        out_specs=(vmem(),) * n_col,
+        compiler_params=params(24),
+        cost_estimate=pl.CostEstimate(
+            flops=2 * len(places) * n_col * side * side * feats,
+            bytes_accessed=2 * len(places) * n_col * side * side,
+            transcendentals=0,
+        ),
+        name="forward",
+    )(resident(dense), *xs, *totals)
+
+
+def backward_kernel(parity, dense, *refs):
+    n_src, n_col = dense.shape[0], dense.shape[1]
+    pieces, out = refs[:n_col], refs[n_col]
+    turned = [piece[...].astype(F32).T.astype(BF16) for piece in pieces]
+    for s in range(n_src // 2):
+        total = jnp.dot(turned[0], dense[2 * s + parity, 0], preferred_element_type=F32)
+        for t in range(1, n_col):
+            total = total + jnp.dot(turned[t], dense[2 * s + parity, t], preferred_element_type=F32)
+        out[s] = total.T.astype(BF16)
+
+
+def backward(dense, parity, pieces):
+    n_src, n_col, side, _ = dense.shape
+    feats = pieces[0].shape[1]
+    n_z = n_src // 2
+    return pl.pallas_call(
+        functools.partial(backward_kernel, parity),
+        out_shape=jax.ShapeDtypeStruct((n_z, side, feats), BF16),
+        in_specs=[vmem()] * (1 + n_col),
+        out_specs=vmem(),
+        compiler_params=params(24),
+        cost_estimate=pl.CostEstimate(
+            flops=2 * n_z * n_col * side * side * feats,
+            bytes_accessed=2 * n_z * n_col * side * side,
+            transcendentals=0,
+        ),
+        name="backward",
+    )(resident(dense), *pieces)
+
+
+def densify_stream_kernel(
     dims, info, rows, cols, count, tiles, out, buffer, head, following, sems
 ):
     n_z, n_col, blocks, slots, groups = dims
@@ -40,7 +206,6 @@
     def _():
         for g in range(groups):
             copy(g).start()
-        z, core, c = info[0], info[1], info[2]
 
         def clear(i, carry):
             head[i] = slots
@@ -52,13 +217,7 @@
 
         def link(slot, carry):
             block_row, block_col = rows[0, 0, slot], cols[0, 0, slot]
-            source, owner = block_col // blocks, block_row // blocks
-            shift = z - source // 2
-            shift = jnp.where(shift < 0, shift + n_z, shift)
-            j = 2 * shift + ((source + core) & 1)
-            t = c - owner
-            t = jnp.where(t < 0, t + n_col, t)
-            place = ((j * n_col + t) * blocks + block_row % blocks) * blocks + block_col % blocks
+            place = place_of((n_z, n_col, blocks), info, block_row, block_col)
             following[slot] = head[place]
             head[place] = slot
             return carry
@@ -96,14 +255,14 @@
     lax.fori_loop(0, per_chunk, fill, 0)
 
 
-def densify(info, rows, cols, count, tiles, n_z, n_col, blocks):
+def densify_stream(info, rows, cols, count, tiles, n_z, n_col, blocks):
     slots, tile = tiles.shape[0], tiles.shape[1]
     n_src = 2 * n_z
     groups = 8
     side = blocks * tile
     shape = (n_src, n_col, side, side)
     return pl.pallas_call(
-        functools.partial(densify_kernel, (n_z, n_col, blocks, slots, groups)),
+        functools.partial(densify_stream_kernel, (n_z, n_col, blocks, slots, groups)),
         grid=(n_src,),
         out_shape=jax.ShapeDtypeStruct(shape, BF16),
         in_specs=[smem(), smem(), smem(), smem(), pl.BlockSpec(memory_space=pl.ANY)],
@@ -122,7 +281,7 @@
     )(info, rows, cols, count, tiles)
 
 
-def forward_kernel(first, a, x0, x1, *rest):
+def forward_stream_kernel(first, a, x0, x1, *rest):
 
     j = pl.program_id(1)
 
@@ -138,13 +297,13 @@
         rest[-1][...] += jnp.dot(a[0, 0], x1[...], preferred_element_type=F32)
 
 
-def forward(dense, shift, x0, x1, total):
+def forward_stream(dense, shift, x0, x1, total):
     _, n_col, side, _ = dense.shape
     feats = x0.shape[1]
     first = total is None
     block = pl.BlockSpec((side, feats), lambda t, j: (t, 0))
     return pl.pallas_call(
-        functools.partial(forward_kernel, first),
+        functools.partial(forward_stream_kernel, first),
         grid=(n_col, 2),
         out_shape=jax.ShapeDtypeStruct((n_col * side, feats), F32),
         in_specs=[
@@ -236,7 +395,7 @@
     )(info, weights, cot_own, cot_other, *own, *other)
 
 
-def backward_kernel(n_col, a, *refs):
+def backward_stream_kernel(n_col, a, *refs):
     pieces, out, turned = refs[:n_col], refs[n_col], refs[n_col + 1]
 
     @pl.when(pl.program_id(0) == 0)
@@ -250,12 +409,12 @@
     out[0] = total.T.astype(BF16)
 
 
-def backward(dense, parity, pieces):
+def backward_stream(dense, parity, pieces):
     n_src, n_col, side, _ = dense.shape
     feats = pieces[0].shape[1]
     n_z = n_src // 2
     return pl.pallas_call(
-        functools.partial(backward_kernel, n_col),
+        functools.partial(backward_stream_kernel, n_col),
         grid=(n_z,),
         out_shape=jax.ShapeDtypeStruct((n_z, side, feats), BF16),
         in_specs=[pl.BlockSpec((1, n_col, side, side), lambda s: (2 * s + parity, 0, 0, 0))]
@@ -303,7 +462,7 @@
         return lax.ppermute(v, "row", [(i, i ^ 1) for i in range(n_row)])
 
     def along_z(v, s):
-        return lax.ppermute(v, "row", [(i, (i + 2 * s) % n_row) for i in range(n_row)])
+        return lax.ppermute(v, "row", [(i, i ^ (2 * s)) for i in range(n_row)])
 
     def other_feat(v):
         return lax.ppermute(v, "feat", [(0, 1), (1, 0)])
@@ -316,16 +475,32 @@
         return lax.ppermute(v, ("col", "feat"), pairs)
 
     same = [features] + [along_z(features, s) for s in range(1, n_z)]
-    cross = [sibling(v) for v in same]
     cot_other = other_feat(cotangent)
-
-    dense = densify(
-        info, tile_rows, tile_cols, tile_count, tile_values[0, 0], n_z, n_col, blocks
-    )
-    total = None
-    for s in range(n_z):
-        total = forward(dense, s, same[s], cross[s], total)
-    parts = total.astype(BF16).reshape(n_col, nodes, half)
+    tiles = tile_values[0, 0]
+    cell = (info, tile_rows, tile_cols, tile_count, tiles, n_z, n_col, blocks)
+    if 2 * n_z * n_col * (blocks * tile) ** 2 <= 8 * MIB:
+        dense = densify(*cell)
+        same = [features] + hold(same[1:], dense)
+        cross = [sibling(v) for v in same]
+        near, far = range(0, n_z // 2), range(n_z // 2, n_z)
+        totals = forward(
+            dense,
+            [2 * s + k for s in near for k in range(2)],
+            [v for s in near for v in (same[s], cross[s])],
+            (),
+            False,
+        )
+        totals = forward(dense, [2 * s for s in far], [same[s] for s in far], totals, False)
+        parts = forward(dense, [2 * s + 1 for s in far], [cross[s] for s in far], totals, True)
+        back_of = backward
+    else:
+        cross = [sibling(v) for v in same]
+        dense = densify_stream(*cell)
+        total = None
+        for s in range(n_z):
+            total = forward_stream(dense, s, same[s], cross[s], total)
+        parts = total.astype(BF16).reshape(n_col, nodes, half)
+        back_of = backward_stream
 
     own = [parts[0]] + [to_group(parts[t], -t, 0) for t in range(1, n_col)]
     other = [to_group(parts[t], -t, 1) for t in range(n_col)]
@@ -338,13 +513,13 @@
     ]
     gathered = [along_z(term, s) for s in range(1, n_z)]
 
-    odd = backward(dense, 1, pieces)
+    odd = back_of(dense, 1, pieces)
     arrived = sibling(odd)
-    even = backward(dense, 0, pieces)
+    even = back_of(dense, 0, pieces)
     sums = pair_sums(even, arrived)
     back = sums[0].astype(F32)
     for s in range(1, n_z):
-        back = back + along_z(sums[s], -s).astype(F32)
+        back = back + along_z(sums[s], s).astype(F32)
 
     grad = term.astype(F32)
     for v in gathered:

time: 94.5 us -> 66.1 us (0.70)
  Pallas kernels: 34.7 us -> 13.9 us
  starting transfers between devices: 30.1 us -> 22.4 us
  local copies, waits for them, and re-layouts: 1.39 us -> 3.4 us
  waiting for transfers between devices: 25 us -> 23.1 us
    pallas_call x7, Pallas kernels: 32.6 us -> 11.8 us  [the longest x1 7.47 us: densify(): pl.pallas_call(functools.partial(densify_kernel, (n_z, n_col, blocks), gr...]
    ppermute x3, starting transfers between devices: 7.58 us -> 3.55 us  [to_group(): return lax.ppermute(v, ('col', 'feat'), pairs)]
    ppermute x9, starting transfers between devices: 18 us -> 14.6 us  [along_z(): return lax.ppermute(v, 'row', [(i, i ^ 2 * s) for i in range(n_row)])]
    ppermute x9, waiting for transfers between devices: 16.8 us -> 13.8 us  [along_z(): return lax.ppermute(v, 'row', [(i, i ^ 2 * s) for i in range(n_row)])]
    unnamed x10 -> x12, local copies, waits for them, and re-layouts: 1.37 us -> 3.4 us
  transfers between devices with their start and end apart: 22 -> 22, of which waited for: 9 -> 11; matrix products, arithmetic and copies ran while one was open for 1% -> 2% of each run, Pallas kernels for 35% -> 18%
where the time goes in v2:
time: 66.1 us; the launch traced here: 66.4 us
  waiting for transfers between devices  23.1 us (35%)
  starting transfers between devices  22.4 us (34%)
  Pallas kernels  13.9 us (21%)
  local copies, waits for them, and re-layouts  3.4 us (5%)
  other arithmetic  2.07 us (3%)
  between operations  1.49 us (2%)
    ppermute x9, starting transfers between devices, along_z(): return lax.ppermute(v, 'row', [(i, i ^ 2 * s) for i in range(n_row)])  14.6 us
    ppermute x9, waiting for transfers between devices, along_z(): return lax.ppermute(v, 'row', [(i, i ^ 2 * s) for i in range(n_row)])  13.8 us
    pallas_call x1, Pallas kernels, densify(): pl.pallas_call(functools.partial(densify_kernel, (n_z, n_col, blocks), gr...  7.47 us
    ppermute x3, waiting for transfers between devices, to_group(): return lax.ppermute(v, ('col', 'feat'), pairs)  5.89 us
    ppermute x3, starting transfers between devices, to_group(): return lax.ppermute(v, ('col', 'feat'), pairs)  3.55 us
    unnamed x12, local copies, waits for them, and re-layouts  3.4 us
    ppermute x1, waiting for transfers between devices, shards(): lax.ppermute(grad, 'col', [(i, (i + t) % n_col) for i in range(n_col)])  2.9 us
    pallas_call x3, Pallas kernels, forward(): pl.pallas_call(functools.partial(forward_kernel, places, last), out_shape...  2.69 us
  transfers between devices with their start and end apart: 22, of which 11 were waited for; matrix products, arithmetic and copies ran while one was open for 2% of the time, Pallas kernels for 18%

profile of v2, /device:TPU:0, one launch (start us, length us, event | category | flops | bytes accessed | tf_op | source)
XLA Modules:
  0.0 66.4 jit_solution(15054642044603867936)
XLA Ops:
  0.6 3.1 %collective-permute-start.1 = (bf16[512,128]{1,0:T(8,128)(2,1)}, bf16[512,128]{1,0:T(8,128)(2,1)S(1)}, u32[]{:S(2)}, u32[]{:S(2)}) collective-permute-start(bf16[512,128]{1,0:T(8,128)(2,1)} %refs_0_.1), channel_id=1, source_target_pairs={{0,8},{4,12},{8,0},{12,4},{16,24},{20,28},{24,16},{28,20},{1,9},{5... | collective-permute-start | bytes 393224 | tf_op jit(solution)/shard_map/ppermute | solution.py:465
  3.7 2.6 %collective-permute-start.2 = (bf16[512,128]{1,0:T(8,128)(2,1)}, bf16[512,128]{1,0:T(8,128)(2,1)S(1)}, u32[]{:S(2)}, u32[]{:S(2)}) collective-permute-start(bf16[512,128]{1,0:T(8,128)(2,1)} %refs_0_.1), channel_id=1, source_target_pairs={{0,16},{4,20},{8,24},{12,28},{16,0},{20,4},{24,8},{28,12},{1,17},{... | collective-permute-start | bytes 393224 | tf_op jit(solution)/shard_map/ppermute | solution.py:465
  6.3 0.0 collective-permute-start.3
  6.3 0.0 collective-permute-start.6
  7.0 0.6 pad_add_fusion.info
  7.6 7.5 %densify.1.refs_3_.dense = bf16[8,2,512,512]{3,2,1,0:T(8,128)(2,1)S(1)} custom-call(s32[4]{0:T(128)} %pad_add_fusion.info, s32[1,1,256]{2,1,0:T(1,128)} %rows.1, s32[1,1,256]{2,1,0:T(1,128)} %cols.1, s32[1,1]{1,0:T(1,128)S(6)} %copy.16.count, bf16[256,128,128]{2,1,0:T(8,128)(2,1)} %bitcast.5), custom_call_target="tpu_custom_call" | custom-call | bytes 25165824 | tf_op jit(solution)/shard_map/densify/pallas_call | solution.py:94
  15.1 0.0 copy-start
  15.1 0.0 copy-start.4
  15.1 0.0 copy-start.2
  15.1 0.0 collective-permute-done.1.refs_0_
  15.1 1.8 %collective-permute-done.2.refs_1_ = bf16[512,128]{1,0:T(8,128)(2,1)S(1)} collective-permute-done((bf16[512,128]{1,0:T(8,128)(2,1)}, bf16[512,128]{1,0:T(8,128)(2,1)S(1)}, u32[]{:S(2)}, u32[]{:S(2)}) %collective-permute-start.2) | collective-permute-done | bytes 131104 | tf_op jit(solution)/shard_map/ppermute | solution.py:465
  16.9 0.0 collective-permute-done.3.refs_2_
  16.9 0.0 collective-permute-start.7
  16.9 0.5 collective-permute-start.4
  17.4 0.1 collective-permute-start.5
  17.4 0.0 copy-done.4
  17.5 1.5 %collective-permute-start = (bf16[512,128]{1,0:T(8,128)(2,1)S(1)}, bf16[512,128]{1,0:T(8,128)(2,1)S(1)}, u32[]{:S(2)}, u32[]{:S(2)}) collective-permute-start(bf16[512,128]{1,0:T(8,128)(2,1)S(1)} %copy-done.4), channel_id=1, source_target_pairs={{0,1},{1,0},{2,3},{3,2},{4,5},{5,4},{6,7},{7,6},{8,9},{9,8},{10,11... | collective-permute-start | bytes 393224 | tf_op jit(solution)/shard_map/ppermute | solution.py:468
  18.9 0.0 collective-permute-done.6.refs_1_
  18.9 0.0 collective-permute-done.7.refs_3_
  19.0 0.0 copy-done.2
  19.0 1.2 %forward.3 = (f32[512,128]{1,0:T(8,128)S(1)}, f32[512,128]{1,0:T(8,128)S(1)}) custom-call(bf16[8,2,512,512]{3,2,1,0:T(8,128)(2,1)S(1)} %densify.1.refs_3_.dense, bf16[512,128]{1,0:T(8,128)(2,1)S(1)} %copy-done.2, bf16[512,128]{1,0:T(8,128)(2,1)S(1)} %collective-permute-done.6.refs_1_, bf16[512,128]{1,0:T(8,128)(2,1)S(1)} %get-tuple-element.22.refs_2_, ...), custom_call_target="tpu_custom_call" | custom-call | flops 536870912 | bytes 4194304 | tf_op jit(solution)/shard_map/forward/pallas_call | solution.py:148
  20.2 0.0 copy-start.3
  20.2 0.0 copy-start.5
  20.2 0.7 %forward.4 = (f32[512,128]{1,0:T(8,128)S(1)}, f32[512,128]{1,0:T(8,128)S(1)}) custom-call(bf16[8,2,512,512]{3,2,1,0:T(8,128)(2,1)S(1)} %densify.1.refs_3_.dense, bf16[512,128]{1,0:T(8,128)(2,1)S(1)} %get-tuple-element.20.refs_0_, bf16[512,128]{1,0:T(8,128)(2,1)S(1)} %get-tuple-element.21.refs_1_, f32[512,128]{1,0:T(8,128)S(1)} %get-tuple-element.23.refs_2_, ...), custom_call_target="tpu_custom_call" | custom-call | flops 268435456 | bytes 2097152 | tf_op jit(solution)/shard_map/forward/pallas_call | solution.py:148
  21.0 0.0 collective-permute-done.4.refs_0_
  21.0 0.0 collective-permute-done.5.refs_1_
  21.0 0.7 %forward.5 = (bf16[512,128]{1,0:T(8,128)(2,1)S(1)}, bf16[512,128]{1,0:T(8,128)(2,1)S(1)}) custom-call(bf16[8,2,512,512]{3,2,1,0:T(8,128)(2,1)S(1)} %densify.1.refs_3_.dense, bf16[512,128]{1,0:T(8,128)(2,1)S(1)} %collective-permute-done.4.refs_0_, bf16[512,128]{1,0:T(8,128)(2,1)S(1)} %collective-permute-done.5.refs_1_, ...), custom_call_target="tpu_custom_call" | custom-call | flops 268435456 | bytes 2097152 | tf_op jit(solution)/shard_map/forward/pallas_call | solution.py:148
  21.7 1.8 %collective-permute-start.10 = (bf16[512,128]{1,0:T(8,128)(2,1)S(1)}, bf16[512,128]{1,0:T(8,128)(2,1)S(1)}, u32[]{:S(2)}, u32[]{:S(2)}) collective-permute-start(bf16[512,128]{1,0:T(8,128)(2,1)S(1)} %get-tuple-element.28), channel_id=1, source_target_pairs={{0,3},{1,2},{2,1},{3,0},{4,7},{5,6},{6,5},{7,4},{8,11},{9,10},{10,... | collective-permute-start | bytes 393224 | tf_op jit(solution)/shard_map/ppermute | solution.py:475
  23.5 0.5 collective-permute-start.8
  24.0 1.3 %collective-permute-start.9 = (bf16[512,128]{1,0:T(8,128)(2,1)S(1)}, bf16[512,128]{1,0:T(8,128)(2,1)S(1)}, u32[]{:S(2)}, u32[]{:S(2)}) collective-permute-start(bf16[512,128]{1,0:T(8,128)(2,1)S(1)} %get-tuple-element.27.refs_0_), channel_id=1, source_target_pairs={{0,1},{1,0},{2,3},{3,2},{4,5},{5,4},{6,7},{7,6},{8,9},{9,8},{10,11... | collective-permute-start | bytes 393224 | tf_op jit(solution)/shard_map/ppermute | solution.py:475
  25.3 0.0 collective-permute-done.cot_other
  25.3 3.7 %collective-permute-done.10.refs_3_ = bf16[512,128]{1,0:T(8,128)(2,1)S(1)} collective-permute-done((bf16[512,128]{1,0:T(8,128)(2,1)S(1)}, bf16[512,128]{1,0:T(8,128)(2,1)S(1)}, u32[]{:S(2)}, u32[]{:S(2)}) %collective-permute-start.10) | collective-permute-done | bytes 131104 | tf_op jit(solution)/shard_map/ppermute | solution.py:475
  29.0 2.0 %collective-permute-done.8.refs_1_ = bf16[512,128]{1,0:T(8,128)(2,1)S(1)} collective-permute-done((bf16[512,128]{1,0:T(8,128)(2,1)S(1)}, bf16[512,128]{1,0:T(8,128)(2,1)S(1)}, u32[]{:S(2)}, u32[]{:S(2)}) %collective-permute-start.8) | collective-permute-done | bytes 131104 | tf_op jit(solution)/shard_map/ppermute | solution.py:475
  31.1 0.1 collective-permute-done.9.refs_2_
  31.2 0.0 copy-done.3
  31.2 1.9 %middle.1 = (bf16[512,128]{1,0:T(8,128)(2,1)}, bf16[512,128]{1,0:T(8,128)(2,1)S(1)}, bf16[64,256]{1,0:T(8,128)(2,1)S(1)}, bf16[64,256]{1,0:T(8,128)(2,1)S(1)}) custom-call(s32[4]{0:T(128)S(1)} %copy-done.5, bf16[256,256]{1,0:T(8,128)(2,1)S(1)} %copy-done.3, bf16[512,128]{1,0:T(8,128)(2,1)S(1)} %copy-done.4, ...), custom_call_target="tpu_custom_call" | custom-call | flops 134217728 | bytes 1048576 | tf_op jit(solution)/shard_map/middle/pallas_call | solution.py:380
  33.1 0.0 collective-permute-start.16
  33.1 0.9 %collective-permute-start.11 = (bf16[512,128]{1,0:T(8,128)(2,1)S(1)}, bf16[512,128]{1,0:T(8,128)(2,1)S(1)}, u32[]{:S(2)}, u32[]{:S(2)}) collective-permute-start(bf16[512,128]{1,0:T(8,128)(2,1)S(1)} %get-tuple-element.30.refs_0_), channel_id=1, source_target_pairs={{0,2},{2,0},{1,3},{3,1},{4,6},{6,4},{5,7},{7,5},{8,10},{10,8},{9,1... | collective-permute-start | bytes 393224 | tf_op jit(solution)/shard_map/ppermute | solution.py:511
  34.0 0.3 collective-permute-done.16
  34.3 2.0 %collective-permute-start.17 = (bf16[64,256]{1,0:T(8,128)(2,1)S(1)}, bf16[64,256]{1,0:T(8,128)(2,1)S(1)}, u32[]{:S(2)}, u32[]{:S(2)}) collective-permute-start(bf16[64,256]{1,0:T(8,128)(2,1)S(1)} %add_convert_fusion.3), channel_id=1, source_target_pairs={{0,8},{4,12},{8,0},{12,4},{16,24},{20,28},{24,16},{28,20},{1,9},{5... | collective-permute-start | bytes 98312 | tf_op jit(solution)/shard_map/ppermute | solution.py:465
  36.4 2.1 %collective-permute-start.18 = (bf16[64,256]{1,0:T(8,128)(2,1)S(1)}, bf16[64,256]{1,0:T(8,128)(2,1)S(1)}, u32[]{:S(2)}, u32[]{:S(2)}) collective-permute-start(bf16[64,256]{1,0:T(8,128)(2,1)S(1)} %add_convert_fusion.3), channel_id=1, source_target_pairs={{0,16},{4,20},{8,24},{12,28},{16,0},{20,4},{24,8},{28,12},{1,17},{... | collective-permute-start | bytes 98312 | tf_op jit(solution)/shard_map/ppermute | solution.py:465
  38.5 0.4 collective-permute-start.19
  38.8 0.2 collective-permute-done.11.refs_1_
  39.0 0.8 %backward.3 = bf16[4,512,128]{2,1,0:T(8,128)(2,1)S(1)} custom-call(bf16[8,2,512,512]{3,2,1,0:T(8,128)(2,1)S(1)} %densify.1.refs_3_.dense, bf16[512,128]{1,0:T(8,128)(2,1)S(1)} %get-tuple-element.30.refs_0_, bf16[512,128]{1,0:T(8,128)(2,1)S(1)} %collective-permute-done.11.refs_1_), custom_call_target="tpu_custom_call" | custom-call | flops 536870912 | bytes 4194304 | tf_op jit(solution)/shard_map/backward/pallas_call | solution.py:178
  39.9 0.1 collective-permute-start.12
  40.0 0.0 collective-permute-done.17
  40.0 1.8 %collective-permute-done.18 = bf16[64,256]{1,0:T(8,128)(2,1)S(1)} collective-permute-done((bf16[64,256]{1,0:T(8,128)(2,1)S(1)}, bf16[64,256]{1,0:T(8,128)(2,1)S(1)}, u32[]{:S(2)}, u32[]{:S(2)}) %collective-permute-start.18) | collective-permute-done | bytes 32800 | tf_op jit(solution)/shard_map/ppermute | solution.py:465
  41.8 2.4 %collective-permute-done.19 = bf16[64,256]{1,0:T(8,128)(2,1)S(1)} collective-permute-done((bf16[64,256]{1,0:T(8,128)(2,1)S(1)}, bf16[64,256]{1,0:T(8,128)(2,1)S(1)}, u32[]{:S(2)}, u32[]{:S(2)}) %collective-permute-start.19) | collective-permute-done | bytes 32800 | tf_op jit(solution)/shard_map/ppermute | solution.py:465
  44.2 1.1 %collective-permute-start.20 = (bf16[64,256]{1,0:T(8,128)(2,1)S(1)}, bf16[64,256]{1,0:T(8,128)(2,1)S(1)}, u32[]{:S(2)}, u32[]{:S(2)}) collective-permute-start(bf16[64,256]{1,0:T(8,128)(2,1)S(1)} %add_convert_fusion.2), channel_id=1, source_target_pairs={{0,2},{2,0},{1,3},{3,1},{4,6},{6,4},{5,7},{7,5},{8,10},{10,8},{9,1... | collective-permute-start | bytes 98312 | tf_op jit(solution)/shard_map/ppermute | solution.py:530
  45.3 2.9 %collective-permute-done.20 = bf16[64,256]{1,0:T(8,128)(2,1)S(1)} collective-permute-done((bf16[64,256]{1,0:T(8,128)(2,1)S(1)}, bf16[64,256]{1,0:T(8,128)(2,1)S(1)}, u32[]{:S(2)}, u32[]{:S(2)}) %collective-permute-start.20) | collective-permute-done | bytes 32800 | tf_op jit(solution)/shard_map/ppermute | solution.py:530
  48.2 0.1 collective-permute-start.21
  48.3 3.4 %copy-done.1 = bf16[8,2,512,512]{3,2,1,0:T(8,128)(2,1)S(1)} copy-done((bf16[8,2,512,512]{3,2,1,0:T(8,128)(2,1)S(1)}, bf16[8,2,512,512]{3,2,1,0:T(8,128)(2,1)}, u32[]{:S(2)}) %copy-start.1) | copy-done | bytes 8388632
  51.7 0.8 %backward.2.own = bf16[4,512,128]{2,1,0:T(8,128)(2,1)S(1)} custom-call(bf16[8,2,512,512]{3,2,1,0:T(8,128)(2,1)S(1)} %copy-done.1, bf16[512,128]{1,0:T(8,128)(2,1)S(1)} %get-tuple-element.30.refs_0_, bf16[512,128]{1,0:T(8,128)(2,1)S(1)} %collective-permute-done.11.refs_1_), custom_call_target="tpu_custom_call" | custom-call | flops 536870912 | bytes 4194304 | tf_op jit(solution)/shard_map/backward/pallas_call | solution.py:178
  52.5 0.0 collective-permute-done.12.arrived
  52.5 0.1 pair_sums.1
  52.7 0.1 collective-permute-start.13
  52.7 1.0 %collective-permute-start.14 = (bf16[512,128]{1,0:T(8,128)(2,1)S(1)}, bf16[512,128]{1,0:T(8,128)(2,1)S(1)}, u32[]{:S(2)}, u32[]{:S(2)}) collective-permute-start(bf16[512,128]{1,0:T(8,128)(2,1)S(1)} %get-tuple-element.33), channel_id=1, source_target_pairs={{0,16},{4,20},{8,24},{12,28},{16,0},{20,4},{24,8},{28,12},{1,17},{... | collective-permute-start | bytes 393224 | tf_op jit(solution)/shard_map/ppermute | solution.py:465
  53.8 3.4 %collective-permute-start.15 = (bf16[512,128]{1,0:T(8,128)(2,1)S(1)}, bf16[512,128]{1,0:T(8,128)(2,1)S(1)}, u32[]{:S(2)}, u32[]{:S(2)}) collective-permute-start(bf16[512,128]{1,0:T(8,128)(2,1)S(1)} %get-tuple-element.34), channel_id=1, source_target_pairs={{0,24},{4,28},{8,16},{12,20},{16,8},{20,12},{24,0},{28,4},{1,25},{... | collective-permute-start | bytes 393224 | tf_op jit(solution)/shard_map/ppermute | solution.py:465
  57.1 0.0 collective-permute-done.21
  57.1 0.7 %convert_multiply_fusion = f32[128,256]{1,0:T(8,128)} fusion(bf16[64,256]{1,0:T(8,128)(2,1)S(1)} %get-tuple-element.38, bf16[64,256]{1,0:T(8,128)(2,1)S(1)} %get-tuple-element.37), kind=kLoop, calls=%fused_computation.1 | loop fusion | flops 163840 | bytes 196608 | tf_op jit(solution)/shard_map/mul | solution.py:537
  57.8 2.1 %collective-permute-done.13 = bf16[512,128]{1,0:T(8,128)(2,1)S(1)} collective-permute-done((bf16[512,128]{1,0:T(8,128)(2,1)S(1)}, bf16[512,128]{1,0:T(8,128)(2,1)S(1)}, u32[]{:S(2)}, u32[]{:S(2)}) %collective-permute-start.13) | collective-permute-done | bytes 131104 | tf_op jit(solution)/shard_map/ppermute | solution.py:465
  59.9 5.8 %collective-permute-done.14 = bf16[512,128]{1,0:T(8,128)(2,1)S(1)} collective-permute-done((bf16[512,128]{1,0:T(8,128)(2,1)S(1)}, bf16[512,128]{1,0:T(8,128)(2,1)S(1)}, u32[]{:S(2)}, u32[]{:S(2)}) %collective-permute-start.14) | collective-permute-done | bytes 131104 | tf_op jit(solution)/shard_map/ppermute | solution.py:465
  65.7 0.0 collective-permute-done.15
  65.7 0.7 %add_convert_fusion = bf16[512,128]{1,0:T(8,128)(2,1)} fusion(bf16[512,128]{1,0:T(8,128)(2,1)S(1)} %collective-permute-done.15, bf16[512,128]{1,0:T(8,128)(2,1)S(1)} %collective-permute-done.14, bf16[512,128]{1,0:T(8,128)(2,1)S(1)} %collective-permute-done.13, bf16[512,128]{1,0:T(8,128)(2,1)S(1)} %get-tuple-element.31), kind=kLoop, calls=%fused_computation | loop fusion | flops 524288 | bytes 655360 | tf_op jit(solution)/shard_map/convert_element_type | solution.py:538
  (8 shorter events, 0.1 us)
Async XLA Ops:
  0.6 14.5 %collective-permute-start.1 = (bf16[512,128]{1,0:T(8,128)(2,1)}, bf16[512,128]{1,0:T(8,128)(2,1)S(1)}, u32[]{:S(2)}, u32[]{:S(2)}) collective-permute-start(bf16[512,128]{1,0:T(8,128)(2,1)} %refs_0_.1), channel_id=1, source_target_pairs={{0,8},{4,12},{8,0},{12,4},{16,24},{20,28},{24,16},{28,20},{1,9},{5... | collective-permute-start | bytes 393224 | tf_op jit(solution)/shard_map/ppermute | solution.py:465
  3.7 13.2 %collective-permute-start.2 = (bf16[512,128]{1,0:T(8,128)(2,1)}, bf16[512,128]{1,0:T(8,128)(2,1)S(1)}, u32[]{:S(2)}, u32[]{:S(2)}) collective-permute-start(bf16[512,128]{1,0:T(8,128)(2,1)} %refs_0_.1), channel_id=1, source_target_pairs={{0,16},{4,20},{8,24},{12,28},{16,0},{20,4},{24,8},{28,12},{1,17},{... | collective-permute-start | bytes 393224 | tf_op jit(solution)/shard_map/ppermute | solution.py:465
  6.3 10.6 %collective-permute-start.3 = (bf16[512,128]{1,0:T(8,128)(2,1)}, bf16[512,128]{1,0:T(8,128)(2,1)S(1)}, u32[]{:S(2)}, u32[]{:S(2)}) collective-permute-start(bf16[512,128]{1,0:T(8,128)(2,1)} %refs_0_.1), channel_id=1, source_target_pairs={{0,24},{4,28},{8,16},{12,20},{16,8},{20,12},{24,0},{28,4},{1,25},{... | collective-permute-start | bytes 393224 | tf_op jit(solution)/shard_map/ppermute | solution.py:465
  6.3 12.6 %collective-permute-start.6 = (bf16[512,128]{1,0:T(8,128)(2,1)}, bf16[512,128]{1,0:T(8,128)(2,1)S(1)}, u32[]{:S(2)}, u32[]{:S(2)}) collective-permute-start(bf16[512,128]{1,0:T(8,128)(2,1)} %refs_0_.1), channel_id=1, source_target_pairs={{0,4},{4,0},{8,12},{12,8},{16,20},{20,16},{24,28},{28,24},{1,5},{5... | collective-permute-start | bytes 393224 | tf_op jit(solution)/shard_map/ppermute | solution.py:462
  15.1 24.0 %copy-start = (bf16[8,2,512,512]{3,2,1,0:T(8,128)(2,1)}, bf16[8,2,512,512]{3,2,1,0:T(8,128)(2,1)S(1)}, u32[]{:S(2)}) copy-start(bf16[8,2,512,512]{3,2,1,0:T(8,128)(2,1)S(1)} %densify.1.refs_3_.dense) | copy-start | bytes 25165828
  15.1 2.4 %copy-start.4 = (bf16[512,128]{1,0:T(8,128)(2,1)S(1)}, bf16[512,128]{1,0:T(8,128)(2,1)}, u32[]{:S(2)}) copy-start(bf16[512,128]{1,0:T(8,128)(2,1)} %cot_own.1) | copy-start | bytes 393220
  15.1 3.9 %copy-start.2 = (bf16[512,128]{1,0:T(8,128)(2,1)S(1)}, bf16[512,128]{1,0:T(8,128)(2,1)}, u32[]{:S(2)}) copy-start(bf16[512,128]{1,0:T(8,128)(2,1)} %refs_0_.1) | copy-start | bytes 393220
  16.9 2.1 %collective-permute-start.7 = (bf16[512,128]{1,0:T(8,128)(2,1)S(1)}, bf16[512,128]{1,0:T(8,128)(2,1)S(1)}, u32[]{:S(2)}, u32[]{:S(2)}) collective-permute-start(bf16[512,128]{1,0:T(8,128)(2,1)S(1)} %get-tuple-element.22.refs_2_), channel_id=1, source_target_pairs={{0,4},{4,0},{8,12},{12,8},{16,20},{20,16},{24,28},{28,24},{1,5},{5... | collective-permute-start | bytes 393224 | tf_op jit(solution)/shard_map/ppermute | solution.py:462
  16.9 4.1 %collective-permute-start.4 = (bf16[512,128]{1,0:T(8,128)(2,1)S(1)}, bf16[512,128]{1,0:T(8,128)(2,1)S(1)}, u32[]{:S(2)}, u32[]{:S(2)}) collective-permute-start(bf16[512,128]{1,0:T(8,128)(2,1)S(1)} %get-tuple-element.20.refs_0_), channel_id=1, source_target_pairs={{0,4},{4,0},{8,12},{12,8},{16,20},{20,16},{24,28},{28,24},{1,5},{5... | collective-permute-start | bytes 393224 | tf_op jit(solution)/shard_map/ppermute | solution.py:462
  17.4 3.6 %collective-permute-start.5 = (bf16[512,128]{1,0:T(8,128)(2,1)S(1)}, bf16[512,128]{1,0:T(8,128)(2,1)S(1)}, u32[]{:S(2)}, u32[]{:S(2)}) collective-permute-start(bf16[512,128]{1,0:T(8,128)(2,1)S(1)} %get-tuple-element.21.refs_1_), channel_id=1, source_target_pairs={{0,4},{4,0},{8,12},{12,8},{16,20},{20,16},{24,28},{28,24},{1,5},{5... | collective-permute-start | bytes 393224 | tf_op jit(solution)/shard_map/ppermute | solution.py:462
  17.5 7.8 %collective-permute-start = (bf16[512,128]{1,0:T(8,128)(2,1)S(1)}, bf16[512,128]{1,0:T(8,128)(2,1)S(1)}, u32[]{:S(2)}, u32[]{:S(2)}) collective-permute-start(bf16[512,128]{1,0:T(8,128)(2,1)S(1)} %copy-done.4), channel_id=1, source_target_pairs={{0,1},{1,0},{2,3},{3,2},{4,5},{5,4},{6,7},{7,6},{8,9},{9,8},{10,11... | collective-permute-start | bytes 393224 | tf_op jit(solution)/shard_map/ppermute | solution.py:468
  20.2 11.0 %copy-start.3 = (bf16[256,256]{1,0:T(8,128)(2,1)S(1)}, bf16[256,256]{1,0:T(8,128)(2,1)}, u32[]{:S(2)}) copy-start(bf16[256,256]{1,0:T(8,128)(2,1)} %weights.1) | copy-start | bytes 393220
  20.2 10.9 %copy-start.5 = (s32[4]{0:T(128)S(1)}, s32[4]{0:T(128)}, u32[]{:S(2)}) copy-start(s32[4]{0:T(128)} %pad_add_fusion.info) | copy-start | bytes 52
  21.7 7.3 %collective-permute-start.10 = (bf16[512,128]{1,0:T(8,128)(2,1)S(1)}, bf16[512,128]{1,0:T(8,128)(2,1)S(1)}, u32[]{:S(2)}, u32[]{:S(2)}) collective-permute-start(bf16[512,128]{1,0:T(8,128)(2,1)S(1)} %get-tuple-element.28), channel_id=1, source_target_pairs={{0,3},{1,2},{2,1},{3,0},{4,7},{5,6},{6,5},{7,4},{8,11},{9,10},{10,... | collective-permute-start | bytes 393224 | tf_op jit(solution)/shard_map/ppermute | solution.py:475
  23.5 7.6 %collective-permute-start.8 = (bf16[512,128]{1,0:T(8,128)(2,1)S(1)}, bf16[512,128]{1,0:T(8,128)(2,1)S(1)}, u32[]{:S(2)}, u32[]{:S(2)}) collective-permute-start(bf16[512,128]{1,0:T(8,128)(2,1)S(1)} %get-tuple-element.28), channel_id=1, source_target_pairs={{0,2},{1,3},{2,0},{3,1},{4,6},{5,7},{6,4},{7,5},{8,10},{9,11},{10,... | collective-permute-start | bytes 393224 | tf_op jit(solution)/shard_map/ppermute | solution.py:475
  24.0 7.2 %collective-permute-start.9 = (bf16[512,128]{1,0:T(8,128)(2,1)S(1)}, bf16[512,128]{1,0:T(8,128)(2,1)S(1)}, u32[]{:S(2)}, u32[]{:S(2)}) collective-permute-start(bf16[512,128]{1,0:T(8,128)(2,1)S(1)} %get-tuple-element.27.refs_0_), channel_id=1, source_target_pairs={{0,1},{1,0},{2,3},{3,2},{4,5},{5,4},{6,7},{7,6},{8,9},{9,8},{10,11... | collective-permute-start | bytes 393224 | tf_op jit(solution)/shard_map/ppermute | solution.py:475
  33.1 1.2 %collective-permute-start.16 = (bf16[64,256]{1,0:T(8,128)(2,1)S(1)}, bf16[64,256]{1,0:T(8,128)(2,1)S(1)}, u32[]{:S(2)}, u32[]{:S(2)}) collective-permute-start(bf16[64,256]{1,0:T(8,128)(2,1)S(1)} %get-tuple-element.36), channel_id=1, source_target_pairs={{0,4},{4,0},{8,12},{12,8},{16,20},{20,16},{24,28},{28,24},{1,5},{5... | collective-permute-start | bytes 98312 | tf_op jit(solution)/shard_map/ppermute | solution.py:462
  33.1 5.9 %collective-permute-start.11 = (bf16[512,128]{1,0:T(8,128)(2,1)S(1)}, bf16[512,128]{1,0:T(8,128)(2,1)S(1)}, u32[]{:S(2)}, u32[]{:S(2)}) collective-permute-start(bf16[512,128]{1,0:T(8,128)(2,1)S(1)} %get-tuple-element.30.refs_0_), channel_id=1, source_target_pairs={{0,2},{2,0},{1,3},{3,1},{4,6},{6,4},{5,7},{7,5},{8,10},{10,8},{9,1... | collective-permute-start | bytes 393224 | tf_op jit(solution)/shard_map/ppermute | solution.py:511
  34.3 5.6 %collective-permute-start.17 = (bf16[64,256]{1,0:T(8,128)(2,1)S(1)}, bf16[64,256]{1,0:T(8,128)(2,1)S(1)}, u32[]{:S(2)}, u32[]{:S(2)}) collective-permute-start(bf16[64,256]{1,0:T(8,128)(2,1)S(1)} %add_convert_fusion.3), channel_id=1, source_target_pairs={{0,8},{4,12},{8,0},{12,4},{16,24},{20,28},{24,16},{28,20},{1,9},{5... | collective-permute-start | bytes 98312 | tf_op jit(solution)/shard_map/ppermute | solution.py:465
  36.4 5.4 %collective-permute-start.18 = (bf16[64,256]{1,0:T(8,128)(2,1)S(1)}, bf16[64,256]{1,0:T(8,128)(2,1)S(1)}, u32[]{:S(2)}, u32[]{:S(2)}) collective-permute-start(bf16[64,256]{1,0:T(8,128)(2,1)S(1)} %add_convert_fusion.3), channel_id=1, source_target_pairs={{0,16},{4,20},{8,24},{12,28},{16,0},{20,4},{24,8},{28,12},{1,17},{... | collective-permute-start | bytes 98312 | tf_op jit(solution)/shard_map/ppermute | solution.py:465
  38.5 5.7 %collective-permute-start.19 = (bf16[64,256]{1,0:T(8,128)(2,1)S(1)}, bf16[64,256]{1,0:T(8,128)(2,1)S(1)}, u32[]{:S(2)}, u32[]{:S(2)}) collective-permute-start(bf16[64,256]{1,0:T(8,128)(2,1)S(1)} %add_convert_fusion.3), channel_id=1, source_target_pairs={{0,24},{4,28},{8,16},{12,20},{16,8},{20,12},{24,0},{28,4},{1,25},{... | collective-permute-start | bytes 98312 | tf_op jit(solution)/shard_map/ppermute | solution.py:465
  39.9 12.6 %collective-permute-start.12 = (bf16[4,512,128]{2,1,0:T(8,128)(2,1)S(1)}, bf16[4,512,128]{2,1,0:T(8,128)(2,1)S(1)}, u32[]{:S(2)}, u32[]{:S(2)}) collective-permute-start(bf16[4,512,128]{2,1,0:T(8,128)(2,1)S(1)} %backward.3), channel_id=1, source_target_pairs={{0,4},{4,0},{8,12},{12,8},{16,20},{20,16},{24,28},{28,24},{1,5},{5... | collective-permute-start | bytes 1572872 | tf_op jit(solution)/shard_map/ppermute | solution.py:462
  44.2 4.0 %collective-permute-start.20 = (bf16[64,256]{1,0:T(8,128)(2,1)S(1)}, bf16[64,256]{1,0:T(8,128)(2,1)S(1)}, u32[]{:S(2)}, u32[]{:S(2)}) collective-permute-start(bf16[64,256]{1,0:T(8,128)(2,1)S(1)} %add_convert_fusion.2), channel_id=1, source_target_pairs={{0,2},{2,0},{1,3},{3,1},{4,6},{6,4},{5,7},{7,5},{8,10},{10,8},{9,1... | collective-permute-start | bytes 98312 | tf_op jit(solution)/shard_map/ppermute | solution.py:530
  48.2 8.9 %collective-permute-start.21 = (bf16[64,256]{1,0:T(8,128)(2,1)S(1)}, bf16[64,256]{1,0:T(8,128)(2,1)S(1)}, u32[]{:S(2)}, u32[]{:S(2)}) collective-permute-start(bf16[64,256]{1,0:T(8,128)(2,1)S(1)} %add_convert_fusion.1), channel_id=1, source_target_pairs={{0,4},{4,0},{8,12},{12,8},{16,20},{20,16},{24,28},{28,24},{1,5},{5... | collective-permute-start | bytes 98312 | tf_op jit(solution)/shard_map/ppermute | solution.py:462
  48.3 3.4 %copy-start.1 = (bf16[8,2,512,512]{3,2,1,0:T(8,128)(2,1)S(1)}, bf16[8,2,512,512]{3,2,1,0:T(8,128)(2,1)}, u32[]{:S(2)}) copy-start(bf16[8,2,512,512]{3,2,1,0:T(8,128)(2,1)} %copy-done) | copy-start | bytes 25165828
  52.7 7.2 %collective-permute-start.13 = (bf16[512,128]{1,0:T(8,128)(2,1)S(1)}, bf16[512,128]{1,0:T(8,128)(2,1)S(1)}, u32[]{:S(2)}, u32[]{:S(2)}) collective-permute-start(bf16[512,128]{1,0:T(8,128)(2,1)S(1)} %get-tuple-element.32), channel_id=1, source_target_pairs={{0,8},{4,12},{8,0},{12,4},{16,24},{20,28},{24,16},{28,20},{1,9},{5... | collective-permute-start | bytes 393224 | tf_op jit(solution)/shard_map/ppermute | solution.py:465
  52.7 12.9 %collective-permute-start.14 = (bf16[512,128]{1,0:T(8,128)(2,1)S(1)}, bf16[512,128]{1,0:T(8,128)(2,1)S(1)}, u32[]{:S(2)}, u32[]{:S(2)}) collective-permute-start(bf16[512,128]{1,0:T(8,128)(2,1)S(1)} %get-tuple-element.33), channel_id=1, source_target_pairs={{0,16},{4,20},{8,24},{12,28},{16,0},{20,4},{24,8},{28,12},{1,17},{... | collective-permute-start | bytes 393224 | tf_op jit(solution)/shard_map/ppermute | solution.py:465
  53.8 11.9 %collective-permute-start.15 = (bf16[512,128]{1,0:T(8,128)(2,1)S(1)}, bf16[512,128]{1,0:T(8,128)(2,1)S(1)}, u32[]{:S(2)}, u32[]{:S(2)}) collective-permute-start(bf16[512,128]{1,0:T(8,128)(2,1)S(1)} %get-tuple-element.34), channel_id=1, source_target_pairs={{0,24},{4,28},{8,16},{12,20},{16,8},{20,12},{24,0},{28,4},{1,25},{... | collective-permute-start | bytes 393224 | tf_op jit(solution)/shard_map/ppermute | solution.py:465

commit v3 on v2

v3 whole, which is shorter than its diff:
```python
import functools

import jax
import jax.numpy as jnp
from jax import lax
from jax.experimental import pallas as pl
from jax.experimental.pallas import tpu as pltpu
from jax.sharding import PartitionSpec as P

F32 = jnp.float32
BF16 = jnp.bfloat16
MIB = 1024 * 1024
COST = pl.CostEstimate(flops=1, bytes_accessed=1, transcendentals=0)


def params(mib=16):
    return pltpu.CompilerParams(vmem_limit_bytes=mib * MIB)


def vmem():
    return pl.BlockSpec(memory_space=pltpu.VMEM)


def smem():
    return pl.BlockSpec(memory_space=pltpu.SMEM)


def place_of(dims, block_row, block_col):
    n_z, n_col, blocks = dims
    r, c = lax.axis_index("row"), lax.axis_index("col")
    z, core = r // 2, r % 2
    source, owner = block_col // blocks, block_row // blocks
    j = 2 * (z ^ (source // 2)) + ((source + core) & 1)
    t = c - owner
    t = jnp.where(t < 0, t + n_col, t)
    return ((j * n_col + t) * blocks + block_row % blocks) * blocks + block_col % blocks


def densify_kernel(dims, groups, rows, cols, count, tiles, out, buffer, total, sems):
    n_z, n_col, blocks = dims
    slots, tile = buffer.shape[0], buffer.shape[1]
    per_group = slots // groups
    places = total.shape[0] - 1
    live = count[0, 0]

    def copy(g):
        part = pl.ds(g * per_group, per_group)
        return pltpu.make_async_copy(tiles.at[part], buffer.at[part], sems.at[g])

    def each_group(action):
        for g in range(groups):

            @pl.when(g * per_group < live)
            def _():
                action(g)

    each_group(lambda g: copy(g).start())

    def clear(i, carry):
        total[i] = jnp.zeros((tile, tile), F32)
        return carry

    lax.fori_loop(0, places, clear, 0, unroll=4)

    def add_group(g):
        copy(g).wait()

        def add(i, carry):
            slot = g * per_group + i
            place = place_of(dims, rows[0, 0, slot], cols[0, 0, slot])
            place = jnp.where(slot < live, place, places)
            total[place] += buffer[slot].astype(F32)
            return carry

        lax.fori_loop(0, per_group, add, 0, unroll=4)

    each_group(add_group)

    def settle(j, carry):
        for t in range(n_col):
            for a in range(blocks):
                for b in range(blocks):
                    value = total[((j * n_col + t) * blocks + a) * blocks + b]
                    out[j, t, a * tile : (a + 1) * tile, b * tile : (b + 1) * tile] = value.astype(BF16)
        return carry

    lax.fori_loop(0, 2 * n_z, settle, 0)


def densify(rows, cols, count, tiles, n_z, n_col, blocks):
    slots, tile = tiles.shape[0], tiles.shape[1]
    n_src = 2 * n_z
    groups = 8
    side = blocks * tile
    places = n_src * n_col * blocks * blocks
    return pl.pallas_call(
        functools.partial(densify_kernel, (n_z, n_col, blocks), groups),
        out_shape=pltpu.VMEM((n_src, n_col, side, side), BF16),
        in_specs=[smem(), smem(), smem(), pl.BlockSpec(memory_space=pltpu.HBM)],
        out_specs=vmem(),
        scratch_shapes=[
            pltpu.VMEM((slots, tile, tile), BF16),
            pltpu.VMEM((places + 1, tile, tile), F32),
            pltpu.SemaphoreType.DMA((groups,)),
        ],
        compiler_params=params(32),
        cost_estimate=COST,
        name="densify",
    )(in_hbm(rows), in_hbm(cols), count, in_hbm(tiles))


def in_hbm(v):
    return pltpu.with_memory_space_constraint(v, pltpu.HBM)


def resident(dense):
    return pltpu.with_memory_space_constraint(dense, pltpu.VMEM)


def hold(arrays, after):
    n = len(arrays)
    outs = pl.pallas_call(
        lambda *refs: None,
        out_shape=tuple(jax.ShapeDtypeStruct(v.shape, v.dtype) for v in arrays),
        in_specs=[pl.BlockSpec(memory_space=pl.ANY)] * n + [vmem()],
        out_specs=(pl.BlockSpec(memory_space=pl.ANY),) * n,
        input_output_aliases={i: i for i in range(n)},
        compiler_params=params(),
        cost_estimate=COST,
        name="hold",
    )(*arrays, resident(after))
    return list(outs)


def forward_kernel(places, last, dense, *refs):
    n = len(places)
    xs, refs = refs[:n], refs[n:]
    n_col, side = dense.shape[1], dense.shape[2]
    outs = refs[-n_col:]
    for t in range(n_col):
        total = jnp.dot(dense[places[0], t], xs[0][...], preferred_element_type=F32)
        for j, x in zip(places[1:], xs[1:]):
            total = total + jnp.dot(dense[j, t], x[...], preferred_element_type=F32)
        if len(refs) > n_col:
            total = total + refs[t][...]
        outs[t][...] = total.astype(BF16) if last else total


def forward(dense, places, xs, totals, last):
    _, n_col, side, _ = dense.shape
    feats = xs[0].shape[1]
    shape = jax.ShapeDtypeStruct((side, feats), BF16 if last else F32)
    return pl.pallas_call(
        functools.partial(forward_kernel, places, last),
        out_shape=(shape,) * n_col,
        in_specs=[vmem()] * (1 + len(xs) + len(totals)),
        out_specs=(vmem(),) * n_col,
        compiler_params=params(),
        cost_estimate=COST,
        name="forward",
    )(resident(dense), *xs, *totals)


def backward_kernel(dense, *refs):
    n_src, n_col = dense.shape[0], dense.shape[1]
    pieces, outs = refs[:n_col], refs[-2:]
    turned = [piece[...].astype(F32).T.astype(BF16) for piece in pieces]
    for j in range(n_src):
        total = jnp.dot(turned[0], dense[j, 0], preferred_element_type=F32)
        for t in range(1, n_col):
            total = total + jnp.dot(turned[t], dense[j, t], preferred_element_type=F32)
        outs[j % 2][j // 2] = total.T.astype(BF16)


def backward(dense, pieces, after):
    n_src, n_col, side, _ = dense.shape
    feats = pieces[0].shape[1]
    return pl.pallas_call(
        backward_kernel,
        out_shape=(jax.ShapeDtypeStruct((n_src // 2, side, feats), BF16),) * 2,
        in_specs=[vmem()] * (1 + n_col) + [pl.BlockSpec(memory_space=pl.ANY)],
        out_specs=(vmem(),) * 2,
        compiler_params=params(),
        cost_estimate=COST,
        name="backward",
    )(resident(dense), *pieces, after)


def densify_stream_kernel(
    dims, rows, cols, count, tiles, out, buffer, head, following, sems
):
    n_z, n_col, blocks, slots, groups = dims
    chunk = pl.program_id(0)
    per_chunk = n_col * blocks * blocks
    per_group = slots // groups

    def copy(g):
        part = pl.ds(g * per_group, per_group)
        return pltpu.make_async_copy(tiles.at[part], buffer.at[part], sems.at[g])

    @pl.when(chunk == 0)
    def _():
        for g in range(groups):
            copy(g).start()

        def clear(i, carry):
            head[i] = slots
            return carry

        lax.fori_loop(0, 2 * n_z * per_chunk, clear, 0, unroll=8)
        following[slots] = slots
        buffer[slots] = jnp.zeros(buffer.shape[1:], buffer.dtype)

        def link(slot, carry):
            block_row, block_col = rows[0, 0, slot], cols[0, 0, slot]
            place = place_of((n_z, n_col, blocks), block_row, block_col)
            following[slot] = head[place]
            head[place] = slot
            return carry

        lax.fori_loop(0, count[0, 0], link, 0)
        for g in range(groups):
            copy(g).wait()

    tile = buffer.shape[1]

    def fill(i, carry):
        first = head[chunk * per_chunk + i]
        t = i // (blocks * blocks)
        a = pl.multiple_of((i // blocks) % blocks * tile, tile)
        b = pl.multiple_of(i % blocks * tile, tile)
        where = (0, t, pl.ds(a, tile), pl.ds(b, tile))
        out[where] = buffer[first]
        second = following[first]

        @pl.when(second != slots)
        def _():
            def more(state):
                slot, total = state
                return following[slot], total + buffer[slot].astype(F32)

            _, total = lax.while_loop(
                lambda state: state[0] != slots,
                more,
                (second, buffer[first].astype(F32)),
            )
            out[where] = total.astype(BF16)

        return carry

    lax.fori_loop(0, per_chunk, fill, 0)


def densify_stream(rows, cols, count, tiles, n_z, n_col, blocks):
    slots, tile = tiles.shape[0], tiles.shape[1]
    n_src = 2 * n_z
    groups = 8
    side = blocks * tile
    shape = (n_src, n_col, side, side)
    return pl.pallas_call(
        functools.partial(densify_stream_kernel, (n_z, n_col, blocks, slots, groups)),
        grid=(n_src,),
        out_shape=jax.ShapeDtypeStruct(shape, BF16),
        in_specs=[smem(), smem(), smem(), pl.BlockSpec(memory_space=pltpu.HBM)],
        out_specs=pl.BlockSpec((1, n_col, side, side), lambda j: (j, 0, 0, 0)),
        scratch_shapes=[
            pltpu.VMEM((slots + 1, tile, tile), BF16),
            pltpu.SMEM((n_src * n_col * blocks * blocks,), jnp.int32),
            pltpu.SMEM((slots + 1,), jnp.int32),
            pltpu.SemaphoreType.DMA((groups,)),
        ],
        compiler_params=params(32),
        cost_estimate=COST,
        name="densify",
    )(rows, cols, count, tiles)


def forward_stream_kernel(first, a, x0, x1, *rest):

    j = pl.program_id(1)

    @pl.when(j == 0)
    def _():
        value = jnp.dot(a[0, 0], x0[...], preferred_element_type=F32)
        if not first:
            value = value + rest[0][...]
        rest[-1][...] = value

    @pl.when(j == 1)
    def _():
        rest[-1][...] += jnp.dot(a[0, 0], x1[...], preferred_element_type=F32)


def forward_stream(dense, shift, x0, x1, total):
    _, n_col, side, _ = dense.shape
    feats = x0.shape[1]
    first = total is None
    block = pl.BlockSpec((side, feats), lambda t, j: (t, 0))
    return pl.pallas_call(
        functools.partial(forward_stream_kernel, first),
        grid=(n_col, 2),
        out_shape=jax.ShapeDtypeStruct((n_col * side, feats), F32),
        in_specs=[
            pl.BlockSpec((1, 1, side, side), lambda t, j: (2 * shift + j, t, 0, 0)),
            vmem(),
            vmem(),
        ]
        + ([] if first else [block]),
        out_specs=block,
        compiler_params=params(32),
        cost_estimate=COST,
        name="forward",
    )(dense, x0, x1, *([] if first else [total]))


def middle_kernel(n_col, weights, cot_own, cot_other, *refs):
    own = refs[:n_col]
    other = refs[n_col : 2 * n_col]
    spread, activated, agg, g_own, g_other = refs[2 * n_col :]
    half = cot_own.shape[1]
    f = lax.axis_index("feat")
    mine = pl.ds(pl.multiple_of(f * half, half), half)
    theirs = pl.ds(pl.multiple_of((1 - f) * half, half), half)

    def gather(parts):
        total = parts[0][...].astype(F32)
        for part in parts[1:]:
            total = total + part[...].astype(F32)
        return total.astype(BF16)

    top = jnp.concatenate([weights[mine, mine], weights[mine, theirs]], axis=1)
    low = jnp.concatenate([weights[theirs, mine], weights[theirs, theirs]], axis=1)
    agg_own = gather(own)
    agg[...] = agg_own
    both = jnp.concatenate([agg_own, gather(other)], axis=1)
    hidden = jnp.dot(both, jnp.concatenate([top, low], axis=0), preferred_element_type=F32)
    decay = jnp.exp(jnp.minimum(hidden, 0.0))
    cot = jnp.concatenate([cot_own[...], cot_other[...]], axis=1).astype(F32)
    g = (cot * decay).astype(BF16)
    spread[...] = lax.dot_general(
        g, top, (((1,), (1,)), ((), ())), preferred_element_type=F32
    ).astype(BF16)
    g_own[...] = g[:, :half]
    g_other[...] = g[:, half:]
    activated[...] = jnp.where(
        hidden[:, :half] > 0, hidden[:, :half], decay[:, :half] - 1.0
    ).astype(BF16)


def middle(weights, cot_own, cot_other, own, other):
    nodes, half = cot_own.shape
    whole = weights.shape[1]
    n_col = len(own)
    return pl.pallas_call(
        functools.partial(middle_kernel, n_col),
        out_shape=(jax.ShapeDtypeStruct((nodes, half), BF16),) * 5,
        in_specs=[vmem()] * (3 + 2 * n_col),
        out_specs=(vmem(),) * 5,
        compiler_params=params(),
        cost_estimate=COST,
        name="middle",
    )(weights, cot_own, cot_other, *own, *other)


def weight_kernel(agg, g_own, g_other, out):
    half = agg.shape[1]
    f = lax.axis_index("feat")
    turned = agg[...].astype(F32).T.astype(BF16)
    for columns, g in ((f * half, g_own), ((1 - f) * half, g_other)):
        columns = pl.ds(pl.multiple_of(columns, half), half)
        out[:, columns] = jnp.dot(turned, g[...], preferred_element_type=F32).astype(BF16)


def weight_term(agg, g_own, g_other):
    half = agg.shape[1]
    return pl.pallas_call(
        weight_kernel,
        out_shape=jax.ShapeDtypeStruct((half, 2 * half), BF16),
        in_specs=[vmem()] * 3,
        out_specs=vmem(),
        compiler_params=params(),
        cost_estimate=COST,
        name="weight_term",
    )(agg, g_own, g_other)


def backward_stream_kernel(n_col, a, *refs):
    pieces, out, turned = refs[:n_col], refs[-2], refs[-1]

    @pl.when(pl.program_id(0) == 0)
    def _():
        for t in range(n_col):
            turned[t] = pieces[t][...].astype(F32).T.astype(BF16)

    total = jnp.dot(turned[0], a[0, 0], preferred_element_type=F32)
    for t in range(1, n_col):
        total = total + jnp.dot(turned[t], a[0, t], preferred_element_type=F32)
    out[0] = total.T.astype(BF16)


def backward_stream(dense, parity, pieces, after):
    n_src, n_col, side, _ = dense.shape
    feats = pieces[0].shape[1]
    n_z = n_src // 2
    return pl.pallas_call(
        functools.partial(backward_stream_kernel, n_col),
        grid=(n_z,),
        out_shape=jax.ShapeDtypeStruct((n_z, side, feats), BF16),
        in_specs=[pl.BlockSpec((1, n_col, side, side), lambda s: (2 * s + parity, 0, 0, 0))]
        + [vmem()] * n_col
        + [pl.BlockSpec(memory_space=pl.ANY)],
        out_specs=pl.BlockSpec((1, side, feats), lambda s: (s, 0, 0)),
        scratch_shapes=[pltpu.VMEM((n_col, feats, side), BF16)],
        compiler_params=params(32),
        cost_estimate=COST,
        name="backward",
    )(dense, *pieces, after)


def add_kernel(a, b, *rest):
    rest[-1][...] = (a[...].astype(F32) + b[...].astype(F32)).astype(BF16)


def add(a, b, *after):
    return pl.pallas_call(
        add_kernel,
        out_shape=jax.ShapeDtypeStruct(a.shape, BF16),
        in_specs=[vmem()] * 2 + [pl.BlockSpec(memory_space=pl.ANY)] * len(after),
        out_specs=vmem(),
        compiler_params=params(),
        cost_estimate=COST,
        name="add",
    )(a, b, *after)


def pair_kernel(own, arrived, *outs):
    for s, out in enumerate(outs):
        out[...] = (own[s].astype(F32) + arrived[s].astype(F32)).astype(BF16)


def pair_sums(own, arrived):
    n_z, side, feats = own.shape
    return pl.pallas_call(
        pair_kernel,
        out_shape=(jax.ShapeDtypeStruct((side, feats), BF16),) * n_z,
        in_specs=[vmem()] * 2,
        out_specs=(vmem(),) * n_z,
        compiler_params=params(),
        cost_estimate=COST,
        name="pair_sums",
    )(own, arrived)


def shards(features, tile_rows, tile_cols, tile_count, tile_values, weights, cotangent):
    tile = tile_values.shape[-1]
    n_row, n_col = lax.axis_size("row"), lax.axis_size("col")
    n_z = n_row // 2
    nodes, half = features.shape
    blocks = nodes // tile
    node_total = nodes * n_row * n_col
    def sibling(v):
        return lax.ppermute(v, "row", [(i, i ^ 1) for i in range(n_row)])

    def along_z(v, s):
        return lax.ppermute(v, "row", [(i, i ^ (2 * s)) for i in range(n_row)])

    def other_feat(v):
        return lax.ppermute(v, "feat", [(0, 1), (1, 0)])

    def to_group(v, shift, flip):
        pairs = []
        for cc in range(n_col):
            for ff in range(2):
                pairs.append((2 * cc + ff, 2 * ((cc + shift) % n_col) + (ff ^ flip)))
        return lax.ppermute(v, ("col", "feat"), pairs)

    same = [features] + [along_z(features, s) for s in range(1, n_z)]
    cot_other = other_feat(cotangent)
    tiles = tile_values[0, 0]
    cell = (tile_rows, tile_cols, tile_count, tiles, n_z, n_col, blocks)
    if 2 * n_z * n_col * (blocks * tile) ** 2 <= 8 * MIB:
        dense = densify(*cell)
        totals = forward(dense, [0, 1], [features, sibling(features)], (), False)
        *same, cot_other = hold(same[1:] + [cot_other], totals[0])
        cross = [sibling(v) for v in same]
        totals = forward(dense, [2 * s for s in range(1, n_z)], same, totals, False)
        parts = forward(dense, [2 * s + 1 for s in range(1, n_z)], cross, totals, True)
        back_of = backward
    else:
        cross = [sibling(v) for v in same]
        dense = densify_stream(*cell)
        total = None
        for s in range(n_z):
            total = forward_stream(dense, s, same[s], cross[s], total)
        parts = total.astype(BF16).reshape(n_col, nodes, half)

        def back_of(*operands):
            return [backward_stream(operands[0], k, *operands[1:]) for k in range(2)]

    own = [parts[0]] + [to_group(parts[t], -t, 0) for t in range(1, n_col)]
    other = [to_group(parts[t], -t, 1) for t in range(n_col)]
    spread, activated, *rest = middle(weights, cotangent, cot_other, own, other)
    pieces = [spread] + [
        lax.ppermute(spread, "col", [(i, (i + t) % n_col) for i in range(n_col)])
        for t in range(1, n_col)
    ]
    term = weight_term(*rest)
    term = add(term, along_z(term, 1))

    even, odd = back_of(dense, pieces, term)
    arrived = sibling(odd)
    sums = pair_sums(even, arrived)
    if n_z > 2:
        term = add(term, along_z(term, 2), sums[0])
    back = sums[0].astype(F32)
    for s in range(1, n_z):
        back = back + along_z(sums[s], s).astype(F32)

    def finish(_, v):
        for step in range(2, n_z.bit_length() - 1):
            v = add(v, along_z(v, 1 << step))
        total = v.astype(F32)
        for t in range(1, n_col):
            total = total + lax.ppermute(
                v, "col", [(i, (i + t) % n_col) for i in range(n_col)]
            ).astype(F32)
        v = total.astype(BF16)
        return add(v, sibling(v))

    once = lax.optimization_barrier(jnp.int32(1))
    whole = lax.fori_loop(0, once, finish, term)
    weight_grad = whole.astype(F32) * node_total ** (-0.5)
    return (activated, back.astype(BF16), weight_grad)


def solution(mesh):
    return jax.shard_map(
        shards,
        mesh=mesh,
        in_specs=(
            P(("col", "row"), "feat"),
            P("row", "col", None),
            P("row", "col", None),
            P("row", "col"),
            P("row", "col", None, None, None),
            P(),
            P(("row", "col"), "feat"),
        ),
        out_specs=(P(("row", "col"), "feat"), P(("col", "row"), "feat"), P("feat", None)),
        check_vma=False,
    )
```

time: 66.1 us -> 57.7 us (0.87)
  waiting for transfers between devices: 23.1 us -> 18.4 us
  local copies, waits for them, and re-layouts: 3.4 us -> 0.01 us
  starting transfers between devices: 22.4 us -> 24.5 us
  Pallas kernels: 13.9 us -> 11.9 us
    ppermute x9 -> x8, waiting for transfers between devices: 13.8 us -> 7.22 us  [along_z(): return lax.ppermute(v, 'row', [(i, i ^ 2 * s) for i in range(n_row)])]
    unnamed x12 -> x6, local copies, waits for them, and re-layouts: 3.4 us -> 0.01 us
    ppermute x7 -> x6, starting transfers between devices: 0.72 us -> 3 us  [sibling(): return lax.ppermute(v, 'row', [(i, i ^ 1) for i in range(n_row)])]
    pallas_call x1, Pallas kernels: 1.95 us -> 0.96 us  [middle(): pl.pallas_call(functools.partial(middle_kernel, n_col), out_shape=(jax.Sh...]
    pallas_call x1, Pallas kernels: 7.47 us -> 6.49 us  [densify(): pl.pallas_call(functools.partial(densify_kernel, (n_z, n_col, blocks), gr...]
    ppermute x7 -> x6, waiting for transfers between devices: 0.3 us -> 1.26 us  [sibling(): return lax.ppermute(v, 'row', [(i, i ^ 1) for i in range(n_row)])]
    ppermute x1, waiting for transfers between devices: 2.9 us -> 3.65 us  [finish(): lax.ppermute(v, 'col', [(i, (i + t) % n_col) for i in range(n_col)])]
    ppermute x9 -> x8, starting transfers between devices: 14.6 us -> 15.2 us  [along_z(): return lax.ppermute(v, 'row', [(i, i ^ 2 * s) for i in range(n_row)])]
  transfers between devices with their start and end apart: 22 -> 20, of which waited for: 11 -> 8; matrix products, arithmetic and copies ran while one was open for 2% -> 1% of each run, Pallas kernels for 18% -> 15%
where the time goes in v3:
time: 57.7 us
  starting transfers between devices  24.5 us (42%)
  waiting for transfers between devices  18.4 us (32%)
  Pallas kernels  11.9 us (21%)
  between operations  1.42 us (2%)
  other arithmetic  1.41 us (2%)
    ppermute x8, starting transfers between devices, along_z(): return lax.ppermute(v, 'row', [(i, i ^ 2 * s) for i in range(n_row)])  15.2 us
    ppermute x8, waiting for transfers between devices, along_z(): return lax.ppermute(v, 'row', [(i, i ^ 2 * s) for i in range(n_row)])  7.22 us
    pallas_call x1, Pallas kernels, densify(): pl.pallas_call(functools.partial(densify_kernel, (n_z, n_col, blocks), gr...  6.49 us
    ppermute x3, waiting for transfers between devices, to_group(): return lax.ppermute(v, ('col', 'feat'), pairs)  6.23 us
    ppermute x1, waiting for transfers between devices, finish(): lax.ppermute(v, 'col', [(i, (i + t) % n_col) for i in range(n_col)])  3.65 us
    ppermute x3, starting transfers between devices, to_group(): return lax.ppermute(v, ('col', 'feat'), pairs)  3.55 us
    ppermute x6, starting transfers between devices, sibling(): return lax.ppermute(v, 'row', [(i, i ^ 1) for i in range(n_row)])  3 us
    pallas_call x3, Pallas kernels, forward(): pl.pallas_call(functools.partial(forward_kernel, places, last), out_shape...  2.66 us
  transfers between devices with their start and end apart: 20, of which 8 were waited for; matrix products, arithmetic and copies ran while one was open for 1% of the time, Pallas kernels for 15%

profile of v3, /device:TPU:0, one launch (start us, length us, event | category | flops | bytes accessed | tf_op | source)
XLA Modules:
  0.0 57.7 jit_solution(18053184414573426928)
XLA Ops:
  0.6 0.5 collective-permute-start.6
  1.1 2.6 %collective-permute-start.2 = (bf16[512,128]{1,0:T(8,128)(2,1)}, bf16[512,128]{1,0:T(8,128)(2,1)S(1)}, u32[]{:S(2)}, u32[]{:S(2)}) collective-permute-start(bf16[512,128]{1,0:T(8,128)(2,1)} %refs_0_.1), channel_id=1, source_target_pairs={{0,8},{4,12},{8,0},{12,4},{16,24},{20,28},{24,16},{28,20},{1,9},{5... | collective-permute-start | bytes 393224 | tf_op jit(solution)/shard_map/ppermute | solution.py:465
  3.8 2.6 %collective-permute-start.3 = (bf16[512,128]{1,0:T(8,128)(2,1)}, bf16[512,128]{1,0:T(8,128)(2,1)S(1)}, u32[]{:S(2)}, u32[]{:S(2)}) collective-permute-start(bf16[512,128]{1,0:T(8,128)(2,1)} %refs_0_.1), channel_id=1, source_target_pairs={{0,16},{4,20},{8,24},{12,28},{16,0},{20,4},{24,8},{28,12},{1,17},{... | collective-permute-start | bytes 393224 | tf_op jit(solution)/shard_map/ppermute | solution.py:465
  6.4 0.0 collective-permute-start.4
  6.4 1.7 %collective-permute-start.5 = (bf16[512,128]{1,0:T(8,128)(2,1)}, bf16[512,128]{1,0:T(8,128)(2,1)S(1)}, u32[]{:S(2)}, u32[]{:S(2)}) collective-permute-start(bf16[512,128]{1,0:T(8,128)(2,1)} %cot_own.1), channel_id=1, source_target_pairs={{0,1},{1,0},{2,3},{3,2},{4,5},{5,4},{6,7},{7,6},{8,9},{9,8},{10,11... | collective-permute-start | bytes 393224 | tf_op jit(solution)/shard_map/ppermute | solution.py:468
  8.8 0.0 copy-start
  8.8 6.5 %densify.1.dense = bf16[8,2,512,512]{3,2,1,0:T(8,128)(2,1)S(1)} custom-call(s32[1,1,256]{2,1,0:T(1,128)} %rows.1, s32[1,1,256]{2,1,0:T(1,128)} %cols.1, s32[1,1]{1,0:T(1,128)S(6)} %copy.25.count, bf16[256,128,128]{2,1,0:T(8,128)(2,1)} %bitcast.1), custom_call_target="tpu_custom_call" | custom-call | flops 1 | bytes 1 | tf_op jit(solution)/shard_map/densify/pallas_call | solution.py:96
  15.3 0.0 collective-permute-done.6.refs_1_
  15.3 0.0 copy-done
  15.3 0.7 %forward.3 = (f32[512,128]{1,0:T(8,128)S(1)}, f32[512,128]{1,0:T(8,128)S(1)}) custom-call(bf16[8,2,512,512]{3,2,1,0:T(8,128)(2,1)S(1)} %densify.1.dense, bf16[512,128]{1,0:T(8,128)(2,1)S(1)} %copy-done, bf16[512,128]{1,0:T(8,128)(2,1)S(1)} %collective-permute-done.6.refs_1_), custom_call_target="tpu_custom_call" | custom-call | flops 1 | bytes 1 | tf_op jit(solution)/shard_map/forward/pallas_call | solution.py:153
  16.0 0.0 collective-permute-done.2.refs_0_
  16.0 0.9 %collective-permute-done.3.refs_1_ = bf16[512,128]{1,0:T(8,128)(2,1)S(1)} collective-permute-done((bf16[512,128]{1,0:T(8,128)(2,1)}, bf16[512,128]{1,0:T(8,128)(2,1)S(1)}, u32[]{:S(2)}, u32[]{:S(2)}) %collective-permute-start.3) | collective-permute-done | bytes 131104 | tf_op jit(solution)/shard_map/ppermute | solution.py:465
  16.9 0.0 collective-permute-done.4.refs_2_
  16.9 0.0 collective-permute-done.5.refs_3_
  16.9 1.8 %collective-permute-start.7 = (bf16[512,128]{1,0:T(8,128)(2,1)S(1)}, bf16[512,128]{1,0:T(8,128)(2,1)S(1)}, u32[]{:S(2)}, u32[]{:S(2)}) collective-permute-start(bf16[512,128]{1,0:T(8,128)(2,1)S(1)} %get-tuple-element.44.refs_0_), channel_id=1, source_target_pairs={{0,4},{4,0},{8,12},{12,8},{16,20},{20,16},{24,28},{28,24},{1,5},{5... | collective-permute-start | bytes 393224 | tf_op jit(solution)/shard_map/ppermute | solution.py:462
  18.8 0.1 collective-permute-start.8
  18.8 0.4 collective-permute-start.9
  19.3 0.0 copy-start.1
  19.3 0.0 copy-start.2
  19.3 1.0 %forward.4 = (f32[512,128]{1,0:T(8,128)S(1)}, f32[512,128]{1,0:T(8,128)S(1)}) custom-call(bf16[8,2,512,512]{3,2,1,0:T(8,128)(2,1)S(1)} %densify.1.dense, bf16[512,128]{1,0:T(8,128)(2,1)S(1)} %get-tuple-element.44.refs_0_, bf16[512,128]{1,0:T(8,128)(2,1)S(1)} %get-tuple-element.45.refs_1_, bf16[512,128]{1,0:T(8,128)(2,1)S(1)} %get-tuple-element.46.refs_2_, ...), custom_call_target="tpu_custom_call" | custom-call | flops 1 | bytes 1 | tf_op jit(solution)/shard_map/forward/pallas_call | solution.py:153
  20.3 0.0 collective-permute-done.7.refs_0_
  20.3 0.0 collective-permute-done.8.refs_1_
  20.3 0.0 collective-permute-done.9.refs_2_
  20.3 1.0 %forward.5 = (bf16[512,128]{1,0:T(8,128)(2,1)S(1)}, bf16[512,128]{1,0:T(8,128)(2,1)S(1)}) custom-call(bf16[8,2,512,512]{3,2,1,0:T(8,128)(2,1)S(1)} %densify.1.dense, bf16[512,128]{1,0:T(8,128)(2,1)S(1)} %collective-permute-done.7.refs_0_, bf16[512,128]{1,0:T(8,128)(2,1)S(1)} %collective-permute-done.8.refs_1_, ...), custom_call_target="tpu_custom_call" | custom-call | flops 1 | bytes 1 | tf_op jit(solution)/shard_map/forward/pallas_call | solution.py:153
  21.3 0.1 collective-permute-start.10
  21.4 1.5 %collective-permute-start.11 = (bf16[512,128]{1,0:T(8,128)(2,1)S(1)}, bf16[512,128]{1,0:T(8,128)(2,1)S(1)}, u32[]{:S(2)}, u32[]{:S(2)}) collective-permute-start(bf16[512,128]{1,0:T(8,128)(2,1)S(1)} %get-tuple-element.50.refs_0_), channel_id=1, source_target_pairs={{0,1},{1,0},{2,3},{3,2},{4,5},{5,4},{6,7},{7,6},{8,9},{9,8},{10,11... | collective-permute-start | bytes 393224 | tf_op jit(solution)/shard_map/ppermute | solution.py:475
  22.9 1.9 %collective-permute-start.12 = (bf16[512,128]{1,0:T(8,128)(2,1)S(1)}, bf16[512,128]{1,0:T(8,128)(2,1)S(1)}, u32[]{:S(2)}, u32[]{:S(2)}) collective-permute-start(bf16[512,128]{1,0:T(8,128)(2,1)S(1)} %get-tuple-element.51), channel_id=1, source_target_pairs={{0,3},{1,2},{2,1},{3,0},{4,7},{5,6},{6,5},{7,4},{8,11},{9,10},{10,... | collective-permute-start | bytes 393224 | tf_op jit(solution)/shard_map/ppermute | solution.py:475
  24.8 2.2 %collective-permute-done.10.refs_1_ = bf16[512,128]{1,0:T(8,128)(2,1)S(1)} collective-permute-done((bf16[512,128]{1,0:T(8,128)(2,1)S(1)}, bf16[512,128]{1,0:T(8,128)(2,1)S(1)}, u32[]{:S(2)}, u32[]{:S(2)}) %collective-permute-start.10) | collective-permute-done | bytes 131104 | tf_op jit(solution)/shard_map/ppermute | solution.py:475
  27.1 0.7 %collective-permute-done.11.refs_2_ = bf16[512,128]{1,0:T(8,128)(2,1)S(1)} collective-permute-done((bf16[512,128]{1,0:T(8,128)(2,1)S(1)}, bf16[512,128]{1,0:T(8,128)(2,1)S(1)}, u32[]{:S(2)}, u32[]{:S(2)}) %collective-permute-start.11) | collective-permute-done | bytes 131104 | tf_op jit(solution)/shard_map/ppermute | solution.py:475
  27.7 3.3 %collective-permute-done.12.refs_3_ = bf16[512,128]{1,0:T(8,128)(2,1)S(1)} collective-permute-done((bf16[512,128]{1,0:T(8,128)(2,1)S(1)}, bf16[512,128]{1,0:T(8,128)(2,1)S(1)}, u32[]{:S(2)}, u32[]{:S(2)}) %collective-permute-start.12) | collective-permute-done | bytes 131104 | tf_op jit(solution)/shard_map/ppermute | solution.py:475
  31.1 0.0 copy-done.1
  31.1 0.0 copy-done.2
  31.1 1.0 %middle.1 = (bf16[512,128]{1,0:T(8,128)(2,1)S(1)}, bf16[512,128]{1,0:T(8,128)(2,1)}, bf16[512,128]{1,0:T(8,128)(2,1)S(1)}, bf16[512,128]{1,0:T(8,128)(2,1)S(1)}, bf16[512,128]{1,0:T(8,128)(2,1)S(1)}) custom-call(bf16[256,256]{1,0:T(8,128)(2,1)S(1)} %copy-done.1, bf16[512,128]{1,0:T(8,128)(2,1)S(1)} %copy-done.2, ...), custom_call_target="tpu_custom_call" | custom-call | flops 1 | bytes 1 | tf_op jit(solution)/shard_map/middle/pallas_call | solution.py:354
  32.0 0.4 collective-permute-start.13
  32.4 0.3 weight_term.1.a
  32.7 2.2 %collective-permute-start.14 = (bf16[128,256]{1,0:T(8,128)(2,1)S(1)}, bf16[128,256]{1,0:T(8,128)(2,1)S(1)}, u32[]{:S(2)}, u32[]{:S(2)}) collective-permute-start(bf16[128,256]{1,0:T(8,128)(2,1)S(1)} %weight_term.1.a), channel_id=1, source_target_pairs={{0,8},{4,12},{8,0},{12,4},{16,24},{20,28},{24,16},{28,20},{1,9},{5... | collective-permute-start | bytes 196616 | tf_op jit(solution)/shard_map/ppermute | solution.py:465
  34.9 2.2 %collective-permute-done.14.b = bf16[128,256]{1,0:T(8,128)(2,1)S(1)} collective-permute-done((bf16[128,256]{1,0:T(8,128)(2,1)S(1)}, bf16[128,256]{1,0:T(8,128)(2,1)S(1)}, u32[]{:S(2)}, u32[]{:S(2)}) %collective-permute-start.14) | collective-permute-done | bytes 65568 | tf_op jit(solution)/shard_map/ppermute | solution.py:465
  37.1 0.0 collective-permute-done.13.refs_1_
  37.1 1.4 %backward.1 = (bf16[4,512,128]{2,1,0:T(8,128)(2,1)S(1)}, bf16[4,512,128]{2,1,0:T(8,128)(2,1)S(1)}) custom-call(bf16[8,2,512,512]{3,2,1,0:T(8,128)(2,1)S(1)} %densify.1.dense, bf16[512,128]{1,0:T(8,128)(2,1)S(1)} %get-tuple-element.53.refs_0_, bf16[512,128]{1,0:T(8,128)(2,1)S(1)} %collective-permute-done.13.refs_1_, bf16[128,256]{1,0:T(8,128)(2,1)S(1)} %add.29.refs_2_.a), custom_call_target="tpu_custom_call" | custom-call | flops 1 | bytes 1 | tf_op jit(solution)/shard_map/backward/pallas_call | solution.py:178
  38.5 0.1 collective-permute-start.15
  38.6 3.2 %collective-permute-start.19 = (bf16[128,256]{1,0:T(8,128)(2,1)S(1)}, bf16[128,256]{1,0:T(8,128)(2,1)S(1)}, u32[]{:S(2)}, u32[]{:S(2)}) collective-permute-start(bf16[128,256]{1,0:T(8,128)(2,1)S(1)} %add.29.refs_2_.a), channel_id=1, source_target_pairs={{0,16},{4,20},{8,24},{12,28},{16,0},{20,4},{24,8},{28,12},{1,17},{... | collective-permute-start | bytes 196616 | tf_op jit(solution)/shard_map/ppermute | solution.py:465
  41.8 0.0 collective-permute-done.15.arrived
  41.8 0.1 pair_sums.1
  41.9 2.1 %collective-permute-start.16 = (bf16[512,128]{1,0:T(8,128)(2,1)S(1)}, bf16[512,128]{1,0:T(8,128)(2,1)S(1)}, u32[]{:S(2)}, u32[]{:S(2)}) collective-permute-start(bf16[512,128]{1,0:T(8,128)(2,1)S(1)} %get-tuple-element.60), channel_id=1, source_target_pairs={{0,8},{4,12},{8,0},{12,4},{16,24},{20,28},{24,16},{28,20},{1,9},{5... | collective-permute-start | bytes 393224 | tf_op jit(solution)/shard_map/ppermute | solution.py:465
  44.0 1.8 %collective-permute-start.17 = (bf16[512,128]{1,0:T(8,128)(2,1)S(1)}, bf16[512,128]{1,0:T(8,128)(2,1)S(1)}, u32[]{:S(2)}, u32[]{:S(2)}) collective-permute-start(bf16[512,128]{1,0:T(8,128)(2,1)S(1)} %get-tuple-element.61), channel_id=1, source_target_pairs={{0,16},{4,20},{8,24},{12,28},{16,0},{20,4},{24,8},{28,12},{1,17},{... | collective-permute-start | bytes 393224 | tf_op jit(solution)/shard_map/ppermute | solution.py:465
  45.9 0.6 %collective-permute-start.18 = (bf16[512,128]{1,0:T(8,128)(2,1)S(1)}, bf16[512,128]{1,0:T(8,128)(2,1)S(1)}, u32[]{:S(2)}, u32[]{:S(2)}) collective-permute-start(bf16[512,128]{1,0:T(8,128)(2,1)S(1)} %get-tuple-element.62), channel_id=1, source_target_pairs={{0,24},{4,28},{8,16},{12,20},{16,8},{20,12},{24,0},{28,4},{1,25},{... | collective-permute-start | bytes 393224 | tf_op jit(solution)/shard_map/ppermute | solution.py:465
  46.5 0.0 collective-permute-done.19.b
  46.5 5.7 %while.10 = (s32[]{:T(128)}, bf16[128,256]{1,0:T(8,128)(2,1)S(1)}, s32[]{:T(128)}, s32[]{:T(128)}) while((s32[]{:T(128)}, bf16[128,256]{1,0:T(8,128)(2,1)S(1)}, s32[]{:T(128)}, s32[]{:T(128)}) %tuple.22), condition=%wide.region_1.0_spmd, body=%wide.region_0.0_spmd.sunk | while | flops 131075 | bytes 721030 | solution.py:531
  46.5 0.7 %collective-permute-start = (bf16[128,256]{1,0:T(8,128)(2,1)S(1)}, bf16[128,256]{1,0:T(8,128)(2,1)S(1)}, u32[]{:S(2)}, u32[]{:S(2)}) collective-permute-start(bf16[128,256]{1,0:T(8,128)(2,1)S(1)} %get-tuple-element.95), channel_id=1, source_target_pairs={{0,2},{2,0},{1,3},{3,1},{4,6},{6,4},{5,7},{7,5},{8,10},{10,8},{9,1... | collective-permute-start | bytes 196616 | tf_op jit(solution)/shard_map/while/body/ppermute | solution.py:524
  47.2 3.6 %collective-permute-done = bf16[128,256]{1,0:T(8,128)(2,1)S(1)} collective-permute-done((bf16[128,256]{1,0:T(8,128)(2,1)S(1)}, bf16[128,256]{1,0:T(8,128)(2,1)S(1)}, u32[]{:S(2)}, u32[]{:S(2)}) %collective-permute-start) | collective-permute-done | bytes 65568 | tf_op jit(solution)/shard_map/while/body/ppermute | solution.py:524
  50.9 0.1 collective-permute-start.1
  50.9 1.2 %collective-permute-done.1.b = bf16[128,256]{1,0:T(8,128)(2,1)S(1)} collective-permute-done((bf16[128,256]{1,0:T(8,128)(2,1)S(1)}, bf16[128,256]{1,0:T(8,128)(2,1)S(1)}, u32[]{:S(2)}, u32[]{:S(2)}) %collective-permute-start.1) | collective-permute-done | bytes 65568 | tf_op jit(solution)/shard_map/while/body/ppermute | solution.py:462
  52.2 0.7 %convert_multiply_fusion = f32[128,256]{1,0:T(8,128)} fusion(bf16[128,256]{1,0:T(8,128)(2,1)S(1)} %get-tuple-element.63), kind=kLoop, calls=%fused_computation.2 | loop fusion | flops 65536 | bytes 196608 | tf_op jit(solution)/shard_map/mul | solution.py:532
  52.9 0.0 collective-permute-done.16
  52.9 4.0 %collective-permute-done.17 = bf16[512,128]{1,0:T(8,128)(2,1)S(1)} collective-permute-done((bf16[512,128]{1,0:T(8,128)(2,1)S(1)}, bf16[512,128]{1,0:T(8,128)(2,1)S(1)}, u32[]{:S(2)}, u32[]{:S(2)}) %collective-permute-start.17) | collective-permute-done | bytes 131104 | tf_op jit(solution)/shard_map/ppermute | solution.py:465
  56.9 0.0 collective-permute-done.18
  56.9 0.7 %add_convert_fusion.1 = bf16[512,128]{1,0:T(8,128)(2,1)} fusion(bf16[512,128]{1,0:T(8,128)(2,1)S(1)} %collective-permute-done.18, bf16[512,128]{1,0:T(8,128)(2,1)S(1)} %collective-permute-done.17, bf16[512,128]{1,0:T(8,128)(2,1)S(1)} %collective-permute-done.16, bf16[512,128]{1,0:T(8,128)(2,1)S(1)} %get-tuple-element.59.rest_0_), kind=kLoop, calls=%fused_computation.1 | loop fusion | flops 524288 | bytes 655360 | tf_op jit(solution)/shard_map/convert_element_type | solution.py:533
  (5 shorter events, 0.1 us)
Async XLA Ops:
  0.6 14.6 %collective-permute-start.6 = (bf16[512,128]{1,0:T(8,128)(2,1)}, bf16[512,128]{1,0:T(8,128)(2,1)S(1)}, u32[]{:S(2)}, u32[]{:S(2)}) collective-permute-start(bf16[512,128]{1,0:T(8,128)(2,1)} %refs_0_.1), channel_id=1, source_target_pairs={{0,4},{4,0},{8,12},{12,8},{16,20},{20,16},{24,28},{28,24},{1,5},{5... | collective-permute-start | bytes 393224 | tf_op jit(solution)/shard_map/ppermute | solution.py:462
  1.1 14.8 %collective-permute-start.2 = (bf16[512,128]{1,0:T(8,128)(2,1)}, bf16[512,128]{1,0:T(8,128)(2,1)S(1)}, u32[]{:S(2)}, u32[]{:S(2)}) collective-permute-start(bf16[512,128]{1,0:T(8,128)(2,1)} %refs_0_.1), channel_id=1, source_target_pairs={{0,8},{4,12},{8,0},{12,4},{16,24},{20,28},{24,16},{28,20},{1,9},{5... | collective-permute-start | bytes 393224 | tf_op jit(solution)/shard_map/ppermute | solution.py:465
  3.8 13.1 %collective-permute-start.3 = (bf16[512,128]{1,0:T(8,128)(2,1)}, bf16[512,128]{1,0:T(8,128)(2,1)S(1)}, u32[]{:S(2)}, u32[]{:S(2)}) collective-permute-start(bf16[512,128]{1,0:T(8,128)(2,1)} %refs_0_.1), channel_id=1, source_target_pairs={{0,16},{4,20},{8,24},{12,28},{16,0},{20,4},{24,8},{28,12},{1,17},{... | collective-permute-start | bytes 393224 | tf_op jit(solution)/shard_map/ppermute | solution.py:465
  6.4 10.5 %collective-permute-start.4 = (bf16[512,128]{1,0:T(8,128)(2,1)}, bf16[512,128]{1,0:T(8,128)(2,1)S(1)}, u32[]{:S(2)}, u32[]{:S(2)}) collective-permute-start(bf16[512,128]{1,0:T(8,128)(2,1)} %refs_0_.1), channel_id=1, source_target_pairs={{0,24},{4,28},{8,16},{12,20},{16,8},{20,12},{24,0},{28,4},{1,25},{... | collective-permute-start | bytes 393224 | tf_op jit(solution)/shard_map/ppermute | solution.py:465
  6.4 10.5 %collective-permute-start.5 = (bf16[512,128]{1,0:T(8,128)(2,1)}, bf16[512,128]{1,0:T(8,128)(2,1)S(1)}, u32[]{:S(2)}, u32[]{:S(2)}) collective-permute-start(bf16[512,128]{1,0:T(8,128)(2,1)} %cot_own.1), channel_id=1, source_target_pairs={{0,1},{1,0},{2,3},{3,2},{4,5},{5,4},{6,7},{7,6},{8,9},{9,8},{10,11... | collective-permute-start | bytes 393224 | tf_op jit(solution)/shard_map/ppermute | solution.py:468
  8.8 6.5 %copy-start = (bf16[512,128]{1,0:T(8,128)(2,1)S(1)}, bf16[512,128]{1,0:T(8,128)(2,1)}, u32[]{:S(2)}) copy-start(bf16[512,128]{1,0:T(8,128)(2,1)} %refs_0_.1) | copy-start | bytes 393220
  16.9 3.3 %collective-permute-start.7 = (bf16[512,128]{1,0:T(8,128)(2,1)S(1)}, bf16[512,128]{1,0:T(8,128)(2,1)S(1)}, u32[]{:S(2)}, u32[]{:S(2)}) collective-permute-start(bf16[512,128]{1,0:T(8,128)(2,1)S(1)} %get-tuple-element.44.refs_0_), channel_id=1, source_target_pairs={{0,4},{4,0},{8,12},{12,8},{16,20},{20,16},{24,28},{28,24},{1,5},{5... | collective-permute-start | bytes 393224 | tf_op jit(solution)/shard_map/ppermute | solution.py:462
  18.8 1.5 %collective-permute-start.8 = (bf16[512,128]{1,0:T(8,128)(2,1)S(1)}, bf16[512,128]{1,0:T(8,128)(2,1)S(1)}, u32[]{:S(2)}, u32[]{:S(2)}) collective-permute-start(bf16[512,128]{1,0:T(8,128)(2,1)S(1)} %get-tuple-element.45.refs_1_), channel_id=1, source_target_pairs={{0,4},{4,0},{8,12},{12,8},{16,20},{20,16},{24,28},{28,24},{1,5},{5... | collective-permute-start | bytes 393224 | tf_op jit(solution)/shard_map/ppermute | solution.py:462
  18.8 1.5 %collective-permute-start.9 = (bf16[512,128]{1,0:T(8,128)(2,1)S(1)}, bf16[512,128]{1,0:T(8,128)(2,1)S(1)}, u32[]{:S(2)}, u32[]{:S(2)}) collective-permute-start(bf16[512,128]{1,0:T(8,128)(2,1)S(1)} %get-tuple-element.46.refs_2_), channel_id=1, source_target_pairs={{0,4},{4,0},{8,12},{12,8},{16,20},{20,16},{24,28},{28,24},{1,5},{5... | collective-permute-start | bytes 393224 | tf_op jit(solution)/shard_map/ppermute | solution.py:462
  19.3 11.8 %copy-start.1 = (bf16[256,256]{1,0:T(8,128)(2,1)S(1)}, bf16[256,256]{1,0:T(8,128)(2,1)}, u32[]{:S(2)}) copy-start(bf16[256,256]{1,0:T(8,128)(2,1)} %weights.1) | copy-start | bytes 393220
  19.3 11.8 %copy-start.2 = (bf16[512,128]{1,0:T(8,128)(2,1)S(1)}, bf16[512,128]{1,0:T(8,128)(2,1)}, u32[]{:S(2)}) copy-start(bf16[512,128]{1,0:T(8,128)(2,1)} %cot_own.1) | copy-start | bytes 393220
  21.3 5.8 %collective-permute-start.10 = (bf16[512,128]{1,0:T(8,128)(2,1)S(1)}, bf16[512,128]{1,0:T(8,128)(2,1)S(1)}, u32[]{:S(2)}, u32[]{:S(2)}) collective-permute-start(bf16[512,128]{1,0:T(8,128)(2,1)S(1)} %get-tuple-element.51), channel_id=1, source_target_pairs={{0,2},{1,3},{2,0},{3,1},{4,6},{5,7},{6,4},{7,5},{8,10},{9,11},{10,... | collective-permute-start | bytes 393224 | tf_op jit(solution)/shard_map/ppermute | solution.py:475
  21.4 6.3 %collective-permute-start.11 = (bf16[512,128]{1,0:T(8,128)(2,1)S(1)}, bf16[512,128]{1,0:T(8,128)(2,1)S(1)}, u32[]{:S(2)}, u32[]{:S(2)}) collective-permute-start(bf16[512,128]{1,0:T(8,128)(2,1)S(1)} %get-tuple-element.50.refs_0_), channel_id=1, source_target_pairs={{0,1},{1,0},{2,3},{3,2},{4,5},{5,4},{6,7},{7,6},{8,9},{9,8},{10,11... | collective-permute-start | bytes 393224 | tf_op jit(solution)/shard_map/ppermute | solution.py:475
  22.9 8.2 %collective-permute-start.12 = (bf16[512,128]{1,0:T(8,128)(2,1)S(1)}, bf16[512,128]{1,0:T(8,128)(2,1)S(1)}, u32[]{:S(2)}, u32[]{:S(2)}) collective-permute-start(bf16[512,128]{1,0:T(8,128)(2,1)S(1)} %get-tuple-element.51), channel_id=1, source_target_pairs={{0,3},{1,2},{2,1},{3,0},{4,7},{5,6},{6,5},{7,4},{8,11},{9,10},{10,... | collective-permute-start | bytes 393224 | tf_op jit(solution)/shard_map/ppermute | solution.py:475
  32.0 5.1 %collective-permute-start.13 = (bf16[512,128]{1,0:T(8,128)(2,1)S(1)}, bf16[512,128]{1,0:T(8,128)(2,1)S(1)}, u32[]{:S(2)}, u32[]{:S(2)}) collective-permute-start(bf16[512,128]{1,0:T(8,128)(2,1)S(1)} %get-tuple-element.53.refs_0_), channel_id=1, source_target_pairs={{0,2},{2,0},{1,3},{3,1},{4,6},{6,4},{5,7},{7,5},{8,10},{10,8},{9,1... | collective-permute-start | bytes 393224 | tf_op jit(solution)/shard_map/ppermute | solution.py:504
  32.7 4.4 %collective-permute-start.14 = (bf16[128,256]{1,0:T(8,128)(2,1)S(1)}, bf16[128,256]{1,0:T(8,128)(2,1)S(1)}, u32[]{:S(2)}, u32[]{:S(2)}) collective-permute-start(bf16[128,256]{1,0:T(8,128)(2,1)S(1)} %weight_term.1.a), channel_id=1, source_target_pairs={{0,8},{4,12},{8,0},{12,4},{16,24},{20,28},{24,16},{28,20},{1,9},{5... | collective-permute-start | bytes 196616 | tf_op jit(solution)/shard_map/ppermute | solution.py:465
  38.5 3.3 %collective-permute-start.15 = (bf16[4,512,128]{2,1,0:T(8,128)(2,1)S(1)}, bf16[4,512,128]{2,1,0:T(8,128)(2,1)S(1)}, u32[]{:S(2)}, u32[]{:S(2)}) collective-permute-start(bf16[4,512,128]{2,1,0:T(8,128)(2,1)S(1)} %get-tuple-element.58), channel_id=1, source_target_pairs={{0,4},{4,0},{8,12},{12,8},{16,20},{20,16},{24,28},{28,24},{1,5},{5... | collective-permute-start | bytes 1572872 | tf_op jit(solution)/shard_map/ppermute | solution.py:462
  38.6 7.9 %collective-permute-start.19 = (bf16[128,256]{1,0:T(8,128)(2,1)S(1)}, bf16[128,256]{1,0:T(8,128)(2,1)S(1)}, u32[]{:S(2)}, u32[]{:S(2)}) collective-permute-start(bf16[128,256]{1,0:T(8,128)(2,1)S(1)} %add.29.refs_2_.a), channel_id=1, source_target_pairs={{0,16},{4,20},{8,24},{12,28},{16,0},{20,4},{24,8},{28,12},{1,17},{... | collective-permute-start | bytes 196616 | tf_op jit(solution)/shard_map/ppermute | solution.py:465
  41.9 10.9 %collective-permute-start.16 = (bf16[512,128]{1,0:T(8,128)(2,1)S(1)}, bf16[512,128]{1,0:T(8,128)(2,1)S(1)}, u32[]{:S(2)}, u32[]{:S(2)}) collective-permute-start(bf16[512,128]{1,0:T(8,128)(2,1)S(1)} %get-tuple-element.60), channel_id=1, source_target_pairs={{0,8},{4,12},{8,0},{12,4},{16,24},{20,28},{24,16},{28,20},{1,9},{5... | collective-permute-start | bytes 393224 | tf_op jit(solution)/shard_map/ppermute | solution.py:465
  44.0 12.9 %collective-permute-start.17 = (bf16[512,128]{1,0:T(8,128)(2,1)S(1)}, bf16[512,128]{1,0:T(8,128)(2,1)S(1)}, u32[]{:S(2)}, u32[]{:S(2)}) collective-permute-start(bf16[512,128]{1,0:T(8,128)(2,1)S(1)} %get-tuple-element.61), channel_id=1, source_target_pairs={{0,16},{4,20},{8,24},{12,28},{16,0},{20,4},{24,8},{28,12},{1,17},{... | collective-permute-start | bytes 393224 | tf_op jit(solution)/shard_map/ppermute | solution.py:465
  45.9 11.1 %collective-permute-start.18 = (bf16[512,128]{1,0:T(8,128)(2,1)S(1)}, bf16[512,128]{1,0:T(8,128)(2,1)S(1)}, u32[]{:S(2)}, u32[]{:S(2)}) collective-permute-start(bf16[512,128]{1,0:T(8,128)(2,1)S(1)} %get-tuple-element.62), channel_id=1, source_target_pairs={{0,24},{4,28},{8,16},{12,20},{16,8},{20,12},{24,0},{28,4},{1,25},{... | collective-permute-start | bytes 393224 | tf_op jit(solution)/shard_map/ppermute | solution.py:465
  46.5 4.3 %collective-permute-start = (bf16[128,256]{1,0:T(8,128)(2,1)S(1)}, bf16[128,256]{1,0:T(8,128)(2,1)S(1)}, u32[]{:S(2)}, u32[]{:S(2)}) collective-permute-start(bf16[128,256]{1,0:T(8,128)(2,1)S(1)} %get-tuple-element.95), channel_id=1, source_target_pairs={{0,2},{2,0},{1,3},{3,1},{4,6},{6,4},{5,7},{7,5},{8,10},{10,8},{9,1... | collective-permute-start | bytes 196616 | tf_op jit(solution)/shard_map/while/body/ppermute | solution.py:524
  50.9 1.3 %collective-permute-start.1 = (bf16[128,256]{1,0:T(8,128)(2,1)S(1)}, bf16[128,256]{1,0:T(8,128)(2,1)S(1)}, u32[]{:S(2)}, u32[]{:S(2)}) collective-permute-start(bf16[128,256]{1,0:T(8,128)(2,1)S(1)} %add_convert_fusion.3.a), channel_id=1, source_target_pairs={{0,4},{4,0},{8,12},{12,8},{16,20},{20,16},{24,28},{28,24},{1,5},{5... | collective-permute-start | bytes 196616 | tf_op jit(solution)/shard_map/while/body/ppermute | solution.py:462

commit v4 on v3

--- a/solution.py
+++ b/solution.py
@@ -27,13 +27,10 @@
 
 def place_of(dims, block_row, block_col):
     n_z, n_col, blocks = dims
-    r, c = lax.axis_index("row"), lax.axis_index("col")
-    z, core = r // 2, r % 2
-    source, owner = block_col // blocks, block_row // blocks
-    j = 2 * (z ^ (source // 2)) + ((source + core) & 1)
-    t = c - owner
-    t = jnp.where(t < 0, t + n_col, t)
-    return ((j * n_col + t) * blocks + block_row % blocks) * blocks + block_col % blocks
+    bits, low = blocks.bit_length() - 1, blocks - 1
+    j = (block_col >> bits) ^ lax.axis_index("row")
+    t = (lax.axis_index("col") - (block_row >> bits)) & (n_col - 1)
+    return ((((j * n_col + t) << bits) | (block_row & low)) << bits) | (block_col & low)
 
 
 def densify_kernel(dims, groups, rows, cols, count, tiles, out, buffer, total, sems):
@@ -72,7 +69,7 @@
             total[place] += buffer[slot].astype(F32)
             return carry
 
-        lax.fori_loop(0, per_group, add, 0, unroll=4)
+        lax.fori_loop(0, per_group, add, 0, unroll=8)
 
     each_group(add_group)
 
@@ -161,29 +158,45 @@
     )(resident(dense), *xs, *totals)
 
 
-def backward_kernel(dense, *refs):
-    n_src, n_col = dense.shape[0], dense.shape[1]
-    pieces, outs = refs[:n_col], refs[-2:]
-    turned = [piece[...].astype(F32).T.astype(BF16) for piece in pieces]
-    for j in range(n_src):
-        total = jnp.dot(turned[0], dense[j, 0], preferred_element_type=F32)
-        for t in range(1, n_col):
-            total = total + jnp.dot(turned[t], dense[j, t], preferred_element_type=F32)
-        outs[j % 2][j // 2] = total.T.astype(BF16)
-
-
-def backward(dense, pieces, after):
+def own_kernel(dense, piece, out):
+    for j in range(dense.shape[0]):
+        out[j] = jnp.dot(piece[...], dense[j, 0], preferred_element_type=F32)
+
+
+def backward_own(dense, piece):
+    n_src, _, side, _ = dense.shape
+    return pl.pallas_call(
+        own_kernel,
+        out_shape=pltpu.VMEM((n_src, piece.shape[0], side), F32),
+        in_specs=[vmem()] * 2,
+        out_specs=vmem(),
+        compiler_params=params(),
+        cost_estimate=COST,
+        name="backward_own",
+    )(resident(dense), piece)
+
+
+def backward_kernel(dense, own, *refs):
+    pieces, outs = refs[: dense.shape[1] - 1], refs[-2:]
+    for j in range(dense.shape[0]):
+        total = own[j]
+        for t, piece in enumerate(pieces):
+            total = total + jnp.dot(piece[...], dense[j, t + 1], preferred_element_type=F32)
+        outs[j % 2][j // 2] = total.astype(BF16)
+
+
+def backward(dense, own, pieces, after):
     n_src, n_col, side, _ = dense.shape
-    feats = pieces[0].shape[1]
+    feats = own.shape[1]
     return pl.pallas_call(
         backward_kernel,
-        out_shape=(jax.ShapeDtypeStruct((n_src // 2, side, feats), BF16),) * 2,
+        out_shape=(jax.ShapeDtypeStruct((n_src // 2, feats, side), BF16),) * 2,
         in_specs=[vmem()] * (1 + n_col) + [pl.BlockSpec(memory_space=pl.ANY)],
         out_specs=(vmem(),) * 2,
         compiler_params=params(),
         cost_estimate=COST,
         name="backward",
-    )(resident(dense), *pieces, after)
+    )(resident(dense), resident(own), *pieces, after)
 
 
 def densify_stream_kernel(
@@ -338,7 +351,7 @@
     cot = jnp.concatenate([cot_own[...], cot_other[...]], axis=1).astype(F32)
     g = (cot * decay).astype(BF16)
     spread[...] = lax.dot_general(
-        g, top, (((1,), (1,)), ((), ())), preferred_element_type=F32
+        top, g, (((1,), (1,)), ((), ())), preferred_element_type=F32
     ).astype(BF16)
     g_own[...] = g[:, :half]
     g_other[...] = g[:, half:]
@@ -353,7 +366,8 @@
     n_col = len(own)
     return pl.pallas_call(
         functools.partial(middle_kernel, n_col),
-        out_shape=(jax.ShapeDtypeStruct((nodes, half), BF16),) * 5,
+        out_shape=(jax.ShapeDtypeStruct((half, nodes), BF16),)
+        + (jax.ShapeDtypeStruct((nodes, half), BF16),) * 4,
         in_specs=[vmem()] * (3 + 2 * n_col),
         out_specs=(vmem(),) * 5,
         compiler_params=params(),
@@ -385,36 +399,28 @@
 
 
 def backward_stream_kernel(n_col, a, *refs):
-    pieces, out, turned = refs[:n_col], refs[-2], refs[-1]
-
-    @pl.when(pl.program_id(0) == 0)
-    def _():
-        for t in range(n_col):
-            turned[t] = pieces[t][...].astype(F32).T.astype(BF16)
-
-    total = jnp.dot(turned[0], a[0, 0], preferred_element_type=F32)
+    pieces, out = refs[:n_col], refs[n_col]
+    total = jnp.dot(pieces[0][...], a[0, 0], preferred_element_type=F32)
     for t in range(1, n_col):
-        total = total + jnp.dot(turned[t], a[0, t], preferred_element_type=F32)
-    out[0] = total.T.astype(BF16)
-
-
-def backward_stream(dense, parity, pieces, after):
+        total = total + jnp.dot(pieces[t][...], a[0, t], preferred_element_type=F32)
+    out[0] = total.astype(BF16)
+
+
+def backward_stream(dense, parity, pieces):
     n_src, n_col, side, _ = dense.shape
-    feats = pieces[0].shape[1]
+    feats = pieces[0].shape[0]
     n_z = n_src // 2
     return pl.pallas_call(
         functools.partial(backward_stream_kernel, n_col),
         grid=(n_z,),
-        out_shape=jax.ShapeDtypeStruct((n_z, side, feats), BF16),
+        out_shape=jax.ShapeDtypeStruct((n_z, feats, side), BF16),
         in_specs=[pl.BlockSpec((1, n_col, side, side), lambda s: (2 * s + parity, 0, 0, 0))]
-        + [vmem()] * n_col
-        + [pl.BlockSpec(memory_space=pl.ANY)],
-        out_specs=pl.BlockSpec((1, side, feats), lambda s: (s, 0, 0)),
-        scratch_shapes=[pltpu.VMEM((n_col, feats, side), BF16)],
+        + [vmem()] * n_col,
+        out_specs=pl.BlockSpec((1, feats, side), lambda s: (s, 0, 0)),
         compiler_params=params(32),
         cost_estimate=COST,
         name="backward",
-    )(dense, *pieces, after)
+    )(dense, *pieces)
 
 
 def add_kernel(a, b, *rest):
@@ -449,6 +455,26 @@
         cost_estimate=COST,
         name="pair_sums",
     )(own, arrived)
+
+
+def turned_kernel(*refs):
+    total = refs[0][...].astype(F32)
+    for part in refs[1:-1]:
+        total = total + part[...].astype(F32)
+    refs[-1][...] = total.T.astype(BF16)
+
+
+def turned_sum(parts):
+    feats, nodes = parts[0].shape
+    return pl.pallas_call(
+        turned_kernel,
+        out_shape=jax.ShapeDtypeStruct((nodes, feats), BF16),
+        in_specs=[vmem()] * len(parts),
+        out_specs=vmem(),
+        compiler_params=params(),
+        cost_estimate=COST,
+        name="turned_sum",
+    )(*parts)
 
 
 def shards(features, tile_rows, tile_cols, tile_count, tile_values, weights, cotangent):
@@ -485,7 +511,10 @@
         cross = [sibling(v) for v in same]
         totals = forward(dense, [2 * s for s in range(1, n_z)], same, totals, False)
         parts = forward(dense, [2 * s + 1 for s in range(1, n_z)], cross, totals, True)
-        back_of = backward
+
+        def back_of(pieces, after):
+            return backward(dense, backward_own(dense, pieces[0]), pieces[1:], after)
+
     else:
         cross = [sibling(v) for v in same]
         dense = densify_stream(*cell)
@@ -494,8 +523,8 @@
             total = forward_stream(dense, s, same[s], cross[s], total)
         parts = total.astype(BF16).reshape(n_col, nodes, half)
 
-        def back_of(*operands):
-            return [backward_stream(operands[0], k, *operands[1:]) for k in range(2)]
+        def back_of(pieces, after):
+            return [backward_stream(dense, k, pieces) for k in range(2)]
 
     own = [parts[0]] + [to_group(parts[t], -t, 0) for t in range(1, n_col)]
     other = [to_group(parts[t], -t, 1) for t in range(n_col)]
@@ -507,14 +536,12 @@
     term = weight_term(*rest)
     term = add(term, along_z(term, 1))
 
-    even, odd = back_of(dense, pieces, term)
+    even, odd = back_of(pieces, term)
     arrived = sibling(odd)
     sums = pair_sums(even, arrived)
     if n_z > 2:
         term = add(term, along_z(term, 2), sums[0])
-    back = sums[0].astype(F32)
-    for s in range(1, n_z):
-        back = back + along_z(sums[s], s).astype(F32)
+    back = turned_sum([sums[0]] + [along_z(sums[s], s) for s in range(1, n_z)])
 
     def finish(_, v):
         for step in range(2, n_z.bit_length() - 1):
@@ -530,7 +557,7 @@
     once = lax.optimization_barrier(jnp.int32(1))
     whole = lax.fori_loop(0, once, finish, term)
     weight_grad = whole.astype(F32) * node_total ** (-0.5)
-    return (activated, back.astype(BF16), weight_grad)
+    return (activated, back, weight_grad)
 
 
 def solution(mesh):

time: 57.7 us -> 55.9 us (0.969)
  other arithmetic: 1.41 us -> 0.69 us
  waiting for transfers between devices: 18.4 us -> 17.7 us
    ppermute x6, starting transfers between devices: 3 us -> 1.3 us  [sibling(): return lax.ppermute(v, 'row', [(i, i ^ 1) for i in range(n_row)])]
    pallas_call x0 -> x2, Pallas kernels: none -> 1.5 us  [the longest x1 0.79 us: turned_sum(): pl.pallas_call(turned_kernel, out_shape=jax.ShapeDtypeStruct((nodes, feat...]
    ppermute x1, starting transfers between devices: 0.36 us -> 1.52 us  [shards(): lax.ppermute(spread, 'col', [(i, (i + t) % n_col) for i in range(n_col)])]
    pallas_call x1, Pallas kernels: 6.49 us -> 5.57 us  [densify(): pl.pallas_call(functools.partial(densify_kernel, (n_z, n_col, blocks), gr...]
    ppermute x8, waiting for transfers between devices: 7.22 us -> 6.3 us  [along_z(): return lax.ppermute(v, 'row', [(i, i ^ 2 * s) for i in range(n_row)])]
    convert_element_type x1 -> x0, other arithmetic: 0.73 us -> none  [shards(): return (activated, back.astype(BF16), weight_grad)]
    pallas_call x1, Pallas kernels: 1.39 us -> 0.71 us  [backward(): pl.pallas_call(backward_kernel, out_shape=(jax.ShapeDtypeStruct((n_src //...]
  transfers between devices with their start and end apart: 20 -> 20, of which waited for: 8 -> 9; matrix products, arithmetic and copies ran while one was open for 1% -> 1% of each run, Pallas kernels for 15% -> 15%
where the time goes in v4:
time: 55.9 us; the launch traced here: 55.7 us
  starting transfers between devices  24 us (43%)
  waiting for transfers between devices  17.7 us (32%)
  Pallas kernels  11.9 us (21%)
  between operations  1.44 us (3%)
  other arithmetic  0.69 us (1%)
    ppermute x8, starting transfers between devices, along_z(): return lax.ppermute(v, 'row', [(i, i ^ 2 * s) for i in range(n_row)])  15.4 us
    ppermute x8, waiting for transfers between devices, along_z(): return lax.ppermute(v, 'row', [(i, i ^ 2 * s) for i in range(n_row)])  6.3 us
    ppermute x3, waiting for transfers between devices, to_group(): return lax.ppermute(v, ('col', 'feat'), pairs)  6.09 us
    pallas_call x1, Pallas kernels, densify(): pl.pallas_call(functools.partial(densify_kernel, (n_z, n_col, blocks), gr...  5.57 us
    ppermute x1, waiting for transfers between devices, finish(): lax.ppermute(v, 'col', [(i, (i + t) % n_col) for i in range(n_col)])  3.77 us
    ppermute x3, starting transfers between devices, to_group(): return lax.ppermute(v, ('col', 'feat'), pairs)  3.55 us
    pallas_call x3, Pallas kernels, forward(): pl.pallas_call(functools.partial(forward_kernel, places, last), out_shape...  2.66 us
    ppermute x1, starting transfers between devices, other_feat(): return lax.ppermute(v, 'feat', [(0, 1), (1, 0)])  1.71 us
  transfers between devices with their start and end apart: 20, of which 9 were waited for; matrix products, arithmetic and copies ran while one was open for 1% of the time, Pallas kernels for 15%

profile of v4, /device:TPU:0, one launch (start us, length us, event | category | flops | bytes accessed | tf_op | source)
XLA Modules:
  0.0 55.7 jit_solution(8264052437119168528)
XLA Ops:
  0.6 0.5 collective-permute-start.6
  1.1 2.6 %collective-permute-start.2 = (bf16[512,128]{1,0:T(8,128)(2,1)}, bf16[512,128]{1,0:T(8,128)(2,1)S(1)}, u32[]{:S(2)}, u32[]{:S(2)}) collective-permute-start(bf16[512,128]{1,0:T(8,128)(2,1)} %refs_0_.1), channel_id=1, source_target_pairs={{0,8},{4,12},{8,0},{12,4},{16,24},{20,28},{24,16},{28,20},{1,9},{5... | collective-permute-start | bytes 393224 | tf_op jit(solution)/shard_map/ppermute | solution.py:491
  3.8 2.6 %collective-permute-start.3 = (bf16[512,128]{1,0:T(8,128)(2,1)}, bf16[512,128]{1,0:T(8,128)(2,1)S(1)}, u32[]{:S(2)}, u32[]{:S(2)}) collective-permute-start(bf16[512,128]{1,0:T(8,128)(2,1)} %refs_0_.1), channel_id=1, source_target_pairs={{0,16},{4,20},{8,24},{12,28},{16,0},{20,4},{24,8},{28,12},{1,17},{... | collective-permute-start | bytes 393224 | tf_op jit(solution)/shard_map/ppermute | solution.py:491
  6.4 0.0 collective-permute-start.4
  6.4 1.7 %collective-permute-start.5 = (bf16[512,128]{1,0:T(8,128)(2,1)}, bf16[512,128]{1,0:T(8,128)(2,1)S(1)}, u32[]{:S(2)}, u32[]{:S(2)}) collective-permute-start(bf16[512,128]{1,0:T(8,128)(2,1)} %cot_own.1), channel_id=1, source_target_pairs={{0,1},{1,0},{2,3},{3,2},{4,5},{5,4},{6,7},{7,6},{8,9},{9,8},{10,11... | collective-permute-start | bytes 393224 | tf_op jit(solution)/shard_map/ppermute | solution.py:494
  8.8 0.0 copy-start
  8.8 5.6 %densify.1.dense = bf16[8,2,512,512]{3,2,1,0:T(8,128)(2,1)S(1)} custom-call(s32[1,1,256]{2,1,0:T(1,128)} %rows.1, s32[1,1,256]{2,1,0:T(1,128)} %cols.1, s32[1,1]{1,0:T(1,128)S(6)} %copy.25.count, bf16[256,128,128]{2,1,0:T(8,128)(2,1)} %bitcast.1), custom_call_target="tpu_custom_call" | custom-call | flops 1 | bytes 1 | tf_op jit(solution)/shard_map/densify/pallas_call | solution.py:93
  14.3 0.0 collective-permute-done.6.refs_1_
  14.4 0.0 copy-done
  14.4 0.7 %forward.3 = (f32[512,128]{1,0:T(8,128)S(1)}, f32[512,128]{1,0:T(8,128)S(1)}) custom-call(bf16[8,2,512,512]{3,2,1,0:T(8,128)(2,1)S(1)} %densify.1.dense, bf16[512,128]{1,0:T(8,128)(2,1)S(1)} %copy-done, bf16[512,128]{1,0:T(8,128)(2,1)S(1)} %collective-permute-done.6.refs_1_), custom_call_target="tpu_custom_call" | custom-call | flops 1 | bytes 1 | tf_op jit(solution)/shard_map/forward/pallas_call | solution.py:150
  15.1 0.0 collective-permute-done.2.refs_0_
  15.1 1.8 %collective-permute-done.3.refs_1_ = bf16[512,128]{1,0:T(8,128)(2,1)S(1)} collective-permute-done((bf16[512,128]{1,0:T(8,128)(2,1)}, bf16[512,128]{1,0:T(8,128)(2,1)S(1)}, u32[]{:S(2)}, u32[]{:S(2)}) %collective-permute-start.3) | collective-permute-done | bytes 131104 | tf_op jit(solution)/shard_map/ppermute | solution.py:491
  16.9 0.0 collective-permute-done.4.refs_2_
  16.9 0.0 collective-permute-done.5.refs_3_
  16.9 0.1 collective-permute-start.7
  17.0 0.5 collective-permute-start.8
  17.5 0.1 collective-permute-start.9
  17.6 0.0 copy-start.1
  17.6 0.0 copy-start.2
  17.6 1.0 %forward.4 = (f32[512,128]{1,0:T(8,128)S(1)}, f32[512,128]{1,0:T(8,128)S(1)}) custom-call(bf16[8,2,512,512]{3,2,1,0:T(8,128)(2,1)S(1)} %densify.1.dense, bf16[512,128]{1,0:T(8,128)(2,1)S(1)} %get-tuple-element.44.refs_0_, bf16[512,128]{1,0:T(8,128)(2,1)S(1)} %get-tuple-element.45.refs_1_, bf16[512,128]{1,0:T(8,128)(2,1)S(1)} %get-tuple-element.46.refs_2_, ...), custom_call_target="tpu_custom_call" | custom-call | flops 1 | bytes 1 | tf_op jit(solution)/shard_map/forward/pallas_call | solution.py:150
  18.6 0.0 collective-permute-done.7.refs_0_
  18.6 0.0 collective-permute-done.8.refs_1_
  18.6 0.3 collective-permute-done.9.refs_2_
  18.8 1.0 %forward.5 = (bf16[512,128]{1,0:T(8,128)(2,1)S(1)}, bf16[512,128]{1,0:T(8,128)(2,1)S(1)}) custom-call(bf16[8,2,512,512]{3,2,1,0:T(8,128)(2,1)S(1)} %densify.1.dense, bf16[512,128]{1,0:T(8,128)(2,1)S(1)} %collective-permute-done.7.refs_0_, bf16[512,128]{1,0:T(8,128)(2,1)S(1)} %collective-permute-done.8.refs_1_, ...), custom_call_target="tpu_custom_call" | custom-call | flops 1 | bytes 1 | tf_op jit(solution)/shard_map/forward/pallas_call | solution.py:150
  19.8 1.6 %collective-permute-start.10 = (bf16[512,128]{1,0:T(8,128)(2,1)S(1)}, bf16[512,128]{1,0:T(8,128)(2,1)S(1)}, u32[]{:S(2)}, u32[]{:S(2)}) collective-permute-start(bf16[512,128]{1,0:T(8,128)(2,1)S(1)} %get-tuple-element.51), channel_id=1, source_target_pairs={{0,2},{1,3},{2,0},{3,1},{4,6},{5,7},{6,4},{7,5},{8,10},{9,11},{10,... | collective-permute-start | bytes 393224 | tf_op jit(solution)/shard_map/ppermute | solution.py:501
  21.4 1.5 %collective-permute-start.11 = (bf16[512,128]{1,0:T(8,128)(2,1)S(1)}, bf16[512,128]{1,0:T(8,128)(2,1)S(1)}, u32[]{:S(2)}, u32[]{:S(2)}) collective-permute-start(bf16[512,128]{1,0:T(8,128)(2,1)S(1)} %get-tuple-element.50.refs_0_), channel_id=1, source_target_pairs={{0,1},{1,0},{2,3},{3,2},{4,5},{5,4},{6,7},{7,6},{8,9},{9,8},{10,11... | collective-permute-start | bytes 393224 | tf_op jit(solution)/shard_map/ppermute | solution.py:501
  22.9 0.5 collective-permute-start.12
  23.4 2.1 %collective-permute-done.10.refs_1_ = bf16[512,128]{1,0:T(8,128)(2,1)S(1)} collective-permute-done((bf16[512,128]{1,0:T(8,128)(2,1)S(1)}, bf16[512,128]{1,0:T(8,128)(2,1)S(1)}, u32[]{:S(2)}, u32[]{:S(2)}) %collective-permute-start.10) | collective-permute-done | bytes 131104 | tf_op jit(solution)/shard_map/ppermute | solution.py:501
  25.5 2.3 %collective-permute-done.11.refs_2_ = bf16[512,128]{1,0:T(8,128)(2,1)S(1)} collective-permute-done((bf16[512,128]{1,0:T(8,128)(2,1)S(1)}, bf16[512,128]{1,0:T(8,128)(2,1)S(1)}, u32[]{:S(2)}, u32[]{:S(2)}) %collective-permute-start.11) | collective-permute-done | bytes 131104 | tf_op jit(solution)/shard_map/ppermute | solution.py:501
  27.8 1.7 %collective-permute-done.12.refs_3_ = bf16[512,128]{1,0:T(8,128)(2,1)S(1)} collective-permute-done((bf16[512,128]{1,0:T(8,128)(2,1)S(1)}, bf16[512,128]{1,0:T(8,128)(2,1)S(1)}, u32[]{:S(2)}, u32[]{:S(2)}) %collective-permute-start.12) | collective-permute-done | bytes 131104 | tf_op jit(solution)/shard_map/ppermute | solution.py:501
  29.5 0.0 copy-done.1
  29.5 0.0 copy-done.2
  29.5 1.0 %middle.1 = (bf16[128,512]{1,0:T(8,128)(2,1)S(1)}, bf16[512,128]{1,0:T(8,128)(2,1)}, bf16[512,128]{1,0:T(8,128)(2,1)S(1)}, bf16[512,128]{1,0:T(8,128)(2,1)S(1)}, bf16[512,128]{1,0:T(8,128)(2,1)S(1)}) custom-call(bf16[256,256]{1,0:T(8,128)(2,1)S(1)} %copy-done.1, bf16[512,128]{1,0:T(8,128)(2,1)S(1)} %copy-done.2, ...), custom_call_target="tpu_custom_call" | custom-call | flops 1 | bytes 1 | tf_op jit(solution)/shard_map/middle/pallas_call | solution.py:367
  30.4 1.5 %collective-permute-start.13 = (bf16[128,512]{1,0:T(8,128)(2,1)S(1)}, bf16[128,512]{1,0:T(8,128)(2,1)S(1)}, u32[]{:S(2)}, u32[]{:S(2)}) collective-permute-start(bf16[128,512]{1,0:T(8,128)(2,1)S(1)} %get-tuple-element.53.piece), channel_id=1, source_target_pairs={{0,2},{2,0},{1,3},{3,1},{4,6},{6,4},{5,7},{7,5},{8,10},{10,8},{9,1... | collective-permute-start | bytes 393224 | tf_op jit(solution)/shard_map/ppermute | solution.py:533
  32.0 0.3 weight_term.1.a
  32.2 2.6 %collective-permute-start.14 = (bf16[128,256]{1,0:T(8,128)(2,1)S(1)}, bf16[128,256]{1,0:T(8,128)(2,1)S(1)}, u32[]{:S(2)}, u32[]{:S(2)}) collective-permute-start(bf16[128,256]{1,0:T(8,128)(2,1)S(1)} %weight_term.1.a), channel_id=1, source_target_pairs={{0,8},{4,12},{8,0},{12,4},{16,24},{20,28},{24,16},{28,20},{1,9},{5... | collective-permute-start | bytes 196616 | tf_op jit(solution)/shard_map/ppermute | solution.py:491
  34.9 0.7 %backward_own.1.own = f32[8,128,512]{2,1,0:T(8,128)S(1)} custom-call(bf16[8,2,512,512]{3,2,1,0:T(8,128)(2,1)S(1)} %densify.1.dense, bf16[128,512]{1,0:T(8,128)(2,1)S(1)} %get-tuple-element.53.piece), custom_call_target="tpu_custom_call" | custom-call | flops 1 | bytes 1 | tf_op jit(solution)/shard_map/backward_own/pallas_call | solution.py:168
  35.6 1.5 %collective-permute-done.14.b = bf16[128,256]{1,0:T(8,128)(2,1)S(1)} collective-permute-done((bf16[128,256]{1,0:T(8,128)(2,1)S(1)}, bf16[128,256]{1,0:T(8,128)(2,1)S(1)}, u32[]{:S(2)}, u32[]{:S(2)}) %collective-permute-start.14) | collective-permute-done | bytes 65568 | tf_op jit(solution)/shard_map/ppermute | solution.py:491
  37.1 0.0 collective-permute-done.13.refs_0_
  37.1 0.7 %backward.1 = (bf16[4,128,512]{2,1,0:T(8,128)(2,1)S(1)}, bf16[4,128,512]{2,1,0:T(8,128)(2,1)S(1)}) custom-call(bf16[8,2,512,512]{3,2,1,0:T(8,128)(2,1)S(1)} %densify.1.dense, f32[8,128,512]{2,1,0:T(8,128)S(1)} %backward_own.1.own, bf16[128,512]{1,0:T(8,128)(2,1)S(1)} %collective-permute-done.13.refs_0_, bf16[128,256]{1,0:T(8,128)(2,1)S(1)} %add.14.refs_1_.a), custom_call_target="tpu_custom_call" | custom-call | flops 1 | bytes 1 | tf_op jit(solution)/shard_map/backward/pallas_call | solution.py:191
  37.9 0.1 collective-permute-start.15
  37.9 3.1 %collective-permute-start.19 = (bf16[128,256]{1,0:T(8,128)(2,1)S(1)}, bf16[128,256]{1,0:T(8,128)(2,1)S(1)}, u32[]{:S(2)}, u32[]{:S(2)}) collective-permute-start(bf16[128,256]{1,0:T(8,128)(2,1)S(1)} %add.14.refs_1_.a), channel_id=1, source_target_pairs={{0,16},{4,20},{8,24},{12,28},{16,0},{20,4},{24,8},{28,12},{1,17},{... | collective-permute-start | bytes 196616 | tf_op jit(solution)/shard_map/ppermute | solution.py:491
  41.0 0.0 collective-permute-done.15.arrived
  41.0 0.1 pair_sums.1
  41.2 0.9 %collective-permute-start.16 = (bf16[128,512]{1,0:T(8,128)(2,1)S(1)}, bf16[128,512]{1,0:T(8,128)(2,1)S(1)}, u32[]{:S(2)}, u32[]{:S(2)}) collective-permute-start(bf16[128,512]{1,0:T(8,128)(2,1)S(1)} %get-tuple-element.60), channel_id=1, source_target_pairs={{0,8},{4,12},{8,0},{12,4},{16,24},{20,28},{24,16},{28,20},{1,9},{5... | collective-permute-start | bytes 393224 | tf_op jit(solution)/shard_map/ppermute | solution.py:491
  42.0 1.1 %collective-permute-start.17 = (bf16[128,512]{1,0:T(8,128)(2,1)S(1)}, bf16[128,512]{1,0:T(8,128)(2,1)S(1)}, u32[]{:S(2)}, u32[]{:S(2)}) collective-permute-start(bf16[128,512]{1,0:T(8,128)(2,1)S(1)} %get-tuple-element.61), channel_id=1, source_target_pairs={{0,16},{4,20},{8,24},{12,28},{16,0},{20,4},{24,8},{28,12},{1,17},{... | collective-permute-start | bytes 393224 | tf_op jit(solution)/shard_map/ppermute | solution.py:491
  43.1 2.5 %collective-permute-start.18 = (bf16[128,512]{1,0:T(8,128)(2,1)S(1)}, bf16[128,512]{1,0:T(8,128)(2,1)S(1)}, u32[]{:S(2)}, u32[]{:S(2)}) collective-permute-start(bf16[128,512]{1,0:T(8,128)(2,1)S(1)} %get-tuple-element.62), channel_id=1, source_target_pairs={{0,24},{4,28},{8,16},{12,20},{16,8},{20,12},{24,0},{28,4},{1,25},{... | collective-permute-start | bytes 393224 | tf_op jit(solution)/shard_map/ppermute | solution.py:491
  45.6 0.0 collective-permute-done.19.b
  45.6 5.7 %while.10 = (s32[]{:T(128)}, bf16[128,256]{1,0:T(8,128)(2,1)S(1)}, s32[]{:T(128)}, s32[]{:T(128)}) while((s32[]{:T(128)}, bf16[128,256]{1,0:T(8,128)(2,1)S(1)}, s32[]{:T(128)}, s32[]{:T(128)}) %tuple.22), condition=%wide.region_1.0_spmd, body=%wide.region_0.0_spmd.sunk | while | flops 131075 | bytes 721030 | solution.py:558
  45.6 0.6 %collective-permute-start = (bf16[128,256]{1,0:T(8,128)(2,1)S(1)}, bf16[128,256]{1,0:T(8,128)(2,1)S(1)}, u32[]{:S(2)}, u32[]{:S(2)}) collective-permute-start(bf16[128,256]{1,0:T(8,128)(2,1)S(1)} %get-tuple-element.95), channel_id=1, source_target_pairs={{0,2},{2,0},{1,3},{3,1},{4,6},{6,4},{5,7},{7,5},{8,10},{10,8},{9,1... | collective-permute-start | bytes 196616 | tf_op jit(solution)/shard_map/while/body/ppermute | solution.py:551
  46.2 3.8 %collective-permute-done = bf16[128,256]{1,0:T(8,128)(2,1)S(1)} collective-permute-done((bf16[128,256]{1,0:T(8,128)(2,1)S(1)}, bf16[128,256]{1,0:T(8,128)(2,1)S(1)}, u32[]{:S(2)}, u32[]{:S(2)}) %collective-permute-start) | collective-permute-done | bytes 65568 | tf_op jit(solution)/shard_map/while/body/ppermute | solution.py:551
  50.0 0.1 collective-permute-start.1
  50.1 1.2 %collective-permute-done.1.b = bf16[128,256]{1,0:T(8,128)(2,1)S(1)} collective-permute-done((bf16[128,256]{1,0:T(8,128)(2,1)S(1)}, bf16[128,256]{1,0:T(8,128)(2,1)S(1)}, u32[]{:S(2)}, u32[]{:S(2)}) %collective-permute-start.1) | collective-permute-done | bytes 65568 | tf_op jit(solution)/shard_map/while/body/ppermute | solution.py:488
  51.4 0.7 %convert_multiply_fusion = f32[128,256]{1,0:T(8,128)} fusion(bf16[128,256]{1,0:T(8,128)(2,1)S(1)} %get-tuple-element.63), kind=kLoop, calls=%fused_computation.1 | loop fusion | flops 65536 | bytes 196608 | tf_op jit(solution)/shard_map/mul | solution.py:559
  52.0 0.0 collective-permute-done.16.refs_1_
  52.0 2.9 %collective-permute-done.17.refs_2_ = bf16[128,512]{1,0:T(8,128)(2,1)S(1)} collective-permute-done((bf16[128,512]{1,0:T(8,128)(2,1)S(1)}, bf16[128,512]{1,0:T(8,128)(2,1)S(1)}, u32[]{:S(2)}, u32[]{:S(2)}) %collective-permute-start.17) | collective-permute-done | bytes 131104 | tf_op jit(solution)/shard_map/ppermute | solution.py:491
  54.9 0.0 collective-permute-done.18.refs_3_
  55.0 0.8 %turned_sum.1 = bf16[512,128]{1,0:T(8,128)(2,1)} custom-call(bf16[128,512]{1,0:T(8,128)(2,1)S(1)} %get-tuple-element.59.refs_0_.rest_0_, bf16[128,512]{1,0:T(8,128)(2,1)S(1)} %collective-permute-done.16.refs_1_, bf16[128,512]{1,0:T(8,128)(2,1)S(1)} %collective-permute-done.17.refs_2_, bf16[128,512]{1,0:T(8,128)(2,1)S(1)} %collective-permute-done.18.refs_3_), custom_call_target="tpu_custom_call" | custom-call | flops 1 | bytes 1 | tf_op jit(solution)/shard_map/turned_sum/pallas_call | solution.py:469
  (5 shorter events, 0.1 us)
Async XLA Ops:
  0.6 13.7 %collective-permute-start.6 = (bf16[512,128]{1,0:T(8,128)(2,1)}, bf16[512,128]{1,0:T(8,128)(2,1)S(1)}, u32[]{:S(2)}, u32[]{:S(2)}) collective-permute-start(bf16[512,128]{1,0:T(8,128)(2,1)} %refs_0_.1), channel_id=1, source_target_pairs={{0,4},{4,0},{8,12},{12,8},{16,20},{20,16},{24,28},{28,24},{1,5},{5... | collective-permute-start | bytes 393224 | tf_op jit(solution)/shard_map/ppermute | solution.py:488
  1.1 13.9 %collective-permute-start.2 = (bf16[512,128]{1,0:T(8,128)(2,1)}, bf16[512,128]{1,0:T(8,128)(2,1)S(1)}, u32[]{:S(2)}, u32[]{:S(2)}) collective-permute-start(bf16[512,128]{1,0:T(8,128)(2,1)} %refs_0_.1), channel_id=1, source_target_pairs={{0,8},{4,12},{8,0},{12,4},{16,24},{20,28},{24,16},{28,20},{1,9},{5... | collective-permute-start | bytes 393224 | tf_op jit(solution)/shard_map/ppermute | solution.py:491
  3.8 13.1 %collective-permute-start.3 = (bf16[512,128]{1,0:T(8,128)(2,1)}, bf16[512,128]{1,0:T(8,128)(2,1)S(1)}, u32[]{:S(2)}, u32[]{:S(2)}) collective-permute-start(bf16[512,128]{1,0:T(8,128)(2,1)} %refs_0_.1), channel_id=1, source_target_pairs={{0,16},{4,20},{8,24},{12,28},{16,0},{20,4},{24,8},{28,12},{1,17},{... | collective-permute-start | bytes 393224 | tf_op jit(solution)/shard_map/ppermute | solution.py:491
  6.4 10.5 %collective-permute-start.4 = (bf16[512,128]{1,0:T(8,128)(2,1)}, bf16[512,128]{1,0:T(8,128)(2,1)S(1)}, u32[]{:S(2)}, u32[]{:S(2)}) collective-permute-start(bf16[512,128]{1,0:T(8,128)(2,1)} %refs_0_.1), channel_id=1, source_target_pairs={{0,24},{4,28},{8,16},{12,20},{16,8},{20,12},{24,0},{28,4},{1,25},{... | collective-permute-start | bytes 393224 | tf_op jit(solution)/shard_map/ppermute | solution.py:491
  6.4 10.5 %collective-permute-start.5 = (bf16[512,128]{1,0:T(8,128)(2,1)}, bf16[512,128]{1,0:T(8,128)(2,1)S(1)}, u32[]{:S(2)}, u32[]{:S(2)}) collective-permute-start(bf16[512,128]{1,0:T(8,128)(2,1)} %cot_own.1), channel_id=1, source_target_pairs={{0,1},{1,0},{2,3},{3,2},{4,5},{5,4},{6,7},{7,6},{8,9},{9,8},{10,11... | collective-permute-start | bytes 393224 | tf_op jit(solution)/shard_map/ppermute | solution.py:494
  8.8 5.6 %copy-start = (bf16[512,128]{1,0:T(8,128)(2,1)S(1)}, bf16[512,128]{1,0:T(8,128)(2,1)}, u32[]{:S(2)}) copy-start(bf16[512,128]{1,0:T(8,128)(2,1)} %refs_0_.1) | copy-start | bytes 393220
  16.9 1.6 %collective-permute-start.7 = (bf16[512,128]{1,0:T(8,128)(2,1)S(1)}, bf16[512,128]{1,0:T(8,128)(2,1)S(1)}, u32[]{:S(2)}, u32[]{:S(2)}) collective-permute-start(bf16[512,128]{1,0:T(8,128)(2,1)S(1)} %get-tuple-element.44.refs_0_), channel_id=1, source_target_pairs={{0,4},{4,0},{8,12},{12,8},{16,20},{20,16},{24,28},{28,24},{1,5},{5... | collective-permute-start | bytes 393224 | tf_op jit(solution)/shard_map/ppermute | solution.py:488
  17.0 1.6 %collective-permute-start.8 = (bf16[512,128]{1,0:T(8,128)(2,1)S(1)}, bf16[512,128]{1,0:T(8,128)(2,1)S(1)}, u32[]{:S(2)}, u32[]{:S(2)}) collective-permute-start(bf16[512,128]{1,0:T(8,128)(2,1)S(1)} %get-tuple-element.45.refs_1_), channel_id=1, source_target_pairs={{0,4},{4,0},{8,12},{12,8},{16,20},{20,16},{24,28},{28,24},{1,5},{5... | collective-permute-start | bytes 393224 | tf_op jit(solution)/shard_map/ppermute | solution.py:488
  17.5 1.3 %collective-permute-start.9 = (bf16[512,128]{1,0:T(8,128)(2,1)S(1)}, bf16[512,128]{1,0:T(8,128)(2,1)S(1)}, u32[]{:S(2)}, u32[]{:S(2)}) collective-permute-start(bf16[512,128]{1,0:T(8,128)(2,1)S(1)} %get-tuple-element.46.refs_2_), channel_id=1, source_target_pairs={{0,4},{4,0},{8,12},{12,8},{16,20},{20,16},{24,28},{28,24},{1,5},{5... | collective-permute-start | bytes 393224 | tf_op jit(solution)/shard_map/ppermute | solution.py:488
  17.6 11.9 %copy-start.1 = (bf16[256,256]{1,0:T(8,128)(2,1)S(1)}, bf16[256,256]{1,0:T(8,128)(2,1)}, u32[]{:S(2)}) copy-start(bf16[256,256]{1,0:T(8,128)(2,1)} %weights.1) | copy-start | bytes 393220
  17.6 11.9 %copy-start.2 = (bf16[512,128]{1,0:T(8,128)(2,1)S(1)}, bf16[512,128]{1,0:T(8,128)(2,1)}, u32[]{:S(2)}) copy-start(bf16[512,128]{1,0:T(8,128)(2,1)} %cot_own.1) | copy-start | bytes 393220
  19.8 5.7 %collective-permute-start.10 = (bf16[512,128]{1,0:T(8,128)(2,1)S(1)}, bf16[512,128]{1,0:T(8,128)(2,1)S(1)}, u32[]{:S(2)}, u32[]{:S(2)}) collective-permute-start(bf16[512,128]{1,0:T(8,128)(2,1)S(1)} %get-tuple-element.51), channel_id=1, source_target_pairs={{0,2},{1,3},{2,0},{3,1},{4,6},{5,7},{6,4},{7,5},{8,10},{9,11},{10,... | collective-permute-start | bytes 393224 | tf_op jit(solution)/shard_map/ppermute | solution.py:501
  21.4 6.4 %collective-permute-start.11 = (bf16[512,128]{1,0:T(8,128)(2,1)S(1)}, bf16[512,128]{1,0:T(8,128)(2,1)S(1)}, u32[]{:S(2)}, u32[]{:S(2)}) collective-permute-start(bf16[512,128]{1,0:T(8,128)(2,1)S(1)} %get-tuple-element.50.refs_0_), channel_id=1, source_target_pairs={{0,1},{1,0},{2,3},{3,2},{4,5},{5,4},{6,7},{7,6},{8,9},{9,8},{10,11... | collective-permute-start | bytes 393224 | tf_op jit(solution)/shard_map/ppermute | solution.py:501
  22.9 6.6 %collective-permute-start.12 = (bf16[512,128]{1,0:T(8,128)(2,1)S(1)}, bf16[512,128]{1,0:T(8,128)(2,1)S(1)}, u32[]{:S(2)}, u32[]{:S(2)}) collective-permute-start(bf16[512,128]{1,0:T(8,128)(2,1)S(1)} %get-tuple-element.51), channel_id=1, source_target_pairs={{0,3},{1,2},{2,1},{3,0},{4,7},{5,6},{6,5},{7,4},{8,11},{9,10},{10,... | collective-permute-start | bytes 393224 | tf_op jit(solution)/shard_map/ppermute | solution.py:501
  30.4 6.7 %collective-permute-start.13 = (bf16[128,512]{1,0:T(8,128)(2,1)S(1)}, bf16[128,512]{1,0:T(8,128)(2,1)S(1)}, u32[]{:S(2)}, u32[]{:S(2)}) collective-permute-start(bf16[128,512]{1,0:T(8,128)(2,1)S(1)} %get-tuple-element.53.piece), channel_id=1, source_target_pairs={{0,2},{2,0},{1,3},{3,1},{4,6},{6,4},{5,7},{7,5},{8,10},{10,8},{9,1... | collective-permute-start | bytes 393224 | tf_op jit(solution)/shard_map/ppermute | solution.py:533
  32.2 4.9 %collective-permute-start.14 = (bf16[128,256]{1,0:T(8,128)(2,1)S(1)}, bf16[128,256]{1,0:T(8,128)(2,1)S(1)}, u32[]{:S(2)}, u32[]{:S(2)}) collective-permute-start(bf16[128,256]{1,0:T(8,128)(2,1)S(1)} %weight_term.1.a), channel_id=1, source_target_pairs={{0,8},{4,12},{8,0},{12,4},{16,24},{20,28},{24,16},{28,20},{1,9},{5... | collective-permute-start | bytes 196616 | tf_op jit(solution)/shard_map/ppermute | solution.py:491
  37.9 3.2 %collective-permute-start.15 = (bf16[4,128,512]{2,1,0:T(8,128)(2,1)S(1)}, bf16[4,128,512]{2,1,0:T(8,128)(2,1)S(1)}, u32[]{:S(2)}, u32[]{:S(2)}) collective-permute-start(bf16[4,128,512]{2,1,0:T(8,128)(2,1)S(1)} %get-tuple-element.58), channel_id=1, source_target_pairs={{0,4},{4,0},{8,12},{12,8},{16,20},{20,16},{24,28},{28,24},{1,5},{5... | collective-permute-start | bytes 1572872 | tf_op jit(solution)/shard_map/ppermute | solution.py:488
  37.9 7.7 %collective-permute-start.19 = (bf16[128,256]{1,0:T(8,128)(2,1)S(1)}, bf16[128,256]{1,0:T(8,128)(2,1)S(1)}, u32[]{:S(2)}, u32[]{:S(2)}) collective-permute-start(bf16[128,256]{1,0:T(8,128)(2,1)S(1)} %add.14.refs_1_.a), channel_id=1, source_target_pairs={{0,16},{4,20},{8,24},{12,28},{16,0},{20,4},{24,8},{28,12},{1,17},{... | collective-permute-start | bytes 196616 | tf_op jit(solution)/shard_map/ppermute | solution.py:491
  41.2 10.9 %collective-permute-start.16 = (bf16[128,512]{1,0:T(8,128)(2,1)S(1)}, bf16[128,512]{1,0:T(8,128)(2,1)S(1)}, u32[]{:S(2)}, u32[]{:S(2)}) collective-permute-start(bf16[128,512]{1,0:T(8,128)(2,1)S(1)} %get-tuple-element.60), channel_id=1, source_target_pairs={{0,8},{4,12},{8,0},{12,4},{16,24},{20,28},{24,16},{28,20},{1,9},{5... | collective-permute-start | bytes 393224 | tf_op jit(solution)/shard_map/ppermute | solution.py:491
  42.0 12.9 %collective-permute-start.17 = (bf16[128,512]{1,0:T(8,128)(2,1)S(1)}, bf16[128,512]{1,0:T(8,128)(2,1)S(1)}, u32[]{:S(2)}, u32[]{:S(2)}) collective-permute-start(bf16[128,512]{1,0:T(8,128)(2,1)S(1)} %get-tuple-element.61), channel_id=1, source_target_pairs={{0,16},{4,20},{8,24},{12,28},{16,0},{20,4},{24,8},{28,12},{1,17},{... | collective-permute-start | bytes 393224 | tf_op jit(solution)/shard_map/ppermute | solution.py:491
  43.1 11.8 %collective-permute-start.18 = (bf16[128,512]{1,0:T(8,128)(2,1)S(1)}, bf16[128,512]{1,0:T(8,128)(2,1)S(1)}, u32[]{:S(2)}, u32[]{:S(2)}) collective-permute-start(bf16[128,512]{1,0:T(8,128)(2,1)S(1)} %get-tuple-element.62), channel_id=1, source_target_pairs={{0,24},{4,28},{8,16},{12,20},{16,8},{20,12},{24,0},{28,4},{1,25},{... | collective-permute-start | bytes 393224 | tf_op jit(solution)/shard_map/ppermute | solution.py:491
  45.6 4.3 %collective-permute-start = (bf16[128,256]{1,0:T(8,128)(2,1)S(1)}, bf16[128,256]{1,0:T(8,128)(2,1)S(1)}, u32[]{:S(2)}, u32[]{:S(2)}) collective-permute-start(bf16[128,256]{1,0:T(8,128)(2,1)S(1)} %get-tuple-element.95), channel_id=1, source_target_pairs={{0,2},{2,0},{1,3},{3,1},{4,6},{6,4},{5,7},{7,5},{8,10},{10,8},{9,1... | collective-permute-start | bytes 196616 | tf_op jit(solution)/shard_map/while/body/ppermute | solution.py:551
  50.0 1.3 %collective-permute-start.1 = (bf16[128,256]{1,0:T(8,128)(2,1)S(1)}, bf16[128,256]{1,0:T(8,128)(2,1)S(1)}, u32[]{:S(2)}, u32[]{:S(2)}) collective-permute-start(bf16[128,256]{1,0:T(8,128)(2,1)S(1)} %add_convert_fusion.2.a), channel_id=1, source_target_pairs={{0,4},{4,0},{8,12},{12,8},{16,20},{20,16},{24,28},{28,24},{1,5},{5... | collective-permute-start | bytes 196616 | tf_op jit(solution)/shard_map/while/body/ppermute | solution.py:488

commit v5 on v4

--- a/solution.py
+++ b/solution.py
@@ -507,7 +507,9 @@
     if 2 * n_z * n_col * (blocks * tile) ** 2 <= 8 * MIB:
         dense = densify(*cell)
         totals = forward(dense, [0, 1], [features, sibling(features)], (), False)
-        *same, cot_other = hold(same[1:] + [cot_other], totals[0])
+        far = range(n_z - 1, 0, -1)
+        *same, cot_other = hold([same[s] for s in far] + [cot_other], totals[0])
+        same.reverse()
         cross = [sibling(v) for v in same]
         totals = forward(dense, [2 * s for s in range(1, n_z)], same, totals, False)
         parts = forward(dense, [2 * s + 1 for s in range(1, n_z)], cross, totals, True)
@@ -541,7 +543,8 @@
     sums = pair_sums(even, arrived)
     if n_z > 2:
         term = add(term, along_z(term, 2), sums[0])
-    back = turned_sum([sums[0]] + [along_z(sums[s], s) for s in range(1, n_z)])
+    order = sorted(range(1, n_z), key=lambda s: (s != n_z // 2, s))
+    back = turned_sum([sums[0]] + [along_z(sums[s], s) for s in order])
 
     def finish(_, v):
         for step in range(2, n_z.bit_length() - 1):

time: 55.9 us -> 54.8 us (0.980)
  starting transfers between devices: 24 us -> 19.5 us
  waiting for transfers between devices: 17.7 us -> 20.5 us
    ppermute x8, starting transfers between devices: 15.4 us -> 10.9 us  [along_z(): return lax.ppermute(v, 'row', [(i, i ^ 2 * s) for i in range(n_row)])]
    ppermute x8, waiting for transfers between devices: 6.3 us -> 8.33 us  [along_z(): return lax.ppermute(v, 'row', [(i, i ^ 2 * s) for i in range(n_row)])]
    ppermute x6, waiting for transfers between devices: 1.51 us -> 2.32 us  [sibling(): return lax.ppermute(v, 'row', [(i, i ^ 1) for i in range(n_row)])]
  transfers between devices with their start and end apart: 20 -> 20, of which waited for: 9 -> 10; matrix products, arithmetic and copies ran while one was open for 1% -> 1% of each run, Pallas kernels for 15% -> 16%
where the time goes in v5:
time: 54.8 us; the launch traced here: 54.4 us
  waiting for transfers between devices  20.5 us (37%)
  starting transfers between devices  19.5 us (36%)
  Pallas kernels  12.2 us (22%)
  between operations  1.45 us (3%)
  other arithmetic  0.69 us (1%)
    ppermute x8, starting transfers between devices, along_z(): return lax.ppermute(v, 'row', [(i, i ^ 2 * s) for i in range(n_row)])  10.9 us
    ppermute x8, waiting for transfers between devices, along_z(): return lax.ppermute(v, 'row', [(i, i ^ 2 * s) for i in range(n_row)])  8.33 us
    ppermute x3, waiting for transfers between devices, to_group(): return lax.ppermute(v, ('col', 'feat'), pairs)  6.09 us
    pallas_call x1, Pallas kernels, densify(): pl.pallas_call(functools.partial(densify_kernel, (n_z, n_col, blocks), gr...  5.9 us
    ppermute x1, waiting for transfers between devices, finish(): lax.ppermute(v, 'col', [(i, (i + t) % n_col) for i in range(n_col)])  3.76 us
    ppermute x3, starting transfers between devices, to_group(): return lax.ppermute(v, ('col', 'feat'), pairs)  3.55 us
    pallas_call x3, Pallas kernels, forward(): pl.pallas_call(functools.partial(forward_kernel, places, last), out_shape...  2.66 us
    ppermute x6, waiting for transfers between devices, sibling(): return lax.ppermute(v, 'row', [(i, i ^ 1) for i in range(n_row)])  2.32 us
  transfers between devices with their start and end apart: 20, of which 10 were waited for; matrix products, arithmetic and copies ran while one was open for 1% of the time, Pallas kernels for 16%

profile of v5, /device:TPU:0, one launch (start us, length us, event | category | flops | bytes accessed | tf_op | source)
XLA Modules:
  0.0 54.4 jit_solution(17416288588648527237)
XLA Ops:
  0.6 0.5 collective-permute-start.6
  1.1 4.7 %collective-permute-start.2 = (bf16[512,128]{1,0:T(8,128)(2,1)}, bf16[512,128]{1,0:T(8,128)(2,1)S(1)}, u32[]{:S(2)}, u32[]{:S(2)}) collective-permute-start(bf16[512,128]{1,0:T(8,128)(2,1)} %refs_0_.1), channel_id=1, source_target_pairs={{0,24},{4,28},{8,16},{12,20},{16,8},{20,12},{24,0},{28,4},{1,25},{... | collective-permute-start | bytes 393224 | tf_op jit(solution)/shard_map/ppermute | solution.py:491
  5.8 0.0 collective-permute-start.3
  5.8 0.7 %collective-permute-start.4 = (bf16[512,128]{1,0:T(8,128)(2,1)}, bf16[512,128]{1,0:T(8,128)(2,1)S(1)}, u32[]{:S(2)}, u32[]{:S(2)}) collective-permute-start(bf16[512,128]{1,0:T(8,128)(2,1)} %refs_0_.1), channel_id=1, source_target_pairs={{0,8},{4,12},{8,0},{12,4},{16,24},{20,28},{24,16},{28,20},{1,9},{5... | collective-permute-start | bytes 393224 | tf_op jit(solution)/shard_map/ppermute | solution.py:491
  6.5 1.6 %collective-permute-start.5 = (bf16[512,128]{1,0:T(8,128)(2,1)}, bf16[512,128]{1,0:T(8,128)(2,1)S(1)}, u32[]{:S(2)}, u32[]{:S(2)}) collective-permute-start(bf16[512,128]{1,0:T(8,128)(2,1)} %cot_own.1), channel_id=1, source_target_pairs={{0,1},{1,0},{2,3},{3,2},{4,5},{5,4},{6,7},{7,6},{8,9},{9,8},{10,11... | collective-permute-start | bytes 393224 | tf_op jit(solution)/shard_map/ppermute | solution.py:494
  8.8 0.0 copy-start
  8.8 5.9 %densify.1.dense = bf16[8,2,512,512]{3,2,1,0:T(8,128)(2,1)S(1)} custom-call(s32[1,1,256]{2,1,0:T(1,128)} %rows.1, s32[1,1,256]{2,1,0:T(1,128)} %cols.1, s32[1,1]{1,0:T(1,128)S(6)} %copy.25.count, bf16[256,128,128]{2,1,0:T(8,128)(2,1)} %bitcast.1), custom_call_target="tpu_custom_call" | custom-call | flops 1 | bytes 1 | tf_op jit(solution)/shard_map/densify/pallas_call | solution.py:93
  14.7 0.0 collective-permute-done.6.refs_1_
  14.7 0.0 copy-done
  14.7 0.7 %forward.3 = (f32[512,128]{1,0:T(8,128)S(1)}, f32[512,128]{1,0:T(8,128)S(1)}) custom-call(bf16[8,2,512,512]{3,2,1,0:T(8,128)(2,1)S(1)} %densify.1.dense, bf16[512,128]{1,0:T(8,128)(2,1)S(1)} %copy-done, bf16[512,128]{1,0:T(8,128)(2,1)S(1)} %collective-permute-done.6.refs_1_), custom_call_target="tpu_custom_call" | custom-call | flops 1 | bytes 1 | tf_op jit(solution)/shard_map/forward/pallas_call | solution.py:150
  15.4 0.0 collective-permute-done.2.refs_0_
  15.4 2.3 %collective-permute-done.3.refs_1_ = bf16[512,128]{1,0:T(8,128)(2,1)S(1)} collective-permute-done((bf16[512,128]{1,0:T(8,128)(2,1)}, bf16[512,128]{1,0:T(8,128)(2,1)S(1)}, u32[]{:S(2)}, u32[]{:S(2)}) %collective-permute-start.3) | collective-permute-done | bytes 131104 | tf_op jit(solution)/shard_map/ppermute | solution.py:491
  17.7 0.0 collective-permute-done.4.refs_2_
  17.7 0.0 collective-permute-done.5.refs_3_
  17.7 0.1 collective-permute-start.7
  17.8 0.5 collective-permute-start.8
  18.3 0.1 collective-permute-start.9
  18.4 0.0 copy-start.1
  18.4 0.0 copy-start.2
  18.4 1.0 %forward.4 = (f32[512,128]{1,0:T(8,128)S(1)}, f32[512,128]{1,0:T(8,128)S(1)}) custom-call(bf16[8,2,512,512]{3,2,1,0:T(8,128)(2,1)S(1)} %densify.1.dense, bf16[512,128]{1,0:T(8,128)(2,1)S(1)} %get-tuple-element.44.refs_0_, bf16[512,128]{1,0:T(8,128)(2,1)S(1)} %get-tuple-element.45.refs_1_, bf16[512,128]{1,0:T(8,128)(2,1)S(1)} %get-tuple-element.46.refs_2_, ...), custom_call_target="tpu_custom_call" | custom-call | flops 1 | bytes 1 | tf_op jit(solution)/shard_map/forward/pallas_call | solution.py:150
  19.4 0.0 collective-permute-done.7.refs_0_
  19.4 0.0 collective-permute-done.8.refs_1_
  19.4 0.3 collective-permute-done.9.refs_2_
  19.6 1.0 %forward.5 = (bf16[512,128]{1,0:T(8,128)(2,1)S(1)}, bf16[512,128]{1,0:T(8,128)(2,1)S(1)}) custom-call(bf16[8,2,512,512]{3,2,1,0:T(8,128)(2,1)S(1)} %densify.1.dense, bf16[512,128]{1,0:T(8,128)(2,1)S(1)} %collective-permute-done.7.refs_0_, bf16[512,128]{1,0:T(8,128)(2,1)S(1)} %collective-permute-done.8.refs_1_, ...), custom_call_target="tpu_custom_call" | custom-call | flops 1 | bytes 1 | tf_op jit(solution)/shard_map/forward/pallas_call | solution.py:150
  20.6 1.6 %collective-permute-start.10 = (bf16[512,128]{1,0:T(8,128)(2,1)S(1)}, bf16[512,128]{1,0:T(8,128)(2,1)S(1)}, u32[]{:S(2)}, u32[]{:S(2)}) collective-permute-start(bf16[512,128]{1,0:T(8,128)(2,1)S(1)} %get-tuple-element.51), channel_id=1, source_target_pairs={{0,2},{1,3},{2,0},{3,1},{4,6},{5,7},{6,4},{7,5},{8,10},{9,11},{10,... | collective-permute-start | bytes 393224 | tf_op jit(solution)/shard_map/ppermute | solution.py:501
  22.2 1.5 %collective-permute-start.11 = (bf16[512,128]{1,0:T(8,128)(2,1)S(1)}, bf16[512,128]{1,0:T(8,128)(2,1)S(1)}, u32[]{:S(2)}, u32[]{:S(2)}) collective-permute-start(bf16[512,128]{1,0:T(8,128)(2,1)S(1)} %get-tuple-element.50.refs_0_), channel_id=1, source_target_pairs={{0,1},{1,0},{2,3},{3,2},{4,5},{5,4},{6,7},{7,6},{8,9},{9,8},{10,11... | collective-permute-start | bytes 393224 | tf_op jit(solution)/shard_map/ppermute | solution.py:501
  23.7 0.5 collective-permute-start.12
  24.2 2.1 %collective-permute-done.10.refs_1_ = bf16[512,128]{1,0:T(8,128)(2,1)S(1)} collective-permute-done((bf16[512,128]{1,0:T(8,128)(2,1)S(1)}, bf16[512,128]{1,0:T(8,128)(2,1)S(1)}, u32[]{:S(2)}, u32[]{:S(2)}) %collective-permute-start.10) | collective-permute-done | bytes 131104 | tf_op jit(solution)/shard_map/ppermute | solution.py:501
  26.3 2.3 %collective-permute-done.11.refs_2_ = bf16[512,128]{1,0:T(8,128)(2,1)S(1)} collective-permute-done((bf16[512,128]{1,0:T(8,128)(2,1)S(1)}, bf16[512,128]{1,0:T(8,128)(2,1)S(1)}, u32[]{:S(2)}, u32[]{:S(2)}) %collective-permute-start.11) | collective-permute-done | bytes 131104 | tf_op jit(solution)/shard_map/ppermute | solution.py:501
  28.6 1.7 %collective-permute-done.12.refs_3_ = bf16[512,128]{1,0:T(8,128)(2,1)S(1)} collective-permute-done((bf16[512,128]{1,0:T(8,128)(2,1)S(1)}, bf16[512,128]{1,0:T(8,128)(2,1)S(1)}, u32[]{:S(2)}, u32[]{:S(2)}) %collective-permute-start.12) | collective-permute-done | bytes 131104 | tf_op jit(solution)/shard_map/ppermute | solution.py:501
  30.3 0.0 copy-done.1
  30.3 0.0 copy-done.2
  30.3 1.0 %middle.1 = (bf16[128,512]{1,0:T(8,128)(2,1)S(1)}, bf16[512,128]{1,0:T(8,128)(2,1)}, bf16[512,128]{1,0:T(8,128)(2,1)S(1)}, bf16[512,128]{1,0:T(8,128)(2,1)S(1)}, bf16[512,128]{1,0:T(8,128)(2,1)S(1)}) custom-call(bf16[256,256]{1,0:T(8,128)(2,1)S(1)} %copy-done.1, bf16[512,128]{1,0:T(8,128)(2,1)S(1)} %copy-done.2, ...), custom_call_target="tpu_custom_call" | custom-call | flops 1 | bytes 1 | tf_op jit(solution)/shard_map/middle/pallas_call | solution.py:367
  31.3 1.5 %collective-permute-start.13 = (bf16[128,512]{1,0:T(8,128)(2,1)S(1)}, bf16[128,512]{1,0:T(8,128)(2,1)S(1)}, u32[]{:S(2)}, u32[]{:S(2)}) collective-permute-start(bf16[128,512]{1,0:T(8,128)(2,1)S(1)} %get-tuple-element.53.piece), channel_id=1, source_target_pairs={{0,2},{2,0},{1,3},{3,1},{4,6},{6,4},{5,7},{7,5},{8,10},{10,8},{9,1... | collective-permute-start | bytes 393224 | tf_op jit(solution)/shard_map/ppermute | solution.py:535
  32.8 0.3 weight_term.1.a
  33.1 0.1 collective-permute-start.14
  33.1 0.7 %backward_own.1.own = f32[8,128,512]{2,1,0:T(8,128)S(1)} custom-call(bf16[8,2,512,512]{3,2,1,0:T(8,128)(2,1)S(1)} %densify.1.dense, bf16[128,512]{1,0:T(8,128)(2,1)S(1)} %get-tuple-element.53.piece), custom_call_target="tpu_custom_call" | custom-call | flops 1 | bytes 1 | tf_op jit(solution)/shard_map/backward_own/pallas_call | solution.py:168
  33.8 3.5 %collective-permute-done.14.b = bf16[128,256]{1,0:T(8,128)(2,1)S(1)} collective-permute-done((bf16[128,256]{1,0:T(8,128)(2,1)S(1)}, bf16[128,256]{1,0:T(8,128)(2,1)S(1)}, u32[]{:S(2)}, u32[]{:S(2)}) %collective-permute-start.14) | collective-permute-done | bytes 65568 | tf_op jit(solution)/shard_map/ppermute | solution.py:491
  37.4 0.0 collective-permute-done.13.refs_0_
  37.4 0.7 %backward.1 = (bf16[4,128,512]{2,1,0:T(8,128)(2,1)S(1)}, bf16[4,128,512]{2,1,0:T(8,128)(2,1)S(1)}) custom-call(bf16[8,2,512,512]{3,2,1,0:T(8,128)(2,1)S(1)} %densify.1.dense, f32[8,128,512]{2,1,0:T(8,128)S(1)} %backward_own.1.own, bf16[128,512]{1,0:T(8,128)(2,1)S(1)} %collective-permute-done.13.refs_0_, bf16[128,256]{1,0:T(8,128)(2,1)S(1)} %add.14.refs_1_.a), custom_call_target="tpu_custom_call" | custom-call | flops 1 | bytes 1 | tf_op jit(solution)/shard_map/backward/pallas_call | solution.py:191
  38.1 0.1 collective-permute-start.15
  38.2 1.1 %collective-permute-start.19 = (bf16[128,256]{1,0:T(8,128)(2,1)S(1)}, bf16[128,256]{1,0:T(8,128)(2,1)S(1)}, u32[]{:S(2)}, u32[]{:S(2)}) collective-permute-start(bf16[128,256]{1,0:T(8,128)(2,1)S(1)} %add.14.refs_1_.a), channel_id=1, source_target_pairs={{0,16},{4,20},{8,24},{12,28},{16,0},{20,4},{24,8},{28,12},{1,17},{... | collective-permute-start | bytes 196616 | tf_op jit(solution)/shard_map/ppermute | solution.py:491
  39.3 0.8 %collective-permute-done.15.arrived = bf16[4,128,512]{2,1,0:T(8,128)(2,1)S(1)} collective-permute-done((bf16[4,128,512]{2,1,0:T(8,128)(2,1)S(1)}, bf16[4,128,512]{2,1,0:T(8,128)(2,1)S(1)}, u32[]{:S(2)}, u32[]{:S(2)}) %collective-permute-start.15) | collective-permute-done | bytes 524320 | tf_op jit(solution)/shard_map/ppermute | solution.py:488
  40.1 0.1 pair_sums.1
  40.2 1.2 %collective-permute-start.16 = (bf16[128,512]{1,0:T(8,128)(2,1)S(1)}, bf16[128,512]{1,0:T(8,128)(2,1)S(1)}, u32[]{:S(2)}, u32[]{:S(2)}) collective-permute-start(bf16[128,512]{1,0:T(8,128)(2,1)S(1)} %get-tuple-element.60), channel_id=1, source_target_pairs={{0,16},{4,20},{8,24},{12,28},{16,0},{20,4},{24,8},{28,12},{1,17},{... | collective-permute-start | bytes 393224 | tf_op jit(solution)/shard_map/ppermute | solution.py:491
  41.4 1.9 %collective-permute-start.17 = (bf16[128,512]{1,0:T(8,128)(2,1)S(1)}, bf16[128,512]{1,0:T(8,128)(2,1)S(1)}, u32[]{:S(2)}, u32[]{:S(2)}) collective-permute-start(bf16[128,512]{1,0:T(8,128)(2,1)S(1)} %get-tuple-element.61), channel_id=1, source_target_pairs={{0,8},{4,12},{8,0},{12,4},{16,24},{20,28},{24,16},{28,20},{1,9},{5... | collective-permute-start | bytes 393224 | tf_op jit(solution)/shard_map/ppermute | solution.py:491
  43.3 1.3 %collective-permute-start.18 = (bf16[128,512]{1,0:T(8,128)(2,1)S(1)}, bf16[128,512]{1,0:T(8,128)(2,1)S(1)}, u32[]{:S(2)}, u32[]{:S(2)}) collective-permute-start(bf16[128,512]{1,0:T(8,128)(2,1)S(1)} %get-tuple-element.62), channel_id=1, source_target_pairs={{0,24},{4,28},{8,16},{12,20},{16,8},{20,12},{24,0},{28,4},{1,25},{... | collective-permute-start | bytes 393224 | tf_op jit(solution)/shard_map/ppermute | solution.py:491
  44.7 2.5 %collective-permute-done.19.b = bf16[128,256]{1,0:T(8,128)(2,1)S(1)} collective-permute-done((bf16[128,256]{1,0:T(8,128)(2,1)S(1)}, bf16[128,256]{1,0:T(8,128)(2,1)S(1)}, u32[]{:S(2)}, u32[]{:S(2)}) %collective-permute-start.19) | collective-permute-done | bytes 65568 | tf_op jit(solution)/shard_map/ppermute | solution.py:491
  47.2 5.7 %while.10 = (s32[]{:T(128)}, bf16[128,256]{1,0:T(8,128)(2,1)S(1)}, s32[]{:T(128)}, s32[]{:T(128)}) while((s32[]{:T(128)}, bf16[128,256]{1,0:T(8,128)(2,1)S(1)}, s32[]{:T(128)}, s32[]{:T(128)}) %tuple.22), condition=%wide.region_1.0_spmd, body=%wide.region_0.0_spmd.sunk | while | flops 131075 | bytes 721030 | solution.py:561
  47.2 0.6 %collective-permute-start = (bf16[128,256]{1,0:T(8,128)(2,1)S(1)}, bf16[128,256]{1,0:T(8,128)(2,1)S(1)}, u32[]{:S(2)}, u32[]{:S(2)}) collective-permute-start(bf16[128,256]{1,0:T(8,128)(2,1)S(1)} %get-tuple-element.95), channel_id=1, source_target_pairs={{0,2},{2,0},{1,3},{3,1},{4,6},{6,4},{5,7},{7,5},{8,10},{10,8},{9,1... | collective-permute-start | bytes 196616 | tf_op jit(solution)/shard_map/while/body/ppermute | solution.py:554
  47.8 3.8 %collective-permute-done = bf16[128,256]{1,0:T(8,128)(2,1)S(1)} collective-permute-done((bf16[128,256]{1,0:T(8,128)(2,1)S(1)}, bf16[128,256]{1,0:T(8,128)(2,1)S(1)}, u32[]{:S(2)}, u32[]{:S(2)}) %collective-permute-start) | collective-permute-done | bytes 65568 | tf_op jit(solution)/shard_map/while/body/ppermute | solution.py:554
  51.6 0.1 collective-permute-start.1
  51.6 1.2 %collective-permute-done.1.b = bf16[128,256]{1,0:T(8,128)(2,1)S(1)} collective-permute-done((bf16[128,256]{1,0:T(8,128)(2,1)S(1)}, bf16[128,256]{1,0:T(8,128)(2,1)S(1)}, u32[]{:S(2)}, u32[]{:S(2)}) %collective-permute-start.1) | collective-permute-done | bytes 65568 | tf_op jit(solution)/shard_map/while/body/ppermute | solution.py:488
  52.9 0.7 %convert_multiply_fusion = f32[128,256]{1,0:T(8,128)} fusion(bf16[128,256]{1,0:T(8,128)(2,1)S(1)} %get-tuple-element.63), kind=kLoop, calls=%fused_computation.1 | loop fusion | flops 65536 | bytes 196608 | tf_op jit(solution)/shard_map/mul | solution.py:562
  53.6 0.0 collective-permute-done.16.refs_1_
  53.6 0.0 collective-permute-done.17.refs_2_
  53.6 0.0 collective-permute-done.18.refs_3_
  53.6 0.8 %turned_sum.1 = bf16[512,128]{1,0:T(8,128)(2,1)} custom-call(bf16[128,512]{1,0:T(8,128)(2,1)S(1)} %get-tuple-element.59.refs_0_.rest_0_, bf16[128,512]{1,0:T(8,128)(2,1)S(1)} %collective-permute-done.16.refs_1_, bf16[128,512]{1,0:T(8,128)(2,1)S(1)} %collective-permute-done.17.refs_2_, bf16[128,512]{1,0:T(8,128)(2,1)S(1)} %collective-permute-done.18.refs_3_), custom_call_target="tpu_custom_call" | custom-call | flops 1 | bytes 1 | tf_op jit(solution)/shard_map/turned_sum/pallas_call | solution.py:469
  (5 shorter events, 0.1 us)
Async XLA Ops:
  0.6 14.0 %collective-permute-start.6 = (bf16[512,128]{1,0:T(8,128)(2,1)}, bf16[512,128]{1,0:T(8,128)(2,1)S(1)}, u32[]{:S(2)}, u32[]{:S(2)}) collective-permute-start(bf16[512,128]{1,0:T(8,128)(2,1)} %refs_0_.1), channel_id=1, source_target_pairs={{0,4},{4,0},{8,12},{12,8},{16,20},{20,16},{24,28},{28,24},{1,5},{5... | collective-permute-start | bytes 393224 | tf_op jit(solution)/shard_map/ppermute | solution.py:488
  1.1 14.3 %collective-permute-start.2 = (bf16[512,128]{1,0:T(8,128)(2,1)}, bf16[512,128]{1,0:T(8,128)(2,1)S(1)}, u32[]{:S(2)}, u32[]{:S(2)}) collective-permute-start(bf16[512,128]{1,0:T(8,128)(2,1)} %refs_0_.1), channel_id=1, source_target_pairs={{0,24},{4,28},{8,16},{12,20},{16,8},{20,12},{24,0},{28,4},{1,25},{... | collective-permute-start | bytes 393224 | tf_op jit(solution)/shard_map/ppermute | solution.py:491
  5.8 11.9 %collective-permute-start.3 = (bf16[512,128]{1,0:T(8,128)(2,1)}, bf16[512,128]{1,0:T(8,128)(2,1)S(1)}, u32[]{:S(2)}, u32[]{:S(2)}) collective-permute-start(bf16[512,128]{1,0:T(8,128)(2,1)} %refs_0_.1), channel_id=1, source_target_pairs={{0,16},{4,20},{8,24},{12,28},{16,0},{20,4},{24,8},{28,12},{1,17},{... | collective-permute-start | bytes 393224 | tf_op jit(solution)/shard_map/ppermute | solution.py:491
  5.8 11.9 %collective-permute-start.4 = (bf16[512,128]{1,0:T(8,128)(2,1)}, bf16[512,128]{1,0:T(8,128)(2,1)S(1)}, u32[]{:S(2)}, u32[]{:S(2)}) collective-permute-start(bf16[512,128]{1,0:T(8,128)(2,1)} %refs_0_.1), channel_id=1, source_target_pairs={{0,8},{4,12},{8,0},{12,4},{16,24},{20,28},{24,16},{28,20},{1,9},{5... | collective-permute-start | bytes 393224 | tf_op jit(solution)/shard_map/ppermute | solution.py:491
  6.5 11.2 %collective-permute-start.5 = (bf16[512,128]{1,0:T(8,128)(2,1)}, bf16[512,128]{1,0:T(8,128)(2,1)S(1)}, u32[]{:S(2)}, u32[]{:S(2)}) collective-permute-start(bf16[512,128]{1,0:T(8,128)(2,1)} %cot_own.1), channel_id=1, source_target_pairs={{0,1},{1,0},{2,3},{3,2},{4,5},{5,4},{6,7},{7,6},{8,9},{9,8},{10,11... | collective-permute-start | bytes 393224 | tf_op jit(solution)/shard_map/ppermute | solution.py:494
  8.8 5.9 %copy-start = (bf16[512,128]{1,0:T(8,128)(2,1)S(1)}, bf16[512,128]{1,0:T(8,128)(2,1)}, u32[]{:S(2)}) copy-start(bf16[512,128]{1,0:T(8,128)(2,1)} %refs_0_.1) | copy-start | bytes 393220
  17.7 1.6 %collective-permute-start.7 = (bf16[512,128]{1,0:T(8,128)(2,1)S(1)}, bf16[512,128]{1,0:T(8,128)(2,1)S(1)}, u32[]{:S(2)}, u32[]{:S(2)}) collective-permute-start(bf16[512,128]{1,0:T(8,128)(2,1)S(1)} %get-tuple-element.44.refs_0_), channel_id=1, source_target_pairs={{0,4},{4,0},{8,12},{12,8},{16,20},{20,16},{24,28},{28,24},{1,5},{5... | collective-permute-start | bytes 393224 | tf_op jit(solution)/shard_map/ppermute | solution.py:488
  17.8 1.6 %collective-permute-start.8 = (bf16[512,128]{1,0:T(8,128)(2,1)S(1)}, bf16[512,128]{1,0:T(8,128)(2,1)S(1)}, u32[]{:S(2)}, u32[]{:S(2)}) collective-permute-start(bf16[512,128]{1,0:T(8,128)(2,1)S(1)} %get-tuple-element.45.refs_1_), channel_id=1, source_target_pairs={{0,4},{4,0},{8,12},{12,8},{16,20},{20,16},{24,28},{28,24},{1,5},{5... | collective-permute-start | bytes 393224 | tf_op jit(solution)/shard_map/ppermute | solution.py:488
  18.3 1.3 %collective-permute-start.9 = (bf16[512,128]{1,0:T(8,128)(2,1)S(1)}, bf16[512,128]{1,0:T(8,128)(2,1)S(1)}, u32[]{:S(2)}, u32[]{:S(2)}) collective-permute-start(bf16[512,128]{1,0:T(8,128)(2,1)S(1)} %get-tuple-element.46.refs_2_), channel_id=1, source_target_pairs={{0,4},{4,0},{8,12},{12,8},{16,20},{20,16},{24,28},{28,24},{1,5},{5... | collective-permute-start | bytes 393224 | tf_op jit(solution)/shard_map/ppermute | solution.py:488
  18.4 11.9 %copy-start.1 = (bf16[256,256]{1,0:T(8,128)(2,1)S(1)}, bf16[256,256]{1,0:T(8,128)(2,1)}, u32[]{:S(2)}) copy-start(bf16[256,256]{1,0:T(8,128)(2,1)} %weights.1) | copy-start | bytes 393220
  18.4 11.9 %copy-start.2 = (bf16[512,128]{1,0:T(8,128)(2,1)S(1)}, bf16[512,128]{1,0:T(8,128)(2,1)}, u32[]{:S(2)}) copy-start(bf16[512,128]{1,0:T(8,128)(2,1)} %cot_own.1) | copy-start | bytes 393220
  20.6 5.7 %collective-permute-start.10 = (bf16[512,128]{1,0:T(8,128)(2,1)S(1)}, bf16[512,128]{1,0:T(8,128)(2,1)S(1)}, u32[]{:S(2)}, u32[]{:S(2)}) collective-permute-start(bf16[512,128]{1,0:T(8,128)(2,1)S(1)} %get-tuple-element.51), channel_id=1, source_target_pairs={{0,2},{1,3},{2,0},{3,1},{4,6},{5,7},{6,4},{7,5},{8,10},{9,11},{10,... | collective-permute-start | bytes 393224 | tf_op jit(solution)/shard_map/ppermute | solution.py:501
  22.2 6.4 %collective-permute-start.11 = (bf16[512,128]{1,0:T(8,128)(2,1)S(1)}, bf16[512,128]{1,0:T(8,128)(2,1)S(1)}, u32[]{:S(2)}, u32[]{:S(2)}) collective-permute-start(bf16[512,128]{1,0:T(8,128)(2,1)S(1)} %get-tuple-element.50.refs_0_), channel_id=1, source_target_pairs={{0,1},{1,0},{2,3},{3,2},{4,5},{5,4},{6,7},{7,6},{8,9},{9,8},{10,11... | collective-permute-start | bytes 393224 | tf_op jit(solution)/shard_map/ppermute | solution.py:501
  23.7 6.6 %collective-permute-start.12 = (bf16[512,128]{1,0:T(8,128)(2,1)S(1)}, bf16[512,128]{1,0:T(8,128)(2,1)S(1)}, u32[]{:S(2)}, u32[]{:S(2)}) collective-permute-start(bf16[512,128]{1,0:T(8,128)(2,1)S(1)} %get-tuple-element.51), channel_id=1, source_target_pairs={{0,3},{1,2},{2,1},{3,0},{4,7},{5,6},{6,5},{7,4},{8,11},{9,10},{10,... | collective-permute-start | bytes 393224 | tf_op jit(solution)/shard_map/ppermute | solution.py:501
  31.3 6.2 %collective-permute-start.13 = (bf16[128,512]{1,0:T(8,128)(2,1)S(1)}, bf16[128,512]{1,0:T(8,128)(2,1)S(1)}, u32[]{:S(2)}, u32[]{:S(2)}) collective-permute-start(bf16[128,512]{1,0:T(8,128)(2,1)S(1)} %get-tuple-element.53.piece), channel_id=1, source_target_pairs={{0,2},{2,0},{1,3},{3,1},{4,6},{6,4},{5,7},{7,5},{8,10},{10,8},{9,1... | collective-permute-start | bytes 393224 | tf_op jit(solution)/shard_map/ppermute | solution.py:535
  33.1 4.3 %collective-permute-start.14 = (bf16[128,256]{1,0:T(8,128)(2,1)S(1)}, bf16[128,256]{1,0:T(8,128)(2,1)S(1)}, u32[]{:S(2)}, u32[]{:S(2)}) collective-permute-start(bf16[128,256]{1,0:T(8,128)(2,1)S(1)} %weight_term.1.a), channel_id=1, source_target_pairs={{0,8},{4,12},{8,0},{12,4},{16,24},{20,28},{24,16},{28,20},{1,9},{5... | collective-permute-start | bytes 196616 | tf_op jit(solution)/shard_map/ppermute | solution.py:491
  38.1 2.0 %collective-permute-start.15 = (bf16[4,128,512]{2,1,0:T(8,128)(2,1)S(1)}, bf16[4,128,512]{2,1,0:T(8,128)(2,1)S(1)}, u32[]{:S(2)}, u32[]{:S(2)}) collective-permute-start(bf16[4,128,512]{2,1,0:T(8,128)(2,1)S(1)} %get-tuple-element.58), channel_id=1, source_target_pairs={{0,4},{4,0},{8,12},{12,8},{16,20},{20,16},{24,28},{28,24},{1,5},{5... | collective-permute-start | bytes 1572872 | tf_op jit(solution)/shard_map/ppermute | solution.py:488
  38.2 8.9 %collective-permute-start.19 = (bf16[128,256]{1,0:T(8,128)(2,1)S(1)}, bf16[128,256]{1,0:T(8,128)(2,1)S(1)}, u32[]{:S(2)}, u32[]{:S(2)}) collective-permute-start(bf16[128,256]{1,0:T(8,128)(2,1)S(1)} %add.14.refs_1_.a), channel_id=1, source_target_pairs={{0,16},{4,20},{8,24},{12,28},{16,0},{20,4},{24,8},{28,12},{1,17},{... | collective-permute-start | bytes 196616 | tf_op jit(solution)/shard_map/ppermute | solution.py:491
  40.2 13.3 %collective-permute-start.16 = (bf16[128,512]{1,0:T(8,128)(2,1)S(1)}, bf16[128,512]{1,0:T(8,128)(2,1)S(1)}, u32[]{:S(2)}, u32[]{:S(2)}) collective-permute-start(bf16[128,512]{1,0:T(8,128)(2,1)S(1)} %get-tuple-element.60), channel_id=1, source_target_pairs={{0,16},{4,20},{8,24},{12,28},{16,0},{20,4},{24,8},{28,12},{1,17},{... | collective-permute-start | bytes 393224 | tf_op jit(solution)/shard_map/ppermute | solution.py:491
  41.4 12.2 %collective-permute-start.17 = (bf16[128,512]{1,0:T(8,128)(2,1)S(1)}, bf16[128,512]{1,0:T(8,128)(2,1)S(1)}, u32[]{:S(2)}, u32[]{:S(2)}) collective-permute-start(bf16[128,512]{1,0:T(8,128)(2,1)S(1)} %get-tuple-element.61), channel_id=1, source_target_pairs={{0,8},{4,12},{8,0},{12,4},{16,24},{20,28},{24,16},{28,20},{1,9},{5... | collective-permute-start | bytes 393224 | tf_op jit(solution)/shard_map/ppermute | solution.py:491
  43.3 10.2 %collective-permute-start.18 = (bf16[128,512]{1,0:T(8,128)(2,1)S(1)}, bf16[128,512]{1,0:T(8,128)(2,1)S(1)}, u32[]{:S(2)}, u32[]{:S(2)}) collective-permute-start(bf16[128,512]{1,0:T(8,128)(2,1)S(1)} %get-tuple-element.62), channel_id=1, source_target_pairs={{0,24},{4,28},{8,16},{12,20},{16,8},{20,12},{24,0},{28,4},{1,25},{... | collective-permute-start | bytes 393224 | tf_op jit(solution)/shard_map/ppermute | solution.py:491
  47.2 4.3 %collective-permute-start = (bf16[128,256]{1,0:T(8,128)(2,1)S(1)}, bf16[128,256]{1,0:T(8,128)(2,1)S(1)}, u32[]{:S(2)}, u32[]{:S(2)}) collective-permute-start(bf16[128,256]{1,0:T(8,128)(2,1)S(1)} %get-tuple-element.95), channel_id=1, source_target_pairs={{0,2},{2,0},{1,3},{3,1},{4,6},{6,4},{5,7},{7,5},{8,10},{10,8},{9,1... | collective-permute-start | bytes 196616 | tf_op jit(solution)/shard_map/while/body/ppermute | solution.py:554
  51.6 1.3 %collective-permute-start.1 = (bf16[128,256]{1,0:T(8,128)(2,1)S(1)}, bf16[128,256]{1,0:T(8,128)(2,1)S(1)}, u32[]{:S(2)}, u32[]{:S(2)}) collective-permute-start(bf16[128,256]{1,0:T(8,128)(2,1)S(1)} %add_convert_fusion.2.a), channel_id=1, source_target_pairs={{0,4},{4,0},{8,12},{12,8},{16,20},{20,16},{24,28},{28,24},{1,5},{5... | collective-permute-start | bytes 196616 | tf_op jit(solution)/shard_map/while/body/ppermute | solution.py:488

commit v6 on v5

--- a/solution.py
+++ b/solution.py
@@ -158,22 +158,30 @@
     )(resident(dense), *xs, *totals)
 
 
-def own_kernel(dense, piece, out):
+def elu(h):
+    return jnp.where(h > 0, h, jnp.exp(jnp.minimum(h, 0.0)) - 1.0).astype(BF16)
+
+
+def own_kernel(dense, piece, hidden, out, activated):
+    activated[...] = elu(hidden[...])
     for j in range(dense.shape[0]):
         out[j] = jnp.dot(piece[...], dense[j, 0], preferred_element_type=F32)
 
 
-def backward_own(dense, piece):
+def backward_own(dense, piece, hidden):
     n_src, _, side, _ = dense.shape
     return pl.pallas_call(
         own_kernel,
-        out_shape=pltpu.VMEM((n_src, piece.shape[0], side), F32),
-        in_specs=[vmem()] * 2,
-        out_specs=vmem(),
+        out_shape=(
+            pltpu.VMEM((n_src, piece.shape[0], side), F32),
+            jax.ShapeDtypeStruct(hidden.shape, BF16),
+        ),
+        in_specs=[vmem()] * 3,
+        out_specs=(vmem(),) * 2,
         compiler_params=params(),
         cost_estimate=COST,
         name="backward_own",
-    )(resident(dense), piece)
+    )(resident(dense), piece, hidden)
 
 
 def backward_kernel(dense, own, *refs):
@@ -185,18 +193,18 @@
         outs[j % 2][j // 2] = total.astype(BF16)
 
 
-def backward(dense, own, pieces, after):
+def backward(dense, own, pieces):
     n_src, n_col, side, _ = dense.shape
     feats = own.shape[1]
     return pl.pallas_call(
         backward_kernel,
         out_shape=(jax.ShapeDtypeStruct((n_src // 2, feats, side), BF16),) * 2,
-        in_specs=[vmem()] * (1 + n_col) + [pl.BlockSpec(memory_space=pl.ANY)],
+        in_specs=[vmem()] * (1 + n_col),
         out_specs=(vmem(),) * 2,
         compiler_params=params(),
         cost_estimate=COST,
         name="backward",
-    )(resident(dense), resident(own), *pieces, after)
+    )(resident(dense), resident(own), *pieces)
 
 
 def densify_stream_kernel(
@@ -329,7 +337,7 @@
 def middle_kernel(n_col, weights, cot_own, cot_other, *refs):
     own = refs[:n_col]
     other = refs[n_col : 2 * n_col]
-    spread, activated, agg, g_own, g_other = refs[2 * n_col :]
+    spread, kept, agg, g_own, g_other = refs[2 * n_col :]
     half = cot_own.shape[1]
     f = lax.axis_index("feat")
     mine = pl.ds(pl.multiple_of(f * half, half), half)
@@ -355,9 +363,7 @@
     ).astype(BF16)
     g_own[...] = g[:, :half]
     g_other[...] = g[:, half:]
-    activated[...] = jnp.where(
-        hidden[:, :half] > 0, hidden[:, :half], decay[:, :half] - 1.0
-    ).astype(BF16)
+    kept[...] = hidden[:, :half]
 
 
 def middle(weights, cot_own, cot_other, own, other):
@@ -366,8 +372,11 @@
     n_col = len(own)
     return pl.pallas_call(
         functools.partial(middle_kernel, n_col),
-        out_shape=(jax.ShapeDtypeStruct((half, nodes), BF16),)
-        + (jax.ShapeDtypeStruct((nodes, half), BF16),) * 4,
+        out_shape=(
+            jax.ShapeDtypeStruct((half, nodes), BF16),
+            jax.ShapeDtypeStruct((nodes, half), F32),
+        )
+        + (jax.ShapeDtypeStruct((nodes, half), BF16),) * 3,
         in_specs=[vmem()] * (3 + 2 * n_col),
         out_specs=(vmem(),) * 5,
         compiler_params=params(),
@@ -376,26 +385,52 @@
     )(weights, cot_own, cot_other, *own, *other)
 
 
-def weight_kernel(agg, g_own, g_other, out):
-    half = agg.shape[1]
-    f = lax.axis_index("feat")
+def weight_kernel(agg, g_own, g_other, keep, send, whole):
+    half, rows = agg.shape[1], keep.shape[0]
+    core, f = lax.axis_index("row") % 2, lax.axis_index("feat")
     turned = agg[...].astype(F32).T.astype(BF16)
     for columns, g in ((f * half, g_own), ((1 - f) * half, g_other)):
         columns = pl.ds(pl.multiple_of(columns, half), half)
-        out[:, columns] = jnp.dot(turned, g[...], preferred_element_type=F32).astype(BF16)
+        whole[:, columns] = jnp.dot(turned, g[...], preferred_element_type=F32)
+        term = whole[:, columns].astype(BF16)
+        first, second = term[:rows], term[rows:]
+        keep[:, columns] = jnp.where(core == 0, first, second)
+        send[:, columns] = jnp.where(core == 0, second, first)
 
 
 def weight_term(agg, g_own, g_other):
     half = agg.shape[1]
     return pl.pallas_call(
         weight_kernel,
-        out_shape=jax.ShapeDtypeStruct((half, 2 * half), BF16),
+        out_shape=(jax.ShapeDtypeStruct((half // 2, 2 * half), BF16),) * 2
+        + (pltpu.VMEM((half, 2 * half), F32),),
         in_specs=[vmem()] * 3,
-        out_specs=vmem(),
+        out_specs=(vmem(),) * 3,
         compiler_params=params(),
         cost_estimate=COST,
         name="weight_term",
     )(agg, g_own, g_other)
+
+
+def assemble_kernel(scale, mine, theirs, out):
+    rows = mine.shape[0]
+    core = lax.axis_index("row") % 2
+    own, other = mine[...].astype(F32) * scale, theirs[...].astype(F32) * scale
+    out[:rows, :] = jnp.where(core == 0, own, other)
+    out[rows:, :] = jnp.where(core == 0, other, own)
+
+
+def assemble(scale, mine, theirs):
+    rows, whole = mine.shape
+    return pl.pallas_call(
+        functools.partial(assemble_kernel, scale),
+        out_shape=jax.ShapeDtypeStruct((2 * rows, whole), F32),
+        in_specs=[vmem()] * 2,
+        out_specs=vmem(),
+        compiler_params=params(),
+        cost_estimate=COST,
+        name="assemble",
+    )(mine, theirs)
 
 
 def backward_stream_kernel(n_col, a, *refs):
@@ -459,22 +494,22 @@
 
 def turned_kernel(*refs):
     total = refs[0][...].astype(F32)
-    for part in refs[1:-1]:
+    for part in refs[1:-2]:
         total = total + part[...].astype(F32)
     refs[-1][...] = total.T.astype(BF16)
 
 
-def turned_sum(parts):
+def turned_sum(parts, after):
     feats, nodes = parts[0].shape
     return pl.pallas_call(
         turned_kernel,
         out_shape=jax.ShapeDtypeStruct((nodes, feats), BF16),
-        in_specs=[vmem()] * len(parts),
+        in_specs=[vmem()] * len(parts) + [pl.BlockSpec(memory_space=pl.ANY)],
         out_specs=vmem(),
         compiler_params=params(),
         cost_estimate=COST,
         name="turned_sum",
-    )(*parts)
+    )(*parts, after)
 
 
 def shards(features, tile_rows, tile_cols, tile_count, tile_values, weights, cotangent):
@@ -514,8 +549,9 @@
         totals = forward(dense, [2 * s for s in range(1, n_z)], same, totals, False)
         parts = forward(dense, [2 * s + 1 for s in range(1, n_z)], cross, totals, True)
 
-        def back_of(pieces, after):
-            return backward(dense, backward_own(dense, pieces[0]), pieces[1:], after)
+        def back_of(pieces, hidden):
+            own, activated = backward_own(dense, pieces[0], hidden)
+            return *backward(dense, own, pieces[1:]), activated
 
     else:
         cross = [sibling(v) for v in same]
@@ -525,28 +561,30 @@
             total = forward_stream(dense, s, same[s], cross[s], total)
         parts = total.astype(BF16).reshape(n_col, nodes, half)
 
-        def back_of(pieces, after):
-            return [backward_stream(dense, k, pieces) for k in range(2)]
+        def back_of(pieces, hidden):
+            even, odd = (backward_stream(dense, k, pieces) for k in range(2))
+            return even, odd, elu(hidden)
 
     own = [parts[0]] + [to_group(parts[t], -t, 0) for t in range(1, n_col)]
     other = [to_group(parts[t], -t, 1) for t in range(n_col)]
-    spread, activated, *rest = middle(weights, cotangent, cot_other, own, other)
+    spread, hidden, *rest = middle(weights, cotangent, cot_other, own, other)
     pieces = [spread] + [
         lax.ppermute(spread, "col", [(i, (i + t) % n_col) for i in range(n_col)])
         for t in range(1, n_col)
     ]
-    term = weight_term(*rest)
-    term = add(term, along_z(term, 1))
-
-    even, odd = back_of(pieces, term)
+    keep, send, weight_grad = weight_term(*rest)
+    term = add(keep, sibling(send))
+    even, odd, activated = back_of(pieces, hidden)
+    term = add(term, along_z(term, 1), odd)
+    (odd,) = hold([odd], term)
     arrived = sibling(odd)
     sums = pair_sums(even, arrived)
     if n_z > 2:
         term = add(term, along_z(term, 2), sums[0])
     order = sorted(range(1, n_z), key=lambda s: (s != n_z // 2, s))
-    back = turned_sum([sums[0]] + [along_z(sums[s], s) for s in order])
-
-    def finish(_, v):
+
+    def finish(_, state):
+        v = state[0]
         for step in range(2, n_z.bit_length() - 1):
             v = add(v, along_z(v, 1 << step))
         total = v.astype(F32)
@@ -555,11 +593,11 @@
                 v, "col", [(i, (i + t) % n_col) for i in range(n_col)]
             ).astype(F32)
         v = total.astype(BF16)
-        return add(v, sibling(v))
+        return v, assemble(node_total ** (-0.5), v, sibling(v))
 
     once = lax.optimization_barrier(jnp.int32(1))
-    whole = lax.fori_loop(0, once, finish, term)
-    weight_grad = whole.astype(F32) * node_total ** (-0.5)
+    _, weight_grad = lax.fori_loop(0, once, finish, (term, weight_grad))
+    back = turned_sum([sums[0]] + [along_z(sums[s], s) for s in order], weight_grad)
     return (activated, back, weight_grad)
 
 

time: 54.8 us -> 53.9 us (0.984)
  Pallas kernels: 12.2 us -> 11.4 us
  other arithmetic: 0.69 us -> 0.01 us
  local copies, waits for them, and re-layouts: 0.01 us -> 0.67 us
    ppermute x8, waiting for transfers between devices: 8.33 us -> 7.2 us  [along_z(): return lax.ppermute(v, 'row', [(i, i ^ 2 * s) for i in range(n_row)])]
    pallas_call x1, Pallas kernels: 5.9 us -> 4.91 us  [densify(): pl.pallas_call(functools.partial(densify_kernel, (n_z, n_col, blocks), gr...]
    ppermute x6 -> x7, waiting for transfers between devices: 2.32 us -> 3.26 us  [sibling(): return lax.ppermute(v, 'row', [(i, i ^ 1) for i in range(n_row)])]
    pallas_call x2 -> x3, Pallas kernels: 0.98 us -> 1.67 us  [the longest x1 1.36 us: backward_own(): pl.pallas_call(own_kernel, out_shape=(pltpu.VMEM((n_src, piece.shape[0],...]
    mul x1 -> x0, other arithmetic: 0.67 us -> none  [shards(): weight_grad = whole.astype(F32) * node_total ** (-0.5)]
    unnamed x6 -> x7, local copies, waits for them, and re-layouts: 0.01 us -> 0.67 us
    ppermute x6 -> x7, starting transfers between devices: 1.3 us -> 1.37 us  [sibling(): return lax.ppermute(v, 'row', [(i, i ^ 1) for i in range(n_row)])]
  transfers between devices with their start and end apart: 20 -> 21, of which waited for: 10 -> 13; matrix products, arithmetic and copies ran while one was open for 1% -> 1% of each run, Pallas kernels for 16% -> 17%
where the time goes in v6:
time: 53.9 us; the launch traced here: 53.8 us
  waiting for transfers between devices  20.4 us (38%)
  starting transfers between devices  19.8 us (37%)
  Pallas kernels  11.4 us (21%)
  between operations  1.45 us (3%)
  local copies, waits for them, and re-layouts  0.67 us (1%)
    ppermute x8, starting transfers between devices, along_z(): return lax.ppermute(v, 'row', [(i, i ^ 2 * s) for i in range(n_row)])  11.1 us
    ppermute x8, waiting for transfers between devices, along_z(): return lax.ppermute(v, 'row', [(i, i ^ 2 * s) for i in range(n_row)])  7.2 us
    ppermute x3, waiting for transfers between devices, to_group(): return lax.ppermute(v, ('col', 'feat'), pairs)  6.09 us
    pallas_call x1, Pallas kernels, densify(): pl.pallas_call(functools.partial(densify_kernel, (n_z, n_col, blocks), gr...  4.91 us
    ppermute x3, starting transfers between devices, to_group(): return lax.ppermute(v, ('col', 'feat'), pairs)  3.55 us
    ppermute x1, waiting for transfers between devices, finish(): lax.ppermute(v, 'col', [(i, (i + t) % n_col) for i in range(n_col)])  3.41 us
    ppermute x7, waiting for transfers between devices, sibling(): return lax.ppermute(v, 'row', [(i, i ^ 1) for i in range(n_row)])  3.26 us
    pallas_call x3, Pallas kernels, forward(): pl.pallas_call(functools.partial(forward_kernel, places, last), out_shape...  2.66 us
  transfers between devices with their start and end apart: 21, of which 13 were waited for; matrix products, arithmetic and copies ran while one was open for 1% of the time, Pallas kernels for 17%

profile of v6, /device:TPU:0, one launch (start us, length us, event | category | flops | bytes accessed | tf_op | source)
XLA Modules:
  0.0 53.8 jit_solution(2167519913353338749)
XLA Ops:
  0.6 0.5 collective-permute-start.6
  1.1 4.7 %collective-permute-start.2 = (bf16[512,128]{1,0:T(8,128)(2,1)}, bf16[512,128]{1,0:T(8,128)(2,1)S(1)}, u32[]{:S(2)}, u32[]{:S(2)}) collective-permute-start(bf16[512,128]{1,0:T(8,128)(2,1)} %refs_0_.1), channel_id=1, source_target_pairs={{0,24},{4,28},{8,16},{12,20},{16,8},{20,12},{24,0},{28,4},{1,25},{... | collective-permute-start | bytes 393224 | tf_op jit(solution)/shard_map/ppermute | solution.py:526
  5.8 0.0 collective-permute-start.3
  5.8 0.7 %collective-permute-start.4 = (bf16[512,128]{1,0:T(8,128)(2,1)}, bf16[512,128]{1,0:T(8,128)(2,1)S(1)}, u32[]{:S(2)}, u32[]{:S(2)}) collective-permute-start(bf16[512,128]{1,0:T(8,128)(2,1)} %refs_0_.1), channel_id=1, source_target_pairs={{0,8},{4,12},{8,0},{12,4},{16,24},{20,28},{24,16},{28,20},{1,9},{5... | collective-permute-start | bytes 393224 | tf_op jit(solution)/shard_map/ppermute | solution.py:526
  6.5 1.6 %collective-permute-start.5 = (bf16[512,128]{1,0:T(8,128)(2,1)}, bf16[512,128]{1,0:T(8,128)(2,1)S(1)}, u32[]{:S(2)}, u32[]{:S(2)}) collective-permute-start(bf16[512,128]{1,0:T(8,128)(2,1)} %cot_own.1), channel_id=1, source_target_pairs={{0,1},{1,0},{2,3},{3,2},{4,5},{5,4},{6,7},{7,6},{8,9},{9,8},{10,11... | collective-permute-start | bytes 393224 | tf_op jit(solution)/shard_map/ppermute | solution.py:529
  8.8 0.0 copy-start
  8.8 4.9 %densify.1.dense = bf16[8,2,512,512]{3,2,1,0:T(8,128)(2,1)S(1)} custom-call(s32[1,1,256]{2,1,0:T(1,128)} %rows.1, s32[1,1,256]{2,1,0:T(1,128)} %cols.1, s32[1,1]{1,0:T(1,128)S(6)} %copy.31.count, bf16[256,128,128]{2,1,0:T(8,128)(2,1)} %bitcast.1), custom_call_target="tpu_custom_call" | custom-call | flops 1 | bytes 1 | tf_op jit(solution)/shard_map/densify/pallas_call | solution.py:93
  13.7 0.0 collective-permute-done.6.refs_1_
  13.7 0.0 copy-done
  13.7 0.7 %forward.3 = (f32[512,128]{1,0:T(8,128)S(1)}, f32[512,128]{1,0:T(8,128)S(1)}) custom-call(bf16[8,2,512,512]{3,2,1,0:T(8,128)(2,1)S(1)} %densify.1.dense, bf16[512,128]{1,0:T(8,128)(2,1)S(1)} %copy-done, bf16[512,128]{1,0:T(8,128)(2,1)S(1)} %collective-permute-done.6.refs_1_), custom_call_target="tpu_custom_call" | custom-call | flops 1 | bytes 1 | tf_op jit(solution)/shard_map/forward/pallas_call | solution.py:150
  14.4 0.0 collective-permute-done.2.refs_0_
  14.4 3.3 %collective-permute-done.3.refs_1_ = bf16[512,128]{1,0:T(8,128)(2,1)S(1)} collective-permute-done((bf16[512,128]{1,0:T(8,128)(2,1)}, bf16[512,128]{1,0:T(8,128)(2,1)S(1)}, u32[]{:S(2)}, u32[]{:S(2)}) %collective-permute-start.3) | collective-permute-done | bytes 131104 | tf_op jit(solution)/shard_map/ppermute | solution.py:526
  17.7 0.0 collective-permute-done.4.refs_2_
  17.7 0.0 collective-permute-done.5.refs_3_
  17.7 0.1 collective-permute-start.7
  17.8 0.5 collective-permute-start.8
  18.3 0.1 collective-permute-start.9
  18.4 0.0 copy-start.1
  18.4 0.0 copy-start.2
  18.4 1.0 %forward.4 = (f32[512,128]{1,0:T(8,128)S(1)}, f32[512,128]{1,0:T(8,128)S(1)}) custom-call(bf16[8,2,512,512]{3,2,1,0:T(8,128)(2,1)S(1)} %densify.1.dense, bf16[512,128]{1,0:T(8,128)(2,1)S(1)} %get-tuple-element.53.refs_0_, bf16[512,128]{1,0:T(8,128)(2,1)S(1)} %get-tuple-element.54.refs_1_, bf16[512,128]{1,0:T(8,128)(2,1)S(1)} %get-tuple-element.55.refs_2_, ...), custom_call_target="tpu_custom_call" | custom-call | flops 1 | bytes 1 | tf_op jit(solution)/shard_map/forward/pallas_call | solution.py:150
  19.4 0.0 collective-permute-done.7.refs_0_
  19.4 0.0 collective-permute-done.8.refs_1_
  19.4 0.3 collective-permute-done.9.refs_2_
  19.6 1.0 %forward.5 = (bf16[512,128]{1,0:T(8,128)(2,1)S(1)}, bf16[512,128]{1,0:T(8,128)(2,1)S(1)}) custom-call(bf16[8,2,512,512]{3,2,1,0:T(8,128)(2,1)S(1)} %densify.1.dense, bf16[512,128]{1,0:T(8,128)(2,1)S(1)} %collective-permute-done.7.refs_0_, bf16[512,128]{1,0:T(8,128)(2,1)S(1)} %collective-permute-done.8.refs_1_, ...), custom_call_target="tpu_custom_call" | custom-call | flops 1 | bytes 1 | tf_op jit(solution)/shard_map/forward/pallas_call | solution.py:150
  20.6 1.6 %collective-permute-start.10 = (bf16[512,128]{1,0:T(8,128)(2,1)S(1)}, bf16[512,128]{1,0:T(8,128)(2,1)S(1)}, u32[]{:S(2)}, u32[]{:S(2)}) collective-permute-start(bf16[512,128]{1,0:T(8,128)(2,1)S(1)} %get-tuple-element.60), channel_id=1, source_target_pairs={{0,2},{1,3},{2,0},{3,1},{4,6},{5,7},{6,4},{7,5},{8,10},{9,11},{10,... | collective-permute-start | bytes 393224 | tf_op jit(solution)/shard_map/ppermute | solution.py:536
  22.2 1.5 %collective-permute-start.11 = (bf16[512,128]{1,0:T(8,128)(2,1)S(1)}, bf16[512,128]{1,0:T(8,128)(2,1)S(1)}, u32[]{:S(2)}, u32[]{:S(2)}) collective-permute-start(bf16[512,128]{1,0:T(8,128)(2,1)S(1)} %get-tuple-element.59.refs_0_), channel_id=1, source_target_pairs={{0,1},{1,0},{2,3},{3,2},{4,5},{5,4},{6,7},{7,6},{8,9},{9,8},{10,11... | collective-permute-start | bytes 393224 | tf_op jit(solution)/shard_map/ppermute | solution.py:536
  23.7 0.5 collective-permute-start.12
  24.2 2.1 %collective-permute-done.10.refs_1_ = bf16[512,128]{1,0:T(8,128)(2,1)S(1)} collective-permute-done((bf16[512,128]{1,0:T(8,128)(2,1)S(1)}, bf16[512,128]{1,0:T(8,128)(2,1)S(1)}, u32[]{:S(2)}, u32[]{:S(2)}) %collective-permute-start.10) | collective-permute-done | bytes 131104 | tf_op jit(solution)/shard_map/ppermute | solution.py:536
  26.3 2.3 %collective-permute-done.11.refs_2_ = bf16[512,128]{1,0:T(8,128)(2,1)S(1)} collective-permute-done((bf16[512,128]{1,0:T(8,128)(2,1)S(1)}, bf16[512,128]{1,0:T(8,128)(2,1)S(1)}, u32[]{:S(2)}, u32[]{:S(2)}) %collective-permute-start.11) | collective-permute-done | bytes 131104 | tf_op jit(solution)/shard_map/ppermute | solution.py:536
  28.6 1.7 %collective-permute-done.12.refs_3_ = bf16[512,128]{1,0:T(8,128)(2,1)S(1)} collective-permute-done((bf16[512,128]{1,0:T(8,128)(2,1)S(1)}, bf16[512,128]{1,0:T(8,128)(2,1)S(1)}, u32[]{:S(2)}, u32[]{:S(2)}) %collective-permute-start.12) | collective-permute-done | bytes 131104 | tf_op jit(solution)/shard_map/ppermute | solution.py:536
  30.3 0.0 copy-done.1
  30.3 0.0 copy-done.2
  30.3 0.5 middle.1
  30.8 1.6 %collective-permute-start.13 = (bf16[128,512]{1,0:T(8,128)(2,1)S(1)}, bf16[128,512]{1,0:T(8,128)(2,1)S(1)}, u32[]{:S(2)}, u32[]{:S(2)}) collective-permute-start(bf16[128,512]{1,0:T(8,128)(2,1)S(1)} %get-tuple-element.61.piece), channel_id=1, source_target_pairs={{0,2},{2,0},{1,3},{3,1},{4,6},{6,4},{5,7},{7,5},{8,10},{10,8},{9,1... | collective-permute-start | bytes 393224 | tf_op jit(solution)/shard_map/ppermute | solution.py:572
  32.3 0.3 weight_term.1
  32.6 0.1 collective-permute-start.14
  32.7 1.2 %collective-permute-done.14.b = bf16[64,256]{1,0:T(8,128)(2,1)S(1)} collective-permute-done((bf16[64,256]{1,0:T(8,128)(2,1)S(1)}, bf16[64,256]{1,0:T(8,128)(2,1)S(1)}, u32[]{:S(2)}, u32[]{:S(2)}) %collective-permute-start.14) | collective-permute-done | bytes 32800 | tf_op jit(solution)/shard_map/ppermute | solution.py:523
  33.9 0.1 collective-permute-start.15
  34.0 1.4 %backward_own.1 = (f32[8,128,512]{2,1,0:T(8,128)S(1)}, bf16[512,128]{1,0:T(8,128)(2,1)}) custom-call(bf16[8,2,512,512]{3,2,1,0:T(8,128)(2,1)S(1)} %densify.1.dense, bf16[128,512]{1,0:T(8,128)(2,1)S(1)} %get-tuple-element.61.piece, f32[512,128]{1,0:T(8,128)S(1)} %get-tuple-element.62.hidden), custom_call_target="tpu_custom_call" | custom-call | flops 1 | bytes 1 | tf_op jit(solution)/shard_map/backward_own/pallas_call | solution.py:173
  35.3 0.4 collective-permute-done.13.refs_0_
  35.8 0.7 %backward.1 = (bf16[4,128,512]{2,1,0:T(8,128)(2,1)S(1)}, bf16[4,128,512]{2,1,0:T(8,128)(2,1)S(1)}) custom-call(bf16[8,2,512,512]{3,2,1,0:T(8,128)(2,1)S(1)} %densify.1.dense, f32[8,128,512]{2,1,0:T(8,128)S(1)} %get-tuple-element.64.own, bf16[128,512]{1,0:T(8,128)(2,1)S(1)} %collective-permute-done.13.refs_0_), custom_call_target="tpu_custom_call" | custom-call | flops 1 | bytes 1 | tf_op jit(solution)/shard_map/backward/pallas_call | solution.py:199
  36.5 1.4 %collective-permute-done.15.b = bf16[64,256]{1,0:T(8,128)(2,1)S(1)} collective-permute-done((bf16[64,256]{1,0:T(8,128)(2,1)S(1)}, bf16[64,256]{1,0:T(8,128)(2,1)S(1)}, u32[]{:S(2)}, u32[]{:S(2)}) %collective-permute-start.15) | collective-permute-done | bytes 32800 | tf_op jit(solution)/shard_map/ppermute | solution.py:526
  37.9 0.1 collective-permute-start.16
  38.0 1.3 %collective-permute-start.20 = (bf16[64,256]{1,0:T(8,128)(2,1)S(1)}, bf16[64,256]{1,0:T(8,128)(2,1)S(1)}, u32[]{:S(2)}, u32[]{:S(2)}) collective-permute-start(bf16[64,256]{1,0:T(8,128)(2,1)S(1)} %add.15.refs_1_.a), channel_id=1, source_target_pairs={{0,16},{4,20},{8,24},{12,28},{16,0},{20,4},{24,8},{28,12},{1,17},{... | collective-permute-start | bytes 98312 | tf_op jit(solution)/shard_map/ppermute | solution.py:526
  39.3 0.6 %collective-permute-done.16.arrived = bf16[4,128,512]{2,1,0:T(8,128)(2,1)S(1)} collective-permute-done((bf16[4,128,512]{2,1,0:T(8,128)(2,1)S(1)}, bf16[4,128,512]{2,1,0:T(8,128)(2,1)S(1)}, u32[]{:S(2)}, u32[]{:S(2)}) %collective-permute-start.16) | collective-permute-done | bytes 524320 | tf_op jit(solution)/shard_map/ppermute | solution.py:523
  39.9 0.1 pair_sums.1
  40.0 1.3 %collective-permute-start.17 = (bf16[128,512]{1,0:T(8,128)(2,1)S(1)}, bf16[128,512]{1,0:T(8,128)(2,1)S(1)}, u32[]{:S(2)}, u32[]{:S(2)}) collective-permute-start(bf16[128,512]{1,0:T(8,128)(2,1)S(1)} %get-tuple-element.73), channel_id=1, source_target_pairs={{0,16},{4,20},{8,24},{12,28},{16,0},{20,4},{24,8},{28,12},{1,17},{... | collective-permute-start | bytes 393224 | tf_op jit(solution)/shard_map/ppermute | solution.py:526
  41.3 1.8 %collective-permute-start.18 = (bf16[128,512]{1,0:T(8,128)(2,1)S(1)}, bf16[128,512]{1,0:T(8,128)(2,1)S(1)}, u32[]{:S(2)}, u32[]{:S(2)}) collective-permute-start(bf16[128,512]{1,0:T(8,128)(2,1)S(1)} %get-tuple-element.74), channel_id=1, source_target_pairs={{0,8},{4,12},{8,0},{12,4},{16,24},{20,28},{24,16},{28,20},{1,9},{5... | collective-permute-start | bytes 393224 | tf_op jit(solution)/shard_map/ppermute | solution.py:526
  43.1 1.3 %collective-permute-start.19 = (bf16[128,512]{1,0:T(8,128)(2,1)S(1)}, bf16[128,512]{1,0:T(8,128)(2,1)S(1)}, u32[]{:S(2)}, u32[]{:S(2)}) collective-permute-start(bf16[128,512]{1,0:T(8,128)(2,1)S(1)} %get-tuple-element.75), channel_id=1, source_target_pairs={{0,24},{4,28},{8,16},{12,20},{16,8},{20,12},{24,0},{28,4},{1,25},{... | collective-permute-start | bytes 393224 | tf_op jit(solution)/shard_map/ppermute | solution.py:526
  44.5 0.0 collective-permute-done.20.b
  44.5 5.3 %while.12 = (s32[]{:T(128)}, bf16[64,256]{1,0:T(8,128)(2,1)S(1)}, f32[128,256]{1,0:T(8,128)S(1)}, s32[]{:T(128)}, s32[]{:T(128)}) while((s32[]{:T(128)}, bf16[64,256]{1,0:T(8,128)(2,1)S(1)}, f32[128,256]{1,0:T(8,128)S(1)}, s32[]{:T(128)}, s32[]{:T(128)}) %tuple.22), condition=%wide.region_1.0_spmd, body=%wide.region_0.0_spmd.sunk | while | flops 65539 | bytes 360590 | solution.py:599
  44.5 0.6 %collective-permute-start = (bf16[64,256]{1,0:T(8,128)(2,1)S(1)}, bf16[64,256]{1,0:T(8,128)(2,1)S(1)}, u32[]{:S(2)}, u32[]{:S(2)}) collective-permute-start(bf16[64,256]{1,0:T(8,128)(2,1)S(1)} %get-tuple-element.116), channel_id=1, source_target_pairs={{0,2},{2,0},{1,3},{3,1},{4,6},{6,4},{5,7},{7,5},{8,10},{10,8},{9,1... | collective-permute-start | bytes 98312 | tf_op jit(solution)/shard_map/while/body/ppermute | solution.py:592
  45.1 3.4 %collective-permute-done = bf16[64,256]{1,0:T(8,128)(2,1)S(1)} collective-permute-done((bf16[64,256]{1,0:T(8,128)(2,1)S(1)}, bf16[64,256]{1,0:T(8,128)(2,1)S(1)}, u32[]{:S(2)}, u32[]{:S(2)}) %collective-permute-start) | collective-permute-done | bytes 32800 | tf_op jit(solution)/shard_map/while/body/ppermute | solution.py:592
  48.5 0.1 collective-permute-start.1
  48.6 1.2 %collective-permute-done.1.theirs = bf16[64,256]{1,0:T(8,128)(2,1)S(1)} collective-permute-done((bf16[64,256]{1,0:T(8,128)(2,1)S(1)}, bf16[64,256]{1,0:T(8,128)(2,1)S(1)}, u32[]{:S(2)}, u32[]{:S(2)}) %collective-permute-start.1) | collective-permute-done | bytes 32800 | tf_op jit(solution)/shard_map/while/body/ppermute | solution.py:523
  49.8 0.7 %copy.30 = f32[128,256]{1,0:T(8,128)} copy(f32[128,256]{1,0:T(8,128)S(1)} %get-tuple-element.127.refs_4_) | data formatting | bytes 262144
  50.5 0.4 collective-permute-done.17.refs_1_
  50.9 0.0 collective-permute-done.18.refs_2_
  50.9 2.1 %collective-permute-done.19.refs_3_ = bf16[128,512]{1,0:T(8,128)(2,1)S(1)} collective-permute-done((bf16[128,512]{1,0:T(8,128)(2,1)S(1)}, bf16[128,512]{1,0:T(8,128)(2,1)S(1)}, u32[]{:S(2)}, u32[]{:S(2)}) %collective-permute-start.19) | collective-permute-done | bytes 131104 | tf_op jit(solution)/shard_map/ppermute | solution.py:526
  53.0 0.8 %turned_sum.1 = bf16[512,128]{1,0:T(8,128)(2,1)} custom-call(bf16[128,512]{1,0:T(8,128)(2,1)S(1)} %get-tuple-element.72.rest_0_.refs_0_, bf16[128,512]{1,0:T(8,128)(2,1)S(1)} %collective-permute-done.17.refs_1_, bf16[128,512]{1,0:T(8,128)(2,1)S(1)} %collective-permute-done.18.refs_2_, bf16[128,512]{1,0:T(8,128)(2,1)S(1)} %collective-permute-done.19.refs_3_, ...), custom_call_target="tpu_custom_call" | custom-call | flops 1 | bytes 1 | tf_op jit(solution)/shard_map/turned_sum/pallas_call | solution.py:504
  (7 shorter events, 0.1 us)
Async XLA Ops:
  0.6 13.0 %collective-permute-start.6 = (bf16[512,128]{1,0:T(8,128)(2,1)}, bf16[512,128]{1,0:T(8,128)(2,1)S(1)}, u32[]{:S(2)}, u32[]{:S(2)}) collective-permute-start(bf16[512,128]{1,0:T(8,128)(2,1)} %refs_0_.1), channel_id=1, source_target_pairs={{0,4},{4,0},{8,12},{12,8},{16,20},{20,16},{24,28},{28,24},{1,5},{5... | collective-permute-start | bytes 393224 | tf_op jit(solution)/shard_map/ppermute | solution.py:523
  1.1 13.3 %collective-permute-start.2 = (bf16[512,128]{1,0:T(8,128)(2,1)}, bf16[512,128]{1,0:T(8,128)(2,1)S(1)}, u32[]{:S(2)}, u32[]{:S(2)}) collective-permute-start(bf16[512,128]{1,0:T(8,128)(2,1)} %refs_0_.1), channel_id=1, source_target_pairs={{0,24},{4,28},{8,16},{12,20},{16,8},{20,12},{24,0},{28,4},{1,25},{... | collective-permute-start | bytes 393224 | tf_op jit(solution)/shard_map/ppermute | solution.py:526
  5.8 11.9 %collective-permute-start.3 = (bf16[512,128]{1,0:T(8,128)(2,1)}, bf16[512,128]{1,0:T(8,128)(2,1)S(1)}, u32[]{:S(2)}, u32[]{:S(2)}) collective-permute-start(bf16[512,128]{1,0:T(8,128)(2,1)} %refs_0_.1), channel_id=1, source_target_pairs={{0,16},{4,20},{8,24},{12,28},{16,0},{20,4},{24,8},{28,12},{1,17},{... | collective-permute-start | bytes 393224 | tf_op jit(solution)/shard_map/ppermute | solution.py:526
  5.8 11.9 %collective-permute-start.4 = (bf16[512,128]{1,0:T(8,128)(2,1)}, bf16[512,128]{1,0:T(8,128)(2,1)S(1)}, u32[]{:S(2)}, u32[]{:S(2)}) collective-permute-start(bf16[512,128]{1,0:T(8,128)(2,1)} %refs_0_.1), channel_id=1, source_target_pairs={{0,8},{4,12},{8,0},{12,4},{16,24},{20,28},{24,16},{28,20},{1,9},{5... | collective-permute-start | bytes 393224 | tf_op jit(solution)/shard_map/ppermute | solution.py:526
  6.5 11.2 %collective-permute-start.5 = (bf16[512,128]{1,0:T(8,128)(2,1)}, bf16[512,128]{1,0:T(8,128)(2,1)S(1)}, u32[]{:S(2)}, u32[]{:S(2)}) collective-permute-start(bf16[512,128]{1,0:T(8,128)(2,1)} %cot_own.1), channel_id=1, source_target_pairs={{0,1},{1,0},{2,3},{3,2},{4,5},{5,4},{6,7},{7,6},{8,9},{9,8},{10,11... | collective-permute-start | bytes 393224 | tf_op jit(solution)/shard_map/ppermute | solution.py:529
  8.8 4.9 %copy-start = (bf16[512,128]{1,0:T(8,128)(2,1)S(1)}, bf16[512,128]{1,0:T(8,128)(2,1)}, u32[]{:S(2)}) copy-start(bf16[512,128]{1,0:T(8,128)(2,1)} %refs_0_.1) | copy-start | bytes 393220
  17.7 1.6 %collective-permute-start.7 = (bf16[512,128]{1,0:T(8,128)(2,1)S(1)}, bf16[512,128]{1,0:T(8,128)(2,1)S(1)}, u32[]{:S(2)}, u32[]{:S(2)}) collective-permute-start(bf16[512,128]{1,0:T(8,128)(2,1)S(1)} %get-tuple-element.53.refs_0_), channel_id=1, source_target_pairs={{0,4},{4,0},{8,12},{12,8},{16,20},{20,16},{24,28},{28,24},{1,5},{5... | collective-permute-start | bytes 393224 | tf_op jit(solution)/shard_map/ppermute | solution.py:523
  17.8 1.6 %collective-permute-start.8 = (bf16[512,128]{1,0:T(8,128)(2,1)S(1)}, bf16[512,128]{1,0:T(8,128)(2,1)S(1)}, u32[]{:S(2)}, u32[]{:S(2)}) collective-permute-start(bf16[512,128]{1,0:T(8,128)(2,1)S(1)} %get-tuple-element.54.refs_1_), channel_id=1, source_target_pairs={{0,4},{4,0},{8,12},{12,8},{16,20},{20,16},{24,28},{28,24},{1,5},{5... | collective-permute-start | bytes 393224 | tf_op jit(solution)/shard_map/ppermute | solution.py:523
  18.3 1.3 %collective-permute-start.9 = (bf16[512,128]{1,0:T(8,128)(2,1)S(1)}, bf16[512,128]{1,0:T(8,128)(2,1)S(1)}, u32[]{:S(2)}, u32[]{:S(2)}) collective-permute-start(bf16[512,128]{1,0:T(8,128)(2,1)S(1)} %get-tuple-element.55.refs_2_), channel_id=1, source_target_pairs={{0,4},{4,0},{8,12},{12,8},{16,20},{20,16},{24,28},{28,24},{1,5},{5... | collective-permute-start | bytes 393224 | tf_op jit(solution)/shard_map/ppermute | solution.py:523
  18.4 11.9 %copy-start.1 = (bf16[256,256]{1,0:T(8,128)(2,1)S(1)}, bf16[256,256]{1,0:T(8,128)(2,1)}, u32[]{:S(2)}) copy-start(bf16[256,256]{1,0:T(8,128)(2,1)} %weights.1) | copy-start | bytes 393220
  18.4 11.9 %copy-start.2 = (bf16[512,128]{1,0:T(8,128)(2,1)S(1)}, bf16[512,128]{1,0:T(8,128)(2,1)}, u32[]{:S(2)}) copy-start(bf16[512,128]{1,0:T(8,128)(2,1)} %cot_own.1) | copy-start | bytes 393220
  20.6 5.7 %collective-permute-start.10 = (bf16[512,128]{1,0:T(8,128)(2,1)S(1)}, bf16[512,128]{1,0:T(8,128)(2,1)S(1)}, u32[]{:S(2)}, u32[]{:S(2)}) collective-permute-start(bf16[512,128]{1,0:T(8,128)(2,1)S(1)} %get-tuple-element.60), channel_id=1, source_target_pairs={{0,2},{1,3},{2,0},{3,1},{4,6},{5,7},{6,4},{7,5},{8,10},{9,11},{10,... | collective-permute-start | bytes 393224 | tf_op jit(solution)/shard_map/ppermute | solution.py:536
  22.2 6.4 %collective-permute-start.11 = (bf16[512,128]{1,0:T(8,128)(2,1)S(1)}, bf16[512,128]{1,0:T(8,128)(2,1)S(1)}, u32[]{:S(2)}, u32[]{:S(2)}) collective-permute-start(bf16[512,128]{1,0:T(8,128)(2,1)S(1)} %get-tuple-element.59.refs_0_), channel_id=1, source_target_pairs={{0,1},{1,0},{2,3},{3,2},{4,5},{5,4},{6,7},{7,6},{8,9},{9,8},{10,11... | collective-permute-start | bytes 393224 | tf_op jit(solution)/shard_map/ppermute | solution.py:536
  23.7 6.6 %collective-permute-start.12 = (bf16[512,128]{1,0:T(8,128)(2,1)S(1)}, bf16[512,128]{1,0:T(8,128)(2,1)S(1)}, u32[]{:S(2)}, u32[]{:S(2)}) collective-permute-start(bf16[512,128]{1,0:T(8,128)(2,1)S(1)} %get-tuple-element.60), channel_id=1, source_target_pairs={{0,3},{1,2},{2,1},{3,0},{4,7},{5,6},{6,5},{7,4},{8,11},{9,10},{10,... | collective-permute-start | bytes 393224 | tf_op jit(solution)/shard_map/ppermute | solution.py:536
  30.8 5.0 %collective-permute-start.13 = (bf16[128,512]{1,0:T(8,128)(2,1)S(1)}, bf16[128,512]{1,0:T(8,128)(2,1)S(1)}, u32[]{:S(2)}, u32[]{:S(2)}) collective-permute-start(bf16[128,512]{1,0:T(8,128)(2,1)S(1)} %get-tuple-element.61.piece), channel_id=1, source_target_pairs={{0,2},{2,0},{1,3},{3,1},{4,6},{6,4},{5,7},{7,5},{8,10},{10,8},{9,1... | collective-permute-start | bytes 393224 | tf_op jit(solution)/shard_map/ppermute | solution.py:572
  32.6 1.3 %collective-permute-start.14 = (bf16[64,256]{1,0:T(8,128)(2,1)S(1)}, bf16[64,256]{1,0:T(8,128)(2,1)S(1)}, u32[]{:S(2)}, u32[]{:S(2)}) collective-permute-start(bf16[64,256]{1,0:T(8,128)(2,1)S(1)} %get-tuple-element.71), channel_id=1, source_target_pairs={{0,4},{4,0},{8,12},{12,8},{16,20},{20,16},{24,28},{28,24},{1,5},{5... | collective-permute-start | bytes 98312 | tf_op jit(solution)/shard_map/ppermute | solution.py:523
  33.9 4.0 %collective-permute-start.15 = (bf16[64,256]{1,0:T(8,128)(2,1)S(1)}, bf16[64,256]{1,0:T(8,128)(2,1)S(1)}, u32[]{:S(2)}, u32[]{:S(2)}) collective-permute-start(bf16[64,256]{1,0:T(8,128)(2,1)S(1)} %add.14.a), channel_id=1, source_target_pairs={{0,8},{4,12},{8,0},{12,4},{16,24},{20,28},{24,16},{28,20},{1,9},{5... | collective-permute-start | bytes 98312 | tf_op jit(solution)/shard_map/ppermute | solution.py:526
  37.9 2.0 %collective-permute-start.16 = (bf16[4,128,512]{2,1,0:T(8,128)(2,1)S(1)}, bf16[4,128,512]{2,1,0:T(8,128)(2,1)S(1)}, u32[]{:S(2)}, u32[]{:S(2)}) collective-permute-start(bf16[4,128,512]{2,1,0:T(8,128)(2,1)S(1)} %hold.3), channel_id=1, source_target_pairs={{0,4},{4,0},{8,12},{12,8},{16,20},{20,16},{24,28},{28,24},{1,5},{5... | collective-permute-start | bytes 1572872 | tf_op jit(solution)/shard_map/ppermute | solution.py:523
  38.0 6.5 %collective-permute-start.20 = (bf16[64,256]{1,0:T(8,128)(2,1)S(1)}, bf16[64,256]{1,0:T(8,128)(2,1)S(1)}, u32[]{:S(2)}, u32[]{:S(2)}) collective-permute-start(bf16[64,256]{1,0:T(8,128)(2,1)S(1)} %add.15.refs_1_.a), channel_id=1, source_target_pairs={{0,16},{4,20},{8,24},{12,28},{16,0},{20,4},{24,8},{28,12},{1,17},{... | collective-permute-start | bytes 98312 | tf_op jit(solution)/shard_map/ppermute | solution.py:526
  40.0 10.8 %collective-permute-start.17 = (bf16[128,512]{1,0:T(8,128)(2,1)S(1)}, bf16[128,512]{1,0:T(8,128)(2,1)S(1)}, u32[]{:S(2)}, u32[]{:S(2)}) collective-permute-start(bf16[128,512]{1,0:T(8,128)(2,1)S(1)} %get-tuple-element.73), channel_id=1, source_target_pairs={{0,16},{4,20},{8,24},{12,28},{16,0},{20,4},{24,8},{28,12},{1,17},{... | collective-permute-start | bytes 393224 | tf_op jit(solution)/shard_map/ppermute | solution.py:526
  41.3 9.6 %collective-permute-start.18 = (bf16[128,512]{1,0:T(8,128)(2,1)S(1)}, bf16[128,512]{1,0:T(8,128)(2,1)S(1)}, u32[]{:S(2)}, u32[]{:S(2)}) collective-permute-start(bf16[128,512]{1,0:T(8,128)(2,1)S(1)} %get-tuple-element.74), channel_id=1, source_target_pairs={{0,8},{4,12},{8,0},{12,4},{16,24},{20,28},{24,16},{28,20},{1,9},{5... | collective-permute-start | bytes 393224 | tf_op jit(solution)/shard_map/ppermute | solution.py:526
  43.1 9.8 %collective-permute-start.19 = (bf16[128,512]{1,0:T(8,128)(2,1)S(1)}, bf16[128,512]{1,0:T(8,128)(2,1)S(1)}, u32[]{:S(2)}, u32[]{:S(2)}) collective-permute-start(bf16[128,512]{1,0:T(8,128)(2,1)S(1)} %get-tuple-element.75), channel_id=1, source_target_pairs={{0,24},{4,28},{8,16},{12,20},{16,8},{20,12},{24,0},{28,4},{1,25},{... | collective-permute-start | bytes 393224 | tf_op jit(solution)/shard_map/ppermute | solution.py:526
  44.5 4.0 %collective-permute-start = (bf16[64,256]{1,0:T(8,128)(2,1)S(1)}, bf16[64,256]{1,0:T(8,128)(2,1)S(1)}, u32[]{:S(2)}, u32[]{:S(2)}) collective-permute-start(bf16[64,256]{1,0:T(8,128)(2,1)S(1)} %get-tuple-element.116), channel_id=1, source_target_pairs={{0,2},{2,0},{1,3},{3,1},{4,6},{6,4},{5,7},{7,5},{8,10},{10,8},{9,1... | collective-permute-start | bytes 98312 | tf_op jit(solution)/shard_map/while/body/ppermute | solution.py:592
  48.5 1.3 %collective-permute-start.1 = (bf16[64,256]{1,0:T(8,128)(2,1)S(1)}, bf16[64,256]{1,0:T(8,128)(2,1)S(1)}, u32[]{:S(2)}, u32[]{:S(2)}) collective-permute-start(bf16[64,256]{1,0:T(8,128)(2,1)S(1)} %add_convert_fusion.2.mine), channel_id=1, source_target_pairs={{0,4},{4,0},{8,12},{12,8},{16,20},{20,16},{24,28},{28,24},{1,5},{5... | collective-permute-start | bytes 98312 | tf_op jit(solution)/shard_map/while/body/ppermute | solution.py:523

commit v7 on v6

--- a/solution.py
+++ b/solution.py
@@ -335,8 +335,8 @@
 
 
 def middle_kernel(n_col, weights, cot_own, cot_other, *refs):
-    own = refs[:n_col]
-    other = refs[n_col : 2 * n_col]
+    other = refs[:n_col]
+    own = refs[n_col : 2 * n_col]
     spread, kept, agg, g_own, g_other = refs[2 * n_col :]
     half = cot_own.shape[1]
     f = lax.axis_index("feat")
@@ -382,7 +382,7 @@
         compiler_params=params(),
         cost_estimate=COST,
         name="middle",
-    )(weights, cot_own, cot_other, *own, *other)
+    )(weights, cot_own, cot_other, *other, *own)
 
 
 def weight_kernel(agg, g_own, g_other, keep, send, whole):
@@ -565,8 +565,8 @@
             even, odd = (backward_stream(dense, k, pieces) for k in range(2))
             return even, odd, elu(hidden)
 
+    other = [to_group(parts[t], -t, 1) for t in range(n_col - 1, -1, -1)]
     own = [parts[0]] + [to_group(parts[t], -t, 0) for t in range(1, n_col)]
-    other = [to_group(parts[t], -t, 1) for t in range(n_col)]
     spread, hidden, *rest = middle(weights, cotangent, cot_other, own, other)
     pieces = [spread] + [
         lax.ppermute(spread, "col", [(i, (i + t) % n_col) for i in range(n_col)])

time: 53.9 us -> 53.6 us (level)
  transfers between devices with their start and end apart: 21 -> 21, of which waited for: 13 -> 12; matrix products, arithmetic and copies ran while one was open for 1% -> 1% of each run, Pallas kernels for 17% -> 16%
where the time goes in v7:
time: 53.6 us; the launch traced here: 53.5 us
  waiting for transfers between devices  20.4 us (38%)
  starting transfers between devices  19.9 us (37%)
  Pallas kernels  11 us (21%)
  between operations  1.45 us (3%)
  local copies, waits for them, and re-layouts  0.67 us (1%)
    ppermute x8, starting transfers between devices, along_z(): return lax.ppermute(v, 'row', [(i, i ^ 2 * s) for i in range(n_row)])  11.1 us
    ppermute x8, waiting for transfers between devices, along_z(): return lax.ppermute(v, 'row', [(i, i ^ 2 * s) for i in range(n_row)])  7.3 us
    ppermute x3, waiting for transfers between devices, to_group(): return lax.ppermute(v, ('col', 'feat'), pairs)  5.87 us
    pallas_call x1, Pallas kernels, densify(): pl.pallas_call(functools.partial(densify_kernel, (n_z, n_col, blocks), gr...  4.57 us
    ppermute x3, starting transfers between devices, to_group(): return lax.ppermute(v, ('col', 'feat'), pairs)  3.55 us
    ppermute x1, waiting for transfers between devices, finish(): lax.ppermute(v, 'col', [(i, (i + t) % n_col) for i in range(n_col)])  3.31 us
    ppermute x7, waiting for transfers between devices, sibling(): return lax.ppermute(v, 'row', [(i, i ^ 1) for i in range(n_row)])  3.26 us
    pallas_call x3, Pallas kernels, forward(): pl.pallas_call(functools.partial(forward_kernel, places, last), out_shape...  2.66 us
  transfers between devices with their start and end apart: 21, of which 12 were waited for; matrix products, arithmetic and copies ran while one was open for 1% of the time, Pallas kernels for 16%

profile of v7, /device:TPU:0, one launch (start us, length us, event | category | flops | bytes accessed | tf_op | source)
XLA Modules:
  0.0 53.5 jit_solution(5215123437360491514)
XLA Ops:
  0.6 0.5 collective-permute-start.6
  1.1 4.7 %collective-permute-start.2 = (bf16[512,128]{1,0:T(8,128)(2,1)}, bf16[512,128]{1,0:T(8,128)(2,1)S(1)}, u32[]{:S(2)}, u32[]{:S(2)}) collective-permute-start(bf16[512,128]{1,0:T(8,128)(2,1)} %refs_0_.1), channel_id=1, source_target_pairs={{0,24},{4,28},{8,16},{12,20},{16,8},{20,12},{24,0},{28,4},{1,25},{... | collective-permute-start | bytes 393224 | tf_op jit(solution)/shard_map/ppermute | solution.py:526
  5.8 0.0 collective-permute-start.3
  5.8 0.7 %collective-permute-start.4 = (bf16[512,128]{1,0:T(8,128)(2,1)}, bf16[512,128]{1,0:T(8,128)(2,1)S(1)}, u32[]{:S(2)}, u32[]{:S(2)}) collective-permute-start(bf16[512,128]{1,0:T(8,128)(2,1)} %refs_0_.1), channel_id=1, source_target_pairs={{0,8},{4,12},{8,0},{12,4},{16,24},{20,28},{24,16},{28,20},{1,9},{5... | collective-permute-start | bytes 393224 | tf_op jit(solution)/shard_map/ppermute | solution.py:526
  6.5 1.6 %collective-permute-start.5 = (bf16[512,128]{1,0:T(8,128)(2,1)}, bf16[512,128]{1,0:T(8,128)(2,1)S(1)}, u32[]{:S(2)}, u32[]{:S(2)}) collective-permute-start(bf16[512,128]{1,0:T(8,128)(2,1)} %cot_own.1), channel_id=1, source_target_pairs={{0,1},{1,0},{2,3},{3,2},{4,5},{5,4},{6,7},{7,6},{8,9},{9,8},{10,11... | collective-permute-start | bytes 393224 | tf_op jit(solution)/shard_map/ppermute | solution.py:529
  8.8 0.0 copy-start
  8.8 4.6 %densify.1.dense = bf16[8,2,512,512]{3,2,1,0:T(8,128)(2,1)S(1)} custom-call(s32[1,1,256]{2,1,0:T(1,128)} %rows.1, s32[1,1,256]{2,1,0:T(1,128)} %cols.1, s32[1,1]{1,0:T(1,128)S(6)} %copy.31.count, bf16[256,128,128]{2,1,0:T(8,128)(2,1)} %bitcast.1), custom_call_target="tpu_custom_call" | custom-call | flops 1 | bytes 1 | tf_op jit(solution)/shard_map/densify/pallas_call | solution.py:93
  13.3 0.0 collective-permute-done.6.refs_1_
  13.4 0.0 copy-done
  13.4 0.7 %forward.3 = (f32[512,128]{1,0:T(8,128)S(1)}, f32[512,128]{1,0:T(8,128)S(1)}) custom-call(bf16[8,2,512,512]{3,2,1,0:T(8,128)(2,1)S(1)} %densify.1.dense, bf16[512,128]{1,0:T(8,128)(2,1)S(1)} %copy-done, bf16[512,128]{1,0:T(8,128)(2,1)S(1)} %collective-permute-done.6.refs_1_), custom_call_target="tpu_custom_call" | custom-call | flops 1 | bytes 1 | tf_op jit(solution)/shard_map/forward/pallas_call | solution.py:150
  14.1 0.0 collective-permute-done.2.refs_0_
  14.1 3.6 %collective-permute-done.3.refs_1_ = bf16[512,128]{1,0:T(8,128)(2,1)S(1)} collective-permute-done((bf16[512,128]{1,0:T(8,128)(2,1)}, bf16[512,128]{1,0:T(8,128)(2,1)S(1)}, u32[]{:S(2)}, u32[]{:S(2)}) %collective-permute-start.3) | collective-permute-done | bytes 131104 | tf_op jit(solution)/shard_map/ppermute | solution.py:526
  17.7 0.0 collective-permute-done.4.refs_2_
  17.7 0.0 collective-permute-done.5.refs_3_
  17.7 0.1 collective-permute-start.7
  17.8 0.5 collective-permute-start.8
  18.3 0.1 collective-permute-start.9
  18.4 0.0 copy-start.1
  18.4 0.0 copy-start.2
  18.4 1.0 %forward.4 = (f32[512,128]{1,0:T(8,128)S(1)}, f32[512,128]{1,0:T(8,128)S(1)}) custom-call(bf16[8,2,512,512]{3,2,1,0:T(8,128)(2,1)S(1)} %densify.1.dense, bf16[512,128]{1,0:T(8,128)(2,1)S(1)} %get-tuple-element.53.refs_0_, bf16[512,128]{1,0:T(8,128)(2,1)S(1)} %get-tuple-element.54.refs_1_, bf16[512,128]{1,0:T(8,128)(2,1)S(1)} %get-tuple-element.55.refs_2_, ...), custom_call_target="tpu_custom_call" | custom-call | flops 1 | bytes 1 | tf_op jit(solution)/shard_map/forward/pallas_call | solution.py:150
  19.4 0.0 collective-permute-done.7.refs_0_
  19.4 0.0 collective-permute-done.8.refs_1_
  19.4 0.3 collective-permute-done.9.refs_2_
  19.6 1.0 %forward.5 = (bf16[512,128]{1,0:T(8,128)(2,1)S(1)}, bf16[512,128]{1,0:T(8,128)(2,1)S(1)}) custom-call(bf16[8,2,512,512]{3,2,1,0:T(8,128)(2,1)S(1)} %densify.1.dense, bf16[512,128]{1,0:T(8,128)(2,1)S(1)} %collective-permute-done.7.refs_0_, bf16[512,128]{1,0:T(8,128)(2,1)S(1)} %collective-permute-done.8.refs_1_, ...), custom_call_target="tpu_custom_call" | custom-call | flops 1 | bytes 1 | tf_op jit(solution)/shard_map/forward/pallas_call | solution.py:150
  20.6 2.5 %collective-permute-start.10 = (bf16[512,128]{1,0:T(8,128)(2,1)S(1)}, bf16[512,128]{1,0:T(8,128)(2,1)S(1)}, u32[]{:S(2)}, u32[]{:S(2)}) collective-permute-start(bf16[512,128]{1,0:T(8,128)(2,1)S(1)} %get-tuple-element.59), channel_id=1, source_target_pairs={{0,3},{1,2},{2,1},{3,0},{4,7},{5,6},{6,5},{7,4},{8,11},{9,10},{10,... | collective-permute-start | bytes 393224 | tf_op jit(solution)/shard_map/ppermute | solution.py:536
  23.2 0.5 %collective-permute-start.11 = (bf16[512,128]{1,0:T(8,128)(2,1)S(1)}, bf16[512,128]{1,0:T(8,128)(2,1)S(1)}, u32[]{:S(2)}, u32[]{:S(2)}) collective-permute-start(bf16[512,128]{1,0:T(8,128)(2,1)S(1)} %get-tuple-element.60.refs_2_), channel_id=1, source_target_pairs={{0,1},{1,0},{2,3},{3,2},{4,5},{5,4},{6,7},{7,6},{8,9},{9,8},{10,11... | collective-permute-start | bytes 393224 | tf_op jit(solution)/shard_map/ppermute | solution.py:536
  23.7 0.5 collective-permute-start.12
  24.2 3.7 %collective-permute-done.10.refs_0_ = bf16[512,128]{1,0:T(8,128)(2,1)S(1)} collective-permute-done((bf16[512,128]{1,0:T(8,128)(2,1)S(1)}, bf16[512,128]{1,0:T(8,128)(2,1)S(1)}, u32[]{:S(2)}, u32[]{:S(2)}) %collective-permute-start.10) | collective-permute-done | bytes 131104 | tf_op jit(solution)/shard_map/ppermute | solution.py:536
  27.9 2.1 %collective-permute-done.11.refs_1_ = bf16[512,128]{1,0:T(8,128)(2,1)S(1)} collective-permute-done((bf16[512,128]{1,0:T(8,128)(2,1)S(1)}, bf16[512,128]{1,0:T(8,128)(2,1)S(1)}, u32[]{:S(2)}, u32[]{:S(2)}) %collective-permute-start.11) | collective-permute-done | bytes 131104 | tf_op jit(solution)/shard_map/ppermute | solution.py:536
  30.1 0.0 collective-permute-done.12.refs_3_
  30.1 0.0 copy-done.1
  30.1 0.0 copy-done.2
  30.1 0.5 middle.1
  30.5 1.5 %collective-permute-start.13 = (bf16[128,512]{1,0:T(8,128)(2,1)S(1)}, bf16[128,512]{1,0:T(8,128)(2,1)S(1)}, u32[]{:S(2)}, u32[]{:S(2)}) collective-permute-start(bf16[128,512]{1,0:T(8,128)(2,1)S(1)} %get-tuple-element.61.piece), channel_id=1, source_target_pairs={{0,2},{2,0},{1,3},{3,1},{4,6},{6,4},{5,7},{7,5},{8,10},{10,8},{9,1... | collective-permute-start | bytes 393224 | tf_op jit(solution)/shard_map/ppermute | solution.py:572
  32.1 0.3 weight_term.1
  32.3 0.1 collective-permute-start.14
  32.4 1.2 %collective-permute-done.14.b = bf16[64,256]{1,0:T(8,128)(2,1)S(1)} collective-permute-done((bf16[64,256]{1,0:T(8,128)(2,1)S(1)}, bf16[64,256]{1,0:T(8,128)(2,1)S(1)}, u32[]{:S(2)}, u32[]{:S(2)}) %collective-permute-start.14) | collective-permute-done | bytes 32800 | tf_op jit(solution)/shard_map/ppermute | solution.py:523
  33.6 0.1 collective-permute-start.15
  33.7 1.4 %backward_own.1 = (f32[8,128,512]{2,1,0:T(8,128)S(1)}, bf16[512,128]{1,0:T(8,128)(2,1)}) custom-call(bf16[8,2,512,512]{3,2,1,0:T(8,128)(2,1)S(1)} %densify.1.dense, bf16[128,512]{1,0:T(8,128)(2,1)S(1)} %get-tuple-element.61.piece, f32[512,128]{1,0:T(8,128)S(1)} %get-tuple-element.62.hidden), custom_call_target="tpu_custom_call" | custom-call | flops 1 | bytes 1 | tf_op jit(solution)/shard_map/backward_own/pallas_call | solution.py:173
  35.1 0.7 %collective-permute-done.13.refs_0_ = bf16[128,512]{1,0:T(8,128)(2,1)S(1)} collective-permute-done((bf16[128,512]{1,0:T(8,128)(2,1)S(1)}, bf16[128,512]{1,0:T(8,128)(2,1)S(1)}, u32[]{:S(2)}, u32[]{:S(2)}) %collective-permute-start.13) | collective-permute-done | bytes 131104 | tf_op jit(solution)/shard_map/ppermute | solution.py:572
  35.7 0.7 %backward.1 = (bf16[4,128,512]{2,1,0:T(8,128)(2,1)S(1)}, bf16[4,128,512]{2,1,0:T(8,128)(2,1)S(1)}) custom-call(bf16[8,2,512,512]{3,2,1,0:T(8,128)(2,1)S(1)} %densify.1.dense, f32[8,128,512]{2,1,0:T(8,128)S(1)} %get-tuple-element.64.own, bf16[128,512]{1,0:T(8,128)(2,1)S(1)} %collective-permute-done.13.refs_0_), custom_call_target="tpu_custom_call" | custom-call | flops 1 | bytes 1 | tf_op jit(solution)/shard_map/backward/pallas_call | solution.py:199
  36.5 1.1 %collective-permute-done.15.b = bf16[64,256]{1,0:T(8,128)(2,1)S(1)} collective-permute-done((bf16[64,256]{1,0:T(8,128)(2,1)S(1)}, bf16[64,256]{1,0:T(8,128)(2,1)S(1)}, u32[]{:S(2)}, u32[]{:S(2)}) %collective-permute-start.15) | collective-permute-done | bytes 32800 | tf_op jit(solution)/shard_map/ppermute | solution.py:526
  37.6 0.1 collective-permute-start.16
  37.7 1.3 %collective-permute-start.20 = (bf16[64,256]{1,0:T(8,128)(2,1)S(1)}, bf16[64,256]{1,0:T(8,128)(2,1)S(1)}, u32[]{:S(2)}, u32[]{:S(2)}) collective-permute-start(bf16[64,256]{1,0:T(8,128)(2,1)S(1)} %add.15.refs_1_.a), channel_id=1, source_target_pairs={{0,16},{4,20},{8,24},{12,28},{16,0},{20,4},{24,8},{28,12},{1,17},{... | collective-permute-start | bytes 98312 | tf_op jit(solution)/shard_map/ppermute | solution.py:526
  39.0 0.6 %collective-permute-done.16.arrived = bf16[4,128,512]{2,1,0:T(8,128)(2,1)S(1)} collective-permute-done((bf16[4,128,512]{2,1,0:T(8,128)(2,1)S(1)}, bf16[4,128,512]{2,1,0:T(8,128)(2,1)S(1)}, u32[]{:S(2)}, u32[]{:S(2)}) %collective-permute-start.16) | collective-permute-done | bytes 524320 | tf_op jit(solution)/shard_map/ppermute | solution.py:523
  39.6 0.1 pair_sums.1
  39.7 1.3 %collective-permute-start.17 = (bf16[128,512]{1,0:T(8,128)(2,1)S(1)}, bf16[128,512]{1,0:T(8,128)(2,1)S(1)}, u32[]{:S(2)}, u32[]{:S(2)}) collective-permute-start(bf16[128,512]{1,0:T(8,128)(2,1)S(1)} %get-tuple-element.73), channel_id=1, source_target_pairs={{0,16},{4,20},{8,24},{12,28},{16,0},{20,4},{24,8},{28,12},{1,17},{... | collective-permute-start | bytes 393224 | tf_op jit(solution)/shard_map/ppermute | solution.py:526
  41.0 1.8 %collective-permute-start.18 = (bf16[128,512]{1,0:T(8,128)(2,1)S(1)}, bf16[128,512]{1,0:T(8,128)(2,1)S(1)}, u32[]{:S(2)}, u32[]{:S(2)}) collective-permute-start(bf16[128,512]{1,0:T(8,128)(2,1)S(1)} %get-tuple-element.74), channel_id=1, source_target_pairs={{0,8},{4,12},{8,0},{12,4},{16,24},{20,28},{24,16},{28,20},{1,9},{5... | collective-permute-start | bytes 393224 | tf_op jit(solution)/shard_map/ppermute | solution.py:526
  42.8 1.3 %collective-permute-start.19 = (bf16[128,512]{1,0:T(8,128)(2,1)S(1)}, bf16[128,512]{1,0:T(8,128)(2,1)S(1)}, u32[]{:S(2)}, u32[]{:S(2)}) collective-permute-start(bf16[128,512]{1,0:T(8,128)(2,1)S(1)} %get-tuple-element.75), channel_id=1, source_target_pairs={{0,24},{4,28},{8,16},{12,20},{16,8},{20,12},{24,0},{28,4},{1,25},{... | collective-permute-start | bytes 393224 | tf_op jit(solution)/shard_map/ppermute | solution.py:526
  44.2 0.0 collective-permute-done.20.b
  44.2 5.3 %while.12 = (s32[]{:T(128)}, bf16[64,256]{1,0:T(8,128)(2,1)S(1)}, f32[128,256]{1,0:T(8,128)S(1)}, s32[]{:T(128)}, s32[]{:T(128)}) while((s32[]{:T(128)}, bf16[64,256]{1,0:T(8,128)(2,1)S(1)}, f32[128,256]{1,0:T(8,128)S(1)}, s32[]{:T(128)}, s32[]{:T(128)}) %tuple.22), condition=%wide.region_1.0_spmd, body=%wide.region_0.0_spmd.sunk | while | flops 65539 | bytes 360590 | solution.py:599
  44.2 0.7 %collective-permute-start = (bf16[64,256]{1,0:T(8,128)(2,1)S(1)}, bf16[64,256]{1,0:T(8,128)(2,1)S(1)}, u32[]{:S(2)}, u32[]{:S(2)}) collective-permute-start(bf16[64,256]{1,0:T(8,128)(2,1)S(1)} %get-tuple-element.116), channel_id=1, source_target_pairs={{0,2},{2,0},{1,3},{3,1},{4,6},{6,4},{5,7},{7,5},{8,10},{10,8},{9,1... | collective-permute-start | bytes 98312 | tf_op jit(solution)/shard_map/while/body/ppermute | solution.py:592
  44.9 3.3 %collective-permute-done = bf16[64,256]{1,0:T(8,128)(2,1)S(1)} collective-permute-done((bf16[64,256]{1,0:T(8,128)(2,1)S(1)}, bf16[64,256]{1,0:T(8,128)(2,1)S(1)}, u32[]{:S(2)}, u32[]{:S(2)}) %collective-permute-start) | collective-permute-done | bytes 32800 | tf_op jit(solution)/shard_map/while/body/ppermute | solution.py:592
  48.2 0.1 collective-permute-start.1
  48.3 1.2 %collective-permute-done.1.theirs = bf16[64,256]{1,0:T(8,128)(2,1)S(1)} collective-permute-done((bf16[64,256]{1,0:T(8,128)(2,1)S(1)}, bf16[64,256]{1,0:T(8,128)(2,1)S(1)}, u32[]{:S(2)}, u32[]{:S(2)}) %collective-permute-start.1) | collective-permute-done | bytes 32800 | tf_op jit(solution)/shard_map/while/body/ppermute | solution.py:523
  49.5 0.7 %copy.30 = f32[128,256]{1,0:T(8,128)} copy(f32[128,256]{1,0:T(8,128)S(1)} %get-tuple-element.127.refs_4_) | data formatting | bytes 262144
  50.2 0.4 collective-permute-done.17.refs_1_
  50.6 0.0 collective-permute-done.18.refs_2_
  50.6 2.1 %collective-permute-done.19.refs_3_ = bf16[128,512]{1,0:T(8,128)(2,1)S(1)} collective-permute-done((bf16[128,512]{1,0:T(8,128)(2,1)S(1)}, bf16[128,512]{1,0:T(8,128)(2,1)S(1)}, u32[]{:S(2)}, u32[]{:S(2)}) %collective-permute-start.19) | collective-permute-done | bytes 131104 | tf_op jit(solution)/shard_map/ppermute | solution.py:526
  52.7 0.8 %turned_sum.1 = bf16[512,128]{1,0:T(8,128)(2,1)} custom-call(bf16[128,512]{1,0:T(8,128)(2,1)S(1)} %get-tuple-element.72.rest_0_.refs_0_, bf16[128,512]{1,0:T(8,128)(2,1)S(1)} %collective-permute-done.17.refs_1_, bf16[128,512]{1,0:T(8,128)(2,1)S(1)} %collective-permute-done.18.refs_2_, bf16[128,512]{1,0:T(8,128)(2,1)S(1)} %collective-permute-done.19.refs_3_, ...), custom_call_target="tpu_custom_call" | custom-call | flops 1 | bytes 1 | tf_op jit(solution)/shard_map/turned_sum/pallas_call | solution.py:504
  (7 shorter events, 0.1 us)
Async XLA Ops:
  0.6 12.7 %collective-permute-start.6 = (bf16[512,128]{1,0:T(8,128)(2,1)}, bf16[512,128]{1,0:T(8,128)(2,1)S(1)}, u32[]{:S(2)}, u32[]{:S(2)}) collective-permute-start(bf16[512,128]{1,0:T(8,128)(2,1)} %refs_0_.1), channel_id=1, source_target_pairs={{0,4},{4,0},{8,12},{12,8},{16,20},{20,16},{24,28},{28,24},{1,5},{5... | collective-permute-start | bytes 393224 | tf_op jit(solution)/shard_map/ppermute | solution.py:523
  1.1 12.9 %collective-permute-start.2 = (bf16[512,128]{1,0:T(8,128)(2,1)}, bf16[512,128]{1,0:T(8,128)(2,1)S(1)}, u32[]{:S(2)}, u32[]{:S(2)}) collective-permute-start(bf16[512,128]{1,0:T(8,128)(2,1)} %refs_0_.1), channel_id=1, source_target_pairs={{0,24},{4,28},{8,16},{12,20},{16,8},{20,12},{24,0},{28,4},{1,25},{... | collective-permute-start | bytes 393224 | tf_op jit(solution)/shard_map/ppermute | solution.py:526
  5.8 11.9 %collective-permute-start.3 = (bf16[512,128]{1,0:T(8,128)(2,1)}, bf16[512,128]{1,0:T(8,128)(2,1)S(1)}, u32[]{:S(2)}, u32[]{:S(2)}) collective-permute-start(bf16[512,128]{1,0:T(8,128)(2,1)} %refs_0_.1), channel_id=1, source_target_pairs={{0,16},{4,20},{8,24},{12,28},{16,0},{20,4},{24,8},{28,12},{1,17},{... | collective-permute-start | bytes 393224 | tf_op jit(solution)/shard_map/ppermute | solution.py:526
  5.8 11.9 %collective-permute-start.4 = (bf16[512,128]{1,0:T(8,128)(2,1)}, bf16[512,128]{1,0:T(8,128)(2,1)S(1)}, u32[]{:S(2)}, u32[]{:S(2)}) collective-permute-start(bf16[512,128]{1,0:T(8,128)(2,1)} %refs_0_.1), channel_id=1, source_target_pairs={{0,8},{4,12},{8,0},{12,4},{16,24},{20,28},{24,16},{28,20},{1,9},{5... | collective-permute-start | bytes 393224 | tf_op jit(solution)/shard_map/ppermute | solution.py:526
  6.5 11.2 %collective-permute-start.5 = (bf16[512,128]{1,0:T(8,128)(2,1)}, bf16[512,128]{1,0:T(8,128)(2,1)S(1)}, u32[]{:S(2)}, u32[]{:S(2)}) collective-permute-start(bf16[512,128]{1,0:T(8,128)(2,1)} %cot_own.1), channel_id=1, source_target_pairs={{0,1},{1,0},{2,3},{3,2},{4,5},{5,4},{6,7},{7,6},{8,9},{9,8},{10,11... | collective-permute-start | bytes 393224 | tf_op jit(solution)/shard_map/ppermute | solution.py:529
  8.8 4.6 %copy-start = (bf16[512,128]{1,0:T(8,128)(2,1)S(1)}, bf16[512,128]{1,0:T(8,128)(2,1)}, u32[]{:S(2)}) copy-start(bf16[512,128]{1,0:T(8,128)(2,1)} %refs_0_.1) | copy-start | bytes 393220
  17.7 1.6 %collective-permute-start.7 = (bf16[512,128]{1,0:T(8,128)(2,1)S(1)}, bf16[512,128]{1,0:T(8,128)(2,1)S(1)}, u32[]{:S(2)}, u32[]{:S(2)}) collective-permute-start(bf16[512,128]{1,0:T(8,128)(2,1)S(1)} %get-tuple-element.53.refs_0_), channel_id=1, source_target_pairs={{0,4},{4,0},{8,12},{12,8},{16,20},{20,16},{24,28},{28,24},{1,5},{5... | collective-permute-start | bytes 393224 | tf_op jit(solution)/shard_map/ppermute | solution.py:523
  17.8 1.6 %collective-permute-start.8 = (bf16[512,128]{1,0:T(8,128)(2,1)S(1)}, bf16[512,128]{1,0:T(8,128)(2,1)S(1)}, u32[]{:S(2)}, u32[]{:S(2)}) collective-permute-start(bf16[512,128]{1,0:T(8,128)(2,1)S(1)} %get-tuple-element.54.refs_1_), channel_id=1, source_target_pairs={{0,4},{4,0},{8,12},{12,8},{16,20},{20,16},{24,28},{28,24},{1,5},{5... | collective-permute-start | bytes 393224 | tf_op jit(solution)/shard_map/ppermute | solution.py:523
  18.3 1.3 %collective-permute-start.9 = (bf16[512,128]{1,0:T(8,128)(2,1)S(1)}, bf16[512,128]{1,0:T(8,128)(2,1)S(1)}, u32[]{:S(2)}, u32[]{:S(2)}) collective-permute-start(bf16[512,128]{1,0:T(8,128)(2,1)S(1)} %get-tuple-element.55.refs_2_), channel_id=1, source_target_pairs={{0,4},{4,0},{8,12},{12,8},{16,20},{20,16},{24,28},{28,24},{1,5},{5... | collective-permute-start | bytes 393224 | tf_op jit(solution)/shard_map/ppermute | solution.py:523
  18.4 11.7 %copy-start.1 = (bf16[256,256]{1,0:T(8,128)(2,1)S(1)}, bf16[256,256]{1,0:T(8,128)(2,1)}, u32[]{:S(2)}) copy-start(bf16[256,256]{1,0:T(8,128)(2,1)} %weights.1) | copy-start | bytes 393220
  18.4 11.7 %copy-start.2 = (bf16[512,128]{1,0:T(8,128)(2,1)S(1)}, bf16[512,128]{1,0:T(8,128)(2,1)}, u32[]{:S(2)}) copy-start(bf16[512,128]{1,0:T(8,128)(2,1)} %cot_own.1) | copy-start | bytes 393220
  20.6 7.3 %collective-permute-start.10 = (bf16[512,128]{1,0:T(8,128)(2,1)S(1)}, bf16[512,128]{1,0:T(8,128)(2,1)S(1)}, u32[]{:S(2)}, u32[]{:S(2)}) collective-permute-start(bf16[512,128]{1,0:T(8,128)(2,1)S(1)} %get-tuple-element.59), channel_id=1, source_target_pairs={{0,3},{1,2},{2,1},{3,0},{4,7},{5,6},{6,5},{7,4},{8,11},{9,10},{10,... | collective-permute-start | bytes 393224 | tf_op jit(solution)/shard_map/ppermute | solution.py:536
  23.2 6.9 %collective-permute-start.11 = (bf16[512,128]{1,0:T(8,128)(2,1)S(1)}, bf16[512,128]{1,0:T(8,128)(2,1)S(1)}, u32[]{:S(2)}, u32[]{:S(2)}) collective-permute-start(bf16[512,128]{1,0:T(8,128)(2,1)S(1)} %get-tuple-element.60.refs_2_), channel_id=1, source_target_pairs={{0,1},{1,0},{2,3},{3,2},{4,5},{5,4},{6,7},{7,6},{8,9},{9,8},{10,11... | collective-permute-start | bytes 393224 | tf_op jit(solution)/shard_map/ppermute | solution.py:536
  23.7 6.4 %collective-permute-start.12 = (bf16[512,128]{1,0:T(8,128)(2,1)S(1)}, bf16[512,128]{1,0:T(8,128)(2,1)S(1)}, u32[]{:S(2)}, u32[]{:S(2)}) collective-permute-start(bf16[512,128]{1,0:T(8,128)(2,1)S(1)} %get-tuple-element.59), channel_id=1, source_target_pairs={{0,2},{1,3},{2,0},{3,1},{4,6},{5,7},{6,4},{7,5},{8,10},{9,11},{10,... | collective-permute-start | bytes 393224 | tf_op jit(solution)/shard_map/ppermute | solution.py:536
  30.5 5.2 %collective-permute-start.13 = (bf16[128,512]{1,0:T(8,128)(2,1)S(1)}, bf16[128,512]{1,0:T(8,128)(2,1)S(1)}, u32[]{:S(2)}, u32[]{:S(2)}) collective-permute-start(bf16[128,512]{1,0:T(8,128)(2,1)S(1)} %get-tuple-element.61.piece), channel_id=1, source_target_pairs={{0,2},{2,0},{1,3},{3,1},{4,6},{6,4},{5,7},{7,5},{8,10},{10,8},{9,1... | collective-permute-start | bytes 393224 | tf_op jit(solution)/shard_map/ppermute | solution.py:572
  32.3 1.3 %collective-permute-start.14 = (bf16[64,256]{1,0:T(8,128)(2,1)S(1)}, bf16[64,256]{1,0:T(8,128)(2,1)S(1)}, u32[]{:S(2)}, u32[]{:S(2)}) collective-permute-start(bf16[64,256]{1,0:T(8,128)(2,1)S(1)} %get-tuple-element.71), channel_id=1, source_target_pairs={{0,4},{4,0},{8,12},{12,8},{16,20},{20,16},{24,28},{28,24},{1,5},{5... | collective-permute-start | bytes 98312 | tf_op jit(solution)/shard_map/ppermute | solution.py:523
  33.6 4.0 %collective-permute-start.15 = (bf16[64,256]{1,0:T(8,128)(2,1)S(1)}, bf16[64,256]{1,0:T(8,128)(2,1)S(1)}, u32[]{:S(2)}, u32[]{:S(2)}) collective-permute-start(bf16[64,256]{1,0:T(8,128)(2,1)S(1)} %add.14.a), channel_id=1, source_target_pairs={{0,8},{4,12},{8,0},{12,4},{16,24},{20,28},{24,16},{28,20},{1,9},{5... | collective-permute-start | bytes 98312 | tf_op jit(solution)/shard_map/ppermute | solution.py:526
  37.6 2.0 %collective-permute-start.16 = (bf16[4,128,512]{2,1,0:T(8,128)(2,1)S(1)}, bf16[4,128,512]{2,1,0:T(8,128)(2,1)S(1)}, u32[]{:S(2)}, u32[]{:S(2)}) collective-permute-start(bf16[4,128,512]{2,1,0:T(8,128)(2,1)S(1)} %hold.3), channel_id=1, source_target_pairs={{0,4},{4,0},{8,12},{12,8},{16,20},{20,16},{24,28},{28,24},{1,5},{5... | collective-permute-start | bytes 1572872 | tf_op jit(solution)/shard_map/ppermute | solution.py:523
  37.7 6.5 %collective-permute-start.20 = (bf16[64,256]{1,0:T(8,128)(2,1)S(1)}, bf16[64,256]{1,0:T(8,128)(2,1)S(1)}, u32[]{:S(2)}, u32[]{:S(2)}) collective-permute-start(bf16[64,256]{1,0:T(8,128)(2,1)S(1)} %add.15.refs_1_.a), channel_id=1, source_target_pairs={{0,16},{4,20},{8,24},{12,28},{16,0},{20,4},{24,8},{28,12},{1,17},{... | collective-permute-start | bytes 98312 | tf_op jit(solution)/shard_map/ppermute | solution.py:526
  39.7 10.8 %collective-permute-start.17 = (bf16[128,512]{1,0:T(8,128)(2,1)S(1)}, bf16[128,512]{1,0:T(8,128)(2,1)S(1)}, u32[]{:S(2)}, u32[]{:S(2)}) collective-permute-start(bf16[128,512]{1,0:T(8,128)(2,1)S(1)} %get-tuple-element.73), channel_id=1, source_target_pairs={{0,16},{4,20},{8,24},{12,28},{16,0},{20,4},{24,8},{28,12},{1,17},{... | collective-permute-start | bytes 393224 | tf_op jit(solution)/shard_map/ppermute | solution.py:526
  41.0 9.6 %collective-permute-start.18 = (bf16[128,512]{1,0:T(8,128)(2,1)S(1)}, bf16[128,512]{1,0:T(8,128)(2,1)S(1)}, u32[]{:S(2)}, u32[]{:S(2)}) collective-permute-start(bf16[128,512]{1,0:T(8,128)(2,1)S(1)} %get-tuple-element.74), channel_id=1, source_target_pairs={{0,8},{4,12},{8,0},{12,4},{16,24},{20,28},{24,16},{28,20},{1,9},{5... | collective-permute-start | bytes 393224 | tf_op jit(solution)/shard_map/ppermute | solution.py:526
  42.8 9.8 %collective-permute-start.19 = (bf16[128,512]{1,0:T(8,128)(2,1)S(1)}, bf16[128,512]{1,0:T(8,128)(2,1)S(1)}, u32[]{:S(2)}, u32[]{:S(2)}) collective-permute-start(bf16[128,512]{1,0:T(8,128)(2,1)S(1)} %get-tuple-element.75), channel_id=1, source_target_pairs={{0,24},{4,28},{8,16},{12,20},{16,8},{20,12},{24,0},{28,4},{1,25},{... | collective-permute-start | bytes 393224 | tf_op jit(solution)/shard_map/ppermute | solution.py:526
  44.2 4.0 %collective-permute-start = (bf16[64,256]{1,0:T(8,128)(2,1)S(1)}, bf16[64,256]{1,0:T(8,128)(2,1)S(1)}, u32[]{:S(2)}, u32[]{:S(2)}) collective-permute-start(bf16[64,256]{1,0:T(8,128)(2,1)S(1)} %get-tuple-element.116), channel_id=1, source_target_pairs={{0,2},{2,0},{1,3},{3,1},{4,6},{6,4},{5,7},{7,5},{8,10},{10,8},{9,1... | collective-permute-start | bytes 98312 | tf_op jit(solution)/shard_map/while/body/ppermute | solution.py:592
  48.2 1.3 %collective-permute-start.1 = (bf16[64,256]{1,0:T(8,128)(2,1)S(1)}, bf16[64,256]{1,0:T(8,128)(2,1)S(1)}, u32[]{:S(2)}, u32[]{:S(2)}) collective-permute-start(bf16[64,256]{1,0:T(8,128)(2,1)S(1)} %add_convert_fusion.2.mine), channel_id=1, source_target_pairs={{0,4},{4,0},{8,12},{12,8},{16,20},{20,16},{24,28},{28,24},{1,5},{5... | collective-permute-start | bytes 98312 | tf_op jit(solution)/shard_map/while/body/ppermute | solution.py:523

commit v8 on v7

--- a/solution.py
+++ b/solution.py
@@ -385,52 +385,26 @@
     )(weights, cot_own, cot_other, *other, *own)
 
 
-def weight_kernel(agg, g_own, g_other, keep, send, whole):
-    half, rows = agg.shape[1], keep.shape[0]
-    core, f = lax.axis_index("row") % 2, lax.axis_index("feat")
+def weight_kernel(agg, g_own, g_other, out):
+    half = agg.shape[1]
+    f = lax.axis_index("feat")
     turned = agg[...].astype(F32).T.astype(BF16)
     for columns, g in ((f * half, g_own), ((1 - f) * half, g_other)):
         columns = pl.ds(pl.multiple_of(columns, half), half)
-        whole[:, columns] = jnp.dot(turned, g[...], preferred_element_type=F32)
-        term = whole[:, columns].astype(BF16)
-        first, second = term[:rows], term[rows:]
-        keep[:, columns] = jnp.where(core == 0, first, second)
-        send[:, columns] = jnp.where(core == 0, second, first)
+        out[:, columns] = jnp.dot(turned, g[...], preferred_element_type=F32).astype(BF16)
 
 
 def weight_term(agg, g_own, g_other):
     half = agg.shape[1]
     return pl.pallas_call(
         weight_kernel,
-        out_shape=(jax.ShapeDtypeStruct((half // 2, 2 * half), BF16),) * 2
-        + (pltpu.VMEM((half, 2 * half), F32),),
+        out_shape=jax.ShapeDtypeStruct((half, 2 * half), BF16),
         in_specs=[vmem()] * 3,
-        out_specs=(vmem(),) * 3,
+        out_specs=vmem(),
         compiler_params=params(),
         cost_estimate=COST,
         name="weight_term",
     )(agg, g_own, g_other)
-
-
-def assemble_kernel(scale, mine, theirs, out):
-    rows = mine.shape[0]
-    core = lax.axis_index("row") % 2
-    own, other = mine[...].astype(F32) * scale, theirs[...].astype(F32) * scale
-    out[:rows, :] = jnp.where(core == 0, own, other)
-    out[rows:, :] = jnp.where(core == 0, other, own)
-
-
-def assemble(scale, mine, theirs):
-    rows, whole = mine.shape
-    return pl.pallas_call(
-        functools.partial(assemble_kernel, scale),
-        out_shape=jax.ShapeDtypeStruct((2 * rows, whole), F32),
-        in_specs=[vmem()] * 2,
-        out_specs=vmem(),
-        compiler_params=params(),
-        cost_estimate=COST,
-        name="assemble",
-    )(mine, theirs)
 
 
 def backward_stream_kernel(n_col, a, *refs):
@@ -494,22 +468,22 @@
 
 def turned_kernel(*refs):
     total = refs[0][...].astype(F32)
-    for part in refs[1:-2]:
+    for part in refs[1:-1]:
         total = total + part[...].astype(F32)
     refs[-1][...] = total.T.astype(BF16)
 
 
-def turned_sum(parts, after):
+def turned_sum(parts):
     feats, nodes = parts[0].shape
     return pl.pallas_call(
         turned_kernel,
         out_shape=jax.ShapeDtypeStruct((nodes, feats), BF16),
-        in_specs=[vmem()] * len(parts) + [pl.BlockSpec(memory_space=pl.ANY)],
+        in_specs=[vmem()] * len(parts),
         out_specs=vmem(),
         compiler_params=params(),
         cost_estimate=COST,
         name="turned_sum",
-    )(*parts, after)
+    )(*parts)
 
 
 def shards(features, tile_rows, tile_cols, tile_count, tile_values, weights, cotangent):
@@ -519,6 +493,7 @@
     nodes, half = features.shape
     blocks = nodes // tile
     node_total = nodes * n_row * n_col
+
     def sibling(v):
         return lax.ppermute(v, "row", [(i, i ^ 1) for i in range(n_row)])
 
@@ -542,9 +517,8 @@
     if 2 * n_z * n_col * (blocks * tile) ** 2 <= 8 * MIB:
         dense = densify(*cell)
         totals = forward(dense, [0, 1], [features, sibling(features)], (), False)
-        far = range(n_z - 1, 0, -1)
-        *same, cot_other = hold([same[s] for s in far] + [cot_other], totals[0])
-        same.reverse()
+        *held, cot_other = hold([same[-1]] + same[1:-1] + [cot_other], totals[0])
+        same = held[1:] + held[:1]
         cross = [sibling(v) for v in same]
         totals = forward(dense, [2 * s for s in range(1, n_z)], same, totals, False)
         parts = forward(dense, [2 * s + 1 for s in range(1, n_z)], cross, totals, True)
@@ -572,8 +546,7 @@
         lax.ppermute(spread, "col", [(i, (i + t) % n_col) for i in range(n_col)])
         for t in range(1, n_col)
     ]
-    keep, send, weight_grad = weight_term(*rest)
-    term = add(keep, sibling(send))
+    term = weight_term(*rest)
     even, odd, activated = back_of(pieces, hidden)
     term = add(term, along_z(term, 1), odd)
     (odd,) = hold([odd], term)
@@ -582,22 +555,19 @@
     if n_z > 2:
         term = add(term, along_z(term, 2), sums[0])
     order = sorted(range(1, n_z), key=lambda s: (s != n_z // 2, s))
-
-    def finish(_, state):
-        v = state[0]
+    back = turned_sum([sums[0]] + [along_z(sums[s], s) for s in order])
+
+    def finish(_, v):
         for step in range(2, n_z.bit_length() - 1):
             v = add(v, along_z(v, 1 << step))
-        total = v.astype(F32)
-        for t in range(1, n_col):
-            total = total + lax.ppermute(
-                v, "col", [(i, (i + t) % n_col) for i in range(n_col)]
-            ).astype(F32)
-        v = total.astype(BF16)
-        return v, assemble(node_total ** (-0.5), v, sibling(v))
+        for step in range(n_col.bit_length() - 1):
+            pairs = [(i, i ^ (1 << step)) for i in range(n_col)]
+            v = add(v, lax.ppermute(v, "col", pairs))
+        return add(v, sibling(v))
 
     once = lax.optimization_barrier(jnp.int32(1))
-    _, weight_grad = lax.fori_loop(0, once, finish, (term, weight_grad))
-    back = turned_sum([sums[0]] + [along_z(sums[s], s) for s in order], weight_grad)
+    whole = lax.fori_loop(0, once, finish, term)
+    weight_grad = whole.astype(F32) * node_total ** (-0.5)
     return (activated, back, weight_grad)
 
 

time: 53.6 us -> 53.3 us (level)
  waiting for transfers between devices: 20.4 us -> 19.2 us
  other arithmetic: 0.01 us -> 0.67 us
  local copies, waits for them, and re-layouts: 0.67 us -> 0.01 us
  starting transfers between devices: 19.9 us -> 20.5 us
    ppermute x1, waiting for transfers between devices: 0.66 us -> 1.97 us  [shards(): lax.ppermute(spread, 'col', [(i, (i + t) % n_col) for i in range(n_col)])]
    ppermute x8, waiting for transfers between devices: 7.3 us -> 6.31 us  [along_z(): return lax.ppermute(v, 'row', [(i, i ^ 2 * s) for i in range(n_row)])]
    ppermute x1, starting transfers between devices: 0.67 us -> 1.61 us  [finish(): v = add(v, lax.ppermute(v, 'col', pairs))]
    ppermute x7 -> x6, waiting for transfers between devices: 3.26 us -> 2.33 us  [sibling(): return lax.ppermute(v, 'row', [(i, i ^ 1) for i in range(n_row)])]
    mul x0 -> x1, other arithmetic: none -> 0.67 us  [shards(): weight_grad = whole.astype(F32) * node_total ** (-0.5)]
    unnamed x7 -> x6, local copies, waits for them, and re-layouts: 0.67 us -> 0.01 us
    ppermute x1, waiting for transfers between devices: 3.31 us -> 2.72 us  [finish(): v = add(v, lax.ppermute(v, 'col', pairs))]
    ppermute x7 -> x6, starting transfers between devices: 1.37 us -> 1.23 us  [sibling(): return lax.ppermute(v, 'row', [(i, i ^ 1) for i in range(n_row)])]
  transfers between devices with their start and end apart: 21 -> 20, of which waited for: 12 -> 10; matrix products, arithmetic and copies ran while one was open for 1% -> 1% of each run, Pallas kernels for 16% -> 17%
where the time goes in v8:
time: 53.3 us; the launch traced here: 52.9 us
  starting transfers between devices  20.5 us (38%)
  waiting for transfers between devices  19.2 us (36%)
  Pallas kernels  11 us (21%)
  between operations  1.45 us (3%)
  other arithmetic  0.67 us (1%)
    ppermute x8, starting transfers between devices, along_z(): return lax.ppermute(v, 'row', [(i, i ^ 2 * s) for i in range(n_row)])  10.9 us
    ppermute x8, waiting for transfers between devices, along_z(): return lax.ppermute(v, 'row', [(i, i ^ 2 * s) for i in range(n_row)])  6.31 us
    ppermute x3, waiting for transfers between devices, to_group(): return lax.ppermute(v, ('col', 'feat'), pairs)  5.87 us
    pallas_call x1, Pallas kernels, densify(): pl.pallas_call(functools.partial(densify_kernel, (n_z, n_col, blocks), gr...  4.57 us
    ppermute x3, starting transfers between devices, to_group(): return lax.ppermute(v, ('col', 'feat'), pairs)  3.55 us
    ppermute x1, waiting for transfers between devices, finish(): v = add(v, lax.ppermute(v, 'col', pairs))  2.72 us
    pallas_call x3, Pallas kernels, forward(): pl.pallas_call(functools.partial(forward_kernel, places, last), out_shape...  2.66 us
    ppermute x6, waiting for transfers between devices, sibling(): return lax.ppermute(v, 'row', [(i, i ^ 1) for i in range(n_row)])  2.33 us
  transfers between devices with their start and end apart: 20, of which 10 were waited for; matrix products, arithmetic and copies ran while one was open for 1% of the time, Pallas kernels for 17%

profile of v8, /device:TPU:0, one launch (start us, length us, event | category | flops | bytes accessed | tf_op | source)
XLA Modules:
  0.0 52.9 jit_solution(15875877826729720583)
XLA Ops:
  0.6 0.5 collective-permute-start.6
  1.1 4.7 %collective-permute-start.2 = (bf16[512,128]{1,0:T(8,128)(2,1)}, bf16[512,128]{1,0:T(8,128)(2,1)S(1)}, u32[]{:S(2)}, u32[]{:S(2)}) collective-permute-start(bf16[512,128]{1,0:T(8,128)(2,1)} %refs_0_.1), channel_id=1, source_target_pairs={{0,24},{4,28},{8,16},{12,20},{16,8},{20,12},{24,0},{28,4},{1,25},{... | collective-permute-start | bytes 393224 | tf_op jit(solution)/shard_map/ppermute | solution.py:501
  5.8 0.0 collective-permute-start.3
  5.8 0.7 %collective-permute-start.4 = (bf16[512,128]{1,0:T(8,128)(2,1)}, bf16[512,128]{1,0:T(8,128)(2,1)S(1)}, u32[]{:S(2)}, u32[]{:S(2)}) collective-permute-start(bf16[512,128]{1,0:T(8,128)(2,1)} %refs_0_.1), channel_id=1, source_target_pairs={{0,16},{4,20},{8,24},{12,28},{16,0},{20,4},{24,8},{28,12},{1,17},{... | collective-permute-start | bytes 393224 | tf_op jit(solution)/shard_map/ppermute | solution.py:501
  6.5 1.6 %collective-permute-start.5 = (bf16[512,128]{1,0:T(8,128)(2,1)}, bf16[512,128]{1,0:T(8,128)(2,1)S(1)}, u32[]{:S(2)}, u32[]{:S(2)}) collective-permute-start(bf16[512,128]{1,0:T(8,128)(2,1)} %cot_own.1), channel_id=1, source_target_pairs={{0,1},{1,0},{2,3},{3,2},{4,5},{5,4},{6,7},{7,6},{8,9},{9,8},{10,11... | collective-permute-start | bytes 393224 | tf_op jit(solution)/shard_map/ppermute | solution.py:504
  8.8 0.0 copy-start
  8.8 4.6 %densify.1.dense = bf16[8,2,512,512]{3,2,1,0:T(8,128)(2,1)S(1)} custom-call(s32[1,1,256]{2,1,0:T(1,128)} %rows.1, s32[1,1,256]{2,1,0:T(1,128)} %cols.1, s32[1,1]{1,0:T(1,128)S(6)} %copy.27.count, bf16[256,128,128]{2,1,0:T(8,128)(2,1)} %bitcast.1), custom_call_target="tpu_custom_call" | custom-call | flops 1 | bytes 1 | tf_op jit(solution)/shard_map/densify/pallas_call | solution.py:93
  13.3 0.0 collective-permute-done.6.refs_1_
  13.4 0.0 copy-done
  13.4 0.7 %forward.3 = (f32[512,128]{1,0:T(8,128)S(1)}, f32[512,128]{1,0:T(8,128)S(1)}) custom-call(bf16[8,2,512,512]{3,2,1,0:T(8,128)(2,1)S(1)} %densify.1.dense, bf16[512,128]{1,0:T(8,128)(2,1)S(1)} %copy-done, bf16[512,128]{1,0:T(8,128)(2,1)S(1)} %collective-permute-done.6.refs_1_), custom_call_target="tpu_custom_call" | custom-call | flops 1 | bytes 1 | tf_op jit(solution)/shard_map/forward/pallas_call | solution.py:150
  14.1 0.0 collective-permute-done.2.refs_0_
  14.1 0.0 collective-permute-done.3.refs_1_
  14.1 3.6 %collective-permute-done.4.refs_2_ = bf16[512,128]{1,0:T(8,128)(2,1)S(1)} collective-permute-done((bf16[512,128]{1,0:T(8,128)(2,1)}, bf16[512,128]{1,0:T(8,128)(2,1)S(1)}, u32[]{:S(2)}, u32[]{:S(2)}) %collective-permute-start.4) | collective-permute-done | bytes 131104 | tf_op jit(solution)/shard_map/ppermute | solution.py:501
  17.7 0.0 collective-permute-done.5.refs_3_
  17.7 0.0 collective-permute-start.7
  17.7 0.5 collective-permute-start.8
  18.2 0.1 collective-permute-start.9
  18.3 0.0 copy-start.1
  18.3 0.0 copy-start.2
  18.3 1.0 %forward.4 = (f32[512,128]{1,0:T(8,128)S(1)}, f32[512,128]{1,0:T(8,128)S(1)}) custom-call(bf16[8,2,512,512]{3,2,1,0:T(8,128)(2,1)S(1)} %densify.1.dense, bf16[512,128]{1,0:T(8,128)(2,1)S(1)} %get-tuple-element.46.refs_0_, bf16[512,128]{1,0:T(8,128)(2,1)S(1)} %get-tuple-element.47.refs_1_, bf16[512,128]{1,0:T(8,128)(2,1)S(1)} %get-tuple-element.48.refs_2_, ...), custom_call_target="tpu_custom_call" | custom-call | flops 1 | bytes 1 | tf_op jit(solution)/shard_map/forward/pallas_call | solution.py:150
  19.3 0.0 collective-permute-done.7.refs_0_
  19.3 0.0 collective-permute-done.8.refs_1_
  19.3 0.3 collective-permute-done.9.refs_2_
  19.6 1.0 %forward.5 = (bf16[512,128]{1,0:T(8,128)(2,1)S(1)}, bf16[512,128]{1,0:T(8,128)(2,1)S(1)}) custom-call(bf16[8,2,512,512]{3,2,1,0:T(8,128)(2,1)S(1)} %densify.1.dense, bf16[512,128]{1,0:T(8,128)(2,1)S(1)} %collective-permute-done.7.refs_0_, bf16[512,128]{1,0:T(8,128)(2,1)S(1)} %collective-permute-done.8.refs_1_, ...), custom_call_target="tpu_custom_call" | custom-call | flops 1 | bytes 1 | tf_op jit(solution)/shard_map/forward/pallas_call | solution.py:150
  20.6 2.5 %collective-permute-start.10 = (bf16[512,128]{1,0:T(8,128)(2,1)S(1)}, bf16[512,128]{1,0:T(8,128)(2,1)S(1)}, u32[]{:S(2)}, u32[]{:S(2)}) collective-permute-start(bf16[512,128]{1,0:T(8,128)(2,1)S(1)} %get-tuple-element.52), channel_id=1, source_target_pairs={{0,3},{1,2},{2,1},{3,0},{4,7},{5,6},{6,5},{7,4},{8,11},{9,10},{10,... | collective-permute-start | bytes 393224 | tf_op jit(solution)/shard_map/ppermute | solution.py:511
  23.1 0.5 %collective-permute-start.11 = (bf16[512,128]{1,0:T(8,128)(2,1)S(1)}, bf16[512,128]{1,0:T(8,128)(2,1)S(1)}, u32[]{:S(2)}, u32[]{:S(2)}) collective-permute-start(bf16[512,128]{1,0:T(8,128)(2,1)S(1)} %get-tuple-element.53.refs_2_), channel_id=1, source_target_pairs={{0,1},{1,0},{2,3},{3,2},{4,5},{5,4},{6,7},{7,6},{8,9},{9,8},{10,11... | collective-permute-start | bytes 393224 | tf_op jit(solution)/shard_map/ppermute | solution.py:511
  23.6 0.5 collective-permute-start.12
  24.1 3.7 %collective-permute-done.10.refs_0_ = bf16[512,128]{1,0:T(8,128)(2,1)S(1)} collective-permute-done((bf16[512,128]{1,0:T(8,128)(2,1)S(1)}, bf16[512,128]{1,0:T(8,128)(2,1)S(1)}, u32[]{:S(2)}, u32[]{:S(2)}) %collective-permute-start.10) | collective-permute-done | bytes 131104 | tf_op jit(solution)/shard_map/ppermute | solution.py:511
  27.9 2.1 %collective-permute-done.11.refs_1_ = bf16[512,128]{1,0:T(8,128)(2,1)S(1)} collective-permute-done((bf16[512,128]{1,0:T(8,128)(2,1)S(1)}, bf16[512,128]{1,0:T(8,128)(2,1)S(1)}, u32[]{:S(2)}, u32[]{:S(2)}) %collective-permute-start.11) | collective-permute-done | bytes 131104 | tf_op jit(solution)/shard_map/ppermute | solution.py:511
  30.0 0.0 collective-permute-done.12.refs_3_
  30.0 0.0 copy-done.1
  30.0 0.0 copy-done.2
  30.0 0.5 middle.1
  30.5 1.5 %collective-permute-start.13 = (bf16[128,512]{1,0:T(8,128)(2,1)S(1)}, bf16[128,512]{1,0:T(8,128)(2,1)S(1)}, u32[]{:S(2)}, u32[]{:S(2)}) collective-permute-start(bf16[128,512]{1,0:T(8,128)(2,1)S(1)} %get-tuple-element.54.piece), channel_id=1, source_target_pairs={{0,2},{2,0},{1,3},{3,1},{4,6},{6,4},{5,7},{7,5},{8,10},{10,8},{9,1... | collective-permute-start | bytes 393224 | tf_op jit(solution)/shard_map/ppermute | solution.py:546
  32.0 0.3 weight_term.1.a
  32.3 0.1 collective-permute-start.14
  32.3 1.4 %backward_own.1 = (f32[8,128,512]{2,1,0:T(8,128)S(1)}, bf16[512,128]{1,0:T(8,128)(2,1)}) custom-call(bf16[8,2,512,512]{3,2,1,0:T(8,128)(2,1)S(1)} %densify.1.dense, bf16[128,512]{1,0:T(8,128)(2,1)S(1)} %get-tuple-element.54.piece, f32[512,128]{1,0:T(8,128)S(1)} %get-tuple-element.55.hidden), custom_call_target="tpu_custom_call" | custom-call | flops 1 | bytes 1 | tf_op jit(solution)/shard_map/backward_own/pallas_call | solution.py:173
  33.7 2.0 %collective-permute-done.13.refs_0_ = bf16[128,512]{1,0:T(8,128)(2,1)S(1)} collective-permute-done((bf16[128,512]{1,0:T(8,128)(2,1)S(1)}, bf16[128,512]{1,0:T(8,128)(2,1)S(1)}, u32[]{:S(2)}, u32[]{:S(2)}) %collective-permute-start.13) | collective-permute-done | bytes 131104 | tf_op jit(solution)/shard_map/ppermute | solution.py:546
  35.7 0.7 %backward.1 = (bf16[4,128,512]{2,1,0:T(8,128)(2,1)S(1)}, bf16[4,128,512]{2,1,0:T(8,128)(2,1)S(1)}) custom-call(bf16[8,2,512,512]{3,2,1,0:T(8,128)(2,1)S(1)} %densify.1.dense, f32[8,128,512]{2,1,0:T(8,128)S(1)} %get-tuple-element.57.own, bf16[128,512]{1,0:T(8,128)(2,1)S(1)} %collective-permute-done.13.refs_0_), custom_call_target="tpu_custom_call" | custom-call | flops 1 | bytes 1 | tf_op jit(solution)/shard_map/backward/pallas_call | solution.py:199
  36.4 0.2 collective-permute-done.14.b
  36.6 0.1 collective-permute-start.15
  36.7 1.1 %collective-permute-start.19 = (bf16[128,256]{1,0:T(8,128)(2,1)S(1)}, bf16[128,256]{1,0:T(8,128)(2,1)S(1)}, u32[]{:S(2)}, u32[]{:S(2)}) collective-permute-start(bf16[128,256]{1,0:T(8,128)(2,1)S(1)} %add.9.refs_1_.a), channel_id=1, source_target_pairs={{0,16},{4,20},{8,24},{12,28},{16,0},{20,4},{24,8},{28,12},{1,17},{... | collective-permute-start | bytes 196616 | tf_op jit(solution)/shard_map/ppermute | solution.py:501
  37.8 0.8 %collective-permute-done.15.arrived = bf16[4,128,512]{2,1,0:T(8,128)(2,1)S(1)} collective-permute-done((bf16[4,128,512]{2,1,0:T(8,128)(2,1)S(1)}, bf16[4,128,512]{2,1,0:T(8,128)(2,1)S(1)}, u32[]{:S(2)}, u32[]{:S(2)}) %collective-permute-start.15) | collective-permute-done | bytes 524320 | tf_op jit(solution)/shard_map/ppermute | solution.py:498
  38.6 0.1 pair_sums.1
  38.7 1.2 %collective-permute-start.16 = (bf16[128,512]{1,0:T(8,128)(2,1)S(1)}, bf16[128,512]{1,0:T(8,128)(2,1)S(1)}, u32[]{:S(2)}, u32[]{:S(2)}) collective-permute-start(bf16[128,512]{1,0:T(8,128)(2,1)S(1)} %get-tuple-element.64), channel_id=1, source_target_pairs={{0,16},{4,20},{8,24},{12,28},{16,0},{20,4},{24,8},{28,12},{1,17},{... | collective-permute-start | bytes 393224 | tf_op jit(solution)/shard_map/ppermute | solution.py:501
  39.9 1.9 %collective-permute-start.17 = (bf16[128,512]{1,0:T(8,128)(2,1)S(1)}, bf16[128,512]{1,0:T(8,128)(2,1)S(1)}, u32[]{:S(2)}, u32[]{:S(2)}) collective-permute-start(bf16[128,512]{1,0:T(8,128)(2,1)S(1)} %get-tuple-element.65), channel_id=1, source_target_pairs={{0,8},{4,12},{8,0},{12,4},{16,24},{20,28},{24,16},{28,20},{1,9},{5... | collective-permute-start | bytes 393224 | tf_op jit(solution)/shard_map/ppermute | solution.py:501
  41.8 1.3 %collective-permute-start.18 = (bf16[128,512]{1,0:T(8,128)(2,1)S(1)}, bf16[128,512]{1,0:T(8,128)(2,1)S(1)}, u32[]{:S(2)}, u32[]{:S(2)}) collective-permute-start(bf16[128,512]{1,0:T(8,128)(2,1)S(1)} %get-tuple-element.66), channel_id=1, source_target_pairs={{0,24},{4,28},{8,16},{12,20},{16,8},{20,12},{24,0},{28,4},{1,25},{... | collective-permute-start | bytes 393224 | tf_op jit(solution)/shard_map/ppermute | solution.py:501
  43.2 2.5 %collective-permute-done.19.b = bf16[128,256]{1,0:T(8,128)(2,1)S(1)} collective-permute-done((bf16[128,256]{1,0:T(8,128)(2,1)S(1)}, bf16[128,256]{1,0:T(8,128)(2,1)S(1)}, u32[]{:S(2)}, u32[]{:S(2)}) %collective-permute-start.19) | collective-permute-done | bytes 65568 | tf_op jit(solution)/shard_map/ppermute | solution.py:501
  45.7 5.7 %while.10 = (s32[]{:T(128)}, bf16[128,256]{1,0:T(8,128)(2,1)S(1)}, s32[]{:T(128)}, s32[]{:T(128)}) while((s32[]{:T(128)}, bf16[128,256]{1,0:T(8,128)(2,1)S(1)}, s32[]{:T(128)}, s32[]{:T(128)}) %tuple.22), condition=%wide.region_1.0_spmd, body=%wide.region_0.0_spmd.sunk | while | flops 4 | bytes 524423 | solution.py:569
  45.7 1.6 %collective-permute-start = (bf16[128,256]{1,0:T(8,128)(2,1)S(1)}, bf16[128,256]{1,0:T(8,128)(2,1)S(1)}, u32[]{:S(2)}, u32[]{:S(2)}) collective-permute-start(bf16[128,256]{1,0:T(8,128)(2,1)S(1)} %get-tuple-element.99.a), channel_id=1, source_target_pairs={{0,2},{2,0},{1,3},{3,1},{4,6},{6,4},{5,7},{7,5},{8,10},{10,8},{9,1... | collective-permute-start | bytes 196616 | tf_op jit(solution)/shard_map/while/body/ppermute | solution.py:565
  47.3 2.7 %collective-permute-done.b = bf16[128,256]{1,0:T(8,128)(2,1)S(1)} collective-permute-done((bf16[128,256]{1,0:T(8,128)(2,1)S(1)}, bf16[128,256]{1,0:T(8,128)(2,1)S(1)}, u32[]{:S(2)}, u32[]{:S(2)}) %collective-permute-start) | collective-permute-done | bytes 65568 | tf_op jit(solution)/shard_map/while/body/ppermute | solution.py:565
  50.0 0.1 collective-permute-start.1
  50.1 1.2 %collective-permute-done.1.b = bf16[128,256]{1,0:T(8,128)(2,1)S(1)} collective-permute-done((bf16[128,256]{1,0:T(8,128)(2,1)S(1)}, bf16[128,256]{1,0:T(8,128)(2,1)S(1)}, u32[]{:S(2)}, u32[]{:S(2)}) %collective-permute-start.1) | collective-permute-done | bytes 65568 | tf_op jit(solution)/shard_map/while/body/ppermute | solution.py:498
  51.4 0.7 %convert_multiply_fusion = f32[128,256]{1,0:T(8,128)} fusion(bf16[128,256]{1,0:T(8,128)(2,1)S(1)} %get-tuple-element.67), kind=kLoop, calls=%fused_computation | loop fusion | flops 65536 | bytes 196608 | tf_op jit(solution)/shard_map/mul | solution.py:570
  52.0 0.0 collective-permute-done.16.refs_1_
  52.1 0.0 collective-permute-done.17.refs_2_
  52.1 0.0 collective-permute-done.18.refs_3_
  52.1 0.8 %turned_sum.1 = bf16[512,128]{1,0:T(8,128)(2,1)} custom-call(bf16[128,512]{1,0:T(8,128)(2,1)S(1)} %get-tuple-element.63.refs_0_.rest_0_, bf16[128,512]{1,0:T(8,128)(2,1)S(1)} %collective-permute-done.16.refs_1_, bf16[128,512]{1,0:T(8,128)(2,1)S(1)} %collective-permute-done.17.refs_2_, bf16[128,512]{1,0:T(8,128)(2,1)S(1)} %collective-permute-done.18.refs_3_), custom_call_target="tpu_custom_call" | custom-call | flops 1 | bytes 1 | tf_op jit(solution)/shard_map/turned_sum/pallas_call | solution.py:478
  (6 shorter events, 0.1 us)
Async XLA Ops:
  0.6 12.7 %collective-permute-start.6 = (bf16[512,128]{1,0:T(8,128)(2,1)}, bf16[512,128]{1,0:T(8,128)(2,1)S(1)}, u32[]{:S(2)}, u32[]{:S(2)}) collective-permute-start(bf16[512,128]{1,0:T(8,128)(2,1)} %refs_0_.1), channel_id=1, source_target_pairs={{0,4},{4,0},{8,12},{12,8},{16,20},{20,16},{24,28},{28,24},{1,5},{5... | collective-permute-start | bytes 393224 | tf_op jit(solution)/shard_map/ppermute | solution.py:498
  1.1 12.9 %collective-permute-start.2 = (bf16[512,128]{1,0:T(8,128)(2,1)}, bf16[512,128]{1,0:T(8,128)(2,1)S(1)}, u32[]{:S(2)}, u32[]{:S(2)}) collective-permute-start(bf16[512,128]{1,0:T(8,128)(2,1)} %refs_0_.1), channel_id=1, source_target_pairs={{0,24},{4,28},{8,16},{12,20},{16,8},{20,12},{24,0},{28,4},{1,25},{... | collective-permute-start | bytes 393224 | tf_op jit(solution)/shard_map/ppermute | solution.py:501
  5.8 8.3 %collective-permute-start.3 = (bf16[512,128]{1,0:T(8,128)(2,1)}, bf16[512,128]{1,0:T(8,128)(2,1)S(1)}, u32[]{:S(2)}, u32[]{:S(2)}) collective-permute-start(bf16[512,128]{1,0:T(8,128)(2,1)} %refs_0_.1), channel_id=1, source_target_pairs={{0,8},{4,12},{8,0},{12,4},{16,24},{20,28},{24,16},{28,20},{1,9},{5... | collective-permute-start | bytes 393224 | tf_op jit(solution)/shard_map/ppermute | solution.py:501
  5.8 11.9 %collective-permute-start.4 = (bf16[512,128]{1,0:T(8,128)(2,1)}, bf16[512,128]{1,0:T(8,128)(2,1)S(1)}, u32[]{:S(2)}, u32[]{:S(2)}) collective-permute-start(bf16[512,128]{1,0:T(8,128)(2,1)} %refs_0_.1), channel_id=1, source_target_pairs={{0,16},{4,20},{8,24},{12,28},{16,0},{20,4},{24,8},{28,12},{1,17},{... | collective-permute-start | bytes 393224 | tf_op jit(solution)/shard_map/ppermute | solution.py:501
  6.5 11.2 %collective-permute-start.5 = (bf16[512,128]{1,0:T(8,128)(2,1)}, bf16[512,128]{1,0:T(8,128)(2,1)S(1)}, u32[]{:S(2)}, u32[]{:S(2)}) collective-permute-start(bf16[512,128]{1,0:T(8,128)(2,1)} %cot_own.1), channel_id=1, source_target_pairs={{0,1},{1,0},{2,3},{3,2},{4,5},{5,4},{6,7},{7,6},{8,9},{9,8},{10,11... | collective-permute-start | bytes 393224 | tf_op jit(solution)/shard_map/ppermute | solution.py:504
  8.8 4.6 %copy-start = (bf16[512,128]{1,0:T(8,128)(2,1)S(1)}, bf16[512,128]{1,0:T(8,128)(2,1)}, u32[]{:S(2)}) copy-start(bf16[512,128]{1,0:T(8,128)(2,1)} %refs_0_.1) | copy-start | bytes 393220
  17.7 1.6 %collective-permute-start.7 = (bf16[512,128]{1,0:T(8,128)(2,1)S(1)}, bf16[512,128]{1,0:T(8,128)(2,1)S(1)}, u32[]{:S(2)}, u32[]{:S(2)}) collective-permute-start(bf16[512,128]{1,0:T(8,128)(2,1)S(1)} %get-tuple-element.46.refs_0_), channel_id=1, source_target_pairs={{0,4},{4,0},{8,12},{12,8},{16,20},{20,16},{24,28},{28,24},{1,5},{5... | collective-permute-start | bytes 393224 | tf_op jit(solution)/shard_map/ppermute | solution.py:498
  17.7 1.6 %collective-permute-start.8 = (bf16[512,128]{1,0:T(8,128)(2,1)S(1)}, bf16[512,128]{1,0:T(8,128)(2,1)S(1)}, u32[]{:S(2)}, u32[]{:S(2)}) collective-permute-start(bf16[512,128]{1,0:T(8,128)(2,1)S(1)} %get-tuple-element.47.refs_1_), channel_id=1, source_target_pairs={{0,4},{4,0},{8,12},{12,8},{16,20},{20,16},{24,28},{28,24},{1,5},{5... | collective-permute-start | bytes 393224 | tf_op jit(solution)/shard_map/ppermute | solution.py:498
  18.2 1.3 %collective-permute-start.9 = (bf16[512,128]{1,0:T(8,128)(2,1)S(1)}, bf16[512,128]{1,0:T(8,128)(2,1)S(1)}, u32[]{:S(2)}, u32[]{:S(2)}) collective-permute-start(bf16[512,128]{1,0:T(8,128)(2,1)S(1)} %get-tuple-element.48.refs_2_), channel_id=1, source_target_pairs={{0,4},{4,0},{8,12},{12,8},{16,20},{20,16},{24,28},{28,24},{1,5},{5... | collective-permute-start | bytes 393224 | tf_op jit(solution)/shard_map/ppermute | solution.py:498
  18.3 11.7 %copy-start.1 = (bf16[256,256]{1,0:T(8,128)(2,1)S(1)}, bf16[256,256]{1,0:T(8,128)(2,1)}, u32[]{:S(2)}) copy-start(bf16[256,256]{1,0:T(8,128)(2,1)} %weights.1) | copy-start | bytes 393220
  18.3 11.7 %copy-start.2 = (bf16[512,128]{1,0:T(8,128)(2,1)S(1)}, bf16[512,128]{1,0:T(8,128)(2,1)}, u32[]{:S(2)}) copy-start(bf16[512,128]{1,0:T(8,128)(2,1)} %cot_own.1) | copy-start | bytes 393220
  20.6 7.3 %collective-permute-start.10 = (bf16[512,128]{1,0:T(8,128)(2,1)S(1)}, bf16[512,128]{1,0:T(8,128)(2,1)S(1)}, u32[]{:S(2)}, u32[]{:S(2)}) collective-permute-start(bf16[512,128]{1,0:T(8,128)(2,1)S(1)} %get-tuple-element.52), channel_id=1, source_target_pairs={{0,3},{1,2},{2,1},{3,0},{4,7},{5,6},{6,5},{7,4},{8,11},{9,10},{10,... | collective-permute-start | bytes 393224 | tf_op jit(solution)/shard_map/ppermute | solution.py:511
  23.1 6.9 %collective-permute-start.11 = (bf16[512,128]{1,0:T(8,128)(2,1)S(1)}, bf16[512,128]{1,0:T(8,128)(2,1)S(1)}, u32[]{:S(2)}, u32[]{:S(2)}) collective-permute-start(bf16[512,128]{1,0:T(8,128)(2,1)S(1)} %get-tuple-element.53.refs_2_), channel_id=1, source_target_pairs={{0,1},{1,0},{2,3},{3,2},{4,5},{5,4},{6,7},{7,6},{8,9},{9,8},{10,11... | collective-permute-start | bytes 393224 | tf_op jit(solution)/shard_map/ppermute | solution.py:511
  23.6 6.4 %collective-permute-start.12 = (bf16[512,128]{1,0:T(8,128)(2,1)S(1)}, bf16[512,128]{1,0:T(8,128)(2,1)S(1)}, u32[]{:S(2)}, u32[]{:S(2)}) collective-permute-start(bf16[512,128]{1,0:T(8,128)(2,1)S(1)} %get-tuple-element.52), channel_id=1, source_target_pairs={{0,2},{1,3},{2,0},{3,1},{4,6},{5,7},{6,4},{7,5},{8,10},{9,11},{10,... | collective-permute-start | bytes 393224 | tf_op jit(solution)/shard_map/ppermute | solution.py:511
  30.5 5.2 %collective-permute-start.13 = (bf16[128,512]{1,0:T(8,128)(2,1)S(1)}, bf16[128,512]{1,0:T(8,128)(2,1)S(1)}, u32[]{:S(2)}, u32[]{:S(2)}) collective-permute-start(bf16[128,512]{1,0:T(8,128)(2,1)S(1)} %get-tuple-element.54.piece), channel_id=1, source_target_pairs={{0,2},{2,0},{1,3},{3,1},{4,6},{6,4},{5,7},{7,5},{8,10},{10,8},{9,1... | collective-permute-start | bytes 393224 | tf_op jit(solution)/shard_map/ppermute | solution.py:546
  32.3 4.3 %collective-permute-start.14 = (bf16[128,256]{1,0:T(8,128)(2,1)S(1)}, bf16[128,256]{1,0:T(8,128)(2,1)S(1)}, u32[]{:S(2)}, u32[]{:S(2)}) collective-permute-start(bf16[128,256]{1,0:T(8,128)(2,1)S(1)} %weight_term.1.a), channel_id=1, source_target_pairs={{0,8},{4,12},{8,0},{12,4},{16,24},{20,28},{24,16},{28,20},{1,9},{5... | collective-permute-start | bytes 196616 | tf_op jit(solution)/shard_map/ppermute | solution.py:501
  36.6 2.0 %collective-permute-start.15 = (bf16[4,128,512]{2,1,0:T(8,128)(2,1)S(1)}, bf16[4,128,512]{2,1,0:T(8,128)(2,1)S(1)}, u32[]{:S(2)}, u32[]{:S(2)}) collective-permute-start(bf16[4,128,512]{2,1,0:T(8,128)(2,1)S(1)} %hold.3), channel_id=1, source_target_pairs={{0,4},{4,0},{8,12},{12,8},{16,20},{20,16},{24,28},{28,24},{1,5},{5... | collective-permute-start | bytes 1572872 | tf_op jit(solution)/shard_map/ppermute | solution.py:498
  36.7 8.9 %collective-permute-start.19 = (bf16[128,256]{1,0:T(8,128)(2,1)S(1)}, bf16[128,256]{1,0:T(8,128)(2,1)S(1)}, u32[]{:S(2)}, u32[]{:S(2)}) collective-permute-start(bf16[128,256]{1,0:T(8,128)(2,1)S(1)} %add.9.refs_1_.a), channel_id=1, source_target_pairs={{0,16},{4,20},{8,24},{12,28},{16,0},{20,4},{24,8},{28,12},{1,17},{... | collective-permute-start | bytes 196616 | tf_op jit(solution)/shard_map/ppermute | solution.py:501
  38.7 13.3 %collective-permute-start.16 = (bf16[128,512]{1,0:T(8,128)(2,1)S(1)}, bf16[128,512]{1,0:T(8,128)(2,1)S(1)}, u32[]{:S(2)}, u32[]{:S(2)}) collective-permute-start(bf16[128,512]{1,0:T(8,128)(2,1)S(1)} %get-tuple-element.64), channel_id=1, source_target_pairs={{0,16},{4,20},{8,24},{12,28},{16,0},{20,4},{24,8},{28,12},{1,17},{... | collective-permute-start | bytes 393224 | tf_op jit(solution)/shard_map/ppermute | solution.py:501
  39.9 12.2 %collective-permute-start.17 = (bf16[128,512]{1,0:T(8,128)(2,1)S(1)}, bf16[128,512]{1,0:T(8,128)(2,1)S(1)}, u32[]{:S(2)}, u32[]{:S(2)}) collective-permute-start(bf16[128,512]{1,0:T(8,128)(2,1)S(1)} %get-tuple-element.65), channel_id=1, source_target_pairs={{0,8},{4,12},{8,0},{12,4},{16,24},{20,28},{24,16},{28,20},{1,9},{5... | collective-permute-start | bytes 393224 | tf_op jit(solution)/shard_map/ppermute | solution.py:501
  41.8 10.2 %collective-permute-start.18 = (bf16[128,512]{1,0:T(8,128)(2,1)S(1)}, bf16[128,512]{1,0:T(8,128)(2,1)S(1)}, u32[]{:S(2)}, u32[]{:S(2)}) collective-permute-start(bf16[128,512]{1,0:T(8,128)(2,1)S(1)} %get-tuple-element.66), channel_id=1, source_target_pairs={{0,24},{4,28},{8,16},{12,20},{16,8},{20,12},{24,0},{28,4},{1,25},{... | collective-permute-start | bytes 393224 | tf_op jit(solution)/shard_map/ppermute | solution.py:501
  45.7 4.3 %collective-permute-start = (bf16[128,256]{1,0:T(8,128)(2,1)S(1)}, bf16[128,256]{1,0:T(8,128)(2,1)S(1)}, u32[]{:S(2)}, u32[]{:S(2)}) collective-permute-start(bf16[128,256]{1,0:T(8,128)(2,1)S(1)} %get-tuple-element.99.a), channel_id=1, source_target_pairs={{0,2},{2,0},{1,3},{3,1},{4,6},{6,4},{5,7},{7,5},{8,10},{10,8},{9,1... | collective-permute-start | bytes 196616 | tf_op jit(solution)/shard_map/while/body/ppermute | solution.py:565
  50.0 1.3 %collective-permute-start.1 = (bf16[128,256]{1,0:T(8,128)(2,1)S(1)}, bf16[128,256]{1,0:T(8,128)(2,1)S(1)}, u32[]{:S(2)}, u32[]{:S(2)}) collective-permute-start(bf16[128,256]{1,0:T(8,128)(2,1)S(1)} %add.11.a), channel_id=1, source_target_pairs={{0,4},{4,0},{8,12},{12,8},{16,20},{20,16},{24,28},{28,24},{1,5},{5... | collective-permute-start | bytes 196616 | tf_op jit(solution)/shard_map/while/body/ppermute | solution.py:498

commit v9 on v8

--- a/solution.py
+++ b/solution.py
@@ -185,12 +185,15 @@
 
 
 def backward_kernel(dense, own, *refs):
-    pieces, outs = refs[: dense.shape[1] - 1], refs[-2:]
+    pieces, outs = refs[: dense.shape[1] - 1], refs[-4:]
     for j in range(dense.shape[0]):
         total = own[j]
         for t, piece in enumerate(pieces):
             total = total + jnp.dot(piece[...], dense[j, t + 1], preferred_element_type=F32)
-        outs[j % 2][j // 2] = total.astype(BF16)
+        if j < 2:
+            outs[j][...] = total.astype(BF16)
+        else:
+            outs[2 + j % 2][j // 2 - 1] = total.astype(BF16)
 
 
 def backward(dense, own, pieces):
@@ -198,9 +201,10 @@
     feats = own.shape[1]
     return pl.pallas_call(
         backward_kernel,
-        out_shape=(jax.ShapeDtypeStruct((n_src // 2, feats, side), BF16),) * 2,
+        out_shape=(jax.ShapeDtypeStruct((feats, side), BF16),) * 2
+        + (jax.ShapeDtypeStruct((n_src // 2 - 1, feats, side), BF16),) * 2,
         in_specs=[vmem()] * (1 + n_col),
-        out_specs=(vmem(),) * 2,
+        out_specs=(vmem(),) * 4,
         compiler_params=params(),
         cost_estimate=COST,
         name="backward",
@@ -537,7 +541,7 @@
 
         def back_of(pieces, hidden):
             even, odd = (backward_stream(dense, k, pieces) for k in range(2))
-            return even, odd, elu(hidden)
+            return even[0], odd[0], even[1:], odd[1:], elu(hidden)
 
     other = [to_group(parts[t], -t, 1) for t in range(n_col - 1, -1, -1)]
     own = [parts[0]] + [to_group(parts[t], -t, 0) for t in range(1, n_col)]
@@ -547,15 +551,14 @@
         for t in range(1, n_col)
     ]
     term = weight_term(*rest)
-    even, odd, activated = back_of(pieces, hidden)
+    here, there, even, odd, activated = back_of(pieces, hidden)
     term = add(term, along_z(term, 1), odd)
     (odd,) = hold([odd], term)
-    arrived = sibling(odd)
-    sums = pair_sums(even, arrived)
+    sums = pair_sums(even, sibling(odd))
     if n_z > 2:
         term = add(term, along_z(term, 2), sums[0])
     order = sorted(range(1, n_z), key=lambda s: (s != n_z // 2, s))
-    back = turned_sum([sums[0]] + [along_z(sums[s], s) for s in order])
+    back = turned_sum([here, sibling(there)] + [along_z(sums[s - 1], s) for s in order])
 
     def finish(_, v):
         for step in range(2, n_z.bit_length() - 1):

time: 53.3 us -> 53.4 us (level)
    ppermute x6 -> x7, waiting for transfers between devices: 2.33 us -> 1.98 us  [sibling(): return lax.ppermute(v, 'row', [(i, i ^ 1) for i in range(n_row)])]
    ppermute x6 -> x7, starting transfers between devices: 1.23 us -> 1.4 us  [sibling(): return lax.ppermute(v, 'row', [(i, i ^ 1) for i in range(n_row)])]
  transfers between devices with their start and end apart: 20 -> 21, of which waited for: 10 -> 12; matrix products, arithmetic and copies ran while one was open for 1% -> 1% of each run, Pallas kernels for 17% -> 16%
where the time goes in v9:
time: 53.4 us; the launch traced here: 52.8 us
  starting transfers between devices  20.6 us (39%)
  waiting for transfers between devices  19.3 us (36%)
  Pallas kernels  10.7 us (20%)
  between operations  1.44 us (3%)
  other arithmetic  0.67 us (1%)
    ppermute x8, starting transfers between devices, along_z(): return lax.ppermute(v, 'row', [(i, i ^ 2 * s) for i in range(n_row)])  10.9 us
    ppermute x8, waiting for transfers between devices, along_z(): return lax.ppermute(v, 'row', [(i, i ^ 2 * s) for i in range(n_row)])  6.79 us
    ppermute x3, waiting for transfers between devices, to_group(): return lax.ppermute(v, ('col', 'feat'), pairs)  5.87 us
    pallas_call x1, Pallas kernels, densify(): pl.pallas_call(functools.partial(densify_kernel, (n_z, n_col, blocks), gr...  4.24 us
    ppermute x3, starting transfers between devices, to_group(): return lax.ppermute(v, ('col', 'feat'), pairs)  3.55 us
    ppermute x1, waiting for transfers between devices, finish(): v = add(v, lax.ppermute(v, 'col', pairs))  2.72 us
    pallas_call x3, Pallas kernels, forward(): pl.pallas_call(functools.partial(forward_kernel, places, last), out_shape...  2.66 us
    ppermute x7, waiting for transfers between devices, sibling(): return lax.ppermute(v, 'row', [(i, i ^ 1) for i in range(n_row)])  1.98 us
  transfers between devices with their start and end apart: 21, of which 12 were waited for; matrix products, arithmetic and copies ran while one was open for 1% of the time, Pallas kernels for 16%

profile of v9, /device:TPU:0, one launch (start us, length us, event | category | flops | bytes accessed | tf_op | source)
XLA Modules:
  0.0 52.8 jit_solution(377672340529191824)
XLA Ops:
  0.6 0.5 collective-permute-start.6
  1.1 4.7 %collective-permute-start.2 = (bf16[512,128]{1,0:T(8,128)(2,1)}, bf16[512,128]{1,0:T(8,128)(2,1)S(1)}, u32[]{:S(2)}, u32[]{:S(2)}) collective-permute-start(bf16[512,128]{1,0:T(8,128)(2,1)} %refs_0_.1), channel_id=1, source_target_pairs={{0,24},{4,28},{8,16},{12,20},{16,8},{20,12},{24,0},{28,4},{1,25},{... | collective-permute-start | bytes 393224 | tf_op jit(solution)/shard_map/ppermute | solution.py:505
  5.8 0.0 collective-permute-start.3
  5.8 0.7 %collective-permute-start.4 = (bf16[512,128]{1,0:T(8,128)(2,1)}, bf16[512,128]{1,0:T(8,128)(2,1)S(1)}, u32[]{:S(2)}, u32[]{:S(2)}) collective-permute-start(bf16[512,128]{1,0:T(8,128)(2,1)} %refs_0_.1), channel_id=1, source_target_pairs={{0,16},{4,20},{8,24},{12,28},{16,0},{20,4},{24,8},{28,12},{1,17},{... | collective-permute-start | bytes 393224 | tf_op jit(solution)/shard_map/ppermute | solution.py:505
  6.5 1.6 %collective-permute-start.5 = (bf16[512,128]{1,0:T(8,128)(2,1)}, bf16[512,128]{1,0:T(8,128)(2,1)S(1)}, u32[]{:S(2)}, u32[]{:S(2)}) collective-permute-start(bf16[512,128]{1,0:T(8,128)(2,1)} %cot_own.1), channel_id=1, source_target_pairs={{0,1},{1,0},{2,3},{3,2},{4,5},{5,4},{6,7},{7,6},{8,9},{9,8},{10,11... | collective-permute-start | bytes 393224 | tf_op jit(solution)/shard_map/ppermute | solution.py:508
  8.8 0.0 copy-start
  8.8 4.2 %densify.1.dense = bf16[8,2,512,512]{3,2,1,0:T(8,128)(2,1)S(1)} custom-call(s32[1,1,256]{2,1,0:T(1,128)} %rows.1, s32[1,1,256]{2,1,0:T(1,128)} %cols.1, s32[1,1]{1,0:T(1,128)S(6)} %copy.27.count, bf16[256,128,128]{2,1,0:T(8,128)(2,1)} %bitcast.1), custom_call_target="tpu_custom_call" | custom-call | flops 1 | bytes 1 | tf_op jit(solution)/shard_map/densify/pallas_call | solution.py:93
  13.0 0.0 collective-permute-done.6.refs_1_
  13.0 0.0 copy-done
  13.0 0.7 %forward.3 = (f32[512,128]{1,0:T(8,128)S(1)}, f32[512,128]{1,0:T(8,128)S(1)}) custom-call(bf16[8,2,512,512]{3,2,1,0:T(8,128)(2,1)S(1)} %densify.1.dense, bf16[512,128]{1,0:T(8,128)(2,1)S(1)} %copy-done, bf16[512,128]{1,0:T(8,128)(2,1)S(1)} %collective-permute-done.6.refs_1_), custom_call_target="tpu_custom_call" | custom-call | flops 1 | bytes 1 | tf_op jit(solution)/shard_map/forward/pallas_call | solution.py:150
  13.7 0.0 collective-permute-done.2.refs_0_
  13.7 0.3 collective-permute-done.3.refs_1_
  14.0 3.7 %collective-permute-done.4.refs_2_ = bf16[512,128]{1,0:T(8,128)(2,1)S(1)} collective-permute-done((bf16[512,128]{1,0:T(8,128)(2,1)}, bf16[512,128]{1,0:T(8,128)(2,1)S(1)}, u32[]{:S(2)}, u32[]{:S(2)}) %collective-permute-start.4) | collective-permute-done | bytes 131104 | tf_op jit(solution)/shard_map/ppermute | solution.py:505
  17.7 0.0 collective-permute-done.5.refs_3_
  17.7 0.0 collective-permute-start.7
  17.7 0.5 collective-permute-start.8
  18.2 0.1 collective-permute-start.9
  18.3 0.0 copy-start.1
  18.3 0.0 copy-start.2
  18.3 1.0 %forward.4 = (f32[512,128]{1,0:T(8,128)S(1)}, f32[512,128]{1,0:T(8,128)S(1)}) custom-call(bf16[8,2,512,512]{3,2,1,0:T(8,128)(2,1)S(1)} %densify.1.dense, bf16[512,128]{1,0:T(8,128)(2,1)S(1)} %get-tuple-element.47.refs_0_, bf16[512,128]{1,0:T(8,128)(2,1)S(1)} %get-tuple-element.48.refs_1_, bf16[512,128]{1,0:T(8,128)(2,1)S(1)} %get-tuple-element.49.refs_2_, ...), custom_call_target="tpu_custom_call" | custom-call | flops 1 | bytes 1 | tf_op jit(solution)/shard_map/forward/pallas_call | solution.py:150
  19.3 0.0 collective-permute-done.7.refs_0_
  19.3 0.0 collective-permute-done.8.refs_1_
  19.3 0.3 collective-permute-done.9.refs_2_
  19.6 1.0 %forward.5 = (bf16[512,128]{1,0:T(8,128)(2,1)S(1)}, bf16[512,128]{1,0:T(8,128)(2,1)S(1)}) custom-call(bf16[8,2,512,512]{3,2,1,0:T(8,128)(2,1)S(1)} %densify.1.dense, bf16[512,128]{1,0:T(8,128)(2,1)S(1)} %collective-permute-done.7.refs_0_, bf16[512,128]{1,0:T(8,128)(2,1)S(1)} %collective-permute-done.8.refs_1_, ...), custom_call_target="tpu_custom_call" | custom-call | flops 1 | bytes 1 | tf_op jit(solution)/shard_map/forward/pallas_call | solution.py:150
  20.6 2.5 %collective-permute-start.10 = (bf16[512,128]{1,0:T(8,128)(2,1)S(1)}, bf16[512,128]{1,0:T(8,128)(2,1)S(1)}, u32[]{:S(2)}, u32[]{:S(2)}) collective-permute-start(bf16[512,128]{1,0:T(8,128)(2,1)S(1)} %get-tuple-element.53), channel_id=1, source_target_pairs={{0,3},{1,2},{2,1},{3,0},{4,7},{5,6},{6,5},{7,4},{8,11},{9,10},{10,... | collective-permute-start | bytes 393224 | tf_op jit(solution)/shard_map/ppermute | solution.py:515
  23.1 0.5 %collective-permute-start.11 = (bf16[512,128]{1,0:T(8,128)(2,1)S(1)}, bf16[512,128]{1,0:T(8,128)(2,1)S(1)}, u32[]{:S(2)}, u32[]{:S(2)}) collective-permute-start(bf16[512,128]{1,0:T(8,128)(2,1)S(1)} %get-tuple-element.54.refs_2_), channel_id=1, source_target_pairs={{0,1},{1,0},{2,3},{3,2},{4,5},{5,4},{6,7},{7,6},{8,9},{9,8},{10,11... | collective-permute-start | bytes 393224 | tf_op jit(solution)/shard_map/ppermute | solution.py:515
  23.6 0.5 collective-permute-start.12
  24.1 3.7 %collective-permute-done.10.refs_0_ = bf16[512,128]{1,0:T(8,128)(2,1)S(1)} collective-permute-done((bf16[512,128]{1,0:T(8,128)(2,1)S(1)}, bf16[512,128]{1,0:T(8,128)(2,1)S(1)}, u32[]{:S(2)}, u32[]{:S(2)}) %collective-permute-start.10) | collective-permute-done | bytes 131104 | tf_op jit(solution)/shard_map/ppermute | solution.py:515
  27.9 2.1 %collective-permute-done.11.refs_1_ = bf16[512,128]{1,0:T(8,128)(2,1)S(1)} collective-permute-done((bf16[512,128]{1,0:T(8,128)(2,1)S(1)}, bf16[512,128]{1,0:T(8,128)(2,1)S(1)}, u32[]{:S(2)}, u32[]{:S(2)}) %collective-permute-start.11) | collective-permute-done | bytes 131104 | tf_op jit(solution)/shard_map/ppermute | solution.py:515
  30.0 0.0 collective-permute-done.12.refs_3_
  30.0 0.0 copy-done.1
  30.0 0.0 copy-done.2
  30.0 0.5 middle.1
  30.5 1.5 %collective-permute-start.13 = (bf16[128,512]{1,0:T(8,128)(2,1)S(1)}, bf16[128,512]{1,0:T(8,128)(2,1)S(1)}, u32[]{:S(2)}, u32[]{:S(2)}) collective-permute-start(bf16[128,512]{1,0:T(8,128)(2,1)S(1)} %get-tuple-element.55.piece), channel_id=1, source_target_pairs={{0,2},{2,0},{1,3},{3,1},{4,6},{6,4},{5,7},{7,5},{8,10},{10,8},{9,1... | collective-permute-start | bytes 393224 | tf_op jit(solution)/shard_map/ppermute | solution.py:550
  32.0 0.3 weight_term.1.a
  32.3 0.1 collective-permute-start.15
  32.3 1.4 %backward_own.1 = (f32[8,128,512]{2,1,0:T(8,128)S(1)}, bf16[512,128]{1,0:T(8,128)(2,1)}) custom-call(bf16[8,2,512,512]{3,2,1,0:T(8,128)(2,1)S(1)} %densify.1.dense, bf16[128,512]{1,0:T(8,128)(2,1)S(1)} %get-tuple-element.55.piece, f32[512,128]{1,0:T(8,128)S(1)} %get-tuple-element.56.hidden), custom_call_target="tpu_custom_call" | custom-call | flops 1 | bytes 1 | tf_op jit(solution)/shard_map/backward_own/pallas_call | solution.py:173
  33.7 2.0 %collective-permute-done.13.refs_0_ = bf16[128,512]{1,0:T(8,128)(2,1)S(1)} collective-permute-done((bf16[128,512]{1,0:T(8,128)(2,1)S(1)}, bf16[128,512]{1,0:T(8,128)(2,1)S(1)}, u32[]{:S(2)}, u32[]{:S(2)}) %collective-permute-start.13) | collective-permute-done | bytes 131104 | tf_op jit(solution)/shard_map/ppermute | solution.py:550
  35.7 0.7 %backward.1 = (bf16[128,512]{1,0:T(8,128)(2,1)S(1)}, bf16[128,512]{1,0:T(8,128)(2,1)S(1)}, bf16[3,128,512]{2,1,0:T(8,128)(2,1)S(1)}, bf16[3,128,512]{2,1,0:T(8,128)(2,1)S(1)}) custom-call(bf16[8,2,512,512]{3,2,1,0:T(8,128)(2,1)S(1)} %densify.1.dense, f32[8,128,512]{2,1,0:T(8,128)S(1)} %get-tuple-element.58.own, ...), custom_call_target="tpu_custom_call" | custom-call | flops 1 | bytes 1 | tf_op jit(solution)/shard_map/backward/pallas_call | solution.py:202
  36.4 0.2 collective-permute-done.15.b
  36.6 0.1 collective-permute-start.16
  36.7 1.1 %collective-permute-start.20 = (bf16[128,256]{1,0:T(8,128)(2,1)S(1)}, bf16[128,256]{1,0:T(8,128)(2,1)S(1)}, u32[]{:S(2)}, u32[]{:S(2)}) collective-permute-start(bf16[128,256]{1,0:T(8,128)(2,1)S(1)} %add.9.refs_1_.a), channel_id=1, source_target_pairs={{0,16},{4,20},{8,24},{12,28},{16,0},{20,4},{24,8},{28,12},{1,17},{... | collective-permute-start | bytes 196616 | tf_op jit(solution)/shard_map/ppermute | solution.py:505
  37.8 0.2 collective-permute-start.14
  38.0 0.5 collective-permute-done.16.arrived
  38.4 0.1 pair_sums.1
  38.5 1.5 %collective-permute-start.17 = (bf16[128,512]{1,0:T(8,128)(2,1)S(1)}, bf16[128,512]{1,0:T(8,128)(2,1)S(1)}, u32[]{:S(2)}, u32[]{:S(2)}) collective-permute-start(bf16[128,512]{1,0:T(8,128)(2,1)S(1)} %get-tuple-element.66), channel_id=1, source_target_pairs={{0,16},{4,20},{8,24},{12,28},{16,0},{20,4},{24,8},{28,12},{1,17},{... | collective-permute-start | bytes 393224 | tf_op jit(solution)/shard_map/ppermute | solution.py:505
  40.0 1.6 %collective-permute-start.18 = (bf16[128,512]{1,0:T(8,128)(2,1)S(1)}, bf16[128,512]{1,0:T(8,128)(2,1)S(1)}, u32[]{:S(2)}, u32[]{:S(2)}) collective-permute-start(bf16[128,512]{1,0:T(8,128)(2,1)S(1)} %get-tuple-element.67.rest_0_), channel_id=1, source_target_pairs={{0,8},{4,12},{8,0},{12,4},{16,24},{20,28},{24,16},{28,20},{1,9},{5... | collective-permute-start | bytes 393224 | tf_op jit(solution)/shard_map/ppermute | solution.py:505
  41.6 1.3 %collective-permute-start.19 = (bf16[128,512]{1,0:T(8,128)(2,1)S(1)}, bf16[128,512]{1,0:T(8,128)(2,1)S(1)}, u32[]{:S(2)}, u32[]{:S(2)}) collective-permute-start(bf16[128,512]{1,0:T(8,128)(2,1)S(1)} %get-tuple-element.68), channel_id=1, source_target_pairs={{0,24},{4,28},{8,16},{12,20},{16,8},{20,12},{24,0},{28,4},{1,25},{... | collective-permute-start | bytes 393224 | tf_op jit(solution)/shard_map/ppermute | solution.py:505
  43.0 0.5 collective-permute-done.20.b
  43.5 5.7 %while.10 = (s32[]{:T(128)}, bf16[128,256]{1,0:T(8,128)(2,1)S(1)}, s32[]{:T(128)}, s32[]{:T(128)}) while((s32[]{:T(128)}, bf16[128,256]{1,0:T(8,128)(2,1)S(1)}, s32[]{:T(128)}, s32[]{:T(128)}) %tuple.22), condition=%wide.region_1.0_spmd, body=%wide.region_0.0_spmd.sunk | while | flops 4 | bytes 524423 | solution.py:572
  43.5 1.6 %collective-permute-start = (bf16[128,256]{1,0:T(8,128)(2,1)S(1)}, bf16[128,256]{1,0:T(8,128)(2,1)S(1)}, u32[]{:S(2)}, u32[]{:S(2)}) collective-permute-start(bf16[128,256]{1,0:T(8,128)(2,1)S(1)} %get-tuple-element.101.a), channel_id=1, source_target_pairs={{0,2},{2,0},{1,3},{3,1},{4,6},{6,4},{5,7},{7,5},{8,10},{10,8},{9,1... | collective-permute-start | bytes 196616 | tf_op jit(solution)/shard_map/while/body/ppermute | solution.py:568
  45.1 2.7 %collective-permute-done.b = bf16[128,256]{1,0:T(8,128)(2,1)S(1)} collective-permute-done((bf16[128,256]{1,0:T(8,128)(2,1)S(1)}, bf16[128,256]{1,0:T(8,128)(2,1)S(1)}, u32[]{:S(2)}, u32[]{:S(2)}) %collective-permute-start) | collective-permute-done | bytes 65568 | tf_op jit(solution)/shard_map/while/body/ppermute | solution.py:568
  47.8 0.1 collective-permute-start.1
  47.9 1.2 %collective-permute-done.1.b = bf16[128,256]{1,0:T(8,128)(2,1)S(1)} collective-permute-done((bf16[128,256]{1,0:T(8,128)(2,1)S(1)}, bf16[128,256]{1,0:T(8,128)(2,1)S(1)}, u32[]{:S(2)}, u32[]{:S(2)}) %collective-permute-start.1) | collective-permute-done | bytes 65568 | tf_op jit(solution)/shard_map/while/body/ppermute | solution.py:502
  49.2 0.7 %convert_multiply_fusion = f32[128,256]{1,0:T(8,128)} fusion(bf16[128,256]{1,0:T(8,128)(2,1)S(1)} %get-tuple-element.69), kind=kLoop, calls=%fused_computation | loop fusion | flops 65536 | bytes 196608 | tf_op jit(solution)/shard_map/mul | solution.py:573
  49.9 0.0 collective-permute-done.14.refs_1_
  49.9 0.0 collective-permute-done.17.refs_2_
  49.9 0.0 collective-permute-done.18.refs_3_
  49.9 2.1 %collective-permute-done.19.refs_4_ = bf16[128,512]{1,0:T(8,128)(2,1)S(1)} collective-permute-done((bf16[128,512]{1,0:T(8,128)(2,1)S(1)}, bf16[128,512]{1,0:T(8,128)(2,1)S(1)}, u32[]{:S(2)}, u32[]{:S(2)}) %collective-permute-start.19) | collective-permute-done | bytes 131104 | tf_op jit(solution)/shard_map/ppermute | solution.py:505
  52.0 0.8 %turned_sum.1 = bf16[512,128]{1,0:T(8,128)(2,1)} custom-call(bf16[128,512]{1,0:T(8,128)(2,1)S(1)} %get-tuple-element.59.refs_0_, bf16[128,512]{1,0:T(8,128)(2,1)S(1)} %collective-permute-done.14.refs_1_, bf16[128,512]{1,0:T(8,128)(2,1)S(1)} %collective-permute-done.17.refs_2_, bf16[128,512]{1,0:T(8,128)(2,1)S(1)} %collective-permute-done.18.refs_3_, ...), custom_call_target="tpu_custom_call" | custom-call | flops 1 | bytes 1 | tf_op jit(solution)/shard_map/turned_sum/pallas_call | solution.py:482
  (6 shorter events, 0.1 us)
Async XLA Ops:
  0.6 12.4 %collective-permute-start.6 = (bf16[512,128]{1,0:T(8,128)(2,1)}, bf16[512,128]{1,0:T(8,128)(2,1)S(1)}, u32[]{:S(2)}, u32[]{:S(2)}) collective-permute-start(bf16[512,128]{1,0:T(8,128)(2,1)} %refs_0_.1), channel_id=1, source_target_pairs={{0,4},{4,0},{8,12},{12,8},{16,20},{20,16},{24,28},{28,24},{1,5},{5... | collective-permute-start | bytes 393224 | tf_op jit(solution)/shard_map/ppermute | solution.py:502
  1.1 12.6 %collective-permute-start.2 = (bf16[512,128]{1,0:T(8,128)(2,1)}, bf16[512,128]{1,0:T(8,128)(2,1)S(1)}, u32[]{:S(2)}, u32[]{:S(2)}) collective-permute-start(bf16[512,128]{1,0:T(8,128)(2,1)} %refs_0_.1), channel_id=1, source_target_pairs={{0,24},{4,28},{8,16},{12,20},{16,8},{20,12},{24,0},{28,4},{1,25},{... | collective-permute-start | bytes 393224 | tf_op jit(solution)/shard_map/ppermute | solution.py:505
  5.8 8.2 %collective-permute-start.3 = (bf16[512,128]{1,0:T(8,128)(2,1)}, bf16[512,128]{1,0:T(8,128)(2,1)S(1)}, u32[]{:S(2)}, u32[]{:S(2)}) collective-permute-start(bf16[512,128]{1,0:T(8,128)(2,1)} %refs_0_.1), channel_id=1, source_target_pairs={{0,8},{4,12},{8,0},{12,4},{16,24},{20,28},{24,16},{28,20},{1,9},{5... | collective-permute-start | bytes 393224 | tf_op jit(solution)/shard_map/ppermute | solution.py:505
  5.8 11.9 %collective-permute-start.4 = (bf16[512,128]{1,0:T(8,128)(2,1)}, bf16[512,128]{1,0:T(8,128)(2,1)S(1)}, u32[]{:S(2)}, u32[]{:S(2)}) collective-permute-start(bf16[512,128]{1,0:T(8,128)(2,1)} %refs_0_.1), channel_id=1, source_target_pairs={{0,16},{4,20},{8,24},{12,28},{16,0},{20,4},{24,8},{28,12},{1,17},{... | collective-permute-start | bytes 393224 | tf_op jit(solution)/shard_map/ppermute | solution.py:505
  6.5 11.2 %collective-permute-start.5 = (bf16[512,128]{1,0:T(8,128)(2,1)}, bf16[512,128]{1,0:T(8,128)(2,1)S(1)}, u32[]{:S(2)}, u32[]{:S(2)}) collective-permute-start(bf16[512,128]{1,0:T(8,128)(2,1)} %cot_own.1), channel_id=1, source_target_pairs={{0,1},{1,0},{2,3},{3,2},{4,5},{5,4},{6,7},{7,6},{8,9},{9,8},{10,11... | collective-permute-start | bytes 393224 | tf_op jit(solution)/shard_map/ppermute | solution.py:508
  8.8 4.3 %copy-start = (bf16[512,128]{1,0:T(8,128)(2,1)S(1)}, bf16[512,128]{1,0:T(8,128)(2,1)}, u32[]{:S(2)}) copy-start(bf16[512,128]{1,0:T(8,128)(2,1)} %refs_0_.1) | copy-start | bytes 393220
  17.7 1.6 %collective-permute-start.7 = (bf16[512,128]{1,0:T(8,128)(2,1)S(1)}, bf16[512,128]{1,0:T(8,128)(2,1)S(1)}, u32[]{:S(2)}, u32[]{:S(2)}) collective-permute-start(bf16[512,128]{1,0:T(8,128)(2,1)S(1)} %get-tuple-element.47.refs_0_), channel_id=1, source_target_pairs={{0,4},{4,0},{8,12},{12,8},{16,20},{20,16},{24,28},{28,24},{1,5},{5... | collective-permute-start | bytes 393224 | tf_op jit(solution)/shard_map/ppermute | solution.py:502
  17.7 1.6 %collective-permute-start.8 = (bf16[512,128]{1,0:T(8,128)(2,1)S(1)}, bf16[512,128]{1,0:T(8,128)(2,1)S(1)}, u32[]{:S(2)}, u32[]{:S(2)}) collective-permute-start(bf16[512,128]{1,0:T(8,128)(2,1)S(1)} %get-tuple-element.48.refs_1_), channel_id=1, source_target_pairs={{0,4},{4,0},{8,12},{12,8},{16,20},{20,16},{24,28},{28,24},{1,5},{5... | collective-permute-start | bytes 393224 | tf_op jit(solution)/shard_map/ppermute | solution.py:502
  18.2 1.3 %collective-permute-start.9 = (bf16[512,128]{1,0:T(8,128)(2,1)S(1)}, bf16[512,128]{1,0:T(8,128)(2,1)S(1)}, u32[]{:S(2)}, u32[]{:S(2)}) collective-permute-start(bf16[512,128]{1,0:T(8,128)(2,1)S(1)} %get-tuple-element.49.refs_2_), channel_id=1, source_target_pairs={{0,4},{4,0},{8,12},{12,8},{16,20},{20,16},{24,28},{28,24},{1,5},{5... | collective-permute-start | bytes 393224 | tf_op jit(solution)/shard_map/ppermute | solution.py:502
  18.3 11.7 %copy-start.1 = (bf16[256,256]{1,0:T(8,128)(2,1)S(1)}, bf16[256,256]{1,0:T(8,128)(2,1)}, u32[]{:S(2)}) copy-start(bf16[256,256]{1,0:T(8,128)(2,1)} %weights.1) | copy-start | bytes 393220
  18.3 11.7 %copy-start.2 = (bf16[512,128]{1,0:T(8,128)(2,1)S(1)}, bf16[512,128]{1,0:T(8,128)(2,1)}, u32[]{:S(2)}) copy-start(bf16[512,128]{1,0:T(8,128)(2,1)} %cot_own.1) | copy-start | bytes 393220
  20.6 7.3 %collective-permute-start.10 = (bf16[512,128]{1,0:T(8,128)(2,1)S(1)}, bf16[512,128]{1,0:T(8,128)(2,1)S(1)}, u32[]{:S(2)}, u32[]{:S(2)}) collective-permute-start(bf16[512,128]{1,0:T(8,128)(2,1)S(1)} %get-tuple-element.53), channel_id=1, source_target_pairs={{0,3},{1,2},{2,1},{3,0},{4,7},{5,6},{6,5},{7,4},{8,11},{9,10},{10,... | collective-permute-start | bytes 393224 | tf_op jit(solution)/shard_map/ppermute | solution.py:515
  23.1 6.9 %collective-permute-start.11 = (bf16[512,128]{1,0:T(8,128)(2,1)S(1)}, bf16[512,128]{1,0:T(8,128)(2,1)S(1)}, u32[]{:S(2)}, u32[]{:S(2)}) collective-permute-start(bf16[512,128]{1,0:T(8,128)(2,1)S(1)} %get-tuple-element.54.refs_2_), channel_id=1, source_target_pairs={{0,1},{1,0},{2,3},{3,2},{4,5},{5,4},{6,7},{7,6},{8,9},{9,8},{10,11... | collective-permute-start | bytes 393224 | tf_op jit(solution)/shard_map/ppermute | solution.py:515
  23.6 6.4 %collective-permute-start.12 = (bf16[512,128]{1,0:T(8,128)(2,1)S(1)}, bf16[512,128]{1,0:T(8,128)(2,1)S(1)}, u32[]{:S(2)}, u32[]{:S(2)}) collective-permute-start(bf16[512,128]{1,0:T(8,128)(2,1)S(1)} %get-tuple-element.53), channel_id=1, source_target_pairs={{0,2},{1,3},{2,0},{3,1},{4,6},{5,7},{6,4},{7,5},{8,10},{9,11},{10,... | collective-permute-start | bytes 393224 | tf_op jit(solution)/shard_map/ppermute | solution.py:515
  30.5 5.2 %collective-permute-start.13 = (bf16[128,512]{1,0:T(8,128)(2,1)S(1)}, bf16[128,512]{1,0:T(8,128)(2,1)S(1)}, u32[]{:S(2)}, u32[]{:S(2)}) collective-permute-start(bf16[128,512]{1,0:T(8,128)(2,1)S(1)} %get-tuple-element.55.piece), channel_id=1, source_target_pairs={{0,2},{2,0},{1,3},{3,1},{4,6},{6,4},{5,7},{7,5},{8,10},{10,8},{9,1... | collective-permute-start | bytes 393224 | tf_op jit(solution)/shard_map/ppermute | solution.py:550
  32.3 4.3 %collective-permute-start.15 = (bf16[128,256]{1,0:T(8,128)(2,1)S(1)}, bf16[128,256]{1,0:T(8,128)(2,1)S(1)}, u32[]{:S(2)}, u32[]{:S(2)}) collective-permute-start(bf16[128,256]{1,0:T(8,128)(2,1)S(1)} %weight_term.1.a), channel_id=1, source_target_pairs={{0,8},{4,12},{8,0},{12,4},{16,24},{20,28},{24,16},{28,20},{1,9},{5... | collective-permute-start | bytes 196616 | tf_op jit(solution)/shard_map/ppermute | solution.py:505
  36.6 1.8 %collective-permute-start.16 = (bf16[3,128,512]{2,1,0:T(8,128)(2,1)S(1)}, bf16[3,128,512]{2,1,0:T(8,128)(2,1)S(1)}, u32[]{:S(2)}, u32[]{:S(2)}) collective-permute-start(bf16[3,128,512]{2,1,0:T(8,128)(2,1)S(1)} %hold.3), channel_id=1, source_target_pairs={{0,4},{4,0},{8,12},{12,8},{16,20},{20,16},{24,28},{28,24},{1,5},{5... | collective-permute-start | bytes 1179656 | tf_op jit(solution)/shard_map/ppermute | solution.py:502
  36.7 6.7 %collective-permute-start.20 = (bf16[128,256]{1,0:T(8,128)(2,1)S(1)}, bf16[128,256]{1,0:T(8,128)(2,1)S(1)}, u32[]{:S(2)}, u32[]{:S(2)}) collective-permute-start(bf16[128,256]{1,0:T(8,128)(2,1)S(1)} %add.9.refs_1_.a), channel_id=1, source_target_pairs={{0,16},{4,20},{8,24},{12,28},{16,0},{20,4},{24,8},{28,12},{1,17},{... | collective-permute-start | bytes 196616 | tf_op jit(solution)/shard_map/ppermute | solution.py:505
  37.8 12.1 %collective-permute-start.14 = (bf16[128,512]{1,0:T(8,128)(2,1)S(1)}, bf16[128,512]{1,0:T(8,128)(2,1)S(1)}, u32[]{:S(2)}, u32[]{:S(2)}) collective-permute-start(bf16[128,512]{1,0:T(8,128)(2,1)S(1)} %get-tuple-element.60), channel_id=1, source_target_pairs={{0,4},{4,0},{8,12},{12,8},{16,20},{20,16},{24,28},{28,24},{1,5},{5... | collective-permute-start | bytes 393224 | tf_op jit(solution)/shard_map/ppermute | solution.py:502
  38.5 11.4 %collective-permute-start.17 = (bf16[128,512]{1,0:T(8,128)(2,1)S(1)}, bf16[128,512]{1,0:T(8,128)(2,1)S(1)}, u32[]{:S(2)}, u32[]{:S(2)}) collective-permute-start(bf16[128,512]{1,0:T(8,128)(2,1)S(1)} %get-tuple-element.66), channel_id=1, source_target_pairs={{0,16},{4,20},{8,24},{12,28},{16,0},{20,4},{24,8},{28,12},{1,17},{... | collective-permute-start | bytes 393224 | tf_op jit(solution)/shard_map/ppermute | solution.py:505
  40.0 9.8 %collective-permute-start.18 = (bf16[128,512]{1,0:T(8,128)(2,1)S(1)}, bf16[128,512]{1,0:T(8,128)(2,1)S(1)}, u32[]{:S(2)}, u32[]{:S(2)}) collective-permute-start(bf16[128,512]{1,0:T(8,128)(2,1)S(1)} %get-tuple-element.67.rest_0_), channel_id=1, source_target_pairs={{0,8},{4,12},{8,0},{12,4},{16,24},{20,28},{24,16},{28,20},{1,9},{5... | collective-permute-start | bytes 393224 | tf_op jit(solution)/shard_map/ppermute | solution.py:505
  41.6 10.4 %collective-permute-start.19 = (bf16[128,512]{1,0:T(8,128)(2,1)S(1)}, bf16[128,512]{1,0:T(8,128)(2,1)S(1)}, u32[]{:S(2)}, u32[]{:S(2)}) collective-permute-start(bf16[128,512]{1,0:T(8,128)(2,1)S(1)} %get-tuple-element.68), channel_id=1, source_target_pairs={{0,24},{4,28},{8,16},{12,20},{16,8},{20,12},{24,0},{28,4},{1,25},{... | collective-permute-start | bytes 393224 | tf_op jit(solution)/shard_map/ppermute | solution.py:505
  43.5 4.3 %collective-permute-start = (bf16[128,256]{1,0:T(8,128)(2,1)S(1)}, bf16[128,256]{1,0:T(8,128)(2,1)S(1)}, u32[]{:S(2)}, u32[]{:S(2)}) collective-permute-start(bf16[128,256]{1,0:T(8,128)(2,1)S(1)} %get-tuple-element.101.a), channel_id=1, source_target_pairs={{0,2},{2,0},{1,3},{3,1},{4,6},{6,4},{5,7},{7,5},{8,10},{10,8},{9,1... | collective-permute-start | bytes 196616 | tf_op jit(solution)/shard_map/while/body/ppermute | solution.py:568
  47.8 1.3 %collective-permute-start.1 = (bf16[128,256]{1,0:T(8,128)(2,1)S(1)}, bf16[128,256]{1,0:T(8,128)(2,1)S(1)}, u32[]{:S(2)}, u32[]{:S(2)}) collective-permute-start(bf16[128,256]{1,0:T(8,128)(2,1)S(1)} %add.11.a), channel_id=1, source_target_pairs={{0,4},{4,0},{8,12},{12,8},{16,20},{20,16},{24,28},{28,24},{1,5},{5... | collective-permute-start | bytes 196616 | tf_op jit(solution)/shard_map/while/body/ppermute | solution.py:502

commit v10 on v9

--- a/solution.py
+++ b/solution.py
@@ -556,7 +556,7 @@
     (odd,) = hold([odd], term)
     sums = pair_sums(even, sibling(odd))
     if n_z > 2:
-        term = add(term, along_z(term, 2), sums[0])
+        term = add(term, along_z(term, 3), sums[0])
     order = sorted(range(1, n_z), key=lambda s: (s != n_z // 2, s))
     back = turned_sum([here, sibling(there)] + [along_z(sums[s - 1], s) for s in order])
 

time: 53.4 us -> 53 us (level)
  waiting for transfers between devices: 19.3 us -> 17.5 us
  starting transfers between devices: 20.6 us -> 22.1 us
    ppermute x8, starting transfers between devices: 10.9 us -> 12.4 us  [along_z(): return lax.ppermute(v, 'row', [(i, i ^ 2 * s) for i in range(n_row)])]
    ppermute x8, waiting for transfers between devices: 6.79 us -> 5.39 us  [along_z(): return lax.ppermute(v, 'row', [(i, i ^ 2 * s) for i in range(n_row)])]
  transfers between devices with their start and end apart: 21 -> 21, of which waited for: 12 -> 10; matrix products, arithmetic and copies ran while one was open for 1% -> 1% of each run, Pallas kernels for 16% -> 16%
where the time goes in v10:
time: 53 us; the launch traced here: 52.4 us
  starting transfers between devices  22.1 us (42%)
  waiting for transfers between devices  17.5 us (33%)
  Pallas kernels  10.7 us (20%)
  between operations  1.44 us (3%)
  other arithmetic  0.67 us (1%)
    ppermute x8, starting transfers between devices, along_z(): return lax.ppermute(v, 'row', [(i, i ^ 2 * s) for i in range(n_row)])  12.4 us
    ppermute x3, waiting for transfers between devices, to_group(): return lax.ppermute(v, ('col', 'feat'), pairs)  5.87 us
    ppermute x8, waiting for transfers between devices, along_z(): return lax.ppermute(v, 'row', [(i, i ^ 2 * s) for i in range(n_row)])  5.39 us
    pallas_call x1, Pallas kernels, densify(): pl.pallas_call(functools.partial(densify_kernel, (n_z, n_col, blocks), gr...  4.24 us
    ppermute x3, starting transfers between devices, to_group(): return lax.ppermute(v, ('col', 'feat'), pairs)  3.55 us
    ppermute x1, waiting for transfers between devices, finish(): v = add(v, lax.ppermute(v, 'col', pairs))  2.72 us
    pallas_call x3, Pallas kernels, forward(): pl.pallas_call(functools.partial(forward_kernel, places, last), out_shape...  2.66 us
    ppermute x1, waiting for transfers between devices, shards(): lax.ppermute(spread, 'col', [(i, (i + t) % n_col) for i in range(n_col)])  1.97 us
  transfers between devices with their start and end apart: 21, of which 10 were waited for; matrix products, arithmetic and copies ran while one was open for 1% of the time, Pallas kernels for 16%

profile of v10, /device:TPU:0, one launch (start us, length us, event | category | flops | bytes accessed | tf_op | source)
XLA Modules:
  0.0 52.4 jit_solution(9939238581194662529)
XLA Ops:
  0.6 0.5 collective-permute-start.6
  1.1 4.7 %collective-permute-start.2 = (bf16[512,128]{1,0:T(8,128)(2,1)}, bf16[512,128]{1,0:T(8,128)(2,1)S(1)}, u32[]{:S(2)}, u32[]{:S(2)}) collective-permute-start(bf16[512,128]{1,0:T(8,128)(2,1)} %refs_0_.1), channel_id=1, source_target_pairs={{0,24},{4,28},{8,16},{12,20},{16,8},{20,12},{24,0},{28,4},{1,25},{... | collective-permute-start | bytes 393224 | tf_op jit(solution)/shard_map/ppermute | solution.py:505
  5.8 0.0 collective-permute-start.3
  5.8 0.7 %collective-permute-start.4 = (bf16[512,128]{1,0:T(8,128)(2,1)}, bf16[512,128]{1,0:T(8,128)(2,1)S(1)}, u32[]{:S(2)}, u32[]{:S(2)}) collective-permute-start(bf16[512,128]{1,0:T(8,128)(2,1)} %refs_0_.1), channel_id=1, source_target_pairs={{0,16},{4,20},{8,24},{12,28},{16,0},{20,4},{24,8},{28,12},{1,17},{... | collective-permute-start | bytes 393224 | tf_op jit(solution)/shard_map/ppermute | solution.py:505
  6.5 1.6 %collective-permute-start.5 = (bf16[512,128]{1,0:T(8,128)(2,1)}, bf16[512,128]{1,0:T(8,128)(2,1)S(1)}, u32[]{:S(2)}, u32[]{:S(2)}) collective-permute-start(bf16[512,128]{1,0:T(8,128)(2,1)} %cot_own.1), channel_id=1, source_target_pairs={{0,1},{1,0},{2,3},{3,2},{4,5},{5,4},{6,7},{7,6},{8,9},{9,8},{10,11... | collective-permute-start | bytes 393224 | tf_op jit(solution)/shard_map/ppermute | solution.py:508
  8.8 0.0 copy-start
  8.8 4.2 %densify.1.dense = bf16[8,2,512,512]{3,2,1,0:T(8,128)(2,1)S(1)} custom-call(s32[1,1,256]{2,1,0:T(1,128)} %rows.1, s32[1,1,256]{2,1,0:T(1,128)} %cols.1, s32[1,1]{1,0:T(1,128)S(6)} %copy.27.count, bf16[256,128,128]{2,1,0:T(8,128)(2,1)} %bitcast.1), custom_call_target="tpu_custom_call" | custom-call | flops 1 | bytes 1 | tf_op jit(solution)/shard_map/densify/pallas_call | solution.py:93
  13.0 0.0 collective-permute-done.6.refs_1_
  13.0 0.0 copy-done
  13.0 0.7 %forward.3 = (f32[512,128]{1,0:T(8,128)S(1)}, f32[512,128]{1,0:T(8,128)S(1)}) custom-call(bf16[8,2,512,512]{3,2,1,0:T(8,128)(2,1)S(1)} %densify.1.dense, bf16[512,128]{1,0:T(8,128)(2,1)S(1)} %copy-done, bf16[512,128]{1,0:T(8,128)(2,1)S(1)} %collective-permute-done.6.refs_1_), custom_call_target="tpu_custom_call" | custom-call | flops 1 | bytes 1 | tf_op jit(solution)/shard_map/forward/pallas_call | solution.py:150
  13.7 0.0 collective-permute-done.2.refs_0_
  13.7 0.3 collective-permute-done.3.refs_1_
  14.0 3.7 %collective-permute-done.4.refs_2_ = bf16[512,128]{1,0:T(8,128)(2,1)S(1)} collective-permute-done((bf16[512,128]{1,0:T(8,128)(2,1)}, bf16[512,128]{1,0:T(8,128)(2,1)S(1)}, u32[]{:S(2)}, u32[]{:S(2)}) %collective-permute-start.4) | collective-permute-done | bytes 131104 | tf_op jit(solution)/shard_map/ppermute | solution.py:505
  17.7 0.0 collective-permute-done.5.refs_3_
  17.7 0.0 collective-permute-start.7
  17.7 0.5 collective-permute-start.8
  18.2 0.1 collective-permute-start.9
  18.3 0.0 copy-start.1
  18.3 0.0 copy-start.2
  18.3 1.0 %forward.4 = (f32[512,128]{1,0:T(8,128)S(1)}, f32[512,128]{1,0:T(8,128)S(1)}) custom-call(bf16[8,2,512,512]{3,2,1,0:T(8,128)(2,1)S(1)} %densify.1.dense, bf16[512,128]{1,0:T(8,128)(2,1)S(1)} %get-tuple-element.47.refs_0_, bf16[512,128]{1,0:T(8,128)(2,1)S(1)} %get-tuple-element.48.refs_1_, bf16[512,128]{1,0:T(8,128)(2,1)S(1)} %get-tuple-element.49.refs_2_, ...), custom_call_target="tpu_custom_call" | custom-call | flops 1 | bytes 1 | tf_op jit(solution)/shard_map/forward/pallas_call | solution.py:150
  19.3 0.0 collective-permute-done.7.refs_0_
  19.3 0.0 collective-permute-done.8.refs_1_
  19.3 0.3 collective-permute-done.9.refs_2_
  19.6 1.0 %forward.5 = (bf16[512,128]{1,0:T(8,128)(2,1)S(1)}, bf16[512,128]{1,0:T(8,128)(2,1)S(1)}) custom-call(bf16[8,2,512,512]{3,2,1,0:T(8,128)(2,1)S(1)} %densify.1.dense, bf16[512,128]{1,0:T(8,128)(2,1)S(1)} %collective-permute-done.7.refs_0_, bf16[512,128]{1,0:T(8,128)(2,1)S(1)} %collective-permute-done.8.refs_1_, ...), custom_call_target="tpu_custom_call" | custom-call | flops 1 | bytes 1 | tf_op jit(solution)/shard_map/forward/pallas_call | solution.py:150
  20.6 2.5 %collective-permute-start.10 = (bf16[512,128]{1,0:T(8,128)(2,1)S(1)}, bf16[512,128]{1,0:T(8,128)(2,1)S(1)}, u32[]{:S(2)}, u32[]{:S(2)}) collective-permute-start(bf16[512,128]{1,0:T(8,128)(2,1)S(1)} %get-tuple-element.53), channel_id=1, source_target_pairs={{0,3},{1,2},{2,1},{3,0},{4,7},{5,6},{6,5},{7,4},{8,11},{9,10},{10,... | collective-permute-start | bytes 393224 | tf_op jit(solution)/shard_map/ppermute | solution.py:515
  23.1 0.5 %collective-permute-start.11 = (bf16[512,128]{1,0:T(8,128)(2,1)S(1)}, bf16[512,128]{1,0:T(8,128)(2,1)S(1)}, u32[]{:S(2)}, u32[]{:S(2)}) collective-permute-start(bf16[512,128]{1,0:T(8,128)(2,1)S(1)} %get-tuple-element.54.refs_2_), channel_id=1, source_target_pairs={{0,1},{1,0},{2,3},{3,2},{4,5},{5,4},{6,7},{7,6},{8,9},{9,8},{10,11... | collective-permute-start | bytes 393224 | tf_op jit(solution)/shard_map/ppermute | solution.py:515
  23.6 0.5 collective-permute-start.12
  24.1 3.7 %collective-permute-done.10.refs_0_ = bf16[512,128]{1,0:T(8,128)(2,1)S(1)} collective-permute-done((bf16[512,128]{1,0:T(8,128)(2,1)S(1)}, bf16[512,128]{1,0:T(8,128)(2,1)S(1)}, u32[]{:S(2)}, u32[]{:S(2)}) %collective-permute-start.10) | collective-permute-done | bytes 131104 | tf_op jit(solution)/shard_map/ppermute | solution.py:515
  27.9 2.1 %collective-permute-done.11.refs_1_ = bf16[512,128]{1,0:T(8,128)(2,1)S(1)} collective-permute-done((bf16[512,128]{1,0:T(8,128)(2,1)S(1)}, bf16[512,128]{1,0:T(8,128)(2,1)S(1)}, u32[]{:S(2)}, u32[]{:S(2)}) %collective-permute-start.11) | collective-permute-done | bytes 131104 | tf_op jit(solution)/shard_map/ppermute | solution.py:515
  30.0 0.0 collective-permute-done.12.refs_3_
  30.0 0.0 copy-done.1
  30.0 0.0 copy-done.2
  30.0 0.5 middle.1
  30.5 1.5 %collective-permute-start.13 = (bf16[128,512]{1,0:T(8,128)(2,1)S(1)}, bf16[128,512]{1,0:T(8,128)(2,1)S(1)}, u32[]{:S(2)}, u32[]{:S(2)}) collective-permute-start(bf16[128,512]{1,0:T(8,128)(2,1)S(1)} %get-tuple-element.55.piece), channel_id=1, source_target_pairs={{0,2},{2,0},{1,3},{3,1},{4,6},{6,4},{5,7},{7,5},{8,10},{10,8},{9,1... | collective-permute-start | bytes 393224 | tf_op jit(solution)/shard_map/ppermute | solution.py:550
  32.0 0.3 weight_term.1.a
  32.3 0.1 collective-permute-start.15
  32.3 1.4 %backward_own.1 = (f32[8,128,512]{2,1,0:T(8,128)S(1)}, bf16[512,128]{1,0:T(8,128)(2,1)}) custom-call(bf16[8,2,512,512]{3,2,1,0:T(8,128)(2,1)S(1)} %densify.1.dense, bf16[128,512]{1,0:T(8,128)(2,1)S(1)} %get-tuple-element.55.piece, f32[512,128]{1,0:T(8,128)S(1)} %get-tuple-element.56.hidden), custom_call_target="tpu_custom_call" | custom-call | flops 1 | bytes 1 | tf_op jit(solution)/shard_map/backward_own/pallas_call | solution.py:173
  33.7 2.0 %collective-permute-done.13.refs_0_ = bf16[128,512]{1,0:T(8,128)(2,1)S(1)} collective-permute-done((bf16[128,512]{1,0:T(8,128)(2,1)S(1)}, bf16[128,512]{1,0:T(8,128)(2,1)S(1)}, u32[]{:S(2)}, u32[]{:S(2)}) %collective-permute-start.13) | collective-permute-done | bytes 131104 | tf_op jit(solution)/shard_map/ppermute | solution.py:550
  35.7 0.7 %backward.1 = (bf16[128,512]{1,0:T(8,128)(2,1)S(1)}, bf16[128,512]{1,0:T(8,128)(2,1)S(1)}, bf16[3,128,512]{2,1,0:T(8,128)(2,1)S(1)}, bf16[3,128,512]{2,1,0:T(8,128)(2,1)S(1)}) custom-call(bf16[8,2,512,512]{3,2,1,0:T(8,128)(2,1)S(1)} %densify.1.dense, f32[8,128,512]{2,1,0:T(8,128)S(1)} %get-tuple-element.58.own, ...), custom_call_target="tpu_custom_call" | custom-call | flops 1 | bytes 1 | tf_op jit(solution)/shard_map/backward/pallas_call | solution.py:202
  36.4 0.2 collective-permute-done.15.b
  36.6 0.1 collective-permute-start.16
  36.7 2.5 %collective-permute-start.20 = (bf16[128,256]{1,0:T(8,128)(2,1)S(1)}, bf16[128,256]{1,0:T(8,128)(2,1)S(1)}, u32[]{:S(2)}, u32[]{:S(2)}) collective-permute-start(bf16[128,256]{1,0:T(8,128)(2,1)S(1)} %add.9.refs_1_.a), channel_id=1, source_target_pairs={{0,24},{4,28},{8,16},{12,20},{16,8},{20,12},{24,0},{28,4},{1,25},{... | collective-permute-start | bytes 196616 | tf_op jit(solution)/shard_map/ppermute | solution.py:505
  39.2 0.2 collective-permute-start.14
  39.4 0.0 collective-permute-done.16.arrived
  39.4 0.1 pair_sums.1
  39.5 0.1 collective-permute-start.17
  39.6 2.0 %collective-permute-start.18 = (bf16[128,512]{1,0:T(8,128)(2,1)S(1)}, bf16[128,512]{1,0:T(8,128)(2,1)S(1)}, u32[]{:S(2)}, u32[]{:S(2)}) collective-permute-start(bf16[128,512]{1,0:T(8,128)(2,1)S(1)} %get-tuple-element.67.rest_0_), channel_id=1, source_target_pairs={{0,8},{4,12},{8,0},{12,4},{16,24},{20,28},{24,16},{28,20},{1,9},{5... | collective-permute-start | bytes 393224 | tf_op jit(solution)/shard_map/ppermute | solution.py:505
  41.6 2.3 %collective-permute-start.19 = (bf16[128,512]{1,0:T(8,128)(2,1)S(1)}, bf16[128,512]{1,0:T(8,128)(2,1)S(1)}, u32[]{:S(2)}, u32[]{:S(2)}) collective-permute-start(bf16[128,512]{1,0:T(8,128)(2,1)S(1)} %get-tuple-element.68), channel_id=1, source_target_pairs={{0,24},{4,28},{8,16},{12,20},{16,8},{20,12},{24,0},{28,4},{1,25},{... | collective-permute-start | bytes 393224 | tf_op jit(solution)/shard_map/ppermute | solution.py:505
  44.0 0.0 collective-permute-done.20.b
  44.0 5.7 %while.10 = (s32[]{:T(128)}, bf16[128,256]{1,0:T(8,128)(2,1)S(1)}, s32[]{:T(128)}, s32[]{:T(128)}) while((s32[]{:T(128)}, bf16[128,256]{1,0:T(8,128)(2,1)S(1)}, s32[]{:T(128)}, s32[]{:T(128)}) %tuple.22), condition=%wide.region_1.0_spmd, body=%wide.region_0.0_spmd.sunk | while | flops 4 | bytes 524423 | solution.py:572
  44.0 1.6 %collective-permute-start = (bf16[128,256]{1,0:T(8,128)(2,1)S(1)}, bf16[128,256]{1,0:T(8,128)(2,1)S(1)}, u32[]{:S(2)}, u32[]{:S(2)}) collective-permute-start(bf16[128,256]{1,0:T(8,128)(2,1)S(1)} %get-tuple-element.101.a), channel_id=1, source_target_pairs={{0,2},{2,0},{1,3},{3,1},{4,6},{6,4},{5,7},{7,5},{8,10},{10,8},{9,1... | collective-permute-start | bytes 196616 | tf_op jit(solution)/shard_map/while/body/ppermute | solution.py:568
  45.6 2.7 %collective-permute-done.b = bf16[128,256]{1,0:T(8,128)(2,1)S(1)} collective-permute-done((bf16[128,256]{1,0:T(8,128)(2,1)S(1)}, bf16[128,256]{1,0:T(8,128)(2,1)S(1)}, u32[]{:S(2)}, u32[]{:S(2)}) %collective-permute-start) | collective-permute-done | bytes 65568 | tf_op jit(solution)/shard_map/while/body/ppermute | solution.py:568
  48.4 0.1 collective-permute-start.1
  48.4 1.2 %collective-permute-done.1.b = bf16[128,256]{1,0:T(8,128)(2,1)S(1)} collective-permute-done((bf16[128,256]{1,0:T(8,128)(2,1)S(1)}, bf16[128,256]{1,0:T(8,128)(2,1)S(1)}, u32[]{:S(2)}, u32[]{:S(2)}) %collective-permute-start.1) | collective-permute-done | bytes 65568 | tf_op jit(solution)/shard_map/while/body/ppermute | solution.py:502
  49.7 0.7 %convert_multiply_fusion = f32[128,256]{1,0:T(8,128)} fusion(bf16[128,256]{1,0:T(8,128)(2,1)S(1)} %get-tuple-element.69), kind=kLoop, calls=%fused_computation | loop fusion | flops 65536 | bytes 196608 | tf_op jit(solution)/shard_map/mul | solution.py:573
  50.4 0.0 collective-permute-done.14.refs_1_
  50.4 0.0 collective-permute-done.17.refs_2_
  50.4 0.0 collective-permute-done.18.refs_3_
  50.4 1.2 %collective-permute-done.19.refs_4_ = bf16[128,512]{1,0:T(8,128)(2,1)S(1)} collective-permute-done((bf16[128,512]{1,0:T(8,128)(2,1)S(1)}, bf16[128,512]{1,0:T(8,128)(2,1)S(1)}, u32[]{:S(2)}, u32[]{:S(2)}) %collective-permute-start.19) | collective-permute-done | bytes 131104 | tf_op jit(solution)/shard_map/ppermute | solution.py:505
  51.6 0.8 %turned_sum.1 = bf16[512,128]{1,0:T(8,128)(2,1)} custom-call(bf16[128,512]{1,0:T(8,128)(2,1)S(1)} %get-tuple-element.59.refs_0_, bf16[128,512]{1,0:T(8,128)(2,1)S(1)} %collective-permute-done.14.refs_1_, bf16[128,512]{1,0:T(8,128)(2,1)S(1)} %collective-permute-done.17.refs_2_, bf16[128,512]{1,0:T(8,128)(2,1)S(1)} %collective-permute-done.18.refs_3_, ...), custom_call_target="tpu_custom_call" | custom-call | flops 1 | bytes 1 | tf_op jit(solution)/shard_map/turned_sum/pallas_call | solution.py:482
  (6 shorter events, 0.1 us)
Async XLA Ops:
  0.6 12.4 %collective-permute-start.6 = (bf16[512,128]{1,0:T(8,128)(2,1)}, bf16[512,128]{1,0:T(8,128)(2,1)S(1)}, u32[]{:S(2)}, u32[]{:S(2)}) collective-permute-start(bf16[512,128]{1,0:T(8,128)(2,1)} %refs_0_.1), channel_id=1, source_target_pairs={{0,4},{4,0},{8,12},{12,8},{16,20},{20,16},{24,28},{28,24},{1,5},{5... | collective-permute-start | bytes 393224 | tf_op jit(solution)/shard_map/ppermute | solution.py:502
  1.1 12.6 %collective-permute-start.2 = (bf16[512,128]{1,0:T(8,128)(2,1)}, bf16[512,128]{1,0:T(8,128)(2,1)S(1)}, u32[]{:S(2)}, u32[]{:S(2)}) collective-permute-start(bf16[512,128]{1,0:T(8,128)(2,1)} %refs_0_.1), channel_id=1, source_target_pairs={{0,24},{4,28},{8,16},{12,20},{16,8},{20,12},{24,0},{28,4},{1,25},{... | collective-permute-start | bytes 393224 | tf_op jit(solution)/shard_map/ppermute | solution.py:505
  5.8 8.2 %collective-permute-start.3 = (bf16[512,128]{1,0:T(8,128)(2,1)}, bf16[512,128]{1,0:T(8,128)(2,1)S(1)}, u32[]{:S(2)}, u32[]{:S(2)}) collective-permute-start(bf16[512,128]{1,0:T(8,128)(2,1)} %refs_0_.1), channel_id=1, source_target_pairs={{0,8},{4,12},{8,0},{12,4},{16,24},{20,28},{24,16},{28,20},{1,9},{5... | collective-permute-start | bytes 393224 | tf_op jit(solution)/shard_map/ppermute | solution.py:505
  5.8 11.9 %collective-permute-start.4 = (bf16[512,128]{1,0:T(8,128)(2,1)}, bf16[512,128]{1,0:T(8,128)(2,1)S(1)}, u32[]{:S(2)}, u32[]{:S(2)}) collective-permute-start(bf16[512,128]{1,0:T(8,128)(2,1)} %refs_0_.1), channel_id=1, source_target_pairs={{0,16},{4,20},{8,24},{12,28},{16,0},{20,4},{24,8},{28,12},{1,17},{... | collective-permute-start | bytes 393224 | tf_op jit(solution)/shard_map/ppermute | solution.py:505
  6.5 11.2 %collective-permute-start.5 = (bf16[512,128]{1,0:T(8,128)(2,1)}, bf16[512,128]{1,0:T(8,128)(2,1)S(1)}, u32[]{:S(2)}, u32[]{:S(2)}) collective-permute-start(bf16[512,128]{1,0:T(8,128)(2,1)} %cot_own.1), channel_id=1, source_target_pairs={{0,1},{1,0},{2,3},{3,2},{4,5},{5,4},{6,7},{7,6},{8,9},{9,8},{10,11... | collective-permute-start | bytes 393224 | tf_op jit(solution)/shard_map/ppermute | solution.py:508
  8.8 4.3 %copy-start = (bf16[512,128]{1,0:T(8,128)(2,1)S(1)}, bf16[512,128]{1,0:T(8,128)(2,1)}, u32[]{:S(2)}) copy-start(bf16[512,128]{1,0:T(8,128)(2,1)} %refs_0_.1) | copy-start | bytes 393220
  17.7 1.6 %collective-permute-start.7 = (bf16[512,128]{1,0:T(8,128)(2,1)S(1)}, bf16[512,128]{1,0:T(8,128)(2,1)S(1)}, u32[]{:S(2)}, u32[]{:S(2)}) collective-permute-start(bf16[512,128]{1,0:T(8,128)(2,1)S(1)} %get-tuple-element.47.refs_0_), channel_id=1, source_target_pairs={{0,4},{4,0},{8,12},{12,8},{16,20},{20,16},{24,28},{28,24},{1,5},{5... | collective-permute-start | bytes 393224 | tf_op jit(solution)/shard_map/ppermute | solution.py:502
  17.7 1.6 %collective-permute-start.8 = (bf16[512,128]{1,0:T(8,128)(2,1)S(1)}, bf16[512,128]{1,0:T(8,128)(2,1)S(1)}, u32[]{:S(2)}, u32[]{:S(2)}) collective-permute-start(bf16[512,128]{1,0:T(8,128)(2,1)S(1)} %get-tuple-element.48.refs_1_), channel_id=1, source_target_pairs={{0,4},{4,0},{8,12},{12,8},{16,20},{20,16},{24,28},{28,24},{1,5},{5... | collective-permute-start | bytes 393224 | tf_op jit(solution)/shard_map/ppermute | solution.py:502
  18.2 1.3 %collective-permute-start.9 = (bf16[512,128]{1,0:T(8,128)(2,1)S(1)}, bf16[512,128]{1,0:T(8,128)(2,1)S(1)}, u32[]{:S(2)}, u32[]{:S(2)}) collective-permute-start(bf16[512,128]{1,0:T(8,128)(2,1)S(1)} %get-tuple-element.49.refs_2_), channel_id=1, source_target_pairs={{0,4},{4,0},{8,12},{12,8},{16,20},{20,16},{24,28},{28,24},{1,5},{5... | collective-permute-start | bytes 393224 | tf_op jit(solution)/shard_map/ppermute | solution.py:502
  18.3 11.7 %copy-start.1 = (bf16[256,256]{1,0:T(8,128)(2,1)S(1)}, bf16[256,256]{1,0:T(8,128)(2,1)}, u32[]{:S(2)}) copy-start(bf16[256,256]{1,0:T(8,128)(2,1)} %weights.1) | copy-start | bytes 393220
  18.3 11.7 %copy-start.2 = (bf16[512,128]{1,0:T(8,128)(2,1)S(1)}, bf16[512,128]{1,0:T(8,128)(2,1)}, u32[]{:S(2)}) copy-start(bf16[512,128]{1,0:T(8,128)(2,1)} %cot_own.1) | copy-start | bytes 393220
  20.6 7.3 %collective-permute-start.10 = (bf16[512,128]{1,0:T(8,128)(2,1)S(1)}, bf16[512,128]{1,0:T(8,128)(2,1)S(1)}, u32[]{:S(2)}, u32[]{:S(2)}) collective-permute-start(bf16[512,128]{1,0:T(8,128)(2,1)S(1)} %get-tuple-element.53), channel_id=1, source_target_pairs={{0,3},{1,2},{2,1},{3,0},{4,7},{5,6},{6,5},{7,4},{8,11},{9,10},{10,... | collective-permute-start | bytes 393224 | tf_op jit(solution)/shard_map/ppermute | solution.py:515
  23.1 6.9 %collective-permute-start.11 = (bf16[512,128]{1,0:T(8,128)(2,1)S(1)}, bf16[512,128]{1,0:T(8,128)(2,1)S(1)}, u32[]{:S(2)}, u32[]{:S(2)}) collective-permute-start(bf16[512,128]{1,0:T(8,128)(2,1)S(1)} %get-tuple-element.54.refs_2_), channel_id=1, source_target_pairs={{0,1},{1,0},{2,3},{3,2},{4,5},{5,4},{6,7},{7,6},{8,9},{9,8},{10,11... | collective-permute-start | bytes 393224 | tf_op jit(solution)/shard_map/ppermute | solution.py:515
  23.6 6.4 %collective-permute-start.12 = (bf16[512,128]{1,0:T(8,128)(2,1)S(1)}, bf16[512,128]{1,0:T(8,128)(2,1)S(1)}, u32[]{:S(2)}, u32[]{:S(2)}) collective-permute-start(bf16[512,128]{1,0:T(8,128)(2,1)S(1)} %get-tuple-element.53), channel_id=1, source_target_pairs={{0,2},{1,3},{2,0},{3,1},{4,6},{5,7},{6,4},{7,5},{8,10},{9,11},{10,... | collective-permute-start | bytes 393224 | tf_op jit(solution)/shard_map/ppermute | solution.py:515
  30.5 5.2 %collective-permute-start.13 = (bf16[128,512]{1,0:T(8,128)(2,1)S(1)}, bf16[128,512]{1,0:T(8,128)(2,1)S(1)}, u32[]{:S(2)}, u32[]{:S(2)}) collective-permute-start(bf16[128,512]{1,0:T(8,128)(2,1)S(1)} %get-tuple-element.55.piece), channel_id=1, source_target_pairs={{0,2},{2,0},{1,3},{3,1},{4,6},{6,4},{5,7},{7,5},{8,10},{10,8},{9,1... | collective-permute-start | bytes 393224 | tf_op jit(solution)/shard_map/ppermute | solution.py:550
  32.3 4.3 %collective-permute-start.15 = (bf16[128,256]{1,0:T(8,128)(2,1)S(1)}, bf16[128,256]{1,0:T(8,128)(2,1)S(1)}, u32[]{:S(2)}, u32[]{:S(2)}) collective-permute-start(bf16[128,256]{1,0:T(8,128)(2,1)S(1)} %weight_term.1.a), channel_id=1, source_target_pairs={{0,8},{4,12},{8,0},{12,4},{16,24},{20,28},{24,16},{28,20},{1,9},{5... | collective-permute-start | bytes 196616 | tf_op jit(solution)/shard_map/ppermute | solution.py:505
  36.6 2.8 %collective-permute-start.16 = (bf16[3,128,512]{2,1,0:T(8,128)(2,1)S(1)}, bf16[3,128,512]{2,1,0:T(8,128)(2,1)S(1)}, u32[]{:S(2)}, u32[]{:S(2)}) collective-permute-start(bf16[3,128,512]{2,1,0:T(8,128)(2,1)S(1)} %hold.3), channel_id=1, source_target_pairs={{0,4},{4,0},{8,12},{12,8},{16,20},{20,16},{24,28},{28,24},{1,5},{5... | collective-permute-start | bytes 1179656 | tf_op jit(solution)/shard_map/ppermute | solution.py:502
  36.7 7.3 %collective-permute-start.20 = (bf16[128,256]{1,0:T(8,128)(2,1)S(1)}, bf16[128,256]{1,0:T(8,128)(2,1)S(1)}, u32[]{:S(2)}, u32[]{:S(2)}) collective-permute-start(bf16[128,256]{1,0:T(8,128)(2,1)S(1)} %add.9.refs_1_.a), channel_id=1, source_target_pairs={{0,24},{4,28},{8,16},{12,20},{16,8},{20,12},{24,0},{28,4},{1,25},{... | collective-permute-start | bytes 196616 | tf_op jit(solution)/shard_map/ppermute | solution.py:505
  39.2 11.1 %collective-permute-start.14 = (bf16[128,512]{1,0:T(8,128)(2,1)S(1)}, bf16[128,512]{1,0:T(8,128)(2,1)S(1)}, u32[]{:S(2)}, u32[]{:S(2)}) collective-permute-start(bf16[128,512]{1,0:T(8,128)(2,1)S(1)} %get-tuple-element.60), channel_id=1, source_target_pairs={{0,4},{4,0},{8,12},{12,8},{16,20},{20,16},{24,28},{28,24},{1,5},{5... | collective-permute-start | bytes 393224 | tf_op jit(solution)/shard_map/ppermute | solution.py:502
  39.5 10.9 %collective-permute-start.17 = (bf16[128,512]{1,0:T(8,128)(2,1)S(1)}, bf16[128,512]{1,0:T(8,128)(2,1)S(1)}, u32[]{:S(2)}, u32[]{:S(2)}) collective-permute-start(bf16[128,512]{1,0:T(8,128)(2,1)S(1)} %get-tuple-element.66), channel_id=1, source_target_pairs={{0,16},{4,20},{8,24},{12,28},{16,0},{20,4},{24,8},{28,12},{1,17},{... | collective-permute-start | bytes 393224 | tf_op jit(solution)/shard_map/ppermute | solution.py:505
  39.6 10.8 %collective-permute-start.18 = (bf16[128,512]{1,0:T(8,128)(2,1)S(1)}, bf16[128,512]{1,0:T(8,128)(2,1)S(1)}, u32[]{:S(2)}, u32[]{:S(2)}) collective-permute-start(bf16[128,512]{1,0:T(8,128)(2,1)S(1)} %get-tuple-element.67.rest_0_), channel_id=1, source_target_pairs={{0,8},{4,12},{8,0},{12,4},{16,24},{20,28},{24,16},{28,20},{1,9},{5... | collective-permute-start | bytes 393224 | tf_op jit(solution)/shard_map/ppermute | solution.py:505
  41.6 10.0 %collective-permute-start.19 = (bf16[128,512]{1,0:T(8,128)(2,1)S(1)}, bf16[128,512]{1,0:T(8,128)(2,1)S(1)}, u32[]{:S(2)}, u32[]{:S(2)}) collective-permute-start(bf16[128,512]{1,0:T(8,128)(2,1)S(1)} %get-tuple-element.68), channel_id=1, source_target_pairs={{0,24},{4,28},{8,16},{12,20},{16,8},{20,12},{24,0},{28,4},{1,25},{... | collective-permute-start | bytes 393224 | tf_op jit(solution)/shard_map/ppermute | solution.py:505
  44.0 4.3 %collective-permute-start = (bf16[128,256]{1,0:T(8,128)(2,1)S(1)}, bf16[128,256]{1,0:T(8,128)(2,1)S(1)}, u32[]{:S(2)}, u32[]{:S(2)}) collective-permute-start(bf16[128,256]{1,0:T(8,128)(2,1)S(1)} %get-tuple-element.101.a), channel_id=1, source_target_pairs={{0,2},{2,0},{1,3},{3,1},{4,6},{6,4},{5,7},{7,5},{8,10},{10,8},{9,1... | collective-permute-start | bytes 196616 | tf_op jit(solution)/shard_map/while/body/ppermute | solution.py:568
  48.4 1.3 %collective-permute-start.1 = (bf16[128,256]{1,0:T(8,128)(2,1)S(1)}, bf16[128,256]{1,0:T(8,128)(2,1)S(1)}, u32[]{:S(2)}, u32[]{:S(2)}) collective-permute-start(bf16[128,256]{1,0:T(8,128)(2,1)S(1)} %add.11.a), channel_id=1, source_target_pairs={{0,4},{4,0},{8,12},{12,8},{16,20},{20,16},{24,28},{28,24},{1,5},{5... | collective-permute-start | bytes 196616 | tf_op jit(solution)/shard_map/while/body/ppermute | solution.py:502

commit v11 on v10

--- a/solution.py
+++ b/solution.py
@@ -521,8 +521,8 @@
     if 2 * n_z * n_col * (blocks * tile) ** 2 <= 8 * MIB:
         dense = densify(*cell)
         totals = forward(dense, [0, 1], [features, sibling(features)], (), False)
-        *held, cot_other = hold([same[-1]] + same[1:-1] + [cot_other], totals[0])
-        same = held[1:] + held[:1]
+        *held, cot_other = hold(same[:0:-1] + [cot_other], totals[0])
+        same = held[::-1]
         cross = [sibling(v) for v in same]
         totals = forward(dense, [2 * s for s in range(1, n_z)], same, totals, False)
         parts = forward(dense, [2 * s + 1 for s in range(1, n_z)], cross, totals, True)

time: 53 us -> 53.1 us (level)
  Pallas kernels: 10.7 us -> 11.4 us
  waiting for transfers between devices: 17.5 us -> 16.8 us
    ppermute x8, waiting for transfers between devices: 5.39 us -> 4.72 us  [along_z(): return lax.ppermute(v, 'row', [(i, i ^ 2 * s) for i in range(n_row)])]
    pallas_call x1, Pallas kernels: 4.24 us -> 4.91 us  [densify(): pl.pallas_call(functools.partial(densify_kernel, (n_z, n_col, blocks), gr...]
  transfers between devices with their start and end apart: 21 -> 21, of which waited for: 10 -> 9; matrix products, arithmetic and copies ran while one was open for 1% -> 1% of each run, Pallas kernels for 16% -> 17%
where the time goes in v11:
time: 53.1 us; the launch traced here: 52.5 us
  starting transfers between devices  22.2 us (42%)
  waiting for transfers between devices  16.8 us (32%)
  Pallas kernels  11.4 us (21%)
  between operations  1.45 us (3%)
  other arithmetic  0.67 us (1%)
    ppermute x8, starting transfers between devices, along_z(): return lax.ppermute(v, 'row', [(i, i ^ 2 * s) for i in range(n_row)])  12.4 us
    ppermute x3, waiting for transfers between devices, to_group(): return lax.ppermute(v, ('col', 'feat'), pairs)  5.87 us
    pallas_call x1, Pallas kernels, densify(): pl.pallas_call(functools.partial(densify_kernel, (n_z, n_col, blocks), gr...  4.91 us
    ppermute x8, waiting for transfers between devices, along_z(): return lax.ppermute(v, 'row', [(i, i ^ 2 * s) for i in range(n_row)])  4.72 us
    ppermute x3, starting transfers between devices, to_group(): return lax.ppermute(v, ('col', 'feat'), pairs)  3.55 us
    ppermute x1, waiting for transfers between devices, finish(): v = add(v, lax.ppermute(v, 'col', pairs))  2.72 us
    pallas_call x3, Pallas kernels, forward(): pl.pallas_call(functools.partial(forward_kernel, places, last), out_shape...  2.66 us
    ppermute x1, waiting for transfers between devices, shards(): lax.ppermute(spread, 'col', [(i, (i + t) % n_col) for i in range(n_col)])  1.96 us
  transfers between devices with their start and end apart: 21, of which 9 were waited for; matrix products, arithmetic and copies ran while one was open for 1% of the time, Pallas kernels for 17%

profile of v11, /device:TPU:0, one launch (start us, length us, event | category | flops | bytes accessed | tf_op | source)
XLA Modules:
  0.0 52.5 jit_solution(16002417969329655078)
XLA Ops:
  0.6 0.5 collective-permute-start.6
  1.1 4.7 %collective-permute-start.2 = (bf16[512,128]{1,0:T(8,128)(2,1)}, bf16[512,128]{1,0:T(8,128)(2,1)S(1)}, u32[]{:S(2)}, u32[]{:S(2)}) collective-permute-start(bf16[512,128]{1,0:T(8,128)(2,1)} %refs_0_.1), channel_id=1, source_target_pairs={{0,24},{4,28},{8,16},{12,20},{16,8},{20,12},{24,0},{28,4},{1,25},{... | collective-permute-start | bytes 393224 | tf_op jit(solution)/shard_map/ppermute | solution.py:505
  5.8 0.0 collective-permute-start.3
  5.8 0.7 %collective-permute-start.4 = (bf16[512,128]{1,0:T(8,128)(2,1)}, bf16[512,128]{1,0:T(8,128)(2,1)S(1)}, u32[]{:S(2)}, u32[]{:S(2)}) collective-permute-start(bf16[512,128]{1,0:T(8,128)(2,1)} %refs_0_.1), channel_id=1, source_target_pairs={{0,8},{4,12},{8,0},{12,4},{16,24},{20,28},{24,16},{28,20},{1,9},{5... | collective-permute-start | bytes 393224 | tf_op jit(solution)/shard_map/ppermute | solution.py:505
  6.5 1.6 %collective-permute-start.5 = (bf16[512,128]{1,0:T(8,128)(2,1)}, bf16[512,128]{1,0:T(8,128)(2,1)S(1)}, u32[]{:S(2)}, u32[]{:S(2)}) collective-permute-start(bf16[512,128]{1,0:T(8,128)(2,1)} %cot_own.1), channel_id=1, source_target_pairs={{0,1},{1,0},{2,3},{3,2},{4,5},{5,4},{6,7},{7,6},{8,9},{9,8},{10,11... | collective-permute-start | bytes 393224 | tf_op jit(solution)/shard_map/ppermute | solution.py:508
  8.8 0.0 copy-start
  8.8 4.9 %densify.1.dense = bf16[8,2,512,512]{3,2,1,0:T(8,128)(2,1)S(1)} custom-call(s32[1,1,256]{2,1,0:T(1,128)} %rows.1, s32[1,1,256]{2,1,0:T(1,128)} %cols.1, s32[1,1]{1,0:T(1,128)S(6)} %copy.27.count, bf16[256,128,128]{2,1,0:T(8,128)(2,1)} %bitcast.1), custom_call_target="tpu_custom_call" | custom-call | flops 1 | bytes 1 | tf_op jit(solution)/shard_map/densify/pallas_call | solution.py:93
  13.7 0.0 collective-permute-done.6.refs_1_
  13.7 0.0 copy-done
  13.7 0.7 %forward.3 = (f32[512,128]{1,0:T(8,128)S(1)}, f32[512,128]{1,0:T(8,128)S(1)}) custom-call(bf16[8,2,512,512]{3,2,1,0:T(8,128)(2,1)S(1)} %densify.1.dense, bf16[512,128]{1,0:T(8,128)(2,1)S(1)} %copy-done, bf16[512,128]{1,0:T(8,128)(2,1)S(1)} %collective-permute-done.6.refs_1_), custom_call_target="tpu_custom_call" | custom-call | flops 1 | bytes 1 | tf_op jit(solution)/shard_map/forward/pallas_call | solution.py:150
  14.4 0.0 collective-permute-done.2.refs_0_
  14.4 3.3 %collective-permute-done.3.refs_1_ = bf16[512,128]{1,0:T(8,128)(2,1)S(1)} collective-permute-done((bf16[512,128]{1,0:T(8,128)(2,1)}, bf16[512,128]{1,0:T(8,128)(2,1)S(1)}, u32[]{:S(2)}, u32[]{:S(2)}) %collective-permute-start.3) | collective-permute-done | bytes 131104 | tf_op jit(solution)/shard_map/ppermute | solution.py:505
  17.7 0.0 collective-permute-done.4.refs_2_
  17.7 0.0 collective-permute-done.5.refs_3_
  17.7 0.1 collective-permute-start.7
  17.8 0.5 collective-permute-start.8
  18.3 0.1 collective-permute-start.9
  18.4 0.0 copy-start.1
  18.4 0.0 copy-start.2
  18.4 1.0 %forward.4 = (f32[512,128]{1,0:T(8,128)S(1)}, f32[512,128]{1,0:T(8,128)S(1)}) custom-call(bf16[8,2,512,512]{3,2,1,0:T(8,128)(2,1)S(1)} %densify.1.dense, bf16[512,128]{1,0:T(8,128)(2,1)S(1)} %get-tuple-element.47.refs_0_, bf16[512,128]{1,0:T(8,128)(2,1)S(1)} %get-tuple-element.48.refs_1_, bf16[512,128]{1,0:T(8,128)(2,1)S(1)} %get-tuple-element.49.refs_2_, ...), custom_call_target="tpu_custom_call" | custom-call | flops 1 | bytes 1 | tf_op jit(solution)/shard_map/forward/pallas_call | solution.py:150
  19.4 0.0 collective-permute-done.7.refs_0_
  19.4 0.0 collective-permute-done.8.refs_1_
  19.4 0.3 collective-permute-done.9.refs_2_
  19.6 1.0 %forward.5 = (bf16[512,128]{1,0:T(8,128)(2,1)S(1)}, bf16[512,128]{1,0:T(8,128)(2,1)S(1)}) custom-call(bf16[8,2,512,512]{3,2,1,0:T(8,128)(2,1)S(1)} %densify.1.dense, bf16[512,128]{1,0:T(8,128)(2,1)S(1)} %collective-permute-done.7.refs_0_, bf16[512,128]{1,0:T(8,128)(2,1)S(1)} %collective-permute-done.8.refs_1_, ...), custom_call_target="tpu_custom_call" | custom-call | flops 1 | bytes 1 | tf_op jit(solution)/shard_map/forward/pallas_call | solution.py:150
  20.6 2.5 %collective-permute-start.10 = (bf16[512,128]{1,0:T(8,128)(2,1)S(1)}, bf16[512,128]{1,0:T(8,128)(2,1)S(1)}, u32[]{:S(2)}, u32[]{:S(2)}) collective-permute-start(bf16[512,128]{1,0:T(8,128)(2,1)S(1)} %get-tuple-element.53), channel_id=1, source_target_pairs={{0,3},{1,2},{2,1},{3,0},{4,7},{5,6},{6,5},{7,4},{8,11},{9,10},{10,... | collective-permute-start | bytes 393224 | tf_op jit(solution)/shard_map/ppermute | solution.py:515
  23.2 0.5 %collective-permute-start.11 = (bf16[512,128]{1,0:T(8,128)(2,1)S(1)}, bf16[512,128]{1,0:T(8,128)(2,1)S(1)}, u32[]{:S(2)}, u32[]{:S(2)}) collective-permute-start(bf16[512,128]{1,0:T(8,128)(2,1)S(1)} %get-tuple-element.54.refs_2_), channel_id=1, source_target_pairs={{0,1},{1,0},{2,3},{3,2},{4,5},{5,4},{6,7},{7,6},{8,9},{9,8},{10,11... | collective-permute-start | bytes 393224 | tf_op jit(solution)/shard_map/ppermute | solution.py:515
  23.7 0.5 collective-permute-start.12
  24.2 3.7 %collective-permute-done.10.refs_0_ = bf16[512,128]{1,0:T(8,128)(2,1)S(1)} collective-permute-done((bf16[512,128]{1,0:T(8,128)(2,1)S(1)}, bf16[512,128]{1,0:T(8,128)(2,1)S(1)}, u32[]{:S(2)}, u32[]{:S(2)}) %collective-permute-start.10) | collective-permute-done | bytes 131104 | tf_op jit(solution)/shard_map/ppermute | solution.py:515
  27.9 2.1 %collective-permute-done.11.refs_1_ = bf16[512,128]{1,0:T(8,128)(2,1)S(1)} collective-permute-done((bf16[512,128]{1,0:T(8,128)(2,1)S(1)}, bf16[512,128]{1,0:T(8,128)(2,1)S(1)}, u32[]{:S(2)}, u32[]{:S(2)}) %collective-permute-start.11) | collective-permute-done | bytes 131104 | tf_op jit(solution)/shard_map/ppermute | solution.py:515
  30.1 0.0 collective-permute-done.12.refs_3_
  30.1 0.0 copy-done.1
  30.1 0.0 copy-done.2
  30.1 0.5 middle.1
  30.5 1.5 %collective-permute-start.13 = (bf16[128,512]{1,0:T(8,128)(2,1)S(1)}, bf16[128,512]{1,0:T(8,128)(2,1)S(1)}, u32[]{:S(2)}, u32[]{:S(2)}) collective-permute-start(bf16[128,512]{1,0:T(8,128)(2,1)S(1)} %get-tuple-element.55.piece), channel_id=1, source_target_pairs={{0,2},{2,0},{1,3},{3,1},{4,6},{6,4},{5,7},{7,5},{8,10},{10,8},{9,1... | collective-permute-start | bytes 393224 | tf_op jit(solution)/shard_map/ppermute | solution.py:550
  32.1 0.3 weight_term.1.a
  32.3 0.1 collective-permute-start.15
  32.4 1.4 %backward_own.1 = (f32[8,128,512]{2,1,0:T(8,128)S(1)}, bf16[512,128]{1,0:T(8,128)(2,1)}) custom-call(bf16[8,2,512,512]{3,2,1,0:T(8,128)(2,1)S(1)} %densify.1.dense, bf16[128,512]{1,0:T(8,128)(2,1)S(1)} %get-tuple-element.55.piece, f32[512,128]{1,0:T(8,128)S(1)} %get-tuple-element.56.hidden), custom_call_target="tpu_custom_call" | custom-call | flops 1 | bytes 1 | tf_op jit(solution)/shard_map/backward_own/pallas_call | solution.py:173
  33.8 2.0 %collective-permute-done.13.refs_0_ = bf16[128,512]{1,0:T(8,128)(2,1)S(1)} collective-permute-done((bf16[128,512]{1,0:T(8,128)(2,1)S(1)}, bf16[128,512]{1,0:T(8,128)(2,1)S(1)}, u32[]{:S(2)}, u32[]{:S(2)}) %collective-permute-start.13) | collective-permute-done | bytes 131104 | tf_op jit(solution)/shard_map/ppermute | solution.py:550
  35.7 0.7 %backward.1 = (bf16[128,512]{1,0:T(8,128)(2,1)S(1)}, bf16[128,512]{1,0:T(8,128)(2,1)S(1)}, bf16[3,128,512]{2,1,0:T(8,128)(2,1)S(1)}, bf16[3,128,512]{2,1,0:T(8,128)(2,1)S(1)}) custom-call(bf16[8,2,512,512]{3,2,1,0:T(8,128)(2,1)S(1)} %densify.1.dense, f32[8,128,512]{2,1,0:T(8,128)S(1)} %get-tuple-element.58.own, ...), custom_call_target="tpu_custom_call" | custom-call | flops 1 | bytes 1 | tf_op jit(solution)/shard_map/backward/pallas_call | solution.py:202
  36.5 0.2 collective-permute-done.15.b
  36.7 0.1 collective-permute-start.16
  36.8 2.5 %collective-permute-start.20 = (bf16[128,256]{1,0:T(8,128)(2,1)S(1)}, bf16[128,256]{1,0:T(8,128)(2,1)S(1)}, u32[]{:S(2)}, u32[]{:S(2)}) collective-permute-start(bf16[128,256]{1,0:T(8,128)(2,1)S(1)} %add.9.refs_1_.a), channel_id=1, source_target_pairs={{0,24},{4,28},{8,16},{12,20},{16,8},{20,12},{24,0},{28,4},{1,25},{... | collective-permute-start | bytes 196616 | tf_op jit(solution)/shard_map/ppermute | solution.py:505
  39.3 0.2 collective-permute-start.14
  39.5 0.0 collective-permute-done.16.arrived
  39.5 0.1 pair_sums.1
  39.6 0.1 collective-permute-start.17
  39.7 2.0 %collective-permute-start.18 = (bf16[128,512]{1,0:T(8,128)(2,1)S(1)}, bf16[128,512]{1,0:T(8,128)(2,1)S(1)}, u32[]{:S(2)}, u32[]{:S(2)}) collective-permute-start(bf16[128,512]{1,0:T(8,128)(2,1)S(1)} %get-tuple-element.67.rest_0_), channel_id=1, source_target_pairs={{0,8},{4,12},{8,0},{12,4},{16,24},{20,28},{24,16},{28,20},{1,9},{5... | collective-permute-start | bytes 393224 | tf_op jit(solution)/shard_map/ppermute | solution.py:505
  41.7 2.3 %collective-permute-start.19 = (bf16[128,512]{1,0:T(8,128)(2,1)S(1)}, bf16[128,512]{1,0:T(8,128)(2,1)S(1)}, u32[]{:S(2)}, u32[]{:S(2)}) collective-permute-start(bf16[128,512]{1,0:T(8,128)(2,1)S(1)} %get-tuple-element.68), channel_id=1, source_target_pairs={{0,24},{4,28},{8,16},{12,20},{16,8},{20,12},{24,0},{28,4},{1,25},{... | collective-permute-start | bytes 393224 | tf_op jit(solution)/shard_map/ppermute | solution.py:505
  44.0 0.0 collective-permute-done.20.b
  44.1 5.7 %while.10 = (s32[]{:T(128)}, bf16[128,256]{1,0:T(8,128)(2,1)S(1)}, s32[]{:T(128)}, s32[]{:T(128)}) while((s32[]{:T(128)}, bf16[128,256]{1,0:T(8,128)(2,1)S(1)}, s32[]{:T(128)}, s32[]{:T(128)}) %tuple.22), condition=%wide.region_1.0_spmd, body=%wide.region_0.0_spmd.sunk | while | flops 4 | bytes 524423 | solution.py:572
  44.1 1.6 %collective-permute-start = (bf16[128,256]{1,0:T(8,128)(2,1)S(1)}, bf16[128,256]{1,0:T(8,128)(2,1)S(1)}, u32[]{:S(2)}, u32[]{:S(2)}) collective-permute-start(bf16[128,256]{1,0:T(8,128)(2,1)S(1)} %get-tuple-element.101.a), channel_id=1, source_target_pairs={{0,2},{2,0},{1,3},{3,1},{4,6},{6,4},{5,7},{7,5},{8,10},{10,8},{9,1... | collective-permute-start | bytes 196616 | tf_op jit(solution)/shard_map/while/body/ppermute | solution.py:568
  45.7 2.7 %collective-permute-done.b = bf16[128,256]{1,0:T(8,128)(2,1)S(1)} collective-permute-done((bf16[128,256]{1,0:T(8,128)(2,1)S(1)}, bf16[128,256]{1,0:T(8,128)(2,1)S(1)}, u32[]{:S(2)}, u32[]{:S(2)}) %collective-permute-start) | collective-permute-done | bytes 65568 | tf_op jit(solution)/shard_map/while/body/ppermute | solution.py:568
  48.4 0.1 collective-permute-start.1
  48.5 1.2 %collective-permute-done.1.b = bf16[128,256]{1,0:T(8,128)(2,1)S(1)} collective-permute-done((bf16[128,256]{1,0:T(8,128)(2,1)S(1)}, bf16[128,256]{1,0:T(8,128)(2,1)S(1)}, u32[]{:S(2)}, u32[]{:S(2)}) %collective-permute-start.1) | collective-permute-done | bytes 65568 | tf_op jit(solution)/shard_map/while/body/ppermute | solution.py:502
  49.8 0.7 %convert_multiply_fusion = f32[128,256]{1,0:T(8,128)} fusion(bf16[128,256]{1,0:T(8,128)(2,1)S(1)} %get-tuple-element.69), kind=kLoop, calls=%fused_computation | loop fusion | flops 65536 | bytes 196608 | tf_op jit(solution)/shard_map/mul | solution.py:573
  50.4 0.0 collective-permute-done.14.refs_1_
  50.4 0.0 collective-permute-done.17.refs_2_
  50.4 0.0 collective-permute-done.18.refs_3_
  50.5 1.2 %collective-permute-done.19.refs_4_ = bf16[128,512]{1,0:T(8,128)(2,1)S(1)} collective-permute-done((bf16[128,512]{1,0:T(8,128)(2,1)S(1)}, bf16[128,512]{1,0:T(8,128)(2,1)S(1)}, u32[]{:S(2)}, u32[]{:S(2)}) %collective-permute-start.19) | collective-permute-done | bytes 131104 | tf_op jit(solution)/shard_map/ppermute | solution.py:505
  51.7 0.8 %turned_sum.1 = bf16[512,128]{1,0:T(8,128)(2,1)} custom-call(bf16[128,512]{1,0:T(8,128)(2,1)S(1)} %get-tuple-element.59.refs_0_, bf16[128,512]{1,0:T(8,128)(2,1)S(1)} %collective-permute-done.14.refs_1_, bf16[128,512]{1,0:T(8,128)(2,1)S(1)} %collective-permute-done.17.refs_2_, bf16[128,512]{1,0:T(8,128)(2,1)S(1)} %collective-permute-done.18.refs_3_, ...), custom_call_target="tpu_custom_call" | custom-call | flops 1 | bytes 1 | tf_op jit(solution)/shard_map/turned_sum/pallas_call | solution.py:482
  (6 shorter events, 0.1 us)
Async XLA Ops:
  0.6 13.0 %collective-permute-start.6 = (bf16[512,128]{1,0:T(8,128)(2,1)}, bf16[512,128]{1,0:T(8,128)(2,1)S(1)}, u32[]{:S(2)}, u32[]{:S(2)}) collective-permute-start(bf16[512,128]{1,0:T(8,128)(2,1)} %refs_0_.1), channel_id=1, source_target_pairs={{0,4},{4,0},{8,12},{12,8},{16,20},{20,16},{24,28},{28,24},{1,5},{5... | collective-permute-start | bytes 393224 | tf_op jit(solution)/shard_map/ppermute | solution.py:502
  1.1 13.3 %collective-permute-start.2 = (bf16[512,128]{1,0:T(8,128)(2,1)}, bf16[512,128]{1,0:T(8,128)(2,1)S(1)}, u32[]{:S(2)}, u32[]{:S(2)}) collective-permute-start(bf16[512,128]{1,0:T(8,128)(2,1)} %refs_0_.1), channel_id=1, source_target_pairs={{0,24},{4,28},{8,16},{12,20},{16,8},{20,12},{24,0},{28,4},{1,25},{... | collective-permute-start | bytes 393224 | tf_op jit(solution)/shard_map/ppermute | solution.py:505
  5.8 11.9 %collective-permute-start.3 = (bf16[512,128]{1,0:T(8,128)(2,1)}, bf16[512,128]{1,0:T(8,128)(2,1)S(1)}, u32[]{:S(2)}, u32[]{:S(2)}) collective-permute-start(bf16[512,128]{1,0:T(8,128)(2,1)} %refs_0_.1), channel_id=1, source_target_pairs={{0,16},{4,20},{8,24},{12,28},{16,0},{20,4},{24,8},{28,12},{1,17},{... | collective-permute-start | bytes 393224 | tf_op jit(solution)/shard_map/ppermute | solution.py:505
  5.8 11.9 %collective-permute-start.4 = (bf16[512,128]{1,0:T(8,128)(2,1)}, bf16[512,128]{1,0:T(8,128)(2,1)S(1)}, u32[]{:S(2)}, u32[]{:S(2)}) collective-permute-start(bf16[512,128]{1,0:T(8,128)(2,1)} %refs_0_.1), channel_id=1, source_target_pairs={{0,8},{4,12},{8,0},{12,4},{16,24},{20,28},{24,16},{28,20},{1,9},{5... | collective-permute-start | bytes 393224 | tf_op jit(solution)/shard_map/ppermute | solution.py:505
  6.5 11.2 %collective-permute-start.5 = (bf16[512,128]{1,0:T(8,128)(2,1)}, bf16[512,128]{1,0:T(8,128)(2,1)S(1)}, u32[]{:S(2)}, u32[]{:S(2)}) collective-permute-start(bf16[512,128]{1,0:T(8,128)(2,1)} %cot_own.1), channel_id=1, source_target_pairs={{0,1},{1,0},{2,3},{3,2},{4,5},{5,4},{6,7},{7,6},{8,9},{9,8},{10,11... | collective-permute-start | bytes 393224 | tf_op jit(solution)/shard_map/ppermute | solution.py:508
  8.8 4.9 %copy-start = (bf16[512,128]{1,0:T(8,128)(2,1)S(1)}, bf16[512,128]{1,0:T(8,128)(2,1)}, u32[]{:S(2)}) copy-start(bf16[512,128]{1,0:T(8,128)(2,1)} %refs_0_.1) | copy-start | bytes 393220
  17.7 1.6 %collective-permute-start.7 = (bf16[512,128]{1,0:T(8,128)(2,1)S(1)}, bf16[512,128]{1,0:T(8,128)(2,1)S(1)}, u32[]{:S(2)}, u32[]{:S(2)}) collective-permute-start(bf16[512,128]{1,0:T(8,128)(2,1)S(1)} %get-tuple-element.47.refs_0_), channel_id=1, source_target_pairs={{0,4},{4,0},{8,12},{12,8},{16,20},{20,16},{24,28},{28,24},{1,5},{5... | collective-permute-start | bytes 393224 | tf_op jit(solution)/shard_map/ppermute | solution.py:502
  17.8 1.6 %collective-permute-start.8 = (bf16[512,128]{1,0:T(8,128)(2,1)S(1)}, bf16[512,128]{1,0:T(8,128)(2,1)S(1)}, u32[]{:S(2)}, u32[]{:S(2)}) collective-permute-start(bf16[512,128]{1,0:T(8,128)(2,1)S(1)} %get-tuple-element.48.refs_1_), channel_id=1, source_target_pairs={{0,4},{4,0},{8,12},{12,8},{16,20},{20,16},{24,28},{28,24},{1,5},{5... | collective-permute-start | bytes 393224 | tf_op jit(solution)/shard_map/ppermute | solution.py:502
  18.3 1.3 %collective-permute-start.9 = (bf16[512,128]{1,0:T(8,128)(2,1)S(1)}, bf16[512,128]{1,0:T(8,128)(2,1)S(1)}, u32[]{:S(2)}, u32[]{:S(2)}) collective-permute-start(bf16[512,128]{1,0:T(8,128)(2,1)S(1)} %get-tuple-element.49.refs_2_), channel_id=1, source_target_pairs={{0,4},{4,0},{8,12},{12,8},{16,20},{20,16},{24,28},{28,24},{1,5},{5... | collective-permute-start | bytes 393224 | tf_op jit(solution)/shard_map/ppermute | solution.py:502
  18.4 11.7 %copy-start.1 = (bf16[256,256]{1,0:T(8,128)(2,1)S(1)}, bf16[256,256]{1,0:T(8,128)(2,1)}, u32[]{:S(2)}) copy-start(bf16[256,256]{1,0:T(8,128)(2,1)} %weights.1) | copy-start | bytes 393220
  18.4 11.7 %copy-start.2 = (bf16[512,128]{1,0:T(8,128)(2,1)S(1)}, bf16[512,128]{1,0:T(8,128)(2,1)}, u32[]{:S(2)}) copy-start(bf16[512,128]{1,0:T(8,128)(2,1)} %cot_own.1) | copy-start | bytes 393220
  20.6 7.3 %collective-permute-start.10 = (bf16[512,128]{1,0:T(8,128)(2,1)S(1)}, bf16[512,128]{1,0:T(8,128)(2,1)S(1)}, u32[]{:S(2)}, u32[]{:S(2)}) collective-permute-start(bf16[512,128]{1,0:T(8,128)(2,1)S(1)} %get-tuple-element.53), channel_id=1, source_target_pairs={{0,3},{1,2},{2,1},{3,0},{4,7},{5,6},{6,5},{7,4},{8,11},{9,10},{10,... | collective-permute-start | bytes 393224 | tf_op jit(solution)/shard_map/ppermute | solution.py:515
  23.2 6.9 %collective-permute-start.11 = (bf16[512,128]{1,0:T(8,128)(2,1)S(1)}, bf16[512,128]{1,0:T(8,128)(2,1)S(1)}, u32[]{:S(2)}, u32[]{:S(2)}) collective-permute-start(bf16[512,128]{1,0:T(8,128)(2,1)S(1)} %get-tuple-element.54.refs_2_), channel_id=1, source_target_pairs={{0,1},{1,0},{2,3},{3,2},{4,5},{5,4},{6,7},{7,6},{8,9},{9,8},{10,11... | collective-permute-start | bytes 393224 | tf_op jit(solution)/shard_map/ppermute | solution.py:515
  23.7 6.4 %collective-permute-start.12 = (bf16[512,128]{1,0:T(8,128)(2,1)S(1)}, bf16[512,128]{1,0:T(8,128)(2,1)S(1)}, u32[]{:S(2)}, u32[]{:S(2)}) collective-permute-start(bf16[512,128]{1,0:T(8,128)(2,1)S(1)} %get-tuple-element.53), channel_id=1, source_target_pairs={{0,2},{1,3},{2,0},{3,1},{4,6},{5,7},{6,4},{7,5},{8,10},{9,11},{10,... | collective-permute-start | bytes 393224 | tf_op jit(solution)/shard_map/ppermute | solution.py:515
  30.5 5.2 %collective-permute-start.13 = (bf16[128,512]{1,0:T(8,128)(2,1)S(1)}, bf16[128,512]{1,0:T(8,128)(2,1)S(1)}, u32[]{:S(2)}, u32[]{:S(2)}) collective-permute-start(bf16[128,512]{1,0:T(8,128)(2,1)S(1)} %get-tuple-element.55.piece), channel_id=1, source_target_pairs={{0,2},{2,0},{1,3},{3,1},{4,6},{6,4},{5,7},{7,5},{8,10},{10,8},{9,1... | collective-permute-start | bytes 393224 | tf_op jit(solution)/shard_map/ppermute | solution.py:550
  32.3 4.3 %collective-permute-start.15 = (bf16[128,256]{1,0:T(8,128)(2,1)S(1)}, bf16[128,256]{1,0:T(8,128)(2,1)S(1)}, u32[]{:S(2)}, u32[]{:S(2)}) collective-permute-start(bf16[128,256]{1,0:T(8,128)(2,1)S(1)} %weight_term.1.a), channel_id=1, source_target_pairs={{0,8},{4,12},{8,0},{12,4},{16,24},{20,28},{24,16},{28,20},{1,9},{5... | collective-permute-start | bytes 196616 | tf_op jit(solution)/shard_map/ppermute | solution.py:505
  36.7 2.8 %collective-permute-start.16 = (bf16[3,128,512]{2,1,0:T(8,128)(2,1)S(1)}, bf16[3,128,512]{2,1,0:T(8,128)(2,1)S(1)}, u32[]{:S(2)}, u32[]{:S(2)}) collective-permute-start(bf16[3,128,512]{2,1,0:T(8,128)(2,1)S(1)} %hold.3), channel_id=1, source_target_pairs={{0,4},{4,0},{8,12},{12,8},{16,20},{20,16},{24,28},{28,24},{1,5},{5... | collective-permute-start | bytes 1179656 | tf_op jit(solution)/shard_map/ppermute | solution.py:502
  36.8 7.3 %collective-permute-start.20 = (bf16[128,256]{1,0:T(8,128)(2,1)S(1)}, bf16[128,256]{1,0:T(8,128)(2,1)S(1)}, u32[]{:S(2)}, u32[]{:S(2)}) collective-permute-start(bf16[128,256]{1,0:T(8,128)(2,1)S(1)} %add.9.refs_1_.a), channel_id=1, source_target_pairs={{0,24},{4,28},{8,16},{12,20},{16,8},{20,12},{24,0},{28,4},{1,25},{... | collective-permute-start | bytes 196616 | tf_op jit(solution)/shard_map/ppermute | solution.py:505
  39.3 11.1 %collective-permute-start.14 = (bf16[128,512]{1,0:T(8,128)(2,1)S(1)}, bf16[128,512]{1,0:T(8,128)(2,1)S(1)}, u32[]{:S(2)}, u32[]{:S(2)}) collective-permute-start(bf16[128,512]{1,0:T(8,128)(2,1)S(1)} %get-tuple-element.60), channel_id=1, source_target_pairs={{0,4},{4,0},{8,12},{12,8},{16,20},{20,16},{24,28},{28,24},{1,5},{5... | collective-permute-start | bytes 393224 | tf_op jit(solution)/shard_map/ppermute | solution.py:502
  39.6 10.9 %collective-permute-start.17 = (bf16[128,512]{1,0:T(8,128)(2,1)S(1)}, bf16[128,512]{1,0:T(8,128)(2,1)S(1)}, u32[]{:S(2)}, u32[]{:S(2)}) collective-permute-start(bf16[128,512]{1,0:T(8,128)(2,1)S(1)} %get-tuple-element.66), channel_id=1, source_target_pairs={{0,16},{4,20},{8,24},{12,28},{16,0},{20,4},{24,8},{28,12},{1,17},{... | collective-permute-start | bytes 393224 | tf_op jit(solution)/shard_map/ppermute | solution.py:505
  39.7 10.8 %collective-permute-start.18 = (bf16[128,512]{1,0:T(8,128)(2,1)S(1)}, bf16[128,512]{1,0:T(8,128)(2,1)S(1)}, u32[]{:S(2)}, u32[]{:S(2)}) collective-permute-start(bf16[128,512]{1,0:T(8,128)(2,1)S(1)} %get-tuple-element.67.rest_0_), channel_id=1, source_target_pairs={{0,8},{4,12},{8,0},{12,4},{16,24},{20,28},{24,16},{28,20},{1,9},{5... | collective-permute-start | bytes 393224 | tf_op jit(solution)/shard_map/ppermute | solution.py:505
  41.7 10.0 %collective-permute-start.19 = (bf16[128,512]{1,0:T(8,128)(2,1)S(1)}, bf16[128,512]{1,0:T(8,128)(2,1)S(1)}, u32[]{:S(2)}, u32[]{:S(2)}) collective-permute-start(bf16[128,512]{1,0:T(8,128)(2,1)S(1)} %get-tuple-element.68), channel_id=1, source_target_pairs={{0,24},{4,28},{8,16},{12,20},{16,8},{20,12},{24,0},{28,4},{1,25},{... | collective-permute-start | bytes 393224 | tf_op jit(solution)/shard_map/ppermute | solution.py:505
  44.1 4.3 %collective-permute-start = (bf16[128,256]{1,0:T(8,128)(2,1)S(1)}, bf16[128,256]{1,0:T(8,128)(2,1)S(1)}, u32[]{:S(2)}, u32[]{:S(2)}) collective-permute-start(bf16[128,256]{1,0:T(8,128)(2,1)S(1)} %get-tuple-element.101.a), channel_id=1, source_target_pairs={{0,2},{2,0},{1,3},{3,1},{4,6},{6,4},{5,7},{7,5},{8,10},{10,8},{9,1... | collective-permute-start | bytes 196616 | tf_op jit(solution)/shard_map/while/body/ppermute | solution.py:568
  48.4 1.3 %collective-permute-start.1 = (bf16[128,256]{1,0:T(8,128)(2,1)S(1)}, bf16[128,256]{1,0:T(8,128)(2,1)S(1)}, u32[]{:S(2)}, u32[]{:S(2)}) collective-permute-start(bf16[128,256]{1,0:T(8,128)(2,1)S(1)} %add.11.a), channel_id=1, source_target_pairs={{0,4},{4,0},{8,12},{12,8},{16,20},{20,16},{24,28},{28,24},{1,5},{5... | collective-permute-start | bytes 196616 | tf_op jit(solution)/shard_map/while/body/ppermute | solution.py:502
